TPU v7x, 32 devices: a whole 2x2x4 slice. The times are simulated.
32 devices in a mesh: ctx: 4 (over z), exp: 8 (over y, x, core).
Axes of the slice: x: 2, y: 2, z: 4, core: 2. Of those that a mesh axis runs over, the one named last changes fastest.
Arguments:
- queries: bfloat16 [1024, 4096], P('ctx', 'exp'), may hold values from -6 to 6
- keys: bfloat16 [1024, 256], P('ctx'), may hold values from -6 to 6
- values: bfloat16 [1024, 256], P('ctx'), may hold values from -6 to 6
- attn_out: bfloat16 [1024, 4096], P('ctx', 'exp'), may hold values from -0.59765625 to 0.59765625
- attn_out_grad: bfloat16 [1024, 4096], P('ctx', 'exp'), may hold values from -6 to 6
- lse_excess: float32 [32, 1024], P('exp', 'ctx'), may hold values from 1 to 2.5
- block_mask: int32 [4, 4], replicated, may hold values from 0 to 1, as said below
- expert_ids: int32 [1024, 8], P('exp'), may hold values from 0 to 15, all different within a row; in each aligned block of 128 rows (0 to 127, 128 to 255, ...) at most 65 rows name the same one
- route_probs: bfloat16 [1024, 8], P('exp'), may hold values from 0.019897461 to 0.5
- moe_grad: bfloat16 [1024, 4096], P('exp'), may hold values from -6 to 6
- shadow_list: int32 [16], replicated, may hold values from -1 to 7, as said below
- stored_hidden_state: bfloat16 [8, 3, 8, 65, 1536], P('exp', None, None, None, 'ctx'), may hold values from -6 to 6
Outputs:
- query_grad: bfloat16 [1024, 4096], P('ctx', 'exp')
- key_grad: bfloat16 [1024, 256], P(('ctx', 'exp'))
- value_grad: bfloat16 [1024, 256], P(('ctx', 'exp'))
- expert_grad: float32 [16, 1536, 4096], P('exp', 'ctx')
Inputs may be any that keep to these rules, and one draw needn't show every extreme that they name: block_mask[i, j] is 1 on the diagonal and 0 above it. `expert_ids`: each token names 8 different experts; among the tokens of one exp index no expert is named more than 65 times, a bound that some block reaches. `shadow_list`: every exp index holds the shadow of exactly one expert, never of one it owns, and exactly one of the 2 experts of each exp index has a shadow.
All inputs are finite; a program needn't handle non-finite values.
Results may differ from a plain program's by a relative error of at most 0.015.
Values may be sent and summed in bfloat16 or wider, within the bound.
No kernel may reach another device: no remote copies, remote signals or barrier semaphores. Data moves between devices by JAX's collectives and lax.ppermute only.
A program may use at most 192 MiB of HBM per device.

v0:
```python
import functools
import math

import jax
import jax.numpy as jnp
from jax import lax
from jax.experimental import pallas as pl
from jax.experimental.pallas import tpu as pltpu
from jax.sharding import PartitionSpec as P

LAST = (((1,), (1,)), ((), ()))
FIRST = (((0,), (0,)), ((), ()))


def full(shape):
    return pl.BlockSpec(shape, lambda *at: (0,) * len(shape))


def attention_kernel(
    place_ref, mask_ref, query_ref, grad_ref, out_ref, lse_ref, *rest
):
    cycle = mask_ref.shape[0]
    pair_refs, query_grad_ref, term_refs = rest[:cycle], rest[cycle], rest[cycle + 1 : -3]
    sums_ref, pairs_ref, terms_ref = rest[-3:]
    rows, width = pairs_ref.shape[1], pairs_ref.shape[2] // 2
    heads = lse_ref.shape[0]
    scale = 1.0 / math.sqrt(width)
    mine = place_ref[0]
    offset = 0.5 * math.log(rows) + lse_ref[...]
    spans = [slice(h * width, (h + 1) * width) for h in range(heads)]
    for step, pair_ref in enumerate(pair_refs):
        pairs_ref[step] = pair_ref[...]
    delta = []
    for span in spans:
        both = grad_ref[:, span].astype(jnp.float32) * out_ref[:, span].astype(jnp.float32)
        delta.append(jnp.sum(both.T, axis=0, keepdims=True))

    def block(step, diagonal):
        key, value = pairs_ref[step, :, :width], pairs_ref[step, :, width:]
        probs, slopes = [], []
        for h, span in enumerate(spans):
            query, grad = query_ref[:, span], grad_ref[:, span]
            scores = lax.dot_general(key, query, LAST, preferred_element_type=jnp.float32)
            prob = jnp.exp(scores * scale - offset[h : h + 1])
            if diagonal:
                at_key = lax.broadcasted_iota(jnp.int32, (rows, rows), 0)
                at_query = lax.broadcasted_iota(jnp.int32, (rows, rows), 1)
                prob = jnp.where(at_key <= at_query, prob, 0.0)
            prob_grad = lax.dot_general(value, grad, LAST, preferred_element_type=jnp.float32)
            slope = (prob * (prob_grad - delta[h]) * scale).astype(jnp.bfloat16)
            probs.append(prob.astype(jnp.bfloat16))
            slopes.append(slope)
            query_term = lax.dot_general(slope, key, FIRST, preferred_element_type=jnp.float32)
            if diagonal:
                sums_ref[:, span] = query_term
            else:
                sums_ref[:, span] += query_term
        queries = jnp.concatenate([query_ref[:, span] for span in spans], axis=0)
        grads = jnp.concatenate([grad_ref[:, span] for span in spans], axis=0)
        key_term = jnp.dot(
            jnp.concatenate(slopes, axis=1), queries, preferred_element_type=jnp.float32
        )
        value_term = jnp.dot(
            jnp.concatenate(probs, axis=1), grads, preferred_element_type=jnp.float32
        )
        terms_ref[step, :, :width] = key_term.astype(jnp.bfloat16)
        terms_ref[step, :, width:] = value_term.astype(jnp.bfloat16)

    block(0, True)

    @pl.loop(1, cycle)
    def _(step):
        source = mine - step
        seen = jnp.logical_and(source >= 0, mask_ref[mine, jnp.maximum(source, 0)] > 0)

        @pl.when(seen)
        def _():
            block(step, False)

        @pl.when(jnp.logical_not(seen))
        def _():
            terms_ref[step] = jnp.zeros_like(terms_ref[step])

    for step, term_ref in enumerate(term_refs):
        term_ref[...] = terms_ref[step]
    query_grad_ref[...] = sums_ref[...].astype(jnp.bfloat16)


def attention(queries, keys, values, attn_out, attn_out_grad, lse_excess, block_mask):
    rows = queries.shape[0]
    heads = lse_excess.shape[0]
    width = queries.shape[1] // heads
    cycle = lax.axis_size("ctx")
    mine = lax.axis_index("ctx")
    owners = lax.axis_size("exp")
    kv_count = keys.shape[1] // width
    kv_head = lax.axis_index("exp") * kv_count // owners
    pair = jnp.concatenate(
        [
            lax.dynamic_slice_in_dim(keys, kv_head * width, width, 1),
            lax.dynamic_slice_in_dim(values, kv_head * width, width, 1),
        ],
        axis=1,
    )
    arrived = [pair] + [
        lax.ppermute(pair, "ctx", [(c, c + step) for c in range(cycle - step)])
        for step in range(1, cycle)
    ]
    operands = (queries, attn_out_grad, attn_out, lse_excess, *arrived)
    query_grad, *terms = pl.pallas_call(
        attention_kernel,
        out_shape=[jax.ShapeDtypeStruct(queries.shape, jnp.bfloat16)]
        + [jax.ShapeDtypeStruct(pair.shape, jnp.bfloat16)] * cycle,
        grid_spec=pltpu.PrefetchScalarGridSpec(
            num_scalar_prefetch=2,
            grid=(1,),
            in_specs=[full(operand.shape) for operand in operands],
            out_specs=[full(queries.shape)] + [full(pair.shape)] * cycle,
            scratch_shapes=[
                pltpu.VMEM(queries.shape, jnp.float32),
                pltpu.VMEM((cycle,) + pair.shape, jnp.bfloat16),
                pltpu.VMEM((cycle,) + pair.shape, jnp.bfloat16),
            ],
        ),
        compiler_params=pltpu.CompilerParams(vmem_limit_bytes=32 * 2**20),
        name="attention",
    )(mine.astype(jnp.int32)[None], block_mask, *operands)
    return query_grad, terms, arrived


def sum_kernel(parts_ref, key_ref, value_ref):
    owners, rows, columns = parts_ref.shape
    kv_count = key_ref.shape[1] * 2 // columns
    group = owners // kv_count
    width = columns // 2
    for k in range(kv_count):
        total = jnp.zeros((rows, columns), jnp.float32)
        for e in range(k * group, (k + 1) * group):
            total += parts_ref[e].astype(jnp.float32)
        key_ref[:, k * width : (k + 1) * width] = total[:, :width].astype(jnp.bfloat16)
        value_ref[:, k * width : (k + 1) * width] = total[:, width:].astype(jnp.bfloat16)


def block_terms(terms):
    cycle = lax.axis_size("ctx")
    total = terms[0].astype(jnp.float32)
    for step in range(1, cycle):
        pairs = [(c, c - step) for c in range(step, cycle)]
        total = total + lax.ppermute(terms[step], "ctx", pairs).astype(jnp.float32)
    return total.astype(jnp.bfloat16)


def summed_terms(total, kv_columns, tiles):
    owners = lax.axis_size("exp")
    rows, columns = total.shape
    parts = lax.all_to_all(
        total.reshape(owners, rows // owners, columns),
        "exp",
        split_axis=0,
        concat_axis=0,
        tiled=True,
    )
    parts, tiles = lax.optimization_barrier((parts, tiles))
    shape = (rows // owners, kv_columns)
    out = jax.ShapeDtypeStruct(shape, jnp.bfloat16)
    key_grad, value_grad = pl.pallas_call(
        sum_kernel,
        out_shape=(out, out),
        grid=(1,),
        in_specs=[full(parts.shape)],
        out_specs=(full(shape), full(shape)),
        compiler_params=pltpu.CompilerParams(vmem_limit_bytes=16 * 2**20),
        name="sums",
    )(parts)
    return key_grad, value_grad, tiles


def pick_kernel(per_dev, shadow_ref, mixed_ref, sent_ref, sems):
    copies = []
    for owner in range(sent_ref.shape[0]):
        host = shadow_ref[owner * per_dev]
        for j in range(1, per_dev):
            host = jnp.maximum(host, shadow_ref[owner * per_dev + j])
        copies.append(
            pltpu.make_async_copy(
                mixed_ref.at[host, pl.ds(0, sent_ref.shape[1])], sent_ref.at[owner], sems.at[owner]
            )
        )
        copies[-1].start()
    for copy in copies:
        copy.wait()


def picked_rows(shadow_list, mixed, limit):
    owners = mixed.shape[0]
    anywhere = pl.BlockSpec(memory_space=pl.ANY)
    return pl.pallas_call(
        functools.partial(pick_kernel, shadow_list.shape[0] // owners),
        out_shape=jax.ShapeDtypeStruct((owners, limit, mixed.shape[2]), jnp.bfloat16),
        grid_spec=pltpu.PrefetchScalarGridSpec(
            num_scalar_prefetch=1,
            grid=(1,),
            in_specs=[anywhere],
            out_specs=anywhere,
            scratch_shapes=[pltpu.SemaphoreType.DMA((owners,))],
        ),
        name="picked",
    )(shadow_list, mixed)


def weight_kernel(orders, own_ref, shadow_ref, mixed_ref, hidden_ref, side_ref, weight_ref):
    owners = mixed_ref.shape[0]
    per_dev, units = hidden_ref.shape[1], hidden_ref.shape[4]
    tokens = weight_ref.shape[1] // owners
    limit = side_ref.shape[1]
    own = own_ref[0]
    earlier = (
        lax.broadcasted_iota(jnp.int32, (tokens, tokens), 0)
        < lax.broadcasted_iota(jnp.int32, (tokens, tokens), 1)
    ).astype(jnp.bfloat16)
    odd = lax.broadcasted_iota(jnp.int32, (1, tokens), 1) % 2 == 1

    def rows_at(named, rows):
        rank = jnp.dot(
            jnp.broadcast_to(named.astype(jnp.float32), (8, tokens)).astype(jnp.bfloat16),
            earlier,
            preferred_element_type=jnp.float32,
        )[:1]
        place = lax.broadcasted_iota(jnp.int32, (rows.shape[0], tokens), 0).astype(jnp.float32)
        chosen = jnp.where(jnp.logical_and(named, rank == place), 1.0, 0.0).astype(jnp.bfloat16)
        return lax.dot_general(rows, chosen, FIRST, preferred_element_type=jnp.float32)

    for i in range(owners):
        source = own ^ jnp.where(own % 2 == 0, orders[0][i], orders[1][i])
        for j in range(per_dev):
            prob = mixed_ref[source, limit + j : limit + j + 1, :tokens].astype(jnp.float32)
            named = prob > 0
            flag = shadow_ref[own * per_dev + j] >= 0
            side = jnp.logical_and(jnp.logical_and(named, odd), flag)
            here = jnp.logical_and(named, jnp.logical_not(side))
            rows = rows_at(here, hidden_ref[0, j, source]) + rows_at(
                side, side_ref[source, :, :units]
            )
            weight_ref[j * units : (j + 1) * units, i * tokens : (i + 1) * tokens] = (
                rows * prob
            ).astype(jnp.bfloat16)


def weighted_rows(own_index, shadow_list, mixed, hidden, shadow_rows, tokens, orders):
    owners = mixed.shape[0]
    per_dev, units = shadow_list.shape[0] // owners, hidden.shape[4]
    shape = (per_dev * units, owners * tokens)
    return pl.pallas_call(
        functools.partial(weight_kernel, orders),
        out_shape=jax.ShapeDtypeStruct(shape, jnp.bfloat16),
        grid_spec=pltpu.PrefetchScalarGridSpec(
            num_scalar_prefetch=2,
            grid=(1,),
            in_specs=[
                full(mixed.shape),
                full((1, per_dev) + hidden.shape[2:]),
                full(shadow_rows.shape),
            ],
            out_specs=full(shape),
        ),
        compiler_params=pltpu.CompilerParams(vmem_limit_bytes=32 * 2**20),
        name="weighted",
    )(own_index.astype(jnp.int32)[None], shadow_list, mixed, hidden, shadow_rows)


def tile_kernel(weight_ref, *refs):
    *block_refs, tile_ref, gathered_ref, held_ref, in_sems, out_sems = refs
    per_dev, units, model = tile_ref.shape
    tokens = block_refs[0].shape[0]
    steps = in_sems.shape[0]
    step = model // steps
    arriving, leaving = [], []
    for i in range(steps):
        columns = pl.ds(i * step, step)
        arriving.append(
            [
                pltpu.make_async_copy(
                    ref.at[:, columns],
                    gathered_ref.at[pl.ds(n * tokens, tokens), columns],
                    in_sems.at[i, n],
                )
                for n, ref in enumerate(block_refs)
            ]
        )
        for copy in arriving[-1]:
            copy.start()
    for i in range(steps):
        for copy in arriving[i]:
            copy.wait()
        columns = slice(i * step, (i + 1) * step)
        held_ref[:, columns] = jnp.dot(
            weight_ref[...], gathered_ref[:, columns], preferred_element_type=jnp.float32
        )
        for j in range(per_dev):
            leaving.append(
                pltpu.make_async_copy(
                    held_ref.at[pl.ds(j * units, units), pl.ds(i * step, step)],
                    tile_ref.at[j, :, pl.ds(i * step, step)],
                    out_sems.at[i, j],
                )
            )
            leaving[-1].start()
    for copy in leaving:
        copy.wait()


def tile_sums(weighted, blocks, per_dev):
    tokens, model = blocks[0].shape
    rows = weighted.shape[0]
    steps = model // 512
    anywhere = pl.BlockSpec(memory_space=pl.ANY)
    return pl.pallas_call(
        tile_kernel,
        out_shape=jax.ShapeDtypeStruct((per_dev, rows // per_dev, model), jnp.float32),
        in_specs=[pl.BlockSpec(memory_space=pltpu.VMEM)] + [anywhere] * len(blocks),
        out_specs=anywhere,
        scratch_shapes=[
            pltpu.VMEM((len(blocks) * tokens, model), jnp.bfloat16),
            pltpu.VMEM((rows, model), jnp.float32),
            pltpu.SemaphoreType.DMA((steps, len(blocks))),
            pltpu.SemaphoreType.DMA((steps, per_dev)),
        ],
        compiler_params=pltpu.CompilerParams(vmem_limit_bytes=32 * 2**20),
        name="tiles",
    )(weighted, *blocks)


def experts(expert_ids, route_probs, shadow_list, stored_hidden_state, first_anchor, near, later):
    owners = lax.axis_size("exp")
    own_index = lax.axis_index("exp")
    swap = functools.partial(
        lax.all_to_all, axis_name="exp", split_axis=0, concat_axis=0, tiled=True
    )
    tokens = expert_ids.shape[0]
    count = shadow_list.shape[0]
    per_dev = count // owners
    capacity, units = stored_hidden_state.shape[3:]
    hit = expert_ids[:, None, :] == jnp.arange(count, dtype=jnp.int32)[None, :, None]
    table = jnp.sum(
        jnp.where(hit, route_probs[:, None, :].astype(jnp.float32), 0.0), axis=2
    ).astype(jnp.bfloat16)
    table = table.T.reshape(owners, per_dev, tokens)
    used = min(capacity, tokens // 2)
    limit = -(-used // 16) * 16
    lanes = max(units, tokens)
    rows = jnp.pad(
        stored_hidden_state[0, per_dev, :, :used],
        ((0, 0), (0, limit - used), (0, lanes - units)),
    )
    mixed = jnp.concatenate([rows, jnp.pad(table, ((0, 0), (0, 0), (0, lanes - tokens)))], axis=1)
    mixed, _ = lax.optimization_barrier((mixed, first_anchor))
    mixed = swap(mixed)
    mixed, near = lax.optimization_barrier((mixed, near))
    shadow_rows = swap(picked_rows(shadow_list, mixed, limit))
    shadow_rows, later = lax.optimization_barrier((shadow_rows, later))
    steps = block_steps(owners)
    orders = [
        [step ^ turn for pair in zip(steps[core], steps[1 - core]) for step, turn in zip(pair, (0, 1))]
        for core in range(2)
    ]
    weighted = weighted_rows(
        own_index, shadow_list, mixed, stored_hidden_state, shadow_rows, tokens, orders
    )
    return weighted, near, later


def block_steps(owners):
    masks = [1 << bit for bit in range(1, owners.bit_length() - 1)]
    steps = []
    for core in range(2):
        first, second = masks[1 - core], masks[core]
        held = [0, first, second, first ^ second]
        for mask in masks[2:]:
            held = held + [step ^ mask for step in held]
        steps.append(held)
    return steps


def moved(value, steps):
    owners = lax.axis_size("exp")
    return lax.ppermute(value, "exp", [(e, e ^ steps[e % 2]) for e in range(owners)])


def near_blocks(moe_grad):
    steps = block_steps(lax.axis_size("exp"))
    first = moved(moe_grad, [held[1] for held in steps])
    second = moved(moe_grad, [held[2] for held in steps])
    return first, second, moved(moe_grad, (1, 1))


def expert_tiles(weighted, moe_grad, near, per_dev):
    owners = lax.axis_size("exp")
    steps = block_steps(owners)
    first, second, beside = near
    far = moved(first, [held[2] for held in steps])
    held = [moe_grad, first, second]
    blocks = [moe_grad, beside] + [
        block for part in held[1:] for block in (part, moved(part, (1, 1)))
    ]
    far, _ = lax.optimization_barrier((far, weighted))
    held = held + [far]
    rest = [far]
    for turn in range(len(steps[0]).bit_length() - 3):
        mask = steps[0][4 << turn]
        more = [moved(part, (mask, mask)) for part in held]
        held, rest = held + more, rest + more
    rest = [block for part in rest for block in (part, moved(part, (1, 1)))]
    return tile_sums(weighted, blocks + rest, per_dev)


def local(
    queries,
    keys,
    values,
    attn_out,
    attn_out_grad,
    lse_excess,
    block_mask,
    expert_ids,
    route_probs,
    moe_grad,
    shadow_list,
    stored_hidden_state,
):
    near = near_blocks(moe_grad)
    query_grad, terms, arrived = attention(
        queries, keys, values, attn_out, attn_out_grad, lse_excess, block_mask
    )
    total = block_terms(terms)
    first, second, beside = near
    weighted, (first, second, _), total = experts(
        expert_ids,
        route_probs,
        shadow_list,
        stored_hidden_state,
        arrived[1],
        (first, second, query_grad),
        total,
    )
    per_dev = shadow_list.shape[0] // lax.axis_size("exp")
    tiles = expert_tiles(weighted, moe_grad, (first, second, beside), per_dev)
    key_grad, value_grad, expert_grad = summed_terms(total, keys.shape[1], tiles)
    return (query_grad, key_grad, value_grad, expert_grad)


def solution(mesh):
    placed = (
        P("ctx", "exp"),
        P("ctx", None),
        P("ctx", None),
        P("ctx", "exp"),
        P("ctx", "exp"),
        P("exp", "ctx"),
        P(),
        P("exp", None),
        P("exp", None),
        P("exp", None),
        P(),
        P("exp", None, None, None, "ctx"),
    )
    return jax.shard_map(
        local,
        mesh=mesh,
        in_specs=placed,
        out_specs=(
            P("ctx", "exp"),
            P(("ctx", "exp"), None),
            P(("ctx", "exp"), None),
            P("exp", "ctx", None),
        ),
        check_vma=False,
    )
```

profile of v0, /device:TPU:27, one launch (start us, length us, event | category | flops | bytes accessed | tf_op | source)
XLA Modules:
  0.0 88.1 jit_solution(9132630081562435610)
XLA Ops:
  0.6 1.3 %collective-permute-start.4 = (bf16[128,4096]{1,0:T(8,128)(2,1)}, bf16[128,4096]{1,0:T(8,128)(2,1)}, u32[]{:S(2)}, u32[]{:S(2)}) collective-permute-start(bf16[128,4096]{1,0:T(8,128)(2,1)} %refs_0_.1), channel_id=1, source_target_pairs={{0,2},{1,5},{2,0},{3,7},{4,6},{5,1},{6,4},{7,3},{8,10},{9,13},{10,... | collective-permute-start | bytes 3145736 | tf_op jit(solution)/shard_map/ppermute | solution.py:386
  1.9 0.3 collective-permute-start.3
  2.2 0.9 constant_dynamic-slice_fusion
  3.1 1.3 %collective-permute-start = (bf16[256,256]{1,0:T(8,128)(2,1)S(1)}, bf16[256,256]{1,0:T(8,128)(2,1)S(1)}, u32[]{:S(2)}, u32[]{:S(2)}) collective-permute-start(bf16[256,256]{1,0:T(8,128)(2,1)S(1)} %pad_maximum_fusion.rest_0_), channel_id=1, source_target_pairs={{0,8},{8,16},{16,24},{1,9},{9,17},{17,25},{2,10},{10,18},{18,26},{... | collective-permute-start | bytes 393224 | tf_op jit(solution)/shard_map/ppermute | solution.py:106
  4.4 0.7 convert_element_type.28
  5.1 1.5 %copy.20.hidden_ref = bf16[1,3,8,65,384]{4,3,2,1,0:T(8,128)(2,1)S(1)} copy(bf16[1,3,8,65,384]{4,2,3,1,0:T(8,128)(2,1)} %param.23) | data formatting | bytes 2396160 | tf_op args[11]
  6.6 0.0 copy-start.4
  6.6 0.0 copy-start.5
  6.6 0.0 copy-start.6
  6.6 0.0 copy-start.7
  6.6 0.0 copy-start.8
  6.7 0.8 fusion.1
  7.5 1.7 %collective-permute-done.rest_1_ = bf16[256,256]{1,0:T(8,128)(2,1)S(1)} collective-permute-done((bf16[256,256]{1,0:T(8,128)(2,1)S(1)}, bf16[256,256]{1,0:T(8,128)(2,1)S(1)}, u32[]{:S(2)}, u32[]{:S(2)}) %collective-permute-start) | collective-permute-done | bytes 131104 | tf_op jit(solution)/shard_map/ppermute | solution.py:106
  9.2 6.5 %all-to-all-start = ((bf16[8,66,384]{2,1,0:T(8,128)(2,1)}), bf16[8,66,384]{2,1,0:T(8,128)(2,1)S(1)}, u32[]{:S(2)}, u32[]{:S(2)}) async-start(bf16[8,66,384]{2,1,0:T(8,128)(2,1)} %fusion.1), calls=%async_computation | async-start | bytes 884736 | tf_op jit(solution)/shard_map/all_to_all | solution.py:357
  15.7 1.3 %collective-permute-start.2 = (bf16[256,256]{1,0:T(8,128)(2,1)S(1)}, bf16[256,256]{1,0:T(8,128)(2,1)S(1)}, u32[]{:S(2)}, u32[]{:S(2)}) collective-permute-start(bf16[256,256]{1,0:T(8,128)(2,1)S(1)} %pad_maximum_fusion.rest_0_), channel_id=1, source_target_pairs={{0,24},{1,25},{2,26},{3,27},{4,28},{5,29},{6,30},{7,31}} | collective-permute-start | bytes 393224 | tf_op jit(solution)/shard_map/ppermute | solution.py:106
  17.0 1.3 %collective-permute-start.1 = (bf16[256,256]{1,0:T(8,128)(2,1)S(1)}, bf16[256,256]{1,0:T(8,128)(2,1)S(1)}, u32[]{:S(2)}, u32[]{:S(2)}) collective-permute-start(bf16[256,256]{1,0:T(8,128)(2,1)S(1)} %pad_maximum_fusion.rest_0_), channel_id=1, source_target_pairs={{0,16},{8,24},{1,17},{9,25},{2,18},{10,26},{3,19},{11,27},{4,20},{... | collective-permute-start | bytes 393224 | tf_op jit(solution)/shard_map/ppermute | solution.py:106
  18.3 5.8 %collective-permute-done.2.rest_3_ = bf16[256,256]{1,0:T(8,128)(2,1)S(1)} collective-permute-done((bf16[256,256]{1,0:T(8,128)(2,1)S(1)}, bf16[256,256]{1,0:T(8,128)(2,1)S(1)}, u32[]{:S(2)}, u32[]{:S(2)}) %collective-permute-start.2) | collective-permute-done | bytes 131104 | tf_op jit(solution)/shard_map/ppermute | solution.py:106
  24.1 6.3 %collective-permute-done.1.rest_2_ = bf16[256,256]{1,0:T(8,128)(2,1)S(1)} collective-permute-done((bf16[256,256]{1,0:T(8,128)(2,1)S(1)}, bf16[256,256]{1,0:T(8,128)(2,1)S(1)}, u32[]{:S(2)}, u32[]{:S(2)}) %collective-permute-start.1) | collective-permute-done | bytes 131104 | tf_op jit(solution)/shard_map/ppermute | solution.py:106
  30.5 4.7 %attention.1 = (bf16[256,512]{1,0:T(8,128)(2,1)}, bf16[256,256]{1,0:T(8,128)(2,1)S(1)}, bf16[256,256]{1,0:T(8,128)(2,1)S(1)}, bf16[256,256]{1,0:T(8,128)(2,1)S(1)}, bf16[256,256]{1,0:T(8,128)(2,1)S(1)}) custom-call(s32[1]{0:T(128)} %bitcast.place_ref, s32[4,4]{1,0:T(4,128)S(1)} %copy-done.8, bf16[256,512]{1,0:T(8,128)(2,1)S(1)} %copy-done.4, ...), custom_call_target="tpu_custom_call" | custom-call | tf_op jit(solution)/shard_map/attention/pallas_call | solution.py:110
  35.2 0.7 copy-done.10
  35.8 0.7 copy-done.11
  36.5 0.0 all-to-all-done.mixed_ref
  36.5 0.0 collective-permute-done.4.refs_4_
  36.5 0.0 collective-permute-done.3.refs_2_
  36.5 1.3 %collective-permute-start.11 = (bf16[128,4096]{1,0:T(8,128)(2,1)}, bf16[128,4096]{1,0:T(8,128)(2,1)}, u32[]{:S(2)}, u32[]{:S(2)}) collective-permute-start(bf16[128,4096]{1,0:T(8,128)(2,1)} %collective-permute-done.3.refs_2_), channel_id=1, source_target_pairs={{0,2},{1,5},{2,0},{3,7},{4,6},{5,1},{6,4},{7,3},{8,10},{9,13},{10,... | collective-permute-start | bytes 3145736 | tf_op jit(solution)/shard_map/ppermute | solution.py:386
  37.8 1.3 %collective-permute-start.5 = (bf16[256,256]{1,0:T(8,128)(2,1)}, bf16[256,256]{1,0:T(8,128)(2,1)S(1)}, u32[]{:S(2)}, u32[]{:S(2)}) collective-permute-start(bf16[256,256]{1,0:T(8,128)(2,1)} %copy-done.11), channel_id=1, source_target_pairs={{8,0},{16,8},{24,16},{9,1},{17,9},{25,17},{10,2},{18,10},{26,18},{... | collective-permute-start | bytes 393224 | tf_op jit(solution)/shard_map/ppermute | solution.py:149
  39.1 1.3 %collective-permute-start.6 = (bf16[256,256]{1,0:T(8,128)(2,1)}, bf16[256,256]{1,0:T(8,128)(2,1)S(1)}, u32[]{:S(2)}, u32[]{:S(2)}) collective-permute-start(bf16[256,256]{1,0:T(8,128)(2,1)} %copy-done.10), channel_id=1, source_target_pairs={{16,0},{24,8},{17,1},{25,9},{18,2},{26,10},{19,3},{27,11},{20,4},{... | collective-permute-start | bytes 393224 | tf_op jit(solution)/shard_map/ppermute | solution.py:149
  40.4 1.3 %collective-permute-start.7 = (bf16[256,256]{1,0:T(8,128)(2,1)S(1)}, bf16[256,256]{1,0:T(8,128)(2,1)S(1)}, u32[]{:S(2)}, u32[]{:S(2)}) collective-permute-start(bf16[256,256]{1,0:T(8,128)(2,1)S(1)} %get-tuple-element.26), channel_id=1, source_target_pairs={{24,0},{25,1},{26,2},{27,3},{28,4},{29,5},{30,6},{31,7}} | collective-permute-start | bytes 393224 | tf_op jit(solution)/shard_map/ppermute | solution.py:149
  41.7 13.8 %picked.1 = bf16[8,64,384]{2,1,0:T(8,128)(2,1)} custom-call(s32[16]{0:T(128)} %shadow_ref.3, bf16[8,66,384]{2,1,0:T(8,128)(2,1)} %copy-done), custom_call_target="tpu_custom_call" | custom-call | tf_op jit(solution)/shard_map/picked/pallas_call | solution.py:197
  55.5 0.0 copy-start.1
  55.5 4.4 %all-to-all-start.1 = ((bf16[8,64,384]{2,1,0:T(8,128)(2,1)}), bf16[8,64,384]{2,1,0:T(8,128)(2,1)S(1)}, u32[]{:S(2)}, u32[]{:S(2)}) async-start(bf16[8,64,384]{2,1,0:T(8,128)(2,1)} %picked.1), calls=%async_computation.1 | async-start | bytes 786432 | tf_op jit(solution)/shard_map/all_to_all | solution.py:359
  59.9 0.4 collective-permute-start.8
  60.3 0.0 collective-permute-done.5
  60.3 0.0 collective-permute-done.6
  60.3 0.7 add_convert_fusion
  61.0 0.1 collective-permute-start.9
  61.2 0.4 collective-permute-start.10
  61.5 5.2 %all-to-all-done.1.side_ref = bf16[8,64,384]{2,1,0:T(8,128)(2,1)S(1)} async-done(((bf16[8,64,384]{2,1,0:T(8,128)(2,1)}), bf16[8,64,384]{2,1,0:T(8,128)(2,1)S(1)}, u32[]{:S(2)}, u32[]{:S(2)}) %all-to-all-start.1) | async-done | bytes 393248 | tf_op jit(solution)/shard_map/all_to_all | solution.py:359
  66.7 0.8 copy-done.2
  67.5 1.0 %copy-done.3 = bf16[8,64,384]{2,1,0:T(8,128)(2,1)S(1)} copy-done((bf16[8,64,384]{2,1,0:T(8,128)(2,1)S(1)}, bf16[8,64,384]{2,1,0:T(8,128)(2,1)}, u32[]{:S(2)}) %copy-start.3) | copy-done | bytes 393240
  68.5 2.9 %weighted.1.weight_ref = bf16[768,1024]{1,0:T(8,128)(2,1)S(1)} custom-call(s32[1]{0:T(128)} %bitcast.5.own_ref, s32[16]{0:T(128)S(1)} %copy-done.9, bf16[8,66,384]{2,1,0:T(8,128)(2,1)S(1)} %copy-done.1, bf16[1,3,8,65,384]{4,3,2,1,0:T(8,128)(2,1)S(1)} %copy.20.hidden_ref, bf16[8,64,384]{2,1,0:T(8,128)(2,1)S(1)} %copy-done.3), custom_call_target="tpu_custom_call" | custom-call | tf_op jit(solution)/shard_map/weighted/pallas_call | solution.py:253
  71.4 0.0 collective-permute-done.11.refs_6_
  71.4 0.5 collective-permute-start.12
  71.9 4.4 %all-to-all-start.2 = ((bf16[8,32,256]{2,1,0:T(8,128)(2,1)}), bf16[8,32,256]{2,1,0:T(8,128)(2,1)S(1)}, u32[]{:S(2)}, u32[]{:S(2)}) async-start(bf16[8,32,256]{2,1,0:T(8,128)(2,1)} %bitcast.4), calls=%async_computation.2 | async-start | bytes 262144 | tf_op jit(solution)/shard_map/all_to_all | solution.py:156
  76.3 0.0 collective-permute-done.8.refs_1_
  76.3 0.0 collective-permute-done.9.refs_3_
  76.3 11.1 %tiles.1 = f32[2,384,4096]{2,1,0:T(8,128)} custom-call(bf16[768,1024]{1,0:T(8,128)(2,1)S(1)} %weighted.1.weight_ref, bf16[128,4096]{1,0:T(8,128)(2,1)} %refs_0_.1, bf16[128,4096]{1,0:T(8,128)(2,1)} %collective-permute-done.8.refs_1_, bf16[128,4096]{1,0:T(8,128)(2,1)} %collective-permute-done.3.refs_2_, bf16[128,4096]{1,0:T(8,128)(2,1)} %collective-permute-done.9.refs_3_, ...), custom_call_target="tpu_custom_call" | custom-call | tf_op jit(solution)/shard_map/tiles/pallas_call | solution.py:317
  87.4 0.6 sums.1
  (23 shorter events, 0.1 us)
Async XLA Ops:
  0.6 35.9 %collective-permute-start.4 = (bf16[128,4096]{1,0:T(8,128)(2,1)}, bf16[128,4096]{1,0:T(8,128)(2,1)}, u32[]{:S(2)}, u32[]{:S(2)}) collective-permute-start(bf16[128,4096]{1,0:T(8,128)(2,1)} %refs_0_.1), channel_id=1, source_target_pairs={{0,2},{1,5},{2,0},{3,7},{4,6},{5,1},{6,4},{7,3},{8,10},{9,13},{10,... | collective-permute-start | bytes 3145736 | tf_op jit(solution)/shard_map/ppermute | solution.py:386
  1.9 34.6 %collective-permute-start.3 = (bf16[128,4096]{1,0:T(8,128)(2,1)}, bf16[128,4096]{1,0:T(8,128)(2,1)}, u32[]{:S(2)}, u32[]{:S(2)}) collective-permute-start(bf16[128,4096]{1,0:T(8,128)(2,1)} %refs_0_.1), channel_id=1, source_target_pairs={{0,4},{1,3},{2,6},{3,1},{4,0},{5,7},{6,2},{7,5},{8,12},{9,11},{10,... | collective-permute-start | bytes 3145736 | tf_op jit(solution)/shard_map/ppermute | solution.py:386
  3.1 6.1 %collective-permute-start = (bf16[256,256]{1,0:T(8,128)(2,1)S(1)}, bf16[256,256]{1,0:T(8,128)(2,1)S(1)}, u32[]{:S(2)}, u32[]{:S(2)}) collective-permute-start(bf16[256,256]{1,0:T(8,128)(2,1)S(1)} %pad_maximum_fusion.rest_0_), channel_id=1, source_target_pairs={{0,8},{8,16},{16,24},{1,9},{9,17},{17,25},{2,10},{10,18},{18,26},{... | collective-permute-start | bytes 393224 | tf_op jit(solution)/shard_map/ppermute | solution.py:106
  5.1 1.6 %copy-start.12 = (s32[128,8]{0,1:T(8,128)S(1)}, s32[128,8]{0,1:T(8,128)}, u32[]{:S(2)}) copy-start(s32[128,8]{0,1:T(8,128)} %param.19) | copy-start | bytes 12292
  6.6 23.9 %copy-start.4 = (bf16[256,512]{1,0:T(8,128)(2,1)S(1)}, bf16[256,512]{1,0:T(8,128)(2,1)}, u32[]{:S(2)}) copy-start(bf16[256,512]{1,0:T(8,128)(2,1)} %query_ref.1) | copy-start | bytes 786436
  6.6 23.9 %copy-start.5 = (bf16[256,512]{1,0:T(8,128)(2,1)S(1)}, bf16[256,512]{1,0:T(8,128)(2,1)}, u32[]{:S(2)}) copy-start(bf16[256,512]{1,0:T(8,128)(2,1)} %grad_ref.1) | copy-start | bytes 786436
  6.6 23.9 %copy-start.6 = (bf16[256,512]{1,0:T(8,128)(2,1)S(1)}, bf16[256,512]{1,0:T(8,128)(2,1)}, u32[]{:S(2)}) copy-start(bf16[256,512]{1,0:T(8,128)(2,1)} %out_ref.1) | copy-start | bytes 786436
  6.6 23.9 %copy-start.7 = (f32[4,256]{1,0:T(4,128)S(1)}, f32[4,256]{1,0:T(4,128)}, u32[]{:S(2)}) copy-start(f32[4,256]{1,0:T(4,128)} %lse_ref.1) | copy-start | bytes 12292
  6.6 23.9 %copy-start.8 = (s32[4,4]{1,0:T(4,128)S(1)}, s32[4,4]{1,0:T(4,128)}, u32[]{:S(2)}) copy-start(s32[4,4]{1,0:T(4,128)} %mask_ref.1) | copy-start | bytes 196
  9.2 27.3 %all-to-all-start = ((bf16[8,66,384]{2,1,0:T(8,128)(2,1)}), bf16[8,66,384]{2,1,0:T(8,128)(2,1)S(1)}, u32[]{:S(2)}, u32[]{:S(2)}) async-start(bf16[8,66,384]{2,1,0:T(8,128)(2,1)} %fusion.1), calls=%async_computation | async-start | bytes 884736 | tf_op jit(solution)/shard_map/all_to_all | solution.py:357
  15.7 8.4 %collective-permute-start.2 = (bf16[256,256]{1,0:T(8,128)(2,1)S(1)}, bf16[256,256]{1,0:T(8,128)(2,1)S(1)}, u32[]{:S(2)}, u32[]{:S(2)}) collective-permute-start(bf16[256,256]{1,0:T(8,128)(2,1)S(1)} %pad_maximum_fusion.rest_0_), channel_id=1, source_target_pairs={{0,24},{1,25},{2,26},{3,27},{4,28},{5,29},{6,30},{7,31}} | collective-permute-start | bytes 393224 | tf_op jit(solution)/shard_map/ppermute | solution.py:106
  17.0 13.4 %collective-permute-start.1 = (bf16[256,256]{1,0:T(8,128)(2,1)S(1)}, bf16[256,256]{1,0:T(8,128)(2,1)S(1)}, u32[]{:S(2)}, u32[]{:S(2)}) collective-permute-start(bf16[256,256]{1,0:T(8,128)(2,1)S(1)} %pad_maximum_fusion.rest_0_), channel_id=1, source_target_pairs={{0,16},{8,24},{1,17},{9,25},{2,18},{10,26},{3,19},{11,27},{4,20},{... | collective-permute-start | bytes 393224 | tf_op jit(solution)/shard_map/ppermute | solution.py:106
  35.2 0.7 copy-start.10
  35.8 0.7 copy-start.11
  36.5 31.0 %copy-start.9 = (s32[16]{0:T(128)S(1)}, s32[16]{0:T(128)}, u32[]{:S(2)}) copy-start(s32[16]{0:T(128)} %shadow_ref.3) | copy-start | bytes 196
  36.5 5.2 %copy-start = (bf16[8,66,384]{2,1,0:T(8,128)(2,1)}, bf16[8,66,384]{2,1,0:T(8,128)(2,1)S(1)}, u32[]{:S(2)}) copy-start(bf16[8,66,384]{2,1,0:T(8,128)(2,1)S(1)} %all-to-all-done.mixed_ref) | copy-start | bytes 1216516
  36.5 34.8 %collective-permute-start.11 = (bf16[128,4096]{1,0:T(8,128)(2,1)}, bf16[128,4096]{1,0:T(8,128)(2,1)}, u32[]{:S(2)}, u32[]{:S(2)}) collective-permute-start(bf16[128,4096]{1,0:T(8,128)(2,1)} %collective-permute-done.3.refs_2_), channel_id=1, source_target_pairs={{0,2},{1,5},{2,0},{3,7},{4,6},{5,1},{6,4},{7,3},{8,10},{9,13},{10,... | collective-permute-start | bytes 3145736 | tf_op jit(solution)/shard_map/ppermute | solution.py:386
  37.8 22.5 %collective-permute-start.5 = (bf16[256,256]{1,0:T(8,128)(2,1)}, bf16[256,256]{1,0:T(8,128)(2,1)S(1)}, u32[]{:S(2)}, u32[]{:S(2)}) collective-permute-start(bf16[256,256]{1,0:T(8,128)(2,1)} %copy-done.11), channel_id=1, source_target_pairs={{8,0},{16,8},{24,16},{9,1},{17,9},{25,17},{10,2},{18,10},{26,18},{... | collective-permute-start | bytes 393224 | tf_op jit(solution)/shard_map/ppermute | solution.py:149
  39.1 21.2 %collective-permute-start.6 = (bf16[256,256]{1,0:T(8,128)(2,1)}, bf16[256,256]{1,0:T(8,128)(2,1)S(1)}, u32[]{:S(2)}, u32[]{:S(2)}) collective-permute-start(bf16[256,256]{1,0:T(8,128)(2,1)} %copy-done.10), channel_id=1, source_target_pairs={{16,0},{24,8},{17,1},{25,9},{18,2},{26,10},{19,3},{27,11},{20,4},{... | collective-permute-start | bytes 393224 | tf_op jit(solution)/shard_map/ppermute | solution.py:149
  40.4 19.9 %collective-permute-start.7 = (bf16[256,256]{1,0:T(8,128)(2,1)S(1)}, bf16[256,256]{1,0:T(8,128)(2,1)S(1)}, u32[]{:S(2)}, u32[]{:S(2)}) collective-permute-start(bf16[256,256]{1,0:T(8,128)(2,1)S(1)} %get-tuple-element.26), channel_id=1, source_target_pairs={{24,0},{25,1},{26,2},{27,3},{28,4},{29,5},{30,6},{31,7}} | collective-permute-start | bytes 393224 | tf_op jit(solution)/shard_map/ppermute | solution.py:149
  55.5 12.0 %copy-start.1 = (bf16[8,66,384]{2,1,0:T(8,128)(2,1)S(1)}, bf16[8,66,384]{2,1,0:T(8,128)(2,1)}, u32[]{:S(2)}) copy-start(bf16[8,66,384]{2,1,0:T(8,128)(2,1)} %copy-done) | copy-start | bytes 1216516
  55.5 11.2 %all-to-all-start.1 = ((bf16[8,64,384]{2,1,0:T(8,128)(2,1)}), bf16[8,64,384]{2,1,0:T(8,128)(2,1)S(1)}, u32[]{:S(2)}, u32[]{:S(2)}) async-start(bf16[8,64,384]{2,1,0:T(8,128)(2,1)} %picked.1), calls=%async_computation.1 | async-start | bytes 786432 | tf_op jit(solution)/shard_map/all_to_all | solution.py:359
  59.9 16.4 %collective-permute-start.8 = (bf16[128,4096]{1,0:T(8,128)(2,1)}, bf16[128,4096]{1,0:T(8,128)(2,1)}, u32[]{:S(2)}, u32[]{:S(2)}) collective-permute-start(bf16[128,4096]{1,0:T(8,128)(2,1)} %refs_0_.1), channel_id=1, source_target_pairs={{0,1},{1,0},{2,3},{3,2},{4,5},{5,4},{6,7},{7,6},{8,9},{9,8},{10,11... | collective-permute-start | bytes 3145736 | tf_op jit(solution)/shard_map/ppermute | solution.py:386
  61.0 15.3 %collective-permute-start.9 = (bf16[128,4096]{1,0:T(8,128)(2,1)}, bf16[128,4096]{1,0:T(8,128)(2,1)}, u32[]{:S(2)}, u32[]{:S(2)}) collective-permute-start(bf16[128,4096]{1,0:T(8,128)(2,1)} %collective-permute-done.3.refs_2_), channel_id=1, source_target_pairs={{0,1},{1,0},{2,3},{3,2},{4,5},{5,4},{6,7},{7,6},{8,9},{9,8},{10,11... | collective-permute-start | bytes 3145736 | tf_op jit(solution)/shard_map/ppermute | solution.py:386
  61.2 15.1 %collective-permute-start.10 = (bf16[128,4096]{1,0:T(8,128)(2,1)}, bf16[128,4096]{1,0:T(8,128)(2,1)}, u32[]{:S(2)}, u32[]{:S(2)}) collective-permute-start(bf16[128,4096]{1,0:T(8,128)(2,1)} %collective-permute-done.4.refs_4_), channel_id=1, source_target_pairs={{0,1},{1,0},{2,3},{3,2},{4,5},{5,4},{6,7},{7,6},{8,9},{9,8},{10,11... | collective-permute-start | bytes 3145736 | tf_op jit(solution)/shard_map/ppermute | solution.py:386
  66.7 0.8 copy-start.2
  67.5 1.0 %copy-start.3 = (bf16[8,64,384]{2,1,0:T(8,128)(2,1)S(1)}, bf16[8,64,384]{2,1,0:T(8,128)(2,1)}, u32[]{:S(2)}) copy-start(bf16[8,64,384]{2,1,0:T(8,128)(2,1)} %copy-done.2) | copy-start | bytes 1179652
  71.4 4.9 %collective-permute-start.12 = (bf16[128,4096]{1,0:T(8,128)(2,1)}, bf16[128,4096]{1,0:T(8,128)(2,1)S(1)}, u32[]{:S(2)}, u32[]{:S(2)}) collective-permute-start(bf16[128,4096]{1,0:T(8,128)(2,1)} %collective-permute-done.11.refs_6_), channel_id=1, source_target_pairs={{0,1},{1,0},{2,3},{3,2},{4,5},{5,4},{6,7},{7,6},{8,9},{9,8},{10,11... | collective-permute-start | bytes 3145736 | tf_op jit(solution)/shard_map/ppermute | solution.py:386
  71.9 15.6 %all-to-all-start.2 = ((bf16[8,32,256]{2,1,0:T(8,128)(2,1)}), bf16[8,32,256]{2,1,0:T(8,128)(2,1)S(1)}, u32[]{:S(2)}, u32[]{:S(2)}) async-start(bf16[8,32,256]{2,1,0:T(8,128)(2,1)} %bitcast.4), calls=%async_computation.2 | async-start | bytes 262144 | tf_op jit(solution)/shard_map/all_to_all | solution.py:156
where the time goes:
time: 88.3 us; the launch traced here: 88.1 us
  Pallas kernels  33 us (37%)
  starting transfers between devices  27.3 us (31%)
  waiting for transfers between devices  19.1 us (22%)
  local copies, waits for them, and re-layouts  5.52 us (6%)
  other arithmetic  2.27 us (3%)
    ppermute x3, waiting for transfers between devices, attention(): lax.ppermute(pair, 'ctx', [(c, c + step) for c in range(cycle - step)])  13.8 us
    pallas_call x1, Pallas kernels, picked_rows(): pl.pallas_call(functools.partial(pick_kernel, shadow_list.shape[0] // own...  13.8 us
    pallas_call x1, Pallas kernels, tile_sums(): pl.pallas_call(tile_kernel, out_shape=jax.ShapeDtypeStruct((per_dev, rows...  11.1 us
    all_to_all x1, starting transfers between devices, experts(): mixed = swap(mixed)  6.49 us
    all_to_all x1, waiting for transfers between devices, experts(): shadow_rows = swap(picked_rows(shadow_list, mixed, limit))  5.2 us
    pallas_call x1, Pallas kernels, attention(): pl.pallas_call(attention_kernel, out_shape=[jax.ShapeDtypeStruct(queries....  4.7 us
    unnamed x27, local copies, waits for them, and re-layouts  4.6 us
    all_to_all x1, starting transfers between devices, experts(): shadow_rows = swap(picked_rows(shadow_list, mixed, limit))  4.43 us
  transfers between devices with their start and end apart: 16, of which 4 were waited for; matrix products, arithmetic and copies ran while one was open for 5% of the time, Pallas kernels for 37%

commit v1 on v0

--- a/solution.py
+++ b/solution.py
@@ -20,8 +20,7 @@
     place_ref, mask_ref, query_ref, grad_ref, out_ref, lse_ref, *rest
 ):
     cycle = mask_ref.shape[0]
-    pair_refs, query_grad_ref, term_refs = rest[:cycle], rest[cycle], rest[cycle + 1 : -3]
-    sums_ref, pairs_ref, terms_ref = rest[-3:]
+    pair_refs, (query_grad_ref, terms_ref, sums_ref, pairs_ref) = rest[:cycle], rest[cycle:]
     rows, width = pairs_ref.shape[1], pairs_ref.shape[2] // 2
     heads = lse_ref.shape[0]
     scale = 1.0 / math.sqrt(width)
@@ -63,35 +62,28 @@
         value_term = jnp.dot(
             jnp.concatenate(probs, axis=1), grads, preferred_element_type=jnp.float32
         )
-        terms_ref[step, :, :width] = key_term.astype(jnp.bfloat16)
-        terms_ref[step, :, width:] = value_term.astype(jnp.bfloat16)
+        terms_ref[mine - step, :, :width] = key_term.astype(jnp.bfloat16)
+        terms_ref[mine - step, :, width:] = value_term.astype(jnp.bfloat16)
 
     block(0, True)
 
-    @pl.loop(1, cycle)
-    def _(step):
-        source = mine - step
-        seen = jnp.logical_and(source >= 0, mask_ref[mine, jnp.maximum(source, 0)] > 0)
+    @pl.loop(0, cycle)
+    def _(source):
+        seen = jnp.logical_and(source < mine, mask_ref[mine, source] > 0)
 
         @pl.when(seen)
         def _():
-            block(step, False)
-
-        @pl.when(jnp.logical_not(seen))
+            block(mine - source, False)
+
+        @pl.when(jnp.logical_and(source != mine, jnp.logical_not(seen)))
         def _():
-            terms_ref[step] = jnp.zeros_like(terms_ref[step])
-
-    for step, term_ref in enumerate(term_refs):
-        term_ref[...] = terms_ref[step]
+            terms_ref[source] = jnp.zeros_like(terms_ref[source])
+
     query_grad_ref[...] = sums_ref[...].astype(jnp.bfloat16)
 
 
-def attention(queries, keys, values, attn_out, attn_out_grad, lse_excess, block_mask):
-    rows = queries.shape[0]
-    heads = lse_excess.shape[0]
-    width = queries.shape[1] // heads
+def key_blocks(keys, values, width):
     cycle = lax.axis_size("ctx")
-    mine = lax.axis_index("ctx")
     owners = lax.axis_size("exp")
     kv_count = keys.shape[1] // width
     kv_head = lax.axis_index("exp") * kv_count // owners
@@ -102,64 +94,62 @@
         ],
         axis=1,
     )
-    arrived = [pair] + [
+    return [pair] + [
         lax.ppermute(pair, "ctx", [(c, c + step) for c in range(cycle - step)])
         for step in range(1, cycle)
     ]
+
+
+def attention(queries, arrived, attn_out, attn_out_grad, lse_excess, block_mask):
+    cycle = lax.axis_size("ctx")
+    mine = lax.axis_index("ctx")
+    pair = arrived[0]
     operands = (queries, attn_out_grad, attn_out, lse_excess, *arrived)
-    query_grad, *terms = pl.pallas_call(
+    return pl.pallas_call(
         attention_kernel,
-        out_shape=[jax.ShapeDtypeStruct(queries.shape, jnp.bfloat16)]
-        + [jax.ShapeDtypeStruct(pair.shape, jnp.bfloat16)] * cycle,
+        out_shape=(
+            jax.ShapeDtypeStruct(queries.shape, jnp.bfloat16),
+            jax.ShapeDtypeStruct((cycle,) + pair.shape, jnp.bfloat16),
+        ),
         grid_spec=pltpu.PrefetchScalarGridSpec(
             num_scalar_prefetch=2,
             grid=(1,),
             in_specs=[full(operand.shape) for operand in operands],
-            out_specs=[full(queries.shape)] + [full(pair.shape)] * cycle,
+            out_specs=(full(queries.shape), full((cycle,) + pair.shape)),
             scratch_shapes=[
                 pltpu.VMEM(queries.shape, jnp.float32),
-                pltpu.VMEM((cycle,) + pair.shape, jnp.bfloat16),
                 pltpu.VMEM((cycle,) + pair.shape, jnp.bfloat16),
             ],
         ),
         compiler_params=pltpu.CompilerParams(vmem_limit_bytes=32 * 2**20),
         name="attention",
     )(mine.astype(jnp.int32)[None], block_mask, *operands)
-    return query_grad, terms, arrived
 
 
 def sum_kernel(parts_ref, key_ref, value_ref):
-    owners, rows, columns = parts_ref.shape
+    cycle, owners, rows, columns = parts_ref.shape
     kv_count = key_ref.shape[1] * 2 // columns
     group = owners // kv_count
     width = columns // 2
     for k in range(kv_count):
         total = jnp.zeros((rows, columns), jnp.float32)
-        for e in range(k * group, (k + 1) * group):
-            total += parts_ref[e].astype(jnp.float32)
+        for c in range(cycle):
+            for e in range(k * group, (k + 1) * group):
+                total += parts_ref[c, e].astype(jnp.float32)
         key_ref[:, k * width : (k + 1) * width] = total[:, :width].astype(jnp.bfloat16)
         value_ref[:, k * width : (k + 1) * width] = total[:, width:].astype(jnp.bfloat16)
 
 
-def block_terms(terms):
-    cycle = lax.axis_size("ctx")
-    total = terms[0].astype(jnp.float32)
-    for step in range(1, cycle):
-        pairs = [(c, c - step) for c in range(step, cycle)]
-        total = total + lax.ppermute(terms[step], "ctx", pairs).astype(jnp.float32)
-    return total.astype(jnp.bfloat16)
-
-
-def summed_terms(total, kv_columns, tiles):
-    owners = lax.axis_size("exp")
-    rows, columns = total.shape
+def summed_terms(terms, kv_columns, tiles):
+    cycle, owners = lax.axis_size("ctx"), lax.axis_size("exp")
+    rows, columns = terms.shape[1:]
     parts = lax.all_to_all(
-        total.reshape(owners, rows // owners, columns),
-        "exp",
+        terms.reshape(cycle * owners, rows // owners, columns),
+        ("ctx", "exp"),
         split_axis=0,
         concat_axis=0,
         tiled=True,
-    )
+    ).reshape(cycle, owners, rows // owners, columns)
     parts, tiles = lax.optimization_barrier((parts, tiles))
     shape = (rows // owners, kv_columns)
     out = jax.ShapeDtypeStruct(shape, jnp.bfloat16)
@@ -175,35 +165,23 @@
     return key_grad, value_grad, tiles
 
 
-def pick_kernel(per_dev, shadow_ref, mixed_ref, sent_ref, sems):
-    copies = []
+def pick_kernel(per_dev, shadow_ref, mixed_ref, sent_ref):
     for owner in range(sent_ref.shape[0]):
         host = shadow_ref[owner * per_dev]
         for j in range(1, per_dev):
             host = jnp.maximum(host, shadow_ref[owner * per_dev + j])
-        copies.append(
-            pltpu.make_async_copy(
-                mixed_ref.at[host, pl.ds(0, sent_ref.shape[1])], sent_ref.at[owner], sems.at[owner]
-            )
-        )
-        copies[-1].start()
-    for copy in copies:
-        copy.wait()
+        sent_ref[owner] = mixed_ref[host, : sent_ref.shape[1]]
 
 
 def picked_rows(shadow_list, mixed, limit):
     owners = mixed.shape[0]
-    anywhere = pl.BlockSpec(memory_space=pl.ANY)
+    whole = pl.BlockSpec(memory_space=pltpu.VMEM)
     return pl.pallas_call(
         functools.partial(pick_kernel, shadow_list.shape[0] // owners),
         out_shape=jax.ShapeDtypeStruct((owners, limit, mixed.shape[2]), jnp.bfloat16),
-        grid_spec=pltpu.PrefetchScalarGridSpec(
-            num_scalar_prefetch=1,
-            grid=(1,),
-            in_specs=[anywhere],
-            out_specs=anywhere,
-            scratch_shapes=[pltpu.SemaphoreType.DMA((owners,))],
-        ),
+        in_specs=[pl.BlockSpec(memory_space=pltpu.SMEM), whole],
+        out_specs=whole,
+        compiler_params=pltpu.CompilerParams(vmem_limit_bytes=4 * 2**20),
         name="picked",
     )(shadow_list, mixed)
 
@@ -287,11 +265,13 @@
                 for n, ref in enumerate(block_refs)
             ]
         )
-        for copy in arriving[-1]:
-            copy.start()
+    for copy in arriving[0] + arriving[1]:
+        copy.start()
     for i in range(steps):
         for copy in arriving[i]:
             copy.wait()
+        for copy in arriving[i + 2] if i + 2 < steps else []:
+            copy.start()
         columns = slice(i * step, (i + 1) * step)
         held_ref[:, columns] = jnp.dot(
             weight_ref[...], gathered_ref[:, columns], preferred_element_type=jnp.float32
@@ -330,12 +310,12 @@
     )(weighted, *blocks)
 
 
-def experts(expert_ids, route_probs, shadow_list, stored_hidden_state, first_anchor, near, later):
+def swapped(value):
+    return lax.all_to_all(value, "exp", split_axis=0, concat_axis=0, tiled=True)
+
+
+def source_rows(expert_ids, route_probs, shadow_list, stored_hidden_state):
     owners = lax.axis_size("exp")
-    own_index = lax.axis_index("exp")
-    swap = functools.partial(
-        lax.all_to_all, axis_name="exp", split_axis=0, concat_axis=0, tiled=True
-    )
     tokens = expert_ids.shape[0]
     count = shadow_list.shape[0]
     per_dev = count // owners
@@ -353,20 +333,20 @@
         ((0, 0), (0, limit - used), (0, lanes - units)),
     )
     mixed = jnp.concatenate([rows, jnp.pad(table, ((0, 0), (0, 0), (0, lanes - tokens)))], axis=1)
-    mixed, _ = lax.optimization_barrier((mixed, first_anchor))
-    mixed = swap(mixed)
-    mixed, near = lax.optimization_barrier((mixed, near))
-    shadow_rows = swap(picked_rows(shadow_list, mixed, limit))
-    shadow_rows, later = lax.optimization_barrier((shadow_rows, later))
-    steps = block_steps(owners)
+    mixed = swapped(mixed)
+    return mixed, picked_rows(shadow_list, mixed, limit)
+
+
+def expert_rows(mixed, shadow_rows, shadow_list, stored_hidden_state, tokens):
+    steps = block_steps(lax.axis_size("exp"))
     orders = [
         [step ^ turn for pair in zip(steps[core], steps[1 - core]) for step, turn in zip(pair, (0, 1))]
         for core in range(2)
     ]
-    weighted = weighted_rows(
+    own_index = lax.axis_index("exp")
+    return weighted_rows(
         own_index, shadow_list, mixed, stored_hidden_state, shadow_rows, tokens, orders
     )
-    return weighted, near, later
 
 
 def block_steps(owners):
@@ -427,24 +407,21 @@
     shadow_list,
     stored_hidden_state,
 ):
-    near = near_blocks(moe_grad)
-    query_grad, terms, arrived = attention(
-        queries, keys, values, attn_out, attn_out_grad, lse_excess, block_mask
-    )
-    total = block_terms(terms)
-    first, second, beside = near
-    weighted, (first, second, _), total = experts(
-        expert_ids,
-        route_probs,
-        shadow_list,
-        stored_hidden_state,
-        arrived[1],
-        (first, second, query_grad),
-        total,
+    first, second, beside = near_blocks(moe_grad)
+    arrived = key_blocks(keys, values, queries.shape[1] // lse_excess.shape[0])
+    mixed, sent = source_rows(expert_ids, route_probs, shadow_list, stored_hidden_state)
+    sent, first, second, arrived = lax.optimization_barrier((sent, first, second, arrived))
+    shadow_rows = swapped(sent)
+    query_grad, terms = attention(
+        queries, arrived, attn_out, attn_out_grad, lse_excess, block_mask
+    )
+    shadow_rows, _ = lax.optimization_barrier((shadow_rows, query_grad))
+    weighted = expert_rows(
+        mixed, shadow_rows, shadow_list, stored_hidden_state, expert_ids.shape[0]
     )
     per_dev = shadow_list.shape[0] // lax.axis_size("exp")
     tiles = expert_tiles(weighted, moe_grad, (first, second, beside), per_dev)
-    key_grad, value_grad, expert_grad = summed_terms(total, keys.shape[1], tiles)
+    key_grad, value_grad, expert_grad = summed_terms(terms, keys.shape[1], tiles)
     return (query_grad, key_grad, value_grad, expert_grad)
 
 

time: 88.3 us -> 80.7 us (0.914)
  the two profiles are of different devices: /device:TPU:27 before, /device:TPU:0 now
where the time goes in v1:
time: 80.7 us; the launch traced here: 80.1 us
  starting transfers between devices  28.6 us (35%)
  waiting for transfers between devices  25.9 us (32%)
  Pallas kernels  19 us (24%)
  local copies, waits for them, and re-layouts  4.11 us (5%)
  other arithmetic  1.54 us (2%)
  between operations  0.9 us (1%)
    all_to_all x2, waiting for transfers between devices, swapped(): return lax.all_to_all(value, 'exp', split_axis=0, concat_axis=0, tiled=True)  21.5 us
    pallas_call x1, Pallas kernels, tile_sums(): pl.pallas_call(tile_kernel, out_shape=jax.ShapeDtypeStruct((per_dev, rows...  11.1 us
    ppermute x3, starting transfers between devices, key_blocks(): lax.ppermute(pair, 'ctx', [(c, c + step) for c in range(cycle - step)])  9.29 us
    ppermute x7, starting transfers between devices, moved(): lax.ppermute(value, 'exp', [(e, e ^ steps[e % 2]) for e in range(owners)])  7.21 us
    all_to_all x2, starting transfers between devices, swapped(): return lax.all_to_all(value, 'exp', split_axis=0, concat_axis=0, tiled=True)  7.07 us
    all_to_all x1, starting transfers between devices, summed_terms(): lax.all_to_all(terms.reshape(cycle * owners, rows // owners, columns), ('...  5.05 us
    all_to_all x1, waiting for transfers between devices, summed_terms(): lax.all_to_all(terms.reshape(cycle * owners, rows // owners, columns), ('...  4.4 us
    unnamed x25, local copies, waits for them, and re-layouts  4.05 us
  transfers between devices with their start and end apart: 13, of which 3 were waited for; matrix products, arithmetic and copies ran while one was open for 4% of the time, Pallas kernels for 23%

profile of v1, /device:TPU:0, one launch (start us, length us, event | category | flops | bytes accessed | tf_op | source)
XLA Modules:
  0.0 80.1 jit_solution(14864629070992857406)
XLA Ops:
  0.6 0.0 copy-start.11
  0.6 3.0 %collective-permute-start.1 = (bf16[128,4096]{1,0:T(8,128)(2,1)}, bf16[128,4096]{1,0:T(8,128)(2,1)}, u32[]{:S(2)}, u32[]{:S(2)}) collective-permute-start(bf16[128,4096]{1,0:T(8,128)(2,1)} %refs_0_.1), channel_id=1, source_target_pairs={{0,2},{1,5},{2,0},{3,7},{4,6},{5,1},{6,4},{7,3},{8,10},{9,13},{10,... | collective-permute-start | bytes 3145736 | tf_op jit(solution)/shard_map/ppermute | solution.py:366
  3.6 1.5 %collective-permute-start = (bf16[128,4096]{1,0:T(8,128)(2,1)}, bf16[128,4096]{1,0:T(8,128)(2,1)}, u32[]{:S(2)}, u32[]{:S(2)}) collective-permute-start(bf16[128,4096]{1,0:T(8,128)(2,1)} %refs_0_.1), channel_id=1, source_target_pairs={{0,4},{1,3},{2,6},{3,1},{4,0},{5,7},{6,2},{7,5},{8,12},{9,11},{10,... | collective-permute-start | bytes 3145736 | tf_op jit(solution)/shard_map/ppermute | solution.py:366
  5.2 0.7 convert_element_type.13
  5.8 1.5 %copy.20.hidden_ref = bf16[1,3,8,65,384]{4,3,2,1,0:T(8,128)(2,1)S(1)} copy(bf16[1,3,8,65,384]{4,2,3,1,0:T(8,128)(2,1)} %param.23) | data formatting | bytes 2396160 | tf_op args[11]
  7.3 0.0 copy-done.11
  7.3 0.0 copy-start.9
  7.3 0.0 copy-start.10
  7.4 0.0 copy-start.8
  7.4 0.8 %fusion.1 = bf16[8,66,384]{2,1,0:T(8,128)(2,1)} fusion(bf16[8,2,128]{2,1,0:T(2,128)(2,1)S(1)} %bitcast.11, bf16[8,64,384]{2,1,0:T(8,128)(2,1)S(1)} %slice_bitcast_fusion), kind=kLoop, calls=%fused_computation.2 | loop fusion | flops 1216512 | bytes 802816 | tf_op jit(solution)/shard_map/concatenate | solution.py:335
  8.2 0.0 copy-start.7
  8.3 3.6 %all-to-all-start = ((bf16[8,66,384]{2,1,0:T(8,128)(2,1)}), bf16[8,66,384]{2,1,0:T(8,128)(2,1)S(1)}, u32[]{:S(2)}, u32[]{:S(2)}) async-start(bf16[8,66,384]{2,1,0:T(8,128)(2,1)} %fusion.1), calls=%async_computation | async-start | bytes 884736 | tf_op jit(solution)/shard_map/all_to_all | solution.py:314
  11.9 0.0 copy-done.9
  11.9 0.0 copy-done.10
  12.0 5.5 %collective-permute-start.4 = (bf16[256,256]{1,0:T(8,128)(2,1)S(1)}, bf16[256,256]{1,0:T(8,128)(2,1)S(1)}, u32[]{:S(2)}, u32[]{:S(2)}) collective-permute-start(bf16[256,256]{1,0:T(8,128)(2,1)S(1)} %pad_maximum_fusion.rest_0_), channel_id=1, source_target_pairs={{0,24},{1,25},{2,26},{3,27},{4,28},{5,29},{6,30},{7,31}} | collective-permute-start | bytes 393224 | tf_op jit(solution)/shard_map/ppermute | solution.py:98
  17.5 1.3 %collective-permute-start.3 = (bf16[256,256]{1,0:T(8,128)(2,1)S(1)}, bf16[256,256]{1,0:T(8,128)(2,1)S(1)}, u32[]{:S(2)}, u32[]{:S(2)}) collective-permute-start(bf16[256,256]{1,0:T(8,128)(2,1)S(1)} %pad_maximum_fusion.rest_0_), channel_id=1, source_target_pairs={{0,16},{8,24},{1,17},{9,25},{2,18},{10,26},{3,19},{11,27},{4,20},{... | collective-permute-start | bytes 393224 | tf_op jit(solution)/shard_map/ppermute | solution.py:98
  18.8 2.5 %collective-permute-start.2 = (bf16[256,256]{1,0:T(8,128)(2,1)S(1)}, bf16[256,256]{1,0:T(8,128)(2,1)S(1)}, u32[]{:S(2)}, u32[]{:S(2)}) collective-permute-start(bf16[256,256]{1,0:T(8,128)(2,1)S(1)} %pad_maximum_fusion.rest_0_), channel_id=1, source_target_pairs={{0,8},{8,16},{16,24},{1,9},{9,17},{17,25},{2,10},{10,18},{18,26},{... | collective-permute-start | bytes 393224 | tf_op jit(solution)/shard_map/ppermute | solution.py:98
  21.3 11.7 %all-to-all-done.mixed_ref = bf16[8,66,384]{2,1,0:T(8,128)(2,1)S(1)} async-done(((bf16[8,66,384]{2,1,0:T(8,128)(2,1)}), bf16[8,66,384]{2,1,0:T(8,128)(2,1)S(1)}, u32[]{:S(2)}, u32[]{:S(2)}) %all-to-all-start) | async-done | bytes 405536 | tf_op jit(solution)/shard_map/all_to_all | solution.py:314
  33.0 0.0 copy-done.8
  33.0 1.3 %picked.1 = bf16[8,64,384]{2,1,0:T(8,128)(2,1)} custom-call(s32[16]{0:T(128)S(1)} %copy-done.8, bf16[8,66,384]{2,1,0:T(8,128)(2,1)S(1)} %all-to-all-done.mixed_ref), custom_call_target="tpu_custom_call" | custom-call | tf_op jit(solution)/shard_map/picked/pallas_call | solution.py:179
  34.4 0.0 collective-permute-done.4.rest_3_
  34.4 0.0 collective-permute-done.3.rest_2_
  34.4 0.0 collective-permute-done.2.rest_1_
  34.4 0.0 collective-permute-done.1.refs_4_
  34.4 0.0 collective-permute-done.refs_2_
  34.4 1.7 %collective-permute-start.8 = (bf16[128,4096]{1,0:T(8,128)(2,1)}, bf16[128,4096]{1,0:T(8,128)(2,1)}, u32[]{:S(2)}, u32[]{:S(2)}) collective-permute-start(bf16[128,4096]{1,0:T(8,128)(2,1)} %collective-permute-done.refs_2_), channel_id=1, source_target_pairs={{0,2},{1,5},{2,0},{3,7},{4,6},{5,1},{6,4},{7,3},{8,10},{9,13},{10,... | collective-permute-start | bytes 3145736 | tf_op jit(solution)/shard_map/ppermute | solution.py:366
  36.1 3.5 %all-to-all-start.2 = ((bf16[8,64,384]{2,1,0:T(8,128)(2,1)}), bf16[8,64,384]{2,1,0:T(8,128)(2,1)S(1)}, u32[]{:S(2)}, u32[]{:S(2)}) async-start(bf16[8,64,384]{2,1,0:T(8,128)(2,1)} %picked.1), calls=%async_computation.2 | async-start | bytes 786432 | tf_op jit(solution)/shard_map/all_to_all | solution.py:314
  39.6 0.4 collective-permute-start.5
  40.0 0.2 collective-permute-start.6
  40.1 0.3 collective-permute-start.7
  40.5 0.0 copy-done.3
  40.5 0.0 copy-done.5
  40.5 3.1 %attention.1 = (bf16[256,512]{1,0:T(8,128)(2,1)}, bf16[4,256,256]{2,1,0:T(8,128)(2,1)S(1)}) custom-call(s32[1]{0:T(128)} %bitcast.place_ref, s32[4,4]{1,0:T(4,128)S(1)} %copy-done.7, bf16[256,512]{1,0:T(8,128)(2,1)S(1)} %copy-done.3, bf16[256,512]{1,0:T(8,128)(2,1)S(1)} %copy-done.4, bf16[256,512]{1,0:T(8,128)(2,1)S(1)} %copy-done.5, ...), custom_call_target="tpu_custom_call" | custom-call | tf_op jit(solution)/shard_map/attention/pallas_call | solution.py:108
  43.6 0.8 %copy-done.2 = bf16[4,256,256]{2,1,0:T(8,128)(2,1)} copy-done((bf16[4,256,256]{2,1,0:T(8,128)(2,1)}, bf16[4,256,256]{2,1,0:T(8,128)(2,1)S(1)}, u32[]{:S(2)}) %copy-start.2) | copy-done | bytes 524312
  44.4 9.8 %all-to-all-done.2.side_ref = bf16[8,64,384]{2,1,0:T(8,128)(2,1)S(1)} async-done(((bf16[8,64,384]{2,1,0:T(8,128)(2,1)}), bf16[8,64,384]{2,1,0:T(8,128)(2,1)S(1)}, u32[]{:S(2)}, u32[]{:S(2)}) %all-to-all-start.2) | async-done | bytes 393248 | tf_op jit(solution)/shard_map/all_to_all | solution.py:314
  54.2 0.7 copy-done
  54.9 1.0 %copy-done.1 = bf16[8,64,384]{2,1,0:T(8,128)(2,1)S(1)} copy-done((bf16[8,64,384]{2,1,0:T(8,128)(2,1)S(1)}, bf16[8,64,384]{2,1,0:T(8,128)(2,1)}, u32[]{:S(2)}) %copy-start.1) | copy-done | bytes 393240
  55.9 2.9 %weighted.1.weight_ref = bf16[768,1024]{1,0:T(8,128)(2,1)S(1)} custom-call(s32[1]{0:T(128)} %bitcast.6.own_ref, s32[16]{0:T(128)S(1)} %copy-done.8, bf16[8,66,384]{2,1,0:T(8,128)(2,1)S(1)} %all-to-all-done.mixed_ref, bf16[1,3,8,65,384]{4,3,2,1,0:T(8,128)(2,1)S(1)} %copy.20.hidden_ref, bf16[8,64,384]{2,1,0:T(8,128)(2,1)S(1)} %copy-done.1), custom_call_target="tpu_custom_call" | custom-call | tf_op jit(solution)/shard_map/weighted/pallas_call | solution.py:231
  58.8 0.0 collective-permute-done.8.refs_6_
  58.8 0.1 collective-permute-start.9
  58.9 5.0 %all-to-all-start.1 = ((bf16[32,32,256]{2,1,0:T(8,128)(2,1)}), bf16[32,32,256]{2,1,0:T(8,128)(2,1)S(1)}, u32[]{:S(2)}, u32[]{:S(2)}) async-start(bf16[32,32,256]{2,1,0:T(8,128)(2,1)} %bitcast.10), calls=%async_computation.1 | async-start | bytes 1048576 | tf_op jit(solution)/shard_map/all_to_all | solution.py:146
  63.9 0.0 collective-permute-done.5.refs_1_
  63.9 0.0 collective-permute-done.7.refs_5_
  63.9 0.0 collective-permute-done.6.refs_3_
  63.9 0.0 collective-permute-done.9.refs_7_
  64.0 11.1 %tiles.1 = f32[2,384,4096]{2,1,0:T(8,128)} custom-call(bf16[768,1024]{1,0:T(8,128)(2,1)S(1)} %weighted.1.weight_ref, bf16[128,4096]{1,0:T(8,128)(2,1)} %refs_0_.1, bf16[128,4096]{1,0:T(8,128)(2,1)} %collective-permute-done.5.refs_1_, bf16[128,4096]{1,0:T(8,128)(2,1)} %collective-permute-done.refs_2_, bf16[128,4096]{1,0:T(8,128)(2,1)} %collective-permute-done.6.refs_3_, ...), custom_call_target="tpu_custom_call" | custom-call | tf_op jit(solution)/shard_map/tiles/pallas_call | solution.py:297
  75.1 4.4 %all-to-all-done.1 = bf16[32,32,256]{2,1,0:T(8,128)(2,1)S(1)} async-done(((bf16[32,32,256]{2,1,0:T(8,128)(2,1)}), bf16[32,32,256]{2,1,0:T(8,128)(2,1)S(1)}, u32[]{:S(2)}, u32[]{:S(2)}) %all-to-all-start.1) | async-done | bytes 524320 | tf_op jit(solution)/shard_map/all_to_all | solution.py:146
  79.5 0.7 sums.1
  (14 shorter events, 0.1 us)
Async XLA Ops:
  0.6 6.7 %copy-start.11 = (s32[128,8]{0,1:T(8,128)S(1)}, s32[128,8]{0,1:T(8,128)}, u32[]{:S(2)}) copy-start(s32[128,8]{0,1:T(8,128)} %param.19) | copy-start | bytes 12292
  0.6 33.7 %collective-permute-start.1 = (bf16[128,4096]{1,0:T(8,128)(2,1)}, bf16[128,4096]{1,0:T(8,128)(2,1)}, u32[]{:S(2)}, u32[]{:S(2)}) collective-permute-start(bf16[128,4096]{1,0:T(8,128)(2,1)} %refs_0_.1), channel_id=1, source_target_pairs={{0,2},{1,5},{2,0},{3,7},{4,6},{5,1},{6,4},{7,3},{8,10},{9,13},{10,... | collective-permute-start | bytes 3145736 | tf_op jit(solution)/shard_map/ppermute | solution.py:366
  3.6 30.8 %collective-permute-start = (bf16[128,4096]{1,0:T(8,128)(2,1)}, bf16[128,4096]{1,0:T(8,128)(2,1)}, u32[]{:S(2)}, u32[]{:S(2)}) collective-permute-start(bf16[128,4096]{1,0:T(8,128)(2,1)} %refs_0_.1), channel_id=1, source_target_pairs={{0,4},{1,3},{2,6},{3,1},{4,0},{5,7},{6,2},{7,5},{8,12},{9,11},{10,... | collective-permute-start | bytes 3145736 | tf_op jit(solution)/shard_map/ppermute | solution.py:366
  7.3 4.6 %copy-start.9 = (bf16[256,256]{1,0:T(8,128)(2,1)S(1)}, bf16[256,256]{1,0:T(8,128)(2,1)}, u32[]{:S(2)}) copy-start(bf16[256,256]{1,0:T(8,128)(2,1)} %param.14) | copy-start | bytes 393220
  7.3 4.6 %copy-start.10 = (bf16[256,256]{1,0:T(8,128)(2,1)S(1)}, bf16[256,256]{1,0:T(8,128)(2,1)}, u32[]{:S(2)}) copy-start(bf16[256,256]{1,0:T(8,128)(2,1)} %param.13) | copy-start | bytes 393220
  7.4 25.6 %copy-start.8 = (s32[16]{0:T(128)S(1)}, s32[16]{0:T(128)}, u32[]{:S(2)}) copy-start(s32[16]{0:T(128)} %shadow_ref.3) | copy-start | bytes 196
  8.2 32.3 %copy-start.3 = (bf16[256,512]{1,0:T(8,128)(2,1)S(1)}, bf16[256,512]{1,0:T(8,128)(2,1)}, u32[]{:S(2)}) copy-start(bf16[256,512]{1,0:T(8,128)(2,1)} %query_ref.1) | copy-start | bytes 786436
  8.2 32.3 %copy-start.4 = (bf16[256,512]{1,0:T(8,128)(2,1)S(1)}, bf16[256,512]{1,0:T(8,128)(2,1)}, u32[]{:S(2)}) copy-start(bf16[256,512]{1,0:T(8,128)(2,1)} %grad_ref.1) | copy-start | bytes 786436
  8.2 32.3 %copy-start.5 = (bf16[256,512]{1,0:T(8,128)(2,1)S(1)}, bf16[256,512]{1,0:T(8,128)(2,1)}, u32[]{:S(2)}) copy-start(bf16[256,512]{1,0:T(8,128)(2,1)} %out_ref.1) | copy-start | bytes 786436
  8.2 32.3 %copy-start.6 = (f32[4,256]{1,0:T(4,128)S(1)}, f32[4,256]{1,0:T(4,128)}, u32[]{:S(2)}) copy-start(f32[4,256]{1,0:T(4,128)} %lse_ref.1) | copy-start | bytes 12292
  8.2 32.3 %copy-start.7 = (s32[4,4]{1,0:T(4,128)S(1)}, s32[4,4]{1,0:T(4,128)}, u32[]{:S(2)}) copy-start(s32[4,4]{1,0:T(4,128)} %mask_ref.1) | copy-start | bytes 196
  8.3 24.8 %all-to-all-start = ((bf16[8,66,384]{2,1,0:T(8,128)(2,1)}), bf16[8,66,384]{2,1,0:T(8,128)(2,1)S(1)}, u32[]{:S(2)}, u32[]{:S(2)}) async-start(bf16[8,66,384]{2,1,0:T(8,128)(2,1)} %fusion.1), calls=%async_computation | async-start | bytes 884736 | tf_op jit(solution)/shard_map/all_to_all | solution.py:314
  12.0 22.4 %collective-permute-start.4 = (bf16[256,256]{1,0:T(8,128)(2,1)S(1)}, bf16[256,256]{1,0:T(8,128)(2,1)S(1)}, u32[]{:S(2)}, u32[]{:S(2)}) collective-permute-start(bf16[256,256]{1,0:T(8,128)(2,1)S(1)} %pad_maximum_fusion.rest_0_), channel_id=1, source_target_pairs={{0,24},{1,25},{2,26},{3,27},{4,28},{5,29},{6,30},{7,31}} | collective-permute-start | bytes 393224 | tf_op jit(solution)/shard_map/ppermute | solution.py:98
  17.5 16.9 %collective-permute-start.3 = (bf16[256,256]{1,0:T(8,128)(2,1)S(1)}, bf16[256,256]{1,0:T(8,128)(2,1)S(1)}, u32[]{:S(2)}, u32[]{:S(2)}) collective-permute-start(bf16[256,256]{1,0:T(8,128)(2,1)S(1)} %pad_maximum_fusion.rest_0_), channel_id=1, source_target_pairs={{0,16},{8,24},{1,17},{9,25},{2,18},{10,26},{3,19},{11,27},{4,20},{... | collective-permute-start | bytes 393224 | tf_op jit(solution)/shard_map/ppermute | solution.py:98
  18.8 15.6 %collective-permute-start.2 = (bf16[256,256]{1,0:T(8,128)(2,1)S(1)}, bf16[256,256]{1,0:T(8,128)(2,1)S(1)}, u32[]{:S(2)}, u32[]{:S(2)}) collective-permute-start(bf16[256,256]{1,0:T(8,128)(2,1)S(1)} %pad_maximum_fusion.rest_0_), channel_id=1, source_target_pairs={{0,8},{8,16},{16,24},{1,9},{9,17},{17,25},{2,10},{10,18},{18,26},{... | collective-permute-start | bytes 393224 | tf_op jit(solution)/shard_map/ppermute | solution.py:98
  34.4 24.4 %collective-permute-start.8 = (bf16[128,4096]{1,0:T(8,128)(2,1)}, bf16[128,4096]{1,0:T(8,128)(2,1)}, u32[]{:S(2)}, u32[]{:S(2)}) collective-permute-start(bf16[128,4096]{1,0:T(8,128)(2,1)} %collective-permute-done.refs_2_), channel_id=1, source_target_pairs={{0,2},{1,5},{2,0},{3,7},{4,6},{5,1},{6,4},{7,3},{8,10},{9,13},{10,... | collective-permute-start | bytes 3145736 | tf_op jit(solution)/shard_map/ppermute | solution.py:366
  36.1 18.1 %all-to-all-start.2 = ((bf16[8,64,384]{2,1,0:T(8,128)(2,1)}), bf16[8,64,384]{2,1,0:T(8,128)(2,1)S(1)}, u32[]{:S(2)}, u32[]{:S(2)}) async-start(bf16[8,64,384]{2,1,0:T(8,128)(2,1)} %picked.1), calls=%async_computation.2 | async-start | bytes 786432 | tf_op jit(solution)/shard_map/all_to_all | solution.py:314
  39.6 24.3 %collective-permute-start.5 = (bf16[128,4096]{1,0:T(8,128)(2,1)}, bf16[128,4096]{1,0:T(8,128)(2,1)}, u32[]{:S(2)}, u32[]{:S(2)}) collective-permute-start(bf16[128,4096]{1,0:T(8,128)(2,1)} %refs_0_.1), channel_id=1, source_target_pairs={{0,1},{1,0},{2,3},{3,2},{4,5},{5,4},{6,7},{7,6},{8,9},{9,8},{10,11... | collective-permute-start | bytes 3145736 | tf_op jit(solution)/shard_map/ppermute | solution.py:366
  40.0 24.0 %collective-permute-start.6 = (bf16[128,4096]{1,0:T(8,128)(2,1)}, bf16[128,4096]{1,0:T(8,128)(2,1)}, u32[]{:S(2)}, u32[]{:S(2)}) collective-permute-start(bf16[128,4096]{1,0:T(8,128)(2,1)} %collective-permute-done.refs_2_), channel_id=1, source_target_pairs={{0,1},{1,0},{2,3},{3,2},{4,5},{5,4},{6,7},{7,6},{8,9},{9,8},{10,11... | collective-permute-start | bytes 3145736 | tf_op jit(solution)/shard_map/ppermute | solution.py:366
  40.1 23.8 %collective-permute-start.7 = (bf16[128,4096]{1,0:T(8,128)(2,1)}, bf16[128,4096]{1,0:T(8,128)(2,1)}, u32[]{:S(2)}, u32[]{:S(2)}) collective-permute-start(bf16[128,4096]{1,0:T(8,128)(2,1)} %collective-permute-done.1.refs_4_), channel_id=1, source_target_pairs={{0,1},{1,0},{2,3},{3,2},{4,5},{5,4},{6,7},{7,6},{8,9},{9,8},{10,11... | collective-permute-start | bytes 3145736 | tf_op jit(solution)/shard_map/ppermute | solution.py:366
  43.6 0.8 %copy-start.2 = (bf16[4,256,256]{2,1,0:T(8,128)(2,1)}, bf16[4,256,256]{2,1,0:T(8,128)(2,1)S(1)}, u32[]{:S(2)}) copy-start(bf16[4,256,256]{2,1,0:T(8,128)(2,1)S(1)} %get-tuple-element.24) | copy-start | bytes 1572868
  54.2 0.7 copy-start
  54.9 1.0 %copy-start.1 = (bf16[8,64,384]{2,1,0:T(8,128)(2,1)S(1)}, bf16[8,64,384]{2,1,0:T(8,128)(2,1)}, u32[]{:S(2)}) copy-start(bf16[8,64,384]{2,1,0:T(8,128)(2,1)} %copy-done) | copy-start | bytes 1179652
  58.8 5.2 %collective-permute-start.9 = (bf16[128,4096]{1,0:T(8,128)(2,1)}, bf16[128,4096]{1,0:T(8,128)(2,1)}, u32[]{:S(2)}, u32[]{:S(2)}) collective-permute-start(bf16[128,4096]{1,0:T(8,128)(2,1)} %collective-permute-done.8.refs_6_), channel_id=1, source_target_pairs={{0,1},{1,0},{2,3},{3,2},{4,5},{5,4},{6,7},{7,6},{8,9},{9,8},{10,11... | collective-permute-start | bytes 3145736 | tf_op jit(solution)/shard_map/ppermute | solution.py:366
  58.9 20.6 %all-to-all-start.1 = ((bf16[32,32,256]{2,1,0:T(8,128)(2,1)}), bf16[32,32,256]{2,1,0:T(8,128)(2,1)S(1)}, u32[]{:S(2)}, u32[]{:S(2)}) async-start(bf16[32,32,256]{2,1,0:T(8,128)(2,1)} %bitcast.10), calls=%async_computation.1 | async-start | bytes 1048576 | tf_op jit(solution)/shard_map/all_to_all | solution.py:146

commit v2 on v1

--- a/solution.py
+++ b/solution.py
@@ -292,7 +292,7 @@
 def tile_sums(weighted, blocks, per_dev):
     tokens, model = blocks[0].shape
     rows = weighted.shape[0]
-    steps = model // 512
+    steps = model // 1024
     anywhere = pl.BlockSpec(memory_space=pl.ANY)
     return pl.pallas_call(
         tile_kernel,
@@ -366,22 +366,12 @@
     return lax.ppermute(value, "exp", [(e, e ^ steps[e % 2]) for e in range(owners)])
 
 
-def near_blocks(moe_grad):
-    steps = block_steps(lax.axis_size("exp"))
-    first = moved(moe_grad, [held[1] for held in steps])
-    second = moved(moe_grad, [held[2] for held in steps])
-    return first, second, moved(moe_grad, (1, 1))
-
-
-def expert_tiles(weighted, moe_grad, near, per_dev):
+def expert_tiles(weighted, near, per_dev):
     owners = lax.axis_size("exp")
     steps = block_steps(owners)
-    first, second, beside = near
-    far = moved(first, [held[2] for held in steps])
-    held = [moe_grad, first, second]
-    blocks = [moe_grad, beside] + [
-        block for part in held[1:] for block in (part, moved(part, (1, 1)))
-    ]
+    far = moved(near[1], [held[2] for held in steps])
+    held = list(near)
+    blocks = [block for part in held for block in (part, moved(part, (1, 1)))]
     far, _ = lax.optimization_barrier((far, weighted))
     held = held + [far]
     rest = [far]
@@ -407,20 +397,24 @@
     shadow_list,
     stored_hidden_state,
 ):
-    first, second, beside = near_blocks(moe_grad)
+    steps = block_steps(lax.axis_size("exp"))
+    first = moved(moe_grad, [held[1] for held in steps])
     arrived = key_blocks(keys, values, queries.shape[1] // lse_excess.shape[0])
     mixed, sent = source_rows(expert_ids, route_probs, shadow_list, stored_hidden_state)
-    sent, first, second, arrived = lax.optimization_barrier((sent, first, second, arrived))
+    moe_grad, _ = lax.optimization_barrier((moe_grad, mixed))
+    second = moved(moe_grad, [held[2] for held in steps])
+    sent, arrived = lax.optimization_barrier((sent, arrived))
     shadow_rows = swapped(sent)
     query_grad, terms = attention(
         queries, arrived, attn_out, attn_out_grad, lse_excess, block_mask
     )
+    first, _ = lax.optimization_barrier((first, query_grad))
     shadow_rows, _ = lax.optimization_barrier((shadow_rows, query_grad))
     weighted = expert_rows(
         mixed, shadow_rows, shadow_list, stored_hidden_state, expert_ids.shape[0]
     )
     per_dev = shadow_list.shape[0] // lax.axis_size("exp")
-    tiles = expert_tiles(weighted, moe_grad, (first, second, beside), per_dev)
+    tiles = expert_tiles(weighted, (moe_grad, first, second), per_dev)
     key_grad, value_grad, expert_grad = summed_terms(terms, keys.shape[1], tiles)
     return (query_grad, key_grad, value_grad, expert_grad)
 

time: 80.7 us -> 86 us (1.066)
  waiting for transfers between devices: 25.9 us -> 29.8 us
  starting transfers between devices: 28.6 us -> 30.5 us
    all_to_all x1, starting transfers between devices: 5.05 us -> 7.47 us  [summed_terms(): lax.all_to_all(terms.reshape(cycle * owners, rows // owners, columns), ('...]
    ppermute x3, waiting for transfers between devices: 0.01 us -> 1.88 us  [key_blocks(): lax.ppermute(pair, 'ctx', [(c, c + step) for c in range(cycle - step)])]
    all_to_all x2, waiting for transfers between devices: 21.5 us -> 23.2 us  [swapped(): return lax.all_to_all(value, 'exp', split_axis=0, concat_axis=0, tiled=True)]
    ppermute x7, starting transfers between devices: 7.21 us -> 6.21 us  [moved(): lax.ppermute(value, 'exp', [(e, e ^ steps[e % 2]) for e in range(owners)])]
  transfers between devices with their start and end apart: 13 -> 13, of which waited for: 3 -> 4; matrix products, arithmetic and copies ran while one was open for 4% -> 4% of each run, Pallas kernels for 23% -> 21%
where the time goes in v2:
time: 86 us; the launch traced here: 85.5 us
  starting transfers between devices  30.5 us (35%)
  waiting for transfers between devices  29.8 us (35%)
  Pallas kernels  18.7 us (22%)
  local copies, waits for them, and re-layouts  4.11 us (5%)
  other arithmetic  1.54 us (2%)
  between operations  0.88 us (1%)
    all_to_all x2, waiting for transfers between devices, swapped(): return lax.all_to_all(value, 'exp', split_axis=0, concat_axis=0, tiled=True)  23.2 us
    pallas_call x1, Pallas kernels, tile_sums(): pl.pallas_call(tile_kernel, out_shape=jax.ShapeDtypeStruct((per_dev, rows...  10.8 us
    ppermute x3, starting transfers between devices, key_blocks(): lax.ppermute(pair, 'ctx', [(c, c + step) for c in range(cycle - step)])  9.29 us
    all_to_all x2, starting transfers between devices, swapped(): return lax.all_to_all(value, 'exp', split_axis=0, concat_axis=0, tiled=True)  7.48 us
    all_to_all x1, starting transfers between devices, summed_terms(): lax.all_to_all(terms.reshape(cycle * owners, rows // owners, columns), ('...  7.47 us
    ppermute x7, starting transfers between devices, moved(): lax.ppermute(value, 'exp', [(e, e ^ steps[e % 2]) for e in range(owners)])  6.21 us
    all_to_all x1, waiting for transfers between devices, summed_terms(): lax.all_to_all(terms.reshape(cycle * owners, rows // owners, columns), ('...  4.72 us
    unnamed x25, local copies, waits for them, and re-layouts  4.05 us
  transfers between devices with their start and end apart: 13, of which 4 were waited for; matrix products, arithmetic and copies ran while one was open for 4% of the time, Pallas kernels for 21%

profile of v2, /device:TPU:0, one launch (start us, length us, event | category | flops | bytes accessed | tf_op | source)
XLA Modules:
  0.0 85.5 jit_solution(16757540943264174467)
XLA Ops:
  0.6 0.0 copy-start.11
  0.6 3.0 %collective-permute-start.4 = (bf16[128,4096]{1,0:T(8,128)(2,1)}, bf16[128,4096]{1,0:T(8,128)(2,1)}, u32[]{:S(2)}, u32[]{:S(2)}) collective-permute-start(bf16[128,4096]{1,0:T(8,128)(2,1)} %refs_0_), channel_id=1, source_target_pairs={{0,4},{1,3},{2,6},{3,1},{4,0},{5,7},{6,2},{7,5},{8,12},{9,11},{10,... | collective-permute-start | bytes 3145736 | tf_op jit(solution)/shard_map/ppermute | solution.py:366
  3.7 0.7 convert_element_type.13
  4.4 1.5 %copy.20.hidden_ref = bf16[1,3,8,65,384]{4,3,2,1,0:T(8,128)(2,1)S(1)} copy(bf16[1,3,8,65,384]{4,2,3,1,0:T(8,128)(2,1)} %param.23) | data formatting | bytes 2396160 | tf_op args[11]
  5.8 0.0 copy-done.11
  5.8 0.0 copy-start.9
  5.8 0.0 copy-start.10
  5.9 0.0 copy-start.8
  5.9 0.8 fusion.1
  6.8 0.0 copy-start.7
  6.8 3.6 %all-to-all-start = ((bf16[8,66,384]{2,1,0:T(8,128)(2,1)}), bf16[8,66,384]{2,1,0:T(8,128)(2,1)S(1)}, u32[]{:S(2)}, u32[]{:S(2)}) async-start(bf16[8,66,384]{2,1,0:T(8,128)(2,1)} %fusion.1), calls=%async_computation | async-start | bytes 884736 | tf_op jit(solution)/shard_map/all_to_all | solution.py:314
  10.4 0.0 copy-done.9
  10.4 0.0 copy-done.10
  10.5 5.5 %collective-permute-start.2 = (bf16[256,256]{1,0:T(8,128)(2,1)S(1)}, bf16[256,256]{1,0:T(8,128)(2,1)S(1)}, u32[]{:S(2)}, u32[]{:S(2)}) collective-permute-start(bf16[256,256]{1,0:T(8,128)(2,1)S(1)} %pad_maximum_fusion.rest_0_), channel_id=1, source_target_pairs={{0,24},{1,25},{2,26},{3,27},{4,28},{5,29},{6,30},{7,31}} | collective-permute-start | bytes 393224 | tf_op jit(solution)/shard_map/ppermute | solution.py:98
  16.0 1.3 %collective-permute-start.1 = (bf16[256,256]{1,0:T(8,128)(2,1)S(1)}, bf16[256,256]{1,0:T(8,128)(2,1)S(1)}, u32[]{:S(2)}, u32[]{:S(2)}) collective-permute-start(bf16[256,256]{1,0:T(8,128)(2,1)S(1)} %pad_maximum_fusion.rest_0_), channel_id=1, source_target_pairs={{0,16},{8,24},{1,17},{9,25},{2,18},{10,26},{3,19},{11,27},{4,20},{... | collective-permute-start | bytes 393224 | tf_op jit(solution)/shard_map/ppermute | solution.py:98
  17.3 2.5 %collective-permute-start = (bf16[256,256]{1,0:T(8,128)(2,1)S(1)}, bf16[256,256]{1,0:T(8,128)(2,1)S(1)}, u32[]{:S(2)}, u32[]{:S(2)}) collective-permute-start(bf16[256,256]{1,0:T(8,128)(2,1)S(1)} %pad_maximum_fusion.rest_0_), channel_id=1, source_target_pairs={{0,8},{8,16},{16,24},{1,9},{9,17},{17,25},{2,10},{10,18},{18,26},{... | collective-permute-start | bytes 393224 | tf_op jit(solution)/shard_map/ppermute | solution.py:98
  19.8 1.9 %all-to-all-done.mixed_ref = bf16[8,66,384]{2,1,0:T(8,128)(2,1)S(1)} async-done(((bf16[8,66,384]{2,1,0:T(8,128)(2,1)}), bf16[8,66,384]{2,1,0:T(8,128)(2,1)S(1)}, u32[]{:S(2)}, u32[]{:S(2)}) %all-to-all-start) | async-done | bytes 405536 | tf_op jit(solution)/shard_map/all_to_all | solution.py:314
  21.7 0.0 copy-done.8
  21.7 1.3 %picked.1 = bf16[8,64,384]{2,1,0:T(8,128)(2,1)} custom-call(s32[16]{0:T(128)S(1)} %copy-done.8, bf16[8,66,384]{2,1,0:T(8,128)(2,1)S(1)} %all-to-all-done.mixed_ref), custom_call_target="tpu_custom_call" | custom-call | tf_op jit(solution)/shard_map/picked/pallas_call | solution.py:179
  23.1 0.0 collective-permute-done.2.rest_3_
  23.1 0.0 collective-permute-done.1.rest_2_
  23.1 1.9 %collective-permute-done.rest_1_ = bf16[256,256]{1,0:T(8,128)(2,1)S(1)} collective-permute-done((bf16[256,256]{1,0:T(8,128)(2,1)S(1)}, bf16[256,256]{1,0:T(8,128)(2,1)S(1)}, u32[]{:S(2)}, u32[]{:S(2)}) %collective-permute-start) | collective-permute-done | bytes 131104 | tf_op jit(solution)/shard_map/ppermute | solution.py:98
  24.9 1.7 %collective-permute-start.6 = (bf16[128,4096]{1,0:T(8,128)(2,1)}, bf16[128,4096]{1,0:T(8,128)(2,1)}, u32[]{:S(2)}, u32[]{:S(2)}) collective-permute-start(bf16[128,4096]{1,0:T(8,128)(2,1)} %refs_0_), channel_id=1, source_target_pairs={{0,2},{1,5},{2,0},{3,7},{4,6},{5,1},{6,4},{7,3},{8,10},{9,13},{10,... | collective-permute-start | bytes 3145736 | tf_op jit(solution)/shard_map/ppermute | solution.py:366
  26.6 0.0 copy-done.3
  26.6 0.0 copy-done.6
  26.6 3.1 %attention.1 = (bf16[256,512]{1,0:T(8,128)(2,1)}, bf16[4,256,256]{2,1,0:T(8,128)(2,1)S(1)}) custom-call(s32[1]{0:T(128)} %bitcast.place_ref, s32[4,4]{1,0:T(4,128)S(1)} %copy-done.7, bf16[256,512]{1,0:T(8,128)(2,1)S(1)} %copy-done.3, bf16[256,512]{1,0:T(8,128)(2,1)S(1)} %copy-done.4, bf16[256,512]{1,0:T(8,128)(2,1)S(1)} %copy-done.5, ...), custom_call_target="tpu_custom_call" | custom-call | tf_op jit(solution)/shard_map/attention/pallas_call | solution.py:108
  29.7 0.8 copy-done.2
  30.5 0.0 collective-permute-done.4.refs_2_
  30.5 0.4 collective-permute-start.8
  30.9 3.9 %all-to-all-start.2 = ((bf16[8,64,384]{2,1,0:T(8,128)(2,1)}), bf16[8,64,384]{2,1,0:T(8,128)(2,1)S(1)}, u32[]{:S(2)}, u32[]{:S(2)}) async-start(bf16[8,64,384]{2,1,0:T(8,128)(2,1)} %picked.1), calls=%async_computation.2 | async-start | bytes 786432 | tf_op jit(solution)/shard_map/all_to_all | solution.py:314
  34.8 0.5 collective-permute-start.3
  35.3 21.2 %all-to-all-done.2.side_ref = bf16[8,64,384]{2,1,0:T(8,128)(2,1)S(1)} async-done(((bf16[8,64,384]{2,1,0:T(8,128)(2,1)}), bf16[8,64,384]{2,1,0:T(8,128)(2,1)S(1)}, u32[]{:S(2)}, u32[]{:S(2)}) %all-to-all-start.2) | async-done | bytes 393248 | tf_op jit(solution)/shard_map/all_to_all | solution.py:314
  56.5 0.7 copy-done
  57.3 1.0 %copy-done.1 = bf16[8,64,384]{2,1,0:T(8,128)(2,1)S(1)} copy-done((bf16[8,64,384]{2,1,0:T(8,128)(2,1)S(1)}, bf16[8,64,384]{2,1,0:T(8,128)(2,1)}, u32[]{:S(2)}) %copy-start.1) | copy-done | bytes 393240
  58.3 2.9 %weighted.1.weight_ref = bf16[768,1024]{1,0:T(8,128)(2,1)S(1)} custom-call(s32[1]{0:T(128)} %bitcast.6.own_ref, s32[16]{0:T(128)S(1)} %copy-done.8, bf16[8,66,384]{2,1,0:T(8,128)(2,1)S(1)} %all-to-all-done.mixed_ref, bf16[1,3,8,65,384]{4,3,2,1,0:T(8,128)(2,1)S(1)} %copy.20.hidden_ref, bf16[8,64,384]{2,1,0:T(8,128)(2,1)S(1)} %copy-done.1), custom_call_target="tpu_custom_call" | custom-call | tf_op jit(solution)/shard_map/weighted/pallas_call | solution.py:231
  61.1 0.1 collective-permute-start.5
  61.2 0.0 collective-permute-done.6.refs_4_
  61.2 0.5 collective-permute-start.7
  61.7 0.0 collective-permute-done.8.refs_6_
  61.7 0.1 collective-permute-start.9
  61.8 7.5 %all-to-all-start.1 = ((bf16[32,32,256]{2,1,0:T(8,128)(2,1)}), bf16[32,32,256]{2,1,0:T(8,128)(2,1)S(1)}, u32[]{:S(2)}, u32[]{:S(2)}) async-start(bf16[32,32,256]{2,1,0:T(8,128)(2,1)} %bitcast.10), calls=%async_computation.1 | async-start | bytes 1048576 | tf_op jit(solution)/shard_map/all_to_all | solution.py:146
  69.3 0.0 collective-permute-done.3.refs_1_
  69.3 0.0 collective-permute-done.5.refs_3_
  69.3 0.0 collective-permute-done.7.refs_5_
  69.3 0.0 collective-permute-done.9.refs_7_
  69.3 10.8 %tiles.1 = f32[2,384,4096]{2,1,0:T(8,128)} custom-call(bf16[768,1024]{1,0:T(8,128)(2,1)S(1)} %weighted.1.weight_ref, bf16[128,4096]{1,0:T(8,128)(2,1)} %refs_0_, bf16[128,4096]{1,0:T(8,128)(2,1)} %collective-permute-done.3.refs_1_, bf16[128,4096]{1,0:T(8,128)(2,1)} %collective-permute-done.4.refs_2_, bf16[128,4096]{1,0:T(8,128)(2,1)} %collective-permute-done.5.refs_3_, ...), custom_call_target="tpu_custom_call" | custom-call | tf_op jit(solution)/shard_map/tiles/pallas_call | solution.py:297
  80.1 4.7 %all-to-all-done.1 = bf16[32,32,256]{2,1,0:T(8,128)(2,1)S(1)} async-done(((bf16[32,32,256]{2,1,0:T(8,128)(2,1)}), bf16[32,32,256]{2,1,0:T(8,128)(2,1)S(1)}, u32[]{:S(2)}, u32[]{:S(2)}) %all-to-all-start.1) | async-done | bytes 524320 | tf_op jit(solution)/shard_map/all_to_all | solution.py:146
  84.8 0.7 sums.1
  (14 shorter events, 0.1 us)
Async XLA Ops:
  0.6 5.2 %copy-start.11 = (s32[128,8]{0,1:T(8,128)S(1)}, s32[128,8]{0,1:T(8,128)}, u32[]{:S(2)}) copy-start(s32[128,8]{0,1:T(8,128)} %param.19) | copy-start | bytes 12292
  0.6 29.9 %collective-permute-start.4 = (bf16[128,4096]{1,0:T(8,128)(2,1)}, bf16[128,4096]{1,0:T(8,128)(2,1)}, u32[]{:S(2)}, u32[]{:S(2)}) collective-permute-start(bf16[128,4096]{1,0:T(8,128)(2,1)} %refs_0_), channel_id=1, source_target_pairs={{0,4},{1,3},{2,6},{3,1},{4,0},{5,7},{6,2},{7,5},{8,12},{9,11},{10,... | collective-permute-start | bytes 3145736 | tf_op jit(solution)/shard_map/ppermute | solution.py:366
  5.8 4.6 %copy-start.9 = (bf16[256,256]{1,0:T(8,128)(2,1)S(1)}, bf16[256,256]{1,0:T(8,128)(2,1)}, u32[]{:S(2)}) copy-start(bf16[256,256]{1,0:T(8,128)(2,1)} %param.14) | copy-start | bytes 393220
  5.8 4.6 %copy-start.10 = (bf16[256,256]{1,0:T(8,128)(2,1)S(1)}, bf16[256,256]{1,0:T(8,128)(2,1)}, u32[]{:S(2)}) copy-start(bf16[256,256]{1,0:T(8,128)(2,1)} %param.13) | copy-start | bytes 393220
  5.9 15.8 %copy-start.8 = (s32[16]{0:T(128)S(1)}, s32[16]{0:T(128)}, u32[]{:S(2)}) copy-start(s32[16]{0:T(128)} %shadow_ref.3) | copy-start | bytes 196
  6.7 19.9 %copy-start.3 = (bf16[256,512]{1,0:T(8,128)(2,1)S(1)}, bf16[256,512]{1,0:T(8,128)(2,1)}, u32[]{:S(2)}) copy-start(bf16[256,512]{1,0:T(8,128)(2,1)} %query_ref.1) | copy-start | bytes 786436
  6.7 19.9 %copy-start.4 = (bf16[256,512]{1,0:T(8,128)(2,1)S(1)}, bf16[256,512]{1,0:T(8,128)(2,1)}, u32[]{:S(2)}) copy-start(bf16[256,512]{1,0:T(8,128)(2,1)} %grad_ref.1) | copy-start | bytes 786436
  6.8 19.9 %copy-start.5 = (bf16[256,512]{1,0:T(8,128)(2,1)S(1)}, bf16[256,512]{1,0:T(8,128)(2,1)}, u32[]{:S(2)}) copy-start(bf16[256,512]{1,0:T(8,128)(2,1)} %out_ref.1) | copy-start | bytes 786436
  6.8 19.9 %copy-start.6 = (f32[4,256]{1,0:T(4,128)S(1)}, f32[4,256]{1,0:T(4,128)}, u32[]{:S(2)}) copy-start(f32[4,256]{1,0:T(4,128)} %lse_ref.1) | copy-start | bytes 12292
  6.8 19.9 %copy-start.7 = (s32[4,4]{1,0:T(4,128)S(1)}, s32[4,4]{1,0:T(4,128)}, u32[]{:S(2)}) copy-start(s32[4,4]{1,0:T(4,128)} %mask_ref.1) | copy-start | bytes 196
  6.8 15.0 %all-to-all-start = ((bf16[8,66,384]{2,1,0:T(8,128)(2,1)}), bf16[8,66,384]{2,1,0:T(8,128)(2,1)S(1)}, u32[]{:S(2)}, u32[]{:S(2)}) async-start(bf16[8,66,384]{2,1,0:T(8,128)(2,1)} %fusion.1), calls=%async_computation | async-start | bytes 884736 | tf_op jit(solution)/shard_map/all_to_all | solution.py:314
  10.5 12.6 %collective-permute-start.2 = (bf16[256,256]{1,0:T(8,128)(2,1)S(1)}, bf16[256,256]{1,0:T(8,128)(2,1)S(1)}, u32[]{:S(2)}, u32[]{:S(2)}) collective-permute-start(bf16[256,256]{1,0:T(8,128)(2,1)S(1)} %pad_maximum_fusion.rest_0_), channel_id=1, source_target_pairs={{0,24},{1,25},{2,26},{3,27},{4,28},{5,29},{6,30},{7,31}} | collective-permute-start | bytes 393224 | tf_op jit(solution)/shard_map/ppermute | solution.py:98
  16.0 7.0 %collective-permute-start.1 = (bf16[256,256]{1,0:T(8,128)(2,1)S(1)}, bf16[256,256]{1,0:T(8,128)(2,1)S(1)}, u32[]{:S(2)}, u32[]{:S(2)}) collective-permute-start(bf16[256,256]{1,0:T(8,128)(2,1)S(1)} %pad_maximum_fusion.rest_0_), channel_id=1, source_target_pairs={{0,16},{8,24},{1,17},{9,25},{2,18},{10,26},{3,19},{11,27},{4,20},{... | collective-permute-start | bytes 393224 | tf_op jit(solution)/shard_map/ppermute | solution.py:98
  17.3 7.6 %collective-permute-start = (bf16[256,256]{1,0:T(8,128)(2,1)S(1)}, bf16[256,256]{1,0:T(8,128)(2,1)S(1)}, u32[]{:S(2)}, u32[]{:S(2)}) collective-permute-start(bf16[256,256]{1,0:T(8,128)(2,1)S(1)} %pad_maximum_fusion.rest_0_), channel_id=1, source_target_pairs={{0,8},{8,16},{16,24},{1,9},{9,17},{17,25},{2,10},{10,18},{18,26},{... | collective-permute-start | bytes 393224 | tf_op jit(solution)/shard_map/ppermute | solution.py:98
  24.9 36.3 %collective-permute-start.6 = (bf16[128,4096]{1,0:T(8,128)(2,1)}, bf16[128,4096]{1,0:T(8,128)(2,1)}, u32[]{:S(2)}, u32[]{:S(2)}) collective-permute-start(bf16[128,4096]{1,0:T(8,128)(2,1)} %refs_0_), channel_id=1, source_target_pairs={{0,2},{1,5},{2,0},{3,7},{4,6},{5,1},{6,4},{7,3},{8,10},{9,13},{10,... | collective-permute-start | bytes 3145736 | tf_op jit(solution)/shard_map/ppermute | solution.py:366
  29.7 0.8 copy-start.2
  30.5 31.2 %collective-permute-start.8 = (bf16[128,4096]{1,0:T(8,128)(2,1)}, bf16[128,4096]{1,0:T(8,128)(2,1)}, u32[]{:S(2)}, u32[]{:S(2)}) collective-permute-start(bf16[128,4096]{1,0:T(8,128)(2,1)} %collective-permute-done.4.refs_2_), channel_id=1, source_target_pairs={{0,2},{1,5},{2,0},{3,7},{4,6},{5,1},{6,4},{7,3},{8,10},{9,13},{10,... | collective-permute-start | bytes 3145736 | tf_op jit(solution)/shard_map/ppermute | solution.py:366
  30.9 25.6 %all-to-all-start.2 = ((bf16[8,64,384]{2,1,0:T(8,128)(2,1)}), bf16[8,64,384]{2,1,0:T(8,128)(2,1)S(1)}, u32[]{:S(2)}, u32[]{:S(2)}) async-start(bf16[8,64,384]{2,1,0:T(8,128)(2,1)} %picked.1), calls=%async_computation.2 | async-start | bytes 786432 | tf_op jit(solution)/shard_map/all_to_all | solution.py:314
  34.8 34.5 %collective-permute-start.3 = (bf16[128,4096]{1,0:T(8,128)(2,1)}, bf16[128,4096]{1,0:T(8,128)(2,1)}, u32[]{:S(2)}, u32[]{:S(2)}) collective-permute-start(bf16[128,4096]{1,0:T(8,128)(2,1)} %refs_0_), channel_id=1, source_target_pairs={{0,1},{1,0},{2,3},{3,2},{4,5},{5,4},{6,7},{7,6},{8,9},{9,8},{10,11... | collective-permute-start | bytes 3145736 | tf_op jit(solution)/shard_map/ppermute | solution.py:366
  56.5 0.7 copy-start
  57.3 1.0 %copy-start.1 = (bf16[8,64,384]{2,1,0:T(8,128)(2,1)S(1)}, bf16[8,64,384]{2,1,0:T(8,128)(2,1)}, u32[]{:S(2)}) copy-start(bf16[8,64,384]{2,1,0:T(8,128)(2,1)} %copy-done) | copy-start | bytes 1179652
  61.1 8.2 %collective-permute-start.5 = (bf16[128,4096]{1,0:T(8,128)(2,1)}, bf16[128,4096]{1,0:T(8,128)(2,1)}, u32[]{:S(2)}, u32[]{:S(2)}) collective-permute-start(bf16[128,4096]{1,0:T(8,128)(2,1)} %collective-permute-done.4.refs_2_), channel_id=1, source_target_pairs={{0,1},{1,0},{2,3},{3,2},{4,5},{5,4},{6,7},{7,6},{8,9},{9,8},{10,11... | collective-permute-start | bytes 3145736 | tf_op jit(solution)/shard_map/ppermute | solution.py:366
  61.2 8.1 %collective-permute-start.7 = (bf16[128,4096]{1,0:T(8,128)(2,1)}, bf16[128,4096]{1,0:T(8,128)(2,1)}, u32[]{:S(2)}, u32[]{:S(2)}) collective-permute-start(bf16[128,4096]{1,0:T(8,128)(2,1)} %collective-permute-done.6.refs_4_), channel_id=1, source_target_pairs={{0,1},{1,0},{2,3},{3,2},{4,5},{5,4},{6,7},{7,6},{8,9},{9,8},{10,11... | collective-permute-start | bytes 3145736 | tf_op jit(solution)/shard_map/ppermute | solution.py:366
  61.7 7.6 %collective-permute-start.9 = (bf16[128,4096]{1,0:T(8,128)(2,1)}, bf16[128,4096]{1,0:T(8,128)(2,1)}, u32[]{:S(2)}, u32[]{:S(2)}) collective-permute-start(bf16[128,4096]{1,0:T(8,128)(2,1)} %collective-permute-done.8.refs_6_), channel_id=1, source_target_pairs={{0,1},{1,0},{2,3},{3,2},{4,5},{5,4},{6,7},{7,6},{8,9},{9,8},{10,11... | collective-permute-start | bytes 3145736 | tf_op jit(solution)/shard_map/ppermute | solution.py:366
  61.8 23.0 %all-to-all-start.1 = ((bf16[32,32,256]{2,1,0:T(8,128)(2,1)}), bf16[32,32,256]{2,1,0:T(8,128)(2,1)S(1)}, u32[]{:S(2)}, u32[]{:S(2)}) async-start(bf16[32,32,256]{2,1,0:T(8,128)(2,1)} %bitcast.10), calls=%async_computation.1 | async-start | bytes 1048576 | tf_op jit(solution)/shard_map/all_to_all | solution.py:146

commit v3 on v2

--- a/solution.py
+++ b/solution.py
@@ -401,15 +401,14 @@
     first = moved(moe_grad, [held[1] for held in steps])
     arrived = key_blocks(keys, values, queries.shape[1] // lse_excess.shape[0])
     mixed, sent = source_rows(expert_ids, route_probs, shadow_list, stored_hidden_state)
-    moe_grad, _ = lax.optimization_barrier((moe_grad, mixed))
+    moe_grad, first = lax.optimization_barrier((moe_grad, first))
     second = moved(moe_grad, [held[2] for held in steps])
     sent, arrived = lax.optimization_barrier((sent, arrived))
     shadow_rows = swapped(sent)
     query_grad, terms = attention(
         queries, arrived, attn_out, attn_out_grad, lse_excess, block_mask
     )
-    first, _ = lax.optimization_barrier((first, query_grad))
-    shadow_rows, _ = lax.optimization_barrier((shadow_rows, query_grad))
+    first, shadow_rows, query_grad = lax.optimization_barrier((first, shadow_rows, query_grad))
     weighted = expert_rows(
         mixed, shadow_rows, shadow_list, stored_hidden_state, expert_ids.shape[0]
     )

time: 86 us -> 88.6 us (1.030)
  waiting for transfers between devices: 29.8 us -> 32.9 us
  starting transfers between devices: 30.5 us -> 29.4 us
    ppermute x7, waiting for transfers between devices: 0.02 us -> 19.9 us  [moved(): lax.ppermute(value, 'exp', [(e, e ^ steps[e % 2]) for e in range(owners)])]
    all_to_all x2, waiting for transfers between devices: 23.2 us -> 6.32 us  [swapped(): return lax.all_to_all(value, 'exp', split_axis=0, concat_axis=0, tiled=True)]
    all_to_all x1, starting transfers between devices: 7.47 us -> 6.51 us  [summed_terms(): lax.all_to_all(terms.reshape(cycle * owners, rows // owners, columns), ('...]
  transfers between devices with their start and end apart: 13 -> 13, of which waited for: 4 -> 6; matrix products, arithmetic and copies ran while one was open for 4% -> 3% of each run, Pallas kernels for 21% -> 21%
where the time goes in v3:
time: 88.6 us; the launch traced here: 87.5 us
  waiting for transfers between devices  32.9 us (37%)
  starting transfers between devices  29.4 us (33%)
  Pallas kernels  18.7 us (21%)
  local copies, waits for them, and re-layouts  4.11 us (5%)
  other arithmetic  1.54 us (2%)
    ppermute x7, waiting for transfers between devices, moved(): lax.ppermute(value, 'exp', [(e, e ^ steps[e % 2]) for e in range(owners)])  19.9 us
    pallas_call x1, Pallas kernels, tile_sums(): pl.pallas_call(tile_kernel, out_shape=jax.ShapeDtypeStruct((per_dev, rows...  10.7 us
    ppermute x3, starting transfers between devices, key_blocks(): lax.ppermute(pair, 'ctx', [(c, c + step) for c in range(cycle - step)])  9.29 us
    all_to_all x2, starting transfers between devices, swapped(): return lax.all_to_all(value, 'exp', split_axis=0, concat_axis=0, tiled=True)  7.48 us
    all_to_all x1, starting transfers between devices, summed_terms(): lax.all_to_all(terms.reshape(cycle * owners, rows // owners, columns), ('...  6.51 us
    all_to_all x2, waiting for transfers between devices, swapped(): return lax.all_to_all(value, 'exp', split_axis=0, concat_axis=0, tiled=True)  6.32 us
    ppermute x7, starting transfers between devices, moved(): lax.ppermute(value, 'exp', [(e, e ^ steps[e % 2]) for e in range(owners)])  6.08 us
    all_to_all x1, waiting for transfers between devices, summed_terms(): lax.all_to_all(terms.reshape(cycle * owners, rows // owners, columns), ('...  4.77 us
  transfers between devices with their start and end apart: 13, of which 6 were waited for; matrix products, arithmetic and copies ran while one was open for 3% of the time, Pallas kernels for 21%

profile of v3, /device:TPU:0, one launch (start us, length us, event | category | flops | bytes accessed | tf_op | source)
XLA Modules:
  0.0 87.5 jit_solution(12192487528429154953)
XLA Ops:
  0.6 0.0 copy-start.11
  0.6 3.0 %collective-permute-start = (bf16[128,4096]{1,0:T(8,128)(2,1)}, bf16[128,4096]{1,0:T(8,128)(2,1)}, u32[]{:S(2)}, u32[]{:S(2)}) collective-permute-start(bf16[128,4096]{1,0:T(8,128)(2,1)} %refs_0_), channel_id=1, source_target_pairs={{0,4},{1,3},{2,6},{3,1},{4,0},{5,7},{6,2},{7,5},{8,12},{9,11},{10,... | collective-permute-start | bytes 3145736 | tf_op jit(solution)/shard_map/ppermute | solution.py:366
  3.7 0.7 convert_element_type.13
  4.4 1.5 %copy.20.hidden_ref = bf16[1,3,8,65,384]{4,3,2,1,0:T(8,128)(2,1)S(1)} copy(bf16[1,3,8,65,384]{4,2,3,1,0:T(8,128)(2,1)} %param.23) | data formatting | bytes 2396160 | tf_op args[11]
  5.8 0.0 copy-done.11
  5.8 0.0 copy-start.9
  5.8 0.0 copy-start.10
  5.9 0.0 copy-start.8
  5.9 0.8 fusion.1
  6.8 0.0 copy-start.7
  6.8 3.6 %all-to-all-start = ((bf16[8,66,384]{2,1,0:T(8,128)(2,1)}), bf16[8,66,384]{2,1,0:T(8,128)(2,1)S(1)}, u32[]{:S(2)}, u32[]{:S(2)}) async-start(bf16[8,66,384]{2,1,0:T(8,128)(2,1)} %fusion.1), calls=%async_computation | async-start | bytes 884736 | tf_op jit(solution)/shard_map/all_to_all | solution.py:314
  10.4 0.0 copy-done.9
  10.4 0.0 copy-done.10
  10.5 5.5 %collective-permute-start.3 = (bf16[256,256]{1,0:T(8,128)(2,1)S(1)}, bf16[256,256]{1,0:T(8,128)(2,1)S(1)}, u32[]{:S(2)}, u32[]{:S(2)}) collective-permute-start(bf16[256,256]{1,0:T(8,128)(2,1)S(1)} %pad_maximum_fusion.rest_0_), channel_id=1, source_target_pairs={{0,24},{1,25},{2,26},{3,27},{4,28},{5,29},{6,30},{7,31}} | collective-permute-start | bytes 393224 | tf_op jit(solution)/shard_map/ppermute | solution.py:98
  16.0 1.3 %collective-permute-start.2 = (bf16[256,256]{1,0:T(8,128)(2,1)S(1)}, bf16[256,256]{1,0:T(8,128)(2,1)S(1)}, u32[]{:S(2)}, u32[]{:S(2)}) collective-permute-start(bf16[256,256]{1,0:T(8,128)(2,1)S(1)} %pad_maximum_fusion.rest_0_), channel_id=1, source_target_pairs={{0,16},{8,24},{1,17},{9,25},{2,18},{10,26},{3,19},{11,27},{4,20},{... | collective-permute-start | bytes 393224 | tf_op jit(solution)/shard_map/ppermute | solution.py:98
  17.3 2.5 %collective-permute-start.1 = (bf16[256,256]{1,0:T(8,128)(2,1)S(1)}, bf16[256,256]{1,0:T(8,128)(2,1)S(1)}, u32[]{:S(2)}, u32[]{:S(2)}) collective-permute-start(bf16[256,256]{1,0:T(8,128)(2,1)S(1)} %pad_maximum_fusion.rest_0_), channel_id=1, source_target_pairs={{0,8},{8,16},{16,24},{1,9},{9,17},{17,25},{2,10},{10,18},{18,26},{... | collective-permute-start | bytes 393224 | tf_op jit(solution)/shard_map/ppermute | solution.py:98
  19.8 1.9 %all-to-all-done.mixed_ref = bf16[8,66,384]{2,1,0:T(8,128)(2,1)S(1)} async-done(((bf16[8,66,384]{2,1,0:T(8,128)(2,1)}), bf16[8,66,384]{2,1,0:T(8,128)(2,1)S(1)}, u32[]{:S(2)}, u32[]{:S(2)}) %all-to-all-start) | async-done | bytes 405536 | tf_op jit(solution)/shard_map/all_to_all | solution.py:314
  21.7 0.0 copy-done.8
  21.7 1.3 %picked.1 = bf16[8,64,384]{2,1,0:T(8,128)(2,1)} custom-call(s32[16]{0:T(128)S(1)} %copy-done.8, bf16[8,66,384]{2,1,0:T(8,128)(2,1)S(1)} %all-to-all-done.mixed_ref), custom_call_target="tpu_custom_call" | custom-call | tf_op jit(solution)/shard_map/picked/pallas_call | solution.py:179
  23.1 0.0 collective-permute-done.3.rest_3_
  23.1 0.0 collective-permute-done.2.rest_2_
  23.1 1.9 %collective-permute-done.1.rest_1_ = bf16[256,256]{1,0:T(8,128)(2,1)S(1)} collective-permute-done((bf16[256,256]{1,0:T(8,128)(2,1)S(1)}, bf16[256,256]{1,0:T(8,128)(2,1)S(1)}, u32[]{:S(2)}, u32[]{:S(2)}) %collective-permute-start.1) | collective-permute-done | bytes 131104 | tf_op jit(solution)/shard_map/ppermute | solution.py:98
  24.9 3.9 %all-to-all-start.1 = ((bf16[8,64,384]{2,1,0:T(8,128)(2,1)}), bf16[8,64,384]{2,1,0:T(8,128)(2,1)S(1)}, u32[]{:S(2)}, u32[]{:S(2)}) async-start(bf16[8,64,384]{2,1,0:T(8,128)(2,1)} %picked.1), calls=%async_computation.1 | async-start | bytes 786432 | tf_op jit(solution)/shard_map/all_to_all | solution.py:314
  28.8 0.0 copy-done.3
  28.8 0.0 copy-done.4
  28.9 3.1 %attention.1 = (bf16[256,512]{1,0:T(8,128)(2,1)}, bf16[4,256,256]{2,1,0:T(8,128)(2,1)S(1)}) custom-call(s32[1]{0:T(128)} %bitcast.3.place_ref, s32[4,4]{1,0:T(4,128)S(1)} %copy-done.7, bf16[256,512]{1,0:T(8,128)(2,1)S(1)} %copy-done.3, bf16[256,512]{1,0:T(8,128)(2,1)S(1)} %copy-done.4, bf16[256,512]{1,0:T(8,128)(2,1)S(1)} %copy-done.5, ...), custom_call_target="tpu_custom_call" | custom-call | tf_op jit(solution)/shard_map/attention/pallas_call | solution.py:108
  31.9 0.8 copy-done.2
  32.7 0.0 collective-permute-done.refs_2_
  32.7 4.4 %all-to-all-done.1.side_ref = bf16[8,64,384]{2,1,0:T(8,128)(2,1)S(1)} async-done(((bf16[8,64,384]{2,1,0:T(8,128)(2,1)}), bf16[8,64,384]{2,1,0:T(8,128)(2,1)S(1)}, u32[]{:S(2)}, u32[]{:S(2)}) %all-to-all-start.1) | async-done | bytes 393248 | tf_op jit(solution)/shard_map/all_to_all | solution.py:314
  37.1 0.7 copy-done
  37.9 0.6 collective-permute-start.8
  38.5 1.5 %collective-permute-start.6 = (bf16[128,4096]{1,0:T(8,128)(2,1)}, bf16[128,4096]{1,0:T(8,128)(2,1)}, u32[]{:S(2)}, u32[]{:S(2)}) collective-permute-start(bf16[128,4096]{1,0:T(8,128)(2,1)} %refs_0_), channel_id=1, source_target_pairs={{0,2},{1,5},{2,0},{3,7},{4,6},{5,1},{6,4},{7,3},{8,10},{9,13},{10,... | collective-permute-start | bytes 3145736 | tf_op jit(solution)/shard_map/ppermute | solution.py:366
  39.9 0.0 collective-permute-start.4
  39.9 0.5 collective-permute-start.5
  40.4 1.0 %copy-done.1 = bf16[8,64,384]{2,1,0:T(8,128)(2,1)S(1)} copy-done((bf16[8,64,384]{2,1,0:T(8,128)(2,1)S(1)}, bf16[8,64,384]{2,1,0:T(8,128)(2,1)}, u32[]{:S(2)}) %copy-start.1) | copy-done | bytes 393240
  41.4 2.9 %weighted.1.weight_ref = bf16[768,1024]{1,0:T(8,128)(2,1)S(1)} custom-call(s32[1]{0:T(128)} %bitcast.6.own_ref, s32[16]{0:T(128)S(1)} %copy-done.8, bf16[8,66,384]{2,1,0:T(8,128)(2,1)S(1)} %all-to-all-done.mixed_ref, bf16[1,3,8,65,384]{4,3,2,1,0:T(8,128)(2,1)S(1)} %copy.20.hidden_ref, bf16[8,64,384]{2,1,0:T(8,128)(2,1)S(1)} %copy-done.1), custom_call_target="tpu_custom_call" | custom-call | tf_op jit(solution)/shard_map/weighted/pallas_call | solution.py:231
  44.3 8.7 %collective-permute-done.8.refs_6_ = bf16[128,4096]{1,0:T(8,128)(2,1)} collective-permute-done((bf16[128,4096]{1,0:T(8,128)(2,1)}, bf16[128,4096]{1,0:T(8,128)(2,1)}, u32[]{:S(2)}, u32[]{:S(2)}) %collective-permute-start.8) | collective-permute-done | bytes 1048608 | tf_op jit(solution)/shard_map/ppermute | solution.py:366
  53.0 11.2 %collective-permute-done.6.refs_4_ = bf16[128,4096]{1,0:T(8,128)(2,1)} collective-permute-done((bf16[128,4096]{1,0:T(8,128)(2,1)}, bf16[128,4096]{1,0:T(8,128)(2,1)}, u32[]{:S(2)}, u32[]{:S(2)}) %collective-permute-start.6) | collective-permute-done | bytes 1048608 | tf_op jit(solution)/shard_map/ppermute | solution.py:366
  64.2 0.0 collective-permute-start.7
  64.2 0.5 collective-permute-start.9
  64.8 6.5 %all-to-all-start.2 = ((bf16[32,32,256]{2,1,0:T(8,128)(2,1)}), bf16[32,32,256]{2,1,0:T(8,128)(2,1)S(1)}, u32[]{:S(2)}, u32[]{:S(2)}) async-start(bf16[32,32,256]{2,1,0:T(8,128)(2,1)} %bitcast.10), calls=%async_computation.2 | async-start | bytes 1048576 | tf_op jit(solution)/shard_map/all_to_all | solution.py:146
  71.3 0.0 collective-permute-done.4.refs_1_
  71.3 0.0 collective-permute-done.5.refs_3_
  71.3 0.0 collective-permute-done.7.refs_5_
  71.3 0.0 collective-permute-done.9.refs_7_
  71.3 10.7 %tiles.1 = f32[2,384,4096]{2,1,0:T(8,128)} custom-call(bf16[768,1024]{1,0:T(8,128)(2,1)S(1)} %weighted.1.weight_ref, bf16[128,4096]{1,0:T(8,128)(2,1)} %refs_0_, bf16[128,4096]{1,0:T(8,128)(2,1)} %collective-permute-done.4.refs_1_, bf16[128,4096]{1,0:T(8,128)(2,1)} %collective-permute-done.refs_2_, bf16[128,4096]{1,0:T(8,128)(2,1)} %collective-permute-done.5.refs_3_, ...), custom_call_target="tpu_custom_call" | custom-call | tf_op jit(solution)/shard_map/tiles/pallas_call | solution.py:297
  82.1 4.8 %all-to-all-done.2 = bf16[32,32,256]{2,1,0:T(8,128)(2,1)S(1)} async-done(((bf16[32,32,256]{2,1,0:T(8,128)(2,1)}), bf16[32,32,256]{2,1,0:T(8,128)(2,1)S(1)}, u32[]{:S(2)}, u32[]{:S(2)}) %all-to-all-start.2) | async-done | bytes 524320 | tf_op jit(solution)/shard_map/all_to_all | solution.py:146
  86.8 0.7 sums.1
  (14 shorter events, 0.1 us)
Async XLA Ops:
  0.6 5.2 %copy-start.11 = (s32[128,8]{0,1:T(8,128)S(1)}, s32[128,8]{0,1:T(8,128)}, u32[]{:S(2)}) copy-start(s32[128,8]{0,1:T(8,128)} %param.19) | copy-start | bytes 12292
  0.6 32.1 %collective-permute-start = (bf16[128,4096]{1,0:T(8,128)(2,1)}, bf16[128,4096]{1,0:T(8,128)(2,1)}, u32[]{:S(2)}, u32[]{:S(2)}) collective-permute-start(bf16[128,4096]{1,0:T(8,128)(2,1)} %refs_0_), channel_id=1, source_target_pairs={{0,4},{1,3},{2,6},{3,1},{4,0},{5,7},{6,2},{7,5},{8,12},{9,11},{10,... | collective-permute-start | bytes 3145736 | tf_op jit(solution)/shard_map/ppermute | solution.py:366
  5.8 4.6 %copy-start.9 = (bf16[256,256]{1,0:T(8,128)(2,1)S(1)}, bf16[256,256]{1,0:T(8,128)(2,1)}, u32[]{:S(2)}) copy-start(bf16[256,256]{1,0:T(8,128)(2,1)} %param.14) | copy-start | bytes 393220
  5.8 4.6 %copy-start.10 = (bf16[256,256]{1,0:T(8,128)(2,1)S(1)}, bf16[256,256]{1,0:T(8,128)(2,1)}, u32[]{:S(2)}) copy-start(bf16[256,256]{1,0:T(8,128)(2,1)} %param.13) | copy-start | bytes 393220
  5.9 15.8 %copy-start.8 = (s32[16]{0:T(128)S(1)}, s32[16]{0:T(128)}, u32[]{:S(2)}) copy-start(s32[16]{0:T(128)} %shadow_ref.3) | copy-start | bytes 196
  6.7 22.1 %copy-start.3 = (bf16[256,512]{1,0:T(8,128)(2,1)S(1)}, bf16[256,512]{1,0:T(8,128)(2,1)}, u32[]{:S(2)}) copy-start(bf16[256,512]{1,0:T(8,128)(2,1)} %query_ref.1) | copy-start | bytes 786436
  6.7 22.1 %copy-start.4 = (bf16[256,512]{1,0:T(8,128)(2,1)S(1)}, bf16[256,512]{1,0:T(8,128)(2,1)}, u32[]{:S(2)}) copy-start(bf16[256,512]{1,0:T(8,128)(2,1)} %grad_ref.1) | copy-start | bytes 786436
  6.8 22.1 %copy-start.5 = (bf16[256,512]{1,0:T(8,128)(2,1)S(1)}, bf16[256,512]{1,0:T(8,128)(2,1)}, u32[]{:S(2)}) copy-start(bf16[256,512]{1,0:T(8,128)(2,1)} %out_ref.1) | copy-start | bytes 786436
  6.8 22.1 %copy-start.6 = (f32[4,256]{1,0:T(4,128)S(1)}, f32[4,256]{1,0:T(4,128)}, u32[]{:S(2)}) copy-start(f32[4,256]{1,0:T(4,128)} %lse_ref.1) | copy-start | bytes 12292
  6.8 22.1 %copy-start.7 = (s32[4,4]{1,0:T(4,128)S(1)}, s32[4,4]{1,0:T(4,128)}, u32[]{:S(2)}) copy-start(s32[4,4]{1,0:T(4,128)} %mask_ref.1) | copy-start | bytes 196
  6.8 15.0 %all-to-all-start = ((bf16[8,66,384]{2,1,0:T(8,128)(2,1)}), bf16[8,66,384]{2,1,0:T(8,128)(2,1)S(1)}, u32[]{:S(2)}, u32[]{:S(2)}) async-start(bf16[8,66,384]{2,1,0:T(8,128)(2,1)} %fusion.1), calls=%async_computation | async-start | bytes 884736 | tf_op jit(solution)/shard_map/all_to_all | solution.py:314
  10.5 12.6 %collective-permute-start.3 = (bf16[256,256]{1,0:T(8,128)(2,1)S(1)}, bf16[256,256]{1,0:T(8,128)(2,1)S(1)}, u32[]{:S(2)}, u32[]{:S(2)}) collective-permute-start(bf16[256,256]{1,0:T(8,128)(2,1)S(1)} %pad_maximum_fusion.rest_0_), channel_id=1, source_target_pairs={{0,24},{1,25},{2,26},{3,27},{4,28},{5,29},{6,30},{7,31}} | collective-permute-start | bytes 393224 | tf_op jit(solution)/shard_map/ppermute | solution.py:98
  16.0 7.0 %collective-permute-start.2 = (bf16[256,256]{1,0:T(8,128)(2,1)S(1)}, bf16[256,256]{1,0:T(8,128)(2,1)S(1)}, u32[]{:S(2)}, u32[]{:S(2)}) collective-permute-start(bf16[256,256]{1,0:T(8,128)(2,1)S(1)} %pad_maximum_fusion.rest_0_), channel_id=1, source_target_pairs={{0,16},{8,24},{1,17},{9,25},{2,18},{10,26},{3,19},{11,27},{4,20},{... | collective-permute-start | bytes 393224 | tf_op jit(solution)/shard_map/ppermute | solution.py:98
  17.3 7.6 %collective-permute-start.1 = (bf16[256,256]{1,0:T(8,128)(2,1)S(1)}, bf16[256,256]{1,0:T(8,128)(2,1)S(1)}, u32[]{:S(2)}, u32[]{:S(2)}) collective-permute-start(bf16[256,256]{1,0:T(8,128)(2,1)S(1)} %pad_maximum_fusion.rest_0_), channel_id=1, source_target_pairs={{0,8},{8,16},{16,24},{1,9},{9,17},{17,25},{2,10},{10,18},{18,26},{... | collective-permute-start | bytes 393224 | tf_op jit(solution)/shard_map/ppermute | solution.py:98
  24.9 12.2 %all-to-all-start.1 = ((bf16[8,64,384]{2,1,0:T(8,128)(2,1)}), bf16[8,64,384]{2,1,0:T(8,128)(2,1)S(1)}, u32[]{:S(2)}, u32[]{:S(2)}) async-start(bf16[8,64,384]{2,1,0:T(8,128)(2,1)} %picked.1), calls=%async_computation.1 | async-start | bytes 786432 | tf_op jit(solution)/shard_map/all_to_all | solution.py:314
  31.9 0.8 copy-start.2
  37.1 0.7 copy-start
  37.9 15.1 %collective-permute-start.8 = (bf16[128,4096]{1,0:T(8,128)(2,1)}, bf16[128,4096]{1,0:T(8,128)(2,1)}, u32[]{:S(2)}, u32[]{:S(2)}) collective-permute-start(bf16[128,4096]{1,0:T(8,128)(2,1)} %collective-permute-done.refs_2_), channel_id=1, source_target_pairs={{0,2},{1,5},{2,0},{3,7},{4,6},{5,1},{6,4},{7,3},{8,10},{9,13},{10,... | collective-permute-start | bytes 3145736 | tf_op jit(solution)/shard_map/ppermute | solution.py:366
  38.5 25.8 %collective-permute-start.6 = (bf16[128,4096]{1,0:T(8,128)(2,1)}, bf16[128,4096]{1,0:T(8,128)(2,1)}, u32[]{:S(2)}, u32[]{:S(2)}) collective-permute-start(bf16[128,4096]{1,0:T(8,128)(2,1)} %refs_0_), channel_id=1, source_target_pairs={{0,2},{1,5},{2,0},{3,7},{4,6},{5,1},{6,4},{7,3},{8,10},{9,13},{10,... | collective-permute-start | bytes 3145736 | tf_op jit(solution)/shard_map/ppermute | solution.py:366
  39.9 31.4 %collective-permute-start.4 = (bf16[128,4096]{1,0:T(8,128)(2,1)}, bf16[128,4096]{1,0:T(8,128)(2,1)}, u32[]{:S(2)}, u32[]{:S(2)}) collective-permute-start(bf16[128,4096]{1,0:T(8,128)(2,1)} %refs_0_), channel_id=1, source_target_pairs={{0,1},{1,0},{2,3},{3,2},{4,5},{5,4},{6,7},{7,6},{8,9},{9,8},{10,11... | collective-permute-start | bytes 3145736 | tf_op jit(solution)/shard_map/ppermute | solution.py:366
  39.9 31.4 %collective-permute-start.5 = (bf16[128,4096]{1,0:T(8,128)(2,1)}, bf16[128,4096]{1,0:T(8,128)(2,1)}, u32[]{:S(2)}, u32[]{:S(2)}) collective-permute-start(bf16[128,4096]{1,0:T(8,128)(2,1)} %collective-permute-done.refs_2_), channel_id=1, source_target_pairs={{0,1},{1,0},{2,3},{3,2},{4,5},{5,4},{6,7},{7,6},{8,9},{9,8},{10,11... | collective-permute-start | bytes 3145736 | tf_op jit(solution)/shard_map/ppermute | solution.py:366
  40.4 1.0 %copy-start.1 = (bf16[8,64,384]{2,1,0:T(8,128)(2,1)S(1)}, bf16[8,64,384]{2,1,0:T(8,128)(2,1)}, u32[]{:S(2)}) copy-start(bf16[8,64,384]{2,1,0:T(8,128)(2,1)} %copy-done) | copy-start | bytes 1179652
  64.2 7.1 %collective-permute-start.7 = (bf16[128,4096]{1,0:T(8,128)(2,1)}, bf16[128,4096]{1,0:T(8,128)(2,1)}, u32[]{:S(2)}, u32[]{:S(2)}) collective-permute-start(bf16[128,4096]{1,0:T(8,128)(2,1)} %collective-permute-done.6.refs_4_), channel_id=1, source_target_pairs={{0,1},{1,0},{2,3},{3,2},{4,5},{5,4},{6,7},{7,6},{8,9},{9,8},{10,11... | collective-permute-start | bytes 3145736 | tf_op jit(solution)/shard_map/ppermute | solution.py:366
  64.2 7.1 %collective-permute-start.9 = (bf16[128,4096]{1,0:T(8,128)(2,1)}, bf16[128,4096]{1,0:T(8,128)(2,1)}, u32[]{:S(2)}, u32[]{:S(2)}) collective-permute-start(bf16[128,4096]{1,0:T(8,128)(2,1)} %collective-permute-done.8.refs_6_), channel_id=1, source_target_pairs={{0,1},{1,0},{2,3},{3,2},{4,5},{5,4},{6,7},{7,6},{8,9},{9,8},{10,11... | collective-permute-start | bytes 3145736 | tf_op jit(solution)/shard_map/ppermute | solution.py:366
  64.8 22.1 %all-to-all-start.2 = ((bf16[32,32,256]{2,1,0:T(8,128)(2,1)}), bf16[32,32,256]{2,1,0:T(8,128)(2,1)S(1)}, u32[]{:S(2)}, u32[]{:S(2)}) async-start(bf16[32,32,256]{2,1,0:T(8,128)(2,1)} %bitcast.10), calls=%async_computation.2 | async-start | bytes 1048576 | tf_op jit(solution)/shard_map/all_to_all | solution.py:146

commit v4 on v3

--- a/solution.py
+++ b/solution.py
@@ -332,9 +332,7 @@
         stored_hidden_state[0, per_dev, :, :used],
         ((0, 0), (0, limit - used), (0, lanes - units)),
     )
-    mixed = jnp.concatenate([rows, jnp.pad(table, ((0, 0), (0, 0), (0, lanes - tokens)))], axis=1)
-    mixed = swapped(mixed)
-    return mixed, picked_rows(shadow_list, mixed, limit)
+    return jnp.concatenate([rows, jnp.pad(table, ((0, 0), (0, 0), (0, lanes - tokens)))], axis=1)
 
 
 def expert_rows(mixed, shadow_rows, shadow_list, stored_hidden_state, tokens):
@@ -366,21 +364,21 @@
     return lax.ppermute(value, "exp", [(e, e ^ steps[e % 2]) for e in range(owners)])
 
 
-def expert_tiles(weighted, near, per_dev):
-    owners = lax.axis_size("exp")
-    steps = block_steps(owners)
-    far = moved(near[1], [held[2] for held in steps])
-    held = list(near)
-    blocks = [block for part in held for block in (part, moved(part, (1, 1)))]
-    far, _ = lax.optimization_barrier((far, weighted))
-    held = held + [far]
-    rest = [far]
-    for turn in range(len(steps[0]).bit_length() - 3):
-        mask = steps[0][4 << turn]
-        more = [moved(part, (mask, mask)) for part in held]
-        held, rest = held + more, rest + more
-    rest = [block for part in rest for block in (part, moved(part, (1, 1)))]
-    return tile_sums(weighted, blocks + rest, per_dev)
+def after(value, *others):
+    return lax.optimization_barrier((value, others))[0]
+
+
+def beside(block):
+    return moved(block, (1, 1))
+
+
+def all_blocks(held):
+    steps = block_steps(lax.axis_size("exp"))[0]
+    for turn in range(len(steps).bit_length() - 3):
+        mask = steps[4 << turn]
+        more = [moved(part, (mask, mask)) for part, _ in held]
+        held = held + [(part, beside(part)) for part in more]
+    return [block for pair in held for block in pair]
 
 
 def local(
@@ -398,22 +396,30 @@
     stored_hidden_state,
 ):
     steps = block_steps(lax.axis_size("exp"))
+    tokens = expert_ids.shape[0]
     first = moved(moe_grad, [held[1] for held in steps])
     arrived = key_blocks(keys, values, queries.shape[1] // lse_excess.shape[0])
-    mixed, sent = source_rows(expert_ids, route_probs, shadow_list, stored_hidden_state)
-    moe_grad, first = lax.optimization_barrier((moe_grad, first))
-    second = moved(moe_grad, [held[2] for held in steps])
-    sent, arrived = lax.optimization_barrier((sent, arrived))
+    payload = source_rows(expert_ids, route_probs, shadow_list, stored_hidden_state)
+    own_beside = beside(after(moe_grad, payload))
+    mixed = swapped(payload)
+    second = moved(after(moe_grad, own_beside), [held[2] for held in steps])
+    per_dev = shadow_list.shape[0] // lax.axis_size("exp")
+    sent = after(picked_rows(shadow_list, mixed, payload.shape[1] - per_dev), arrived)
+    first_beside = beside(after(first, sent))
     shadow_rows = swapped(sent)
+    far = moved(after(first, first_beside), [held[2] for held in steps])
     query_grad, terms = attention(
-        queries, arrived, attn_out, attn_out_grad, lse_excess, block_mask
-    )
-    first, shadow_rows, query_grad = lax.optimization_barrier((first, shadow_rows, query_grad))
+        queries, after(arrived, first_beside), attn_out, attn_out_grad, lse_excess, block_mask
+    )
     weighted = expert_rows(
-        mixed, shadow_rows, shadow_list, stored_hidden_state, expert_ids.shape[0]
-    )
-    per_dev = shadow_list.shape[0] // lax.axis_size("exp")
-    tiles = expert_tiles(weighted, (moe_grad, first, second), per_dev)
+        mixed, after(shadow_rows, query_grad), shadow_list, stored_hidden_state, tokens
+    )
+    second_beside = beside(after(second, weighted))
+    far = after(far, second_beside)
+    blocks = all_blocks(
+        [(moe_grad, own_beside), (first, first_beside), (second, second_beside), (far, beside(far))]
+    )
+    tiles = tile_sums(weighted, blocks, per_dev)
     key_grad, value_grad, expert_grad = summed_terms(terms, keys.shape[1], tiles)
     return (query_grad, key_grad, value_grad, expert_grad)
 

time: 88.6 us -> 88.6 us (level)
  waiting for transfers between devices: 32.9 us -> 24.5 us
  local copies, waits for them, and re-layouts: 4.11 us -> 10.3 us
  starting transfers between devices: 29.4 us -> 31.1 us
  Pallas kernels: 18.7 us -> 19.6 us
    ppermute x7, waiting for transfers between devices: 19.9 us -> 10.2 us  [moved(): lax.ppermute(value, 'exp', [(e, e ^ steps[e % 2]) for e in range(owners)])]
    unnamed x25 -> x31, local copies, waits for them, and re-layouts: 4.05 us -> 9.42 us
    all_to_all x2, waiting for transfers between devices: 6.32 us -> 9.28 us  [swapped(): return lax.all_to_all(value, 'exp', split_axis=0, concat_axis=0, tiled=True)]
    all_to_all x1, waiting for transfers between devices: 4.77 us -> 2.43 us  [summed_terms(): lax.all_to_all(terms.reshape(cycle * owners, rows // owners, columns), ('...]
    ppermute x3, starting transfers between devices: 9.29 us -> 10.6 us  [key_blocks(): lax.ppermute(pair, 'ctx', [(c, c + step) for c in range(cycle - step)])]
    all_to_all x1, starting transfers between devices: 6.51 us -> 7.67 us  [summed_terms(): lax.all_to_all(terms.reshape(cycle * owners, rows // owners, columns), ('...]
    pallas_call x1, Pallas kernels: 3.08 us -> 4.1 us  [attention(): pl.pallas_call(attention_kernel, out_shape=(jax.ShapeDtypeStruct(queries....]
  transfers between devices with their start and end apart: 13 -> 13, of which waited for: 6 -> 5; matrix products, arithmetic and copies ran while one was open for 3% -> 4% of each run, Pallas kernels for 21% -> 22%
where the time goes in v4:
time: 88.6 us; the launch traced here: 87.9 us
  starting transfers between devices  31.1 us (35%)
  waiting for transfers between devices  24.5 us (28%)
  Pallas kernels  19.6 us (22%)
  local copies, waits for them, and re-layouts  10.3 us (12%)
  other arithmetic  1.54 us (2%)
    pallas_call x1, Pallas kernels, tile_sums(): pl.pallas_call(tile_kernel, out_shape=jax.ShapeDtypeStruct((per_dev, rows...  10.6 us
    ppermute x3, starting transfers between devices, key_blocks(): lax.ppermute(pair, 'ctx', [(c, c + step) for c in range(cycle - step)])  10.6 us
    ppermute x7, waiting for transfers between devices, moved(): lax.ppermute(value, 'exp', [(e, e ^ steps[e % 2]) for e in range(owners)])  10.2 us
    unnamed x31, local copies, waits for them, and re-layouts  9.42 us
    all_to_all x2, waiting for transfers between devices, swapped(): return lax.all_to_all(value, 'exp', split_axis=0, concat_axis=0, tiled=True)  9.28 us
    all_to_all x1, starting transfers between devices, summed_terms(): lax.all_to_all(terms.reshape(cycle * owners, rows // owners, columns), ('...  7.67 us
    all_to_all x2, starting transfers between devices, swapped(): return lax.all_to_all(value, 'exp', split_axis=0, concat_axis=0, tiled=True)  7.06 us
    ppermute x7, starting transfers between devices, moved(): lax.ppermute(value, 'exp', [(e, e ^ steps[e % 2]) for e in range(owners)])  5.8 us
  transfers between devices with their start and end apart: 13, of which 5 were waited for; matrix products, arithmetic and copies ran while one was open for 4% of the time, Pallas kernels for 22%

profile of v4, /device:TPU:0, one launch (start us, length us, event | category | flops | bytes accessed | tf_op | source)
XLA Modules:
  0.0 87.9 jit_solution(12698031277710065588)
XLA Ops:
  0.6 3.0 %collective-permute-start.3 = (bf16[128,4096]{1,0:T(8,128)(2,1)}, bf16[128,4096]{1,0:T(8,128)(2,1)}, u32[]{:S(2)}, u32[]{:S(2)}) collective-permute-start(bf16[128,4096]{1,0:T(8,128)(2,1)} %refs_0_.1), channel_id=1, source_target_pairs={{0,4},{1,3},{2,6},{3,1},{4,0},{5,7},{6,2},{7,5},{8,12},{9,11},{10,... | collective-permute-start | bytes 3145736 | tf_op jit(solution)/shard_map/ppermute | solution.py:364
  3.7 0.7 convert_element_type.13
  4.3 1.5 %copy.20.hidden_ref = bf16[1,3,8,65,384]{4,3,2,1,0:T(8,128)(2,1)S(1)} copy(bf16[1,3,8,65,384]{4,2,3,1,0:T(8,128)(2,1)} %param.23) | data formatting | bytes 2396160 | tf_op args[11]
  5.8 0.0 copy-start.13
  5.9 0.0 copy-start.12
  5.9 0.8 fusion.1
  6.8 0.1 collective-permute-start.5
  6.8 3.6 %all-to-all-start = ((bf16[8,66,384]{2,1,0:T(8,128)(2,1)}), bf16[8,66,384]{2,1,0:T(8,128)(2,1)S(1)}, u32[]{:S(2)}, u32[]{:S(2)}) async-start(bf16[8,66,384]{2,1,0:T(8,128)(2,1)} %fusion.1), calls=%async_computation | async-start | bytes 884736 | tf_op jit(solution)/shard_map/all_to_all | solution.py:314
  10.5 0.9 constant_dynamic-slice_fusion
  11.4 6.2 %collective-permute-start.2 = (bf16[256,256]{1,0:T(8,128)(2,1)S(1)}, bf16[256,256]{1,0:T(8,128)(2,1)}, u32[]{:S(2)}, u32[]{:S(2)}) collective-permute-start(bf16[256,256]{1,0:T(8,128)(2,1)S(1)} %pad_maximum_fusion.rest_0_), channel_id=1, source_target_pairs={{0,24},{1,25},{2,26},{3,27},{4,28},{5,29},{6,30},{7,31}} | collective-permute-start | bytes 393224 | tf_op jit(solution)/shard_map/ppermute | solution.py:98
  17.5 1.9 %collective-permute-start.1 = (bf16[256,256]{1,0:T(8,128)(2,1)S(1)}, bf16[256,256]{1,0:T(8,128)(2,1)}, u32[]{:S(2)}, u32[]{:S(2)}) collective-permute-start(bf16[256,256]{1,0:T(8,128)(2,1)S(1)} %pad_maximum_fusion.rest_0_), channel_id=1, source_target_pairs={{0,16},{8,24},{1,17},{9,25},{2,18},{10,26},{3,19},{11,27},{4,20},{... | collective-permute-start | bytes 393224 | tf_op jit(solution)/shard_map/ppermute | solution.py:98
  19.5 2.5 %collective-permute-start = (bf16[256,256]{1,0:T(8,128)(2,1)S(1)}, bf16[256,256]{1,0:T(8,128)(2,1)}, u32[]{:S(2)}, u32[]{:S(2)}) collective-permute-start(bf16[256,256]{1,0:T(8,128)(2,1)S(1)} %pad_maximum_fusion.rest_0_), channel_id=1, source_target_pairs={{0,8},{8,16},{16,24},{1,9},{9,17},{17,25},{2,10},{10,18},{18,26},{... | collective-permute-start | bytes 393224 | tf_op jit(solution)/shard_map/ppermute | solution.py:98
  22.0 0.0 all-to-all-done.mixed_ref
  22.0 1.3 %picked.1 = bf16[8,64,384]{2,1,0:T(8,128)(2,1)} custom-call(s32[16]{0:T(128)S(1)} %copy-done.12, bf16[8,66,384]{2,1,0:T(8,128)(2,1)S(1)} %all-to-all-done.mixed_ref), custom_call_target="tpu_custom_call" | custom-call | tf_op jit(solution)/shard_map/picked/pallas_call | solution.py:179
  23.3 0.0 collective-permute-done.2.rest_3_
  23.3 0.3 collective-permute-done.1.rest_2_
  23.6 2.3 %collective-permute-done.rest_1_ = bf16[256,256]{1,0:T(8,128)(2,1)} collective-permute-done((bf16[256,256]{1,0:T(8,128)(2,1)S(1)}, bf16[256,256]{1,0:T(8,128)(2,1)}, u32[]{:S(2)}, u32[]{:S(2)}) %collective-permute-start) | collective-permute-done | bytes 131104 | tf_op jit(solution)/shard_map/ppermute | solution.py:98
  25.8 0.0 collective-permute-done.3.refs_2_
  25.8 0.0 collective-permute-start.4
  25.8 0.0 collective-permute-done.5.refs_1_
  25.8 0.0 copy-start.2
  25.8 1.0 %copy-done.2 = bf16[128,4096]{1,0:T(8,128)(2,1)} copy-done((bf16[128,4096]{1,0:T(8,128)(2,1)}, bf16[128,4096]{1,0:T(8,128)(2,1)S(1)}, u32[]{:S(2)}) %copy-start.2) | copy-done | bytes 1048600
  26.8 1.7 %collective-permute-start.6 = (bf16[128,4096]{1,0:T(8,128)(2,1)}, bf16[128,4096]{1,0:T(8,128)(2,1)}, u32[]{:S(2)}, u32[]{:S(2)}) collective-permute-start(bf16[128,4096]{1,0:T(8,128)(2,1)} %refs_0_.1), channel_id=1, source_target_pairs={{0,2},{1,5},{2,0},{3,7},{4,6},{5,1},{6,4},{7,3},{8,10},{9,13},{10,... | collective-permute-start | bytes 3145736 | tf_op jit(solution)/shard_map/ppermute | solution.py:364
  28.5 3.5 %all-to-all-start.2 = ((bf16[8,64,384]{2,1,0:T(8,128)(2,1)}), bf16[8,64,384]{2,1,0:T(8,128)(2,1)S(1)}, u32[]{:S(2)}, u32[]{:S(2)}) async-start(bf16[8,64,384]{2,1,0:T(8,128)(2,1)} %picked.1), calls=%async_computation.2 | async-start | bytes 786432 | tf_op jit(solution)/shard_map/all_to_all | solution.py:314
  31.9 0.0 collective-permute-done.4.refs_3_
  32.0 0.0 copy-start.9
  32.0 0.9 %copy-done.9 = bf16[256,512]{1,0:T(8,128)(2,1)S(1)} copy-done((bf16[256,512]{1,0:T(8,128)(2,1)S(1)}, bf16[256,512]{1,0:T(8,128)(2,1)}, u32[]{:S(2)}) %copy-start.9) | copy-done | bytes 262168
  32.9 4.1 %attention.1 = (bf16[256,512]{1,0:T(8,128)(2,1)}, bf16[4,256,256]{2,1,0:T(8,128)(2,1)S(1)}) custom-call(s32[1]{0:T(128)} %bitcast.place_ref, s32[4,4]{1,0:T(4,128)S(1)} %copy-done.11, bf16[256,512]{1,0:T(8,128)(2,1)S(1)} %copy-done.7, bf16[256,512]{1,0:T(8,128)(2,1)S(1)} %copy-done.8, bf16[256,512]{1,0:T(8,128)(2,1)S(1)} %copy-done.9, ...), custom_call_target="tpu_custom_call" | custom-call | tf_op jit(solution)/shard_map/attention/pallas_call | solution.py:108
  37.0 0.8 copy-done.6
  37.9 9.3 %all-to-all-done.2.side_ref = bf16[8,64,384]{2,1,0:T(8,128)(2,1)S(1)} async-done(((bf16[8,64,384]{2,1,0:T(8,128)(2,1)}), bf16[8,64,384]{2,1,0:T(8,128)(2,1)S(1)}, u32[]{:S(2)}, u32[]{:S(2)}) %all-to-all-start.2) | async-done | bytes 393248 | tf_op jit(solution)/shard_map/all_to_all | solution.py:314
  47.1 0.8 copy-done
  47.9 0.9 %collective-permute-start.8 = (bf16[128,4096]{1,0:T(8,128)(2,1)}, bf16[128,4096]{1,0:T(8,128)(2,1)}, u32[]{:S(2)}, u32[]{:S(2)}) collective-permute-start(bf16[128,4096]{1,0:T(8,128)(2,1)} %collective-permute-done.3.refs_2_), channel_id=1, source_target_pairs={{0,2},{1,5},{2,0},{3,7},{4,6},{5,1},{6,4},{7,3},{8,10},{9,13},{10,... | collective-permute-start | bytes 3145736 | tf_op jit(solution)/shard_map/ppermute | solution.py:364
  48.9 1.0 %copy-done.1 = bf16[8,64,384]{2,1,0:T(8,128)(2,1)S(1)} copy-done((bf16[8,64,384]{2,1,0:T(8,128)(2,1)S(1)}, bf16[8,64,384]{2,1,0:T(8,128)(2,1)}, u32[]{:S(2)}) %copy-start.1) | copy-done | bytes 393240
  49.9 2.8 %weighted.1.weight_ref = bf16[768,1024]{1,0:T(8,128)(2,1)S(1)} custom-call(s32[1]{0:T(128)} %bitcast.6.own_ref, s32[16]{0:T(128)S(1)} %copy-done.12, bf16[8,66,384]{2,1,0:T(8,128)(2,1)S(1)} %all-to-all-done.mixed_ref, bf16[1,3,8,65,384]{4,3,2,1,0:T(8,128)(2,1)S(1)} %copy.20.hidden_ref, bf16[8,64,384]{2,1,0:T(8,128)(2,1)S(1)} %copy-done.1), custom_call_target="tpu_custom_call" | custom-call | tf_op jit(solution)/shard_map/weighted/pallas_call | solution.py:231
  52.7 0.0 collective-permute-done.6.refs_4_
  52.7 0.1 collective-permute-start.7
  52.8 10.2 %collective-permute-done.8.refs_6_ = bf16[128,4096]{1,0:T(8,128)(2,1)} collective-permute-done((bf16[128,4096]{1,0:T(8,128)(2,1)}, bf16[128,4096]{1,0:T(8,128)(2,1)}, u32[]{:S(2)}, u32[]{:S(2)}) %collective-permute-start.8) | collective-permute-done | bytes 1048608 | tf_op jit(solution)/shard_map/ppermute | solution.py:364
  63.0 0.0 collective-permute-done.7.refs_5_
  63.0 1.0 %copy-done.4 = bf16[128,4096]{1,0:T(8,128)(2,1)} copy-done((bf16[128,4096]{1,0:T(8,128)(2,1)}, bf16[128,4096]{1,0:T(8,128)(2,1)S(1)}, u32[]{:S(2)}) %copy-start.4) | copy-done | bytes 1048600
  64.0 0.0 collective-permute-start.9
  64.0 7.7 %all-to-all-start.1 = ((bf16[32,32,256]{2,1,0:T(8,128)(2,1)}), bf16[32,32,256]{2,1,0:T(8,128)(2,1)S(1)}, u32[]{:S(2)}, u32[]{:S(2)}) async-start(bf16[32,32,256]{2,1,0:T(8,128)(2,1)} %bitcast.10), calls=%async_computation.1 | async-start | bytes 1048576 | tf_op jit(solution)/shard_map/all_to_all | solution.py:146
  71.7 0.0 collective-permute-done.9.refs_7_
  71.7 0.0 copy-start.3
  71.7 1.2 %copy-done.3 = bf16[128,4096]{1,0:T(8,128)(2,1)S(1)} copy-done((bf16[128,4096]{1,0:T(8,128)(2,1)S(1)}, bf16[128,4096]{1,0:T(8,128)(2,1)}, u32[]{:S(2)}) %copy-start.3) | copy-done | bytes 1048600
  72.9 1.2 %copy-done.5 = bf16[128,4096]{1,0:T(8,128)(2,1)S(1)} copy-done((bf16[128,4096]{1,0:T(8,128)(2,1)S(1)}, bf16[128,4096]{1,0:T(8,128)(2,1)}, u32[]{:S(2)}) %copy-start.5) | copy-done | bytes 1048600
  74.2 10.6 %tiles.1 = f32[2,384,4096]{2,1,0:T(8,128)} custom-call(bf16[768,1024]{1,0:T(8,128)(2,1)S(1)} %weighted.1.weight_ref, bf16[128,4096]{1,0:T(8,128)(2,1)} %refs_0_.1, bf16[128,4096]{1,0:T(8,128)(2,1)S(1)} %copy-done.3, bf16[128,4096]{1,0:T(8,128)(2,1)} %collective-permute-done.3.refs_2_, bf16[128,4096]{1,0:T(8,128)(2,1)} %collective-permute-done.4.refs_3_, ...), custom_call_target="tpu_custom_call" | custom-call | tf_op jit(solution)/shard_map/tiles/pallas_call | solution.py:297
  84.8 2.4 %all-to-all-done.1 = bf16[32,32,256]{2,1,0:T(8,128)(2,1)S(1)} async-done(((bf16[32,32,256]{2,1,0:T(8,128)(2,1)}), bf16[32,32,256]{2,1,0:T(8,128)(2,1)S(1)}, u32[]{:S(2)}, u32[]{:S(2)}) %all-to-all-start.1) | async-done | bytes 524320 | tf_op jit(solution)/shard_map/all_to_all | solution.py:146
  87.3 0.7 sums.1
  (20 shorter events, 0.1 us)
Async XLA Ops:
  0.6 25.2 %collective-permute-start.3 = (bf16[128,4096]{1,0:T(8,128)(2,1)}, bf16[128,4096]{1,0:T(8,128)(2,1)}, u32[]{:S(2)}, u32[]{:S(2)}) collective-permute-start(bf16[128,4096]{1,0:T(8,128)(2,1)} %refs_0_.1), channel_id=1, source_target_pairs={{0,4},{1,3},{2,6},{3,1},{4,0},{5,7},{6,2},{7,5},{8,12},{9,11},{10,... | collective-permute-start | bytes 3145736 | tf_op jit(solution)/shard_map/ppermute | solution.py:364
  4.3 1.5 %copy-start.14 = (s32[128,8]{0,1:T(8,128)S(1)}, s32[128,8]{0,1:T(8,128)}, u32[]{:S(2)}) copy-start(s32[128,8]{0,1:T(8,128)} %param.19) | copy-start | bytes 12292
  5.8 4.7 %copy-start.13 = (bf16[256,256]{1,0:T(8,128)(2,1)S(1)}, bf16[256,256]{1,0:T(8,128)(2,1)}, u32[]{:S(2)}) copy-start(bf16[256,256]{1,0:T(8,128)(2,1)} %param.14) | copy-start | bytes 393220
  5.9 16.1 %copy-start.12 = (s32[16]{0:T(128)S(1)}, s32[16]{0:T(128)}, u32[]{:S(2)}) copy-start(s32[16]{0:T(128)} %shadow_ref.3) | copy-start | bytes 196
  6.7 25.2 %copy-start.7 = (bf16[256,512]{1,0:T(8,128)(2,1)S(1)}, bf16[256,512]{1,0:T(8,128)(2,1)}, u32[]{:S(2)}) copy-start(bf16[256,512]{1,0:T(8,128)(2,1)} %query_ref.1) | copy-start | bytes 786436
  6.7 25.2 %copy-start.8 = (bf16[256,512]{1,0:T(8,128)(2,1)S(1)}, bf16[256,512]{1,0:T(8,128)(2,1)}, u32[]{:S(2)}) copy-start(bf16[256,512]{1,0:T(8,128)(2,1)} %grad_ref.1) | copy-start | bytes 786436
  6.7 25.2 %copy-start.10 = (f32[4,256]{1,0:T(4,128)S(1)}, f32[4,256]{1,0:T(4,128)}, u32[]{:S(2)}) copy-start(f32[4,256]{1,0:T(4,128)} %lse_ref.1) | copy-start | bytes 12292
  6.7 25.2 %copy-start.11 = (s32[4,4]{1,0:T(4,128)S(1)}, s32[4,4]{1,0:T(4,128)}, u32[]{:S(2)}) copy-start(s32[4,4]{1,0:T(4,128)} %mask_ref.1) | copy-start | bytes 196
  6.8 19.1 %collective-permute-start.5 = (bf16[128,4096]{1,0:T(8,128)(2,1)}, bf16[128,4096]{1,0:T(8,128)(2,1)S(1)}, u32[]{:S(2)}, u32[]{:S(2)}) collective-permute-start(bf16[128,4096]{1,0:T(8,128)(2,1)} %refs_0_.1), channel_id=1, source_target_pairs={{0,1},{1,0},{2,3},{3,2},{4,5},{5,4},{6,7},{7,6},{8,9},{9,8},{10,11... | collective-permute-start | bytes 3145736 | tf_op jit(solution)/shard_map/ppermute | solution.py:364
  6.8 15.1 %all-to-all-start = ((bf16[8,66,384]{2,1,0:T(8,128)(2,1)}), bf16[8,66,384]{2,1,0:T(8,128)(2,1)S(1)}, u32[]{:S(2)}, u32[]{:S(2)}) async-start(bf16[8,66,384]{2,1,0:T(8,128)(2,1)} %fusion.1), calls=%async_computation | async-start | bytes 884736 | tf_op jit(solution)/shard_map/all_to_all | solution.py:314
  11.4 11.9 %collective-permute-start.2 = (bf16[256,256]{1,0:T(8,128)(2,1)S(1)}, bf16[256,256]{1,0:T(8,128)(2,1)}, u32[]{:S(2)}, u32[]{:S(2)}) collective-permute-start(bf16[256,256]{1,0:T(8,128)(2,1)S(1)} %pad_maximum_fusion.rest_0_), channel_id=1, source_target_pairs={{0,24},{1,25},{2,26},{3,27},{4,28},{5,29},{6,30},{7,31}} | collective-permute-start | bytes 393224 | tf_op jit(solution)/shard_map/ppermute | solution.py:98
  17.5 6.0 %collective-permute-start.1 = (bf16[256,256]{1,0:T(8,128)(2,1)S(1)}, bf16[256,256]{1,0:T(8,128)(2,1)}, u32[]{:S(2)}, u32[]{:S(2)}) collective-permute-start(bf16[256,256]{1,0:T(8,128)(2,1)S(1)} %pad_maximum_fusion.rest_0_), channel_id=1, source_target_pairs={{0,16},{8,24},{1,17},{9,25},{2,18},{10,26},{3,19},{11,27},{4,20},{... | collective-permute-start | bytes 393224 | tf_op jit(solution)/shard_map/ppermute | solution.py:98
  19.5 6.4 %collective-permute-start = (bf16[256,256]{1,0:T(8,128)(2,1)S(1)}, bf16[256,256]{1,0:T(8,128)(2,1)}, u32[]{:S(2)}, u32[]{:S(2)}) collective-permute-start(bf16[256,256]{1,0:T(8,128)(2,1)S(1)} %pad_maximum_fusion.rest_0_), channel_id=1, source_target_pairs={{0,8},{8,16},{16,24},{1,9},{9,17},{17,25},{2,10},{10,18},{18,26},{... | collective-permute-start | bytes 393224 | tf_op jit(solution)/shard_map/ppermute | solution.py:98
  25.8 6.1 %collective-permute-start.4 = (bf16[128,4096]{1,0:T(8,128)(2,1)}, bf16[128,4096]{1,0:T(8,128)(2,1)}, u32[]{:S(2)}, u32[]{:S(2)}) collective-permute-start(bf16[128,4096]{1,0:T(8,128)(2,1)} %collective-permute-done.3.refs_2_), channel_id=1, source_target_pairs={{0,1},{1,0},{2,3},{3,2},{4,5},{5,4},{6,7},{7,6},{8,9},{9,8},{10,11... | collective-permute-start | bytes 3145736 | tf_op jit(solution)/shard_map/ppermute | solution.py:364
  25.8 1.0 %copy-start.2 = (bf16[128,4096]{1,0:T(8,128)(2,1)}, bf16[128,4096]{1,0:T(8,128)(2,1)S(1)}, u32[]{:S(2)}) copy-start(bf16[128,4096]{1,0:T(8,128)(2,1)S(1)} %collective-permute-done.5.refs_1_) | copy-start | bytes 3145732
  26.8 25.9 %collective-permute-start.6 = (bf16[128,4096]{1,0:T(8,128)(2,1)}, bf16[128,4096]{1,0:T(8,128)(2,1)}, u32[]{:S(2)}, u32[]{:S(2)}) collective-permute-start(bf16[128,4096]{1,0:T(8,128)(2,1)} %refs_0_.1), channel_id=1, source_target_pairs={{0,2},{1,5},{2,0},{3,7},{4,6},{5,1},{6,4},{7,3},{8,10},{9,13},{10,... | collective-permute-start | bytes 3145736 | tf_op jit(solution)/shard_map/ppermute | solution.py:364
  28.5 18.7 %all-to-all-start.2 = ((bf16[8,64,384]{2,1,0:T(8,128)(2,1)}), bf16[8,64,384]{2,1,0:T(8,128)(2,1)S(1)}, u32[]{:S(2)}, u32[]{:S(2)}) async-start(bf16[8,64,384]{2,1,0:T(8,128)(2,1)} %picked.1), calls=%async_computation.2 | async-start | bytes 786432 | tf_op jit(solution)/shard_map/all_to_all | solution.py:314
  32.0 1.0 %copy-start.9 = (bf16[256,512]{1,0:T(8,128)(2,1)S(1)}, bf16[256,512]{1,0:T(8,128)(2,1)}, u32[]{:S(2)}) copy-start(bf16[256,512]{1,0:T(8,128)(2,1)} %out_ref.1) | copy-start | bytes 786436
  37.0 0.8 copy-start.6
  47.1 0.8 copy-start
  47.9 15.1 %collective-permute-start.8 = (bf16[128,4096]{1,0:T(8,128)(2,1)}, bf16[128,4096]{1,0:T(8,128)(2,1)}, u32[]{:S(2)}, u32[]{:S(2)}) collective-permute-start(bf16[128,4096]{1,0:T(8,128)(2,1)} %collective-permute-done.3.refs_2_), channel_id=1, source_target_pairs={{0,2},{1,5},{2,0},{3,7},{4,6},{5,1},{6,4},{7,3},{8,10},{9,13},{10,... | collective-permute-start | bytes 3145736 | tf_op jit(solution)/shard_map/ppermute | solution.py:364
  48.9 1.0 %copy-start.1 = (bf16[8,64,384]{2,1,0:T(8,128)(2,1)S(1)}, bf16[8,64,384]{2,1,0:T(8,128)(2,1)}, u32[]{:S(2)}) copy-start(bf16[8,64,384]{2,1,0:T(8,128)(2,1)} %copy-done) | copy-start | bytes 1179652
  52.7 10.3 %collective-permute-start.7 = (bf16[128,4096]{1,0:T(8,128)(2,1)}, bf16[128,4096]{1,0:T(8,128)(2,1)S(1)}, u32[]{:S(2)}, u32[]{:S(2)}) collective-permute-start(bf16[128,4096]{1,0:T(8,128)(2,1)} %collective-permute-done.6.refs_4_), channel_id=1, source_target_pairs={{0,1},{1,0},{2,3},{3,2},{4,5},{5,4},{6,7},{7,6},{8,9},{9,8},{10,11... | collective-permute-start | bytes 3145736 | tf_op jit(solution)/shard_map/ppermute | solution.py:364
  63.0 1.0 %copy-start.4 = (bf16[128,4096]{1,0:T(8,128)(2,1)}, bf16[128,4096]{1,0:T(8,128)(2,1)S(1)}, u32[]{:S(2)}) copy-start(bf16[128,4096]{1,0:T(8,128)(2,1)S(1)} %collective-permute-done.7.refs_5_) | copy-start | bytes 3145732
  64.0 7.7 %collective-permute-start.9 = (bf16[128,4096]{1,0:T(8,128)(2,1)}, bf16[128,4096]{1,0:T(8,128)(2,1)}, u32[]{:S(2)}, u32[]{:S(2)}) collective-permute-start(bf16[128,4096]{1,0:T(8,128)(2,1)} %collective-permute-done.8.refs_6_), channel_id=1, source_target_pairs={{0,1},{1,0},{2,3},{3,2},{4,5},{5,4},{6,7},{7,6},{8,9},{9,8},{10,11... | collective-permute-start | bytes 3145736 | tf_op jit(solution)/shard_map/ppermute | solution.py:364
  64.0 23.2 %all-to-all-start.1 = ((bf16[32,32,256]{2,1,0:T(8,128)(2,1)}), bf16[32,32,256]{2,1,0:T(8,128)(2,1)S(1)}, u32[]{:S(2)}, u32[]{:S(2)}) async-start(bf16[32,32,256]{2,1,0:T(8,128)(2,1)} %bitcast.10), calls=%async_computation.1 | async-start | bytes 1048576 | tf_op jit(solution)/shard_map/all_to_all | solution.py:146
  71.7 1.2 %copy-start.3 = (bf16[128,4096]{1,0:T(8,128)(2,1)S(1)}, bf16[128,4096]{1,0:T(8,128)(2,1)}, u32[]{:S(2)}) copy-start(bf16[128,4096]{1,0:T(8,128)(2,1)} %copy-done.2) | copy-start | bytes 3145732
  72.9 1.2 %copy-start.5 = (bf16[128,4096]{1,0:T(8,128)(2,1)S(1)}, bf16[128,4096]{1,0:T(8,128)(2,1)}, u32[]{:S(2)}) copy-start(bf16[128,4096]{1,0:T(8,128)(2,1)} %copy-done.4) | copy-start | bytes 3145732

commit v5 on v4

--- a/solution.py
+++ b/solution.py
@@ -140,7 +140,7 @@
         value_ref[:, k * width : (k + 1) * width] = total[:, width:].astype(jnp.bfloat16)
 
 
-def summed_terms(terms, kv_columns, tiles):
+def summed_terms(terms, kv_columns):
     cycle, owners = lax.axis_size("ctx"), lax.axis_size("exp")
     rows, columns = terms.shape[1:]
     parts = lax.all_to_all(
@@ -150,10 +150,9 @@
         concat_axis=0,
         tiled=True,
     ).reshape(cycle, owners, rows // owners, columns)
-    parts, tiles = lax.optimization_barrier((parts, tiles))
     shape = (rows // owners, kv_columns)
     out = jax.ShapeDtypeStruct(shape, jnp.bfloat16)
-    key_grad, value_grad = pl.pallas_call(
+    return pl.pallas_call(
         sum_kernel,
         out_shape=(out, out),
         grid=(1,),
@@ -162,36 +161,27 @@
         compiler_params=pltpu.CompilerParams(vmem_limit_bytes=16 * 2**20),
         name="sums",
     )(parts)
-    return key_grad, value_grad, tiles
-
-
-def pick_kernel(per_dev, shadow_ref, mixed_ref, sent_ref):
-    for owner in range(sent_ref.shape[0]):
-        host = shadow_ref[owner * per_dev]
-        for j in range(1, per_dev):
-            host = jnp.maximum(host, shadow_ref[owner * per_dev + j])
-        sent_ref[owner] = mixed_ref[host, : sent_ref.shape[1]]
-
-
-def picked_rows(shadow_list, mixed, limit):
-    owners = mixed.shape[0]
-    whole = pl.BlockSpec(memory_space=pltpu.VMEM)
-    return pl.pallas_call(
-        functools.partial(pick_kernel, shadow_list.shape[0] // owners),
-        out_shape=jax.ShapeDtypeStruct((owners, limit, mixed.shape[2]), jnp.bfloat16),
-        in_specs=[pl.BlockSpec(memory_space=pltpu.SMEM), whole],
-        out_specs=whole,
-        compiler_params=pltpu.CompilerParams(vmem_limit_bytes=4 * 2**20),
-        name="picked",
-    )(shadow_list, mixed)
-
-
-def weight_kernel(orders, own_ref, shadow_ref, mixed_ref, hidden_ref, side_ref, weight_ref):
-    owners = mixed_ref.shape[0]
+
+
+def weight_kernel(orders, own_ref, shadow_ref, hidden_ref, *refs):
+    *payload_refs, weight_ref, side_ref = refs
+    owners = len(payload_refs)
     per_dev, units = hidden_ref.shape[1], hidden_ref.shape[4]
     tokens = weight_ref.shape[1] // owners
     limit = side_ref.shape[1]
     own = own_ref[0]
+    sources = [
+        own ^ jnp.where(own % 2 == 0, orders[0][i], orders[1][i]) for i in range(owners)
+    ]
+    host = shadow_ref[own * per_dev]
+    for j in range(1, per_dev):
+        host = jnp.maximum(host, shadow_ref[own * per_dev + j])
+    for source, payload_ref in zip(sources, payload_refs):
+
+        @pl.when(source == host)
+        def _(payload_ref=payload_ref):
+            side_ref[...] = payload_ref[:, :limit]
+
     earlier = (
         lax.broadcasted_iota(jnp.int32, (tokens, tokens), 0)
         < lax.broadcasted_iota(jnp.int32, (tokens, tokens), 1)
@@ -208,10 +198,9 @@
         chosen = jnp.where(jnp.logical_and(named, rank == place), 1.0, 0.0).astype(jnp.bfloat16)
         return lax.dot_general(rows, chosen, FIRST, preferred_element_type=jnp.float32)
 
-    for i in range(owners):
-        source = own ^ jnp.where(own % 2 == 0, orders[0][i], orders[1][i])
+    for i, (source, payload_ref) in enumerate(zip(sources, payload_refs)):
         for j in range(per_dev):
-            prob = mixed_ref[source, limit + j : limit + j + 1, :tokens].astype(jnp.float32)
+            prob = payload_ref[own, limit + j : limit + j + 1, :tokens].astype(jnp.float32)
             named = prob > 0
             flag = shadow_ref[own * per_dev + j] >= 0
             side = jnp.logical_and(jnp.logical_and(named, odd), flag)
@@ -224,26 +213,31 @@
             ).astype(jnp.bfloat16)
 
 
-def weighted_rows(own_index, shadow_list, mixed, hidden, shadow_rows, tokens, orders):
-    owners = mixed.shape[0]
+def weighted_rows(shadow_list, hidden, payloads, tokens, anchors):
+    owners = len(payloads)
+    own_index = lax.axis_index("exp")
     per_dev, units = shadow_list.shape[0] // owners, hidden.shape[4]
     shape = (per_dev * units, owners * tokens)
+    steps = block_steps(owners)
+    orders = [
+        [step ^ turn for pair in zip(steps[core], steps[1 - core]) for step, turn in zip(pair, (0, 1))]
+        for core in range(2)
+    ]
+    blocks, rows, lanes = payloads[0].shape
     return pl.pallas_call(
         functools.partial(weight_kernel, orders),
         out_shape=jax.ShapeDtypeStruct(shape, jnp.bfloat16),
         grid_spec=pltpu.PrefetchScalarGridSpec(
             num_scalar_prefetch=2,
             grid=(1,),
-            in_specs=[
-                full(mixed.shape),
-                full((1, per_dev) + hidden.shape[2:]),
-                full(shadow_rows.shape),
-            ],
+            in_specs=[full((1, per_dev) + hidden.shape[2:])]
+            + [full(payload.shape) for payload in payloads],
             out_specs=full(shape),
+            scratch_shapes=[pltpu.VMEM((blocks, rows - per_dev, lanes), jnp.bfloat16)],
         ),
         compiler_params=pltpu.CompilerParams(vmem_limit_bytes=32 * 2**20),
         name="weighted",
-    )(own_index.astype(jnp.int32)[None], shadow_list, mixed, hidden, shadow_rows)
+    )(own_index.astype(jnp.int32)[None], shadow_list, after(hidden, anchors), *payloads)
 
 
 def tile_kernel(weight_ref, *refs):
@@ -310,10 +304,6 @@
     )(weighted, *blocks)
 
 
-def swapped(value):
-    return lax.all_to_all(value, "exp", split_axis=0, concat_axis=0, tiled=True)
-
-
 def source_rows(expert_ids, route_probs, shadow_list, stored_hidden_state):
     owners = lax.axis_size("exp")
     tokens = expert_ids.shape[0]
@@ -335,18 +325,6 @@
     return jnp.concatenate([rows, jnp.pad(table, ((0, 0), (0, 0), (0, lanes - tokens)))], axis=1)
 
 
-def expert_rows(mixed, shadow_rows, shadow_list, stored_hidden_state, tokens):
-    steps = block_steps(lax.axis_size("exp"))
-    orders = [
-        [step ^ turn for pair in zip(steps[core], steps[1 - core]) for step, turn in zip(pair, (0, 1))]
-        for core in range(2)
-    ]
-    own_index = lax.axis_index("exp")
-    return weighted_rows(
-        own_index, shadow_list, mixed, stored_hidden_state, shadow_rows, tokens, orders
-    )
-
-
 def block_steps(owners):
     masks = [1 << bit for bit in range(1, owners.bit_length() - 1)]
     steps = []
@@ -370,6 +348,14 @@
 
 def beside(block):
     return moved(block, (1, 1))
+
+
+def near_and_far(block, anchor=None):
+    steps = block_steps(lax.axis_size("exp"))
+    first = moved(block, [held[1] for held in steps])
+    second = moved(block, [held[2] for held in steps])
+    far = moved(first if anchor is None else after(first, anchor), [held[2] for held in steps])
+    return [block, first, second, far]
 
 
 def all_blocks(held):
@@ -395,32 +381,26 @@
     shadow_list,
     stored_hidden_state,
 ):
-    steps = block_steps(lax.axis_size("exp"))
-    tokens = expert_ids.shape[0]
-    first = moved(moe_grad, [held[1] for held in steps])
     arrived = key_blocks(keys, values, queries.shape[1] // lse_excess.shape[0])
+    query_grad, terms = attention(
+        queries, arrived, attn_out, attn_out_grad, lse_excess, block_mask
+    )
+    key_grad, value_grad = summed_terms(terms, keys.shape[1])
+    *near, far = near_and_far(moe_grad, query_grad)
+    held = [(block, beside(after(block, query_grad))) for block in near]
     payload = source_rows(expert_ids, route_probs, shadow_list, stored_hidden_state)
-    own_beside = beside(after(moe_grad, payload))
-    mixed = swapped(payload)
-    second = moved(after(moe_grad, own_beside), [held[2] for held in steps])
+    payloads = all_blocks([(block, beside(block)) for block in near_and_far(payload)])
+    weighted = weighted_rows(
+        shadow_list,
+        stored_hidden_state,
+        payloads,
+        expert_ids.shape[0],
+        [block for _, block in held],
+    )
+    far = after(far, weighted, key_grad, value_grad)
+    blocks = all_blocks(held + [(far, beside(far))])
     per_dev = shadow_list.shape[0] // lax.axis_size("exp")
-    sent = after(picked_rows(shadow_list, mixed, payload.shape[1] - per_dev), arrived)
-    first_beside = beside(after(first, sent))
-    shadow_rows = swapped(sent)
-    far = moved(after(first, first_beside), [held[2] for held in steps])
-    query_grad, terms = attention(
-        queries, after(arrived, first_beside), attn_out, attn_out_grad, lse_excess, block_mask
-    )
-    weighted = expert_rows(
-        mixed, after(shadow_rows, query_grad), shadow_list, stored_hidden_state, tokens
-    )
-    second_beside = beside(after(second, weighted))
-    far = after(far, second_beside)
-    blocks = all_blocks(
-        [(moe_grad, own_beside), (first, first_beside), (second, second_beside), (far, beside(far))]
-    )
-    tiles = tile_sums(weighted, blocks, per_dev)
-    key_grad, value_grad, expert_grad = summed_terms(terms, keys.shape[1], tiles)
+    expert_grad = tile_sums(weighted, blocks, per_dev)
     return (query_grad, key_grad, value_grad, expert_grad)
 
 

time: 88.6 us -> 88.6 us (level)
  waiting for transfers between devices: 24.5 us -> 35.3 us
  local copies, waits for them, and re-layouts: 10.3 us -> 3.46 us
  starting transfers between devices: 31.1 us -> 28.3 us
    ppermute x7 -> x14, waiting for transfers between devices: 10.2 us -> 33.1 us  [moved(): lax.ppermute(value, 'exp', [(e, e ^ steps[e % 2]) for e in range(owners)])]
    unnamed x31 -> x19, local copies, waits for them, and re-layouts: 9.42 us -> 0.09 us
    all_to_all x2 -> x0, waiting for transfers between devices: 9.28 us -> none  [swapped(): return lax.all_to_all(value, 'exp', split_axis=0, concat_axis=0, tiled=True)]
    ppermute x7 -> x14, starting transfers between devices: 5.8 us -> 13.4 us  [moved(): lax.ppermute(value, 'exp', [(e, e ^ steps[e % 2]) for e in range(owners)])]
    all_to_all x2 -> x0, starting transfers between devices: 7.06 us -> none  [swapped(): return lax.all_to_all(value, 'exp', split_axis=0, concat_axis=0, tiled=True)]
    all_to_all x1, waiting for transfers between devices: 2.43 us -> 0.01 us  [summed_terms(): lax.all_to_all(terms.reshape(cycle * owners, rows // owners, columns), ('...]
    all_to_all x1, starting transfers between devices: 7.67 us -> 5.45 us  [summed_terms(): lax.all_to_all(terms.reshape(cycle * owners, rows // owners, columns), ('...]
    pallas_call x1, Pallas kernels: 2.85 us -> 4.59 us  [weighted_rows(): pl.pallas_call(functools.partial(weight_kernel, orders), out_shape=jax.Sh...]
  transfers between devices with their start and end apart: 13 -> 18, of which waited for: 5 -> 8; matrix products, arithmetic and copies ran while one was open for 4% -> 5% of each run, Pallas kernels for 22% -> 10%
where the time goes in v5:
time: 88.6 us; the launch traced here: 87.7 us
  waiting for transfers between devices  35.3 us (40%)
  starting transfers between devices  28.3 us (32%)
  Pallas kernels  19 us (21%)
  local copies, waits for them, and re-layouts  3.46 us (4%)
    ppermute x14, waiting for transfers between devices, moved(): lax.ppermute(value, 'exp', [(e, e ^ steps[e % 2]) for e in range(owners)])  33.1 us
    ppermute x14, starting transfers between devices, moved(): lax.ppermute(value, 'exp', [(e, e ^ steps[e % 2]) for e in range(owners)])  13.4 us
    pallas_call x1, Pallas kernels, tile_sums(): pl.pallas_call(tile_kernel, out_shape=jax.ShapeDtypeStruct((per_dev, rows...  10.6 us
    ppermute x3, starting transfers between devices, key_blocks(): lax.ppermute(pair, 'ctx', [(c, c + step) for c in range(cycle - step)])  9.41 us
    all_to_all x1, starting transfers between devices, summed_terms(): lax.all_to_all(terms.reshape(cycle * owners, rows // owners, columns), ('...  5.45 us
    pallas_call x1, Pallas kernels, weighted_rows(): pl.pallas_call(functools.partial(weight_kernel, orders), out_shape=jax.Sh...  4.59 us
    pallas_call x1, Pallas kernels, attention(): pl.pallas_call(attention_kernel, out_shape=(jax.ShapeDtypeStruct(queries....  3.08 us
    ppermute x3, waiting for transfers between devices, key_blocks(): lax.ppermute(pair, 'ctx', [(c, c + step) for c in range(cycle - step)])  2.21 us
  transfers between devices with their start and end apart: 18, of which 8 were waited for; matrix products, arithmetic and copies ran while one was open for 5% of the time, Pallas kernels for 10%

profile of v5, /device:TPU:0, one launch (start us, length us, event | category | flops | bytes accessed | tf_op | source)
XLA Modules:
  0.0 87.7 jit_solution(5293151773223798012)
XLA Ops:
  0.6 0.0 copy-start.8
  0.6 0.0 copy-start.6
  0.7 3.0 %collective-permute-start.4 = (bf16[128,4096]{1,0:T(8,128)(2,1)}, bf16[128,4096]{1,0:T(8,128)(2,1)S(1)}, u32[]{:S(2)}, u32[]{:S(2)}) collective-permute-start(bf16[128,4096]{1,0:T(8,128)(2,1)} %refs_0_.1), channel_id=1, source_target_pairs={{0,4},{1,3},{2,6},{3,1},{4,0},{5,7},{6,2},{7,5},{8,12},{9,11},{10,... | collective-permute-start | bytes 3145736 | tf_op jit(solution)/shard_map/ppermute | solution.py:342
  3.7 1.5 %collective-permute-start.6 = (bf16[128,4096]{1,0:T(8,128)(2,1)}, bf16[128,4096]{1,0:T(8,128)(2,1)}, u32[]{:S(2)}, u32[]{:S(2)}) collective-permute-start(bf16[128,4096]{1,0:T(8,128)(2,1)} %refs_0_.1), channel_id=1, source_target_pairs={{0,2},{1,5},{2,0},{3,7},{4,6},{5,1},{6,4},{7,3},{8,10},{9,13},{10,... | collective-permute-start | bytes 3145736 | tf_op jit(solution)/shard_map/ppermute | solution.py:342
  5.2 0.9 %constant_dynamic-slice_fusion = (bf16[256,128]{1,0:T(8,128)(2,1)S(1)}, bf16[256,128]{1,0:T(8,128)(2,1)S(1)}) fusion(bf16[256,256]{1,0:T(8,128)(2,1)} %param.14, s32[]{:T(128)S(6)} %select_n.14, bf16[256,256]{1,0:T(8,128)(2,1)} %param.13), kind=kLoop, calls=%fused_computation.7 | loop fusion | bytes 262148 | tf_op jit(solution)/shard_map/dynamic_slice | solution.py:93
  6.1 0.0 copy-start
  6.1 5.6 %collective-permute-start.2 = (bf16[256,256]{1,0:T(8,128)(2,1)S(1)}, bf16[256,256]{1,0:T(8,128)(2,1)S(1)}, u32[]{:S(2)}, u32[]{:S(2)}) collective-permute-start(bf16[256,256]{1,0:T(8,128)(2,1)S(1)} %pad_maximum_fusion.rest_0_), channel_id=1, source_target_pairs={{0,24},{1,25},{2,26},{3,27},{4,28},{5,29},{6,30},{7,31}} | collective-permute-start | bytes 393224 | tf_op jit(solution)/shard_map/ppermute | solution.py:98
  11.8 1.3 %collective-permute-start.1 = (bf16[256,256]{1,0:T(8,128)(2,1)S(1)}, bf16[256,256]{1,0:T(8,128)(2,1)S(1)}, u32[]{:S(2)}, u32[]{:S(2)}) collective-permute-start(bf16[256,256]{1,0:T(8,128)(2,1)S(1)} %pad_maximum_fusion.rest_0_), channel_id=1, source_target_pairs={{0,16},{8,24},{1,17},{9,25},{2,18},{10,26},{3,19},{11,27},{4,20},{... | collective-permute-start | bytes 393224 | tf_op jit(solution)/shard_map/ppermute | solution.py:98
  13.1 2.5 %collective-permute-start = (bf16[256,256]{1,0:T(8,128)(2,1)S(1)}, bf16[256,256]{1,0:T(8,128)(2,1)S(1)}, u32[]{:S(2)}, u32[]{:S(2)}) collective-permute-start(bf16[256,256]{1,0:T(8,128)(2,1)S(1)} %pad_maximum_fusion.rest_0_), channel_id=1, source_target_pairs={{0,8},{8,16},{16,24},{1,9},{9,17},{17,25},{2,10},{10,18},{18,26},{... | collective-permute-start | bytes 393224 | tf_op jit(solution)/shard_map/ppermute | solution.py:98
  15.6 0.7 convert_element_type.13
  16.3 1.0 %slice.3 = bf16[1,1,8,64,384]{4,2,3,1,0:T(8,128)(2,1)S(1)} slice(bf16[1,3,8,65,384]{4,2,3,1,0:T(8,128)(2,1)} %param.23), slice={[0:1], [2:3], [0:8], [0:64], [0:384]} | slice | bytes 786432 | tf_op jit(solution)/shard_map/slice | solution.py:322
  17.4 0.0 collective-permute-done.2.rest_3_
  17.4 0.8 collective-permute-done.1.rest_2_
  18.2 1.4 %collective-permute-done.rest_1_ = bf16[256,256]{1,0:T(8,128)(2,1)S(1)} collective-permute-done((bf16[256,256]{1,0:T(8,128)(2,1)S(1)}, bf16[256,256]{1,0:T(8,128)(2,1)S(1)}, u32[]{:S(2)}, u32[]{:S(2)}) %collective-permute-start) | collective-permute-done | bytes 131104 | tf_op jit(solution)/shard_map/ppermute | solution.py:98
  19.6 3.1 %attention.1 = (bf16[256,512]{1,0:T(8,128)(2,1)}, bf16[4,256,256]{2,1,0:T(8,128)(2,1)S(1)}) custom-call(s32[1]{0:T(128)} %bitcast.place_ref, s32[4,4]{1,0:T(4,128)S(1)} %copy-done.6, bf16[256,512]{1,0:T(8,128)(2,1)S(1)} %copy-done.2, bf16[256,512]{1,0:T(8,128)(2,1)S(1)} %copy-done.3, bf16[256,512]{1,0:T(8,128)(2,1)S(1)} %copy-done.4, ...), custom_call_target="tpu_custom_call" | custom-call | tf_op jit(solution)/shard_map/attention/pallas_call | solution.py:108
  22.7 0.0 collective-permute-start.3
  22.7 4.8 %collective-permute-done.4.refs_2_ = bf16[128,4096]{1,0:T(8,128)(2,1)S(1)} collective-permute-done((bf16[128,4096]{1,0:T(8,128)(2,1)}, bf16[128,4096]{1,0:T(8,128)(2,1)S(1)}, u32[]{:S(2)}, u32[]{:S(2)}) %collective-permute-start.4) | collective-permute-done | bytes 1048608 | tf_op jit(solution)/shard_map/ppermute | solution.py:342
  27.5 0.0 collective-permute-start.5
  27.5 0.0 collective-permute-done.6.refs_4_
  27.5 0.5 collective-permute-start.7
  28.1 1.5 %collective-permute-start.11 = (bf16[8,66,384]{2,1,0:T(8,128)(2,1)S(1)}, bf16[8,66,384]{2,1,0:T(8,128)(2,1)S(1)}, u32[]{:S(2)}, u32[]{:S(2)}) collective-permute-start(bf16[8,66,384]{2,1,0:T(8,128)(2,1)S(1)} %fusion.1.refs_0_), channel_id=1, source_target_pairs={{0,2},{1,5},{2,0},{3,7},{4,6},{5,1},{6,4},{7,3},{8,10},{9,13},{10,... | collective-permute-start | bytes 1216520 | tf_op jit(solution)/shard_map/ppermute | solution.py:342
  29.5 1.7 %collective-permute-start.9 = (bf16[8,66,384]{2,1,0:T(8,128)(2,1)S(1)}, bf16[8,66,384]{2,1,0:T(8,128)(2,1)}, u32[]{:S(2)}, u32[]{:S(2)}) collective-permute-start(bf16[8,66,384]{2,1,0:T(8,128)(2,1)S(1)} %fusion.1.refs_0_), channel_id=1, source_target_pairs={{0,4},{1,3},{2,6},{3,1},{4,0},{5,7},{6,2},{7,5},{8,12},{9,11},{10,... | collective-permute-start | bytes 1216520 | tf_op jit(solution)/shard_map/ppermute | solution.py:342
  31.2 8.8 %collective-permute-done.11.refs_4_ = bf16[8,66,384]{2,1,0:T(8,128)(2,1)S(1)} collective-permute-done((bf16[8,66,384]{2,1,0:T(8,128)(2,1)S(1)}, bf16[8,66,384]{2,1,0:T(8,128)(2,1)S(1)}, u32[]{:S(2)}, u32[]{:S(2)}) %collective-permute-start.11) | collective-permute-done | bytes 405536 | tf_op jit(solution)/shard_map/ppermute | solution.py:342
  40.0 2.2 %collective-permute-start.15 = (bf16[128,4096]{1,0:T(8,128)(2,1)S(1)}, bf16[128,4096]{1,0:T(8,128)(2,1)}, u32[]{:S(2)}, u32[]{:S(2)}) collective-permute-start(bf16[128,4096]{1,0:T(8,128)(2,1)S(1)} %collective-permute-done.4.refs_2_), channel_id=1, source_target_pairs={{0,2},{1,5},{2,0},{3,7},{4,6},{5,1},{6,4},{7,3},{8,10},{9,13},{10,... | collective-permute-start | bytes 3145736 | tf_op jit(solution)/shard_map/ppermute | solution.py:342
  42.2 5.5 %all-to-all-start = ((bf16[32,32,256]{2,1,0:T(8,128)(2,1)}), bf16[32,32,256]{2,1,0:T(8,128)(2,1)S(1)}, u32[]{:S(2)}, u32[]{:S(2)}) async-start(bf16[32,32,256]{2,1,0:T(8,128)(2,1)} %bitcast.11), calls=%async_computation | async-start | bytes 1048576 | tf_op jit(solution)/shard_map/all_to_all | solution.py:146
  47.7 0.0 copy-start.7
  47.7 0.0 collective-permute-done.9.refs_2_
  47.7 1.8 %collective-permute-start.13 = (bf16[8,66,384]{2,1,0:T(8,128)(2,1)}, bf16[8,66,384]{2,1,0:T(8,128)(2,1)}, u32[]{:S(2)}, u32[]{:S(2)}) collective-permute-start(bf16[8,66,384]{2,1,0:T(8,128)(2,1)} %collective-permute-done.9.refs_2_), channel_id=1, source_target_pairs={{0,2},{1,5},{2,0},{3,7},{4,6},{5,1},{6,4},{7,3},{8,10},{9,13},{10,... | collective-permute-start | bytes 1216520 | tf_op jit(solution)/shard_map/ppermute | solution.py:342
  49.6 15.9 %collective-permute-done.13.refs_6_ = bf16[8,66,384]{2,1,0:T(8,128)(2,1)} collective-permute-done((bf16[8,66,384]{2,1,0:T(8,128)(2,1)}, bf16[8,66,384]{2,1,0:T(8,128)(2,1)}, u32[]{:S(2)}, u32[]{:S(2)}) %collective-permute-start.13) | collective-permute-done | bytes 405536 | tf_op jit(solution)/shard_map/ppermute | solution.py:342
  65.5 0.0 collective-permute-start.8
  65.5 0.0 collective-permute-done.3.refs_1_
  65.5 0.5 collective-permute-start.10
  66.0 0.0 collective-permute-done.5.refs_3_
  66.0 0.1 collective-permute-start.12
  66.1 0.0 collective-permute-done.7.refs_5_
  66.1 0.4 collective-permute-start.14
  66.5 0.0 all-to-all-done
  66.5 0.7 sums.1
  67.2 1.5 %copy.21.hidden_ref = bf16[1,3,8,65,384]{4,3,2,1,0:T(8,128)(2,1)S(1)} copy(bf16[1,3,8,65,384]{4,2,3,1,0:T(8,128)(2,1)} %param.23) | data formatting | bytes 2396160 | tf_op jit(solution)/shard_map/optimization_barrier | solution.py:346
  68.7 0.0 collective-permute-done.8.refs_1_
  68.7 0.6 collective-permute-done.12.refs_5_
  69.2 0.0 collective-permute-done.10.refs_3_
  69.2 0.3 collective-permute-done.14.refs_7_
  69.5 4.6 %weighted.1.weight_ref = bf16[768,1024]{1,0:T(8,128)(2,1)S(1)} custom-call(s32[1]{0:T(128)} %bitcast.3.own_ref, s32[16]{0:T(128)S(1)} %copy-done.7, bf16[1,3,8,65,384]{4,3,2,1,0:T(8,128)(2,1)S(1)} %copy.21.hidden_ref, bf16[8,66,384]{2,1,0:T(8,128)(2,1)S(1)} %fusion.1.refs_0_, bf16[8,66,384]{2,1,0:T(8,128)(2,1)} %collective-permute-done.8.refs_1_, ...), custom_call_target="tpu_custom_call" | custom-call | tf_op jit(solution)/shard_map/weighted/pallas_call | solution.py:227
  74.1 0.0 collective-permute-done.15.refs_6_
  74.1 0.2 collective-permute-start.16
  74.3 2.7 %collective-permute-done.16.refs_7_ = bf16[128,4096]{1,0:T(8,128)(2,1)S(1)} collective-permute-done((bf16[128,4096]{1,0:T(8,128)(2,1)}, bf16[128,4096]{1,0:T(8,128)(2,1)S(1)}, u32[]{:S(2)}, u32[]{:S(2)}) %collective-permute-start.16) | collective-permute-done | bytes 1048608 | tf_op jit(solution)/shard_map/ppermute | solution.py:342
  77.1 10.6 %tiles.1 = f32[2,384,4096]{2,1,0:T(8,128)} custom-call(bf16[768,1024]{1,0:T(8,128)(2,1)S(1)} %weighted.1.weight_ref, bf16[128,4096]{1,0:T(8,128)(2,1)S(1)} %copy-done, bf16[128,4096]{1,0:T(8,128)(2,1)} %collective-permute-done.3.refs_1_, bf16[128,4096]{1,0:T(8,128)(2,1)S(1)} %collective-permute-done.4.refs_2_, ...), custom_call_target="tpu_custom_call" | custom-call | tf_op jit(solution)/shard_map/tiles/pallas_call | solution.py:291
  (18 shorter events, 0.2 us)
Async XLA Ops:
  0.6 16.7 %copy-start.8 = (s32[128,8]{0,1:T(8,128)S(1)}, s32[128,8]{0,1:T(8,128)}, u32[]{:S(2)}) copy-start(s32[128,8]{0,1:T(8,128)} %param.19) | copy-start | bytes 12292
  0.6 19.0 %copy-start.6 = (s32[4,4]{1,0:T(4,128)S(1)}, s32[4,4]{1,0:T(4,128)}, u32[]{:S(2)}) copy-start(s32[4,4]{1,0:T(4,128)} %mask_ref.1) | copy-start | bytes 196
  0.7 19.0 %copy-start.5 = (f32[4,256]{1,0:T(4,128)S(1)}, f32[4,256]{1,0:T(4,128)}, u32[]{:S(2)}) copy-start(f32[4,256]{1,0:T(4,128)} %lse_ref.1) | copy-start | bytes 12292
  0.7 19.0 %copy-start.3 = (bf16[256,512]{1,0:T(8,128)(2,1)S(1)}, bf16[256,512]{1,0:T(8,128)(2,1)}, u32[]{:S(2)}) copy-start(bf16[256,512]{1,0:T(8,128)(2,1)} %grad_ref.1) | copy-start | bytes 786436
  0.7 19.0 %copy-start.4 = (bf16[256,512]{1,0:T(8,128)(2,1)S(1)}, bf16[256,512]{1,0:T(8,128)(2,1)}, u32[]{:S(2)}) copy-start(bf16[256,512]{1,0:T(8,128)(2,1)} %out_ref.1) | copy-start | bytes 786436
  0.7 19.0 %copy-start.2 = (bf16[256,512]{1,0:T(8,128)(2,1)S(1)}, bf16[256,512]{1,0:T(8,128)(2,1)}, u32[]{:S(2)}) copy-start(bf16[256,512]{1,0:T(8,128)(2,1)} %query_ref.1) | copy-start | bytes 786436
  0.7 26.8 %collective-permute-start.4 = (bf16[128,4096]{1,0:T(8,128)(2,1)}, bf16[128,4096]{1,0:T(8,128)(2,1)S(1)}, u32[]{:S(2)}, u32[]{:S(2)}) collective-permute-start(bf16[128,4096]{1,0:T(8,128)(2,1)} %refs_0_.1), channel_id=1, source_target_pairs={{0,4},{1,3},{2,6},{3,1},{4,0},{5,7},{6,2},{7,5},{8,12},{9,11},{10,... | collective-permute-start | bytes 3145736 | tf_op jit(solution)/shard_map/ppermute | solution.py:342
  3.7 23.8 %collective-permute-start.6 = (bf16[128,4096]{1,0:T(8,128)(2,1)}, bf16[128,4096]{1,0:T(8,128)(2,1)}, u32[]{:S(2)}, u32[]{:S(2)}) collective-permute-start(bf16[128,4096]{1,0:T(8,128)(2,1)} %refs_0_.1), channel_id=1, source_target_pairs={{0,2},{1,5},{2,0},{3,7},{4,6},{5,1},{6,4},{7,3},{8,10},{9,13},{10,... | collective-permute-start | bytes 3145736 | tf_op jit(solution)/shard_map/ppermute | solution.py:342
  6.1 16.6 %copy-start = (bf16[128,4096]{1,0:T(8,128)(2,1)S(1)}, bf16[128,4096]{1,0:T(8,128)(2,1)}, u32[]{:S(2)}) copy-start(bf16[128,4096]{1,0:T(8,128)(2,1)} %refs_0_.1) | copy-start | bytes 3145732
  6.1 11.3 %collective-permute-start.2 = (bf16[256,256]{1,0:T(8,128)(2,1)S(1)}, bf16[256,256]{1,0:T(8,128)(2,1)S(1)}, u32[]{:S(2)}, u32[]{:S(2)}) collective-permute-start(bf16[256,256]{1,0:T(8,128)(2,1)S(1)} %pad_maximum_fusion.rest_0_), channel_id=1, source_target_pairs={{0,24},{1,25},{2,26},{3,27},{4,28},{5,29},{6,30},{7,31}} | collective-permute-start | bytes 393224 | tf_op jit(solution)/shard_map/ppermute | solution.py:98
  11.8 6.4 %collective-permute-start.1 = (bf16[256,256]{1,0:T(8,128)(2,1)S(1)}, bf16[256,256]{1,0:T(8,128)(2,1)S(1)}, u32[]{:S(2)}, u32[]{:S(2)}) collective-permute-start(bf16[256,256]{1,0:T(8,128)(2,1)S(1)} %pad_maximum_fusion.rest_0_), channel_id=1, source_target_pairs={{0,16},{8,24},{1,17},{9,25},{2,18},{10,26},{3,19},{11,27},{4,20},{... | collective-permute-start | bytes 393224 | tf_op jit(solution)/shard_map/ppermute | solution.py:98
  13.1 6.5 %collective-permute-start = (bf16[256,256]{1,0:T(8,128)(2,1)S(1)}, bf16[256,256]{1,0:T(8,128)(2,1)S(1)}, u32[]{:S(2)}, u32[]{:S(2)}) collective-permute-start(bf16[256,256]{1,0:T(8,128)(2,1)S(1)} %pad_maximum_fusion.rest_0_), channel_id=1, source_target_pairs={{0,8},{8,16},{16,24},{1,9},{9,17},{17,25},{2,10},{10,18},{18,26},{... | collective-permute-start | bytes 393224 | tf_op jit(solution)/shard_map/ppermute | solution.py:98
  22.7 19.5 %copy-start.1 = (bf16[4,256,256]{2,1,0:T(8,128)(2,1)}, bf16[4,256,256]{2,1,0:T(8,128)(2,1)S(1)}, u32[]{:S(2)}) copy-start(bf16[4,256,256]{2,1,0:T(8,128)(2,1)S(1)} %get-tuple-element.14) | copy-start | bytes 1572868
  22.7 42.8 %collective-permute-start.3 = (bf16[128,4096]{1,0:T(8,128)(2,1)S(1)}, bf16[128,4096]{1,0:T(8,128)(2,1)}, u32[]{:S(2)}, u32[]{:S(2)}) collective-permute-start(bf16[128,4096]{1,0:T(8,128)(2,1)S(1)} %copy-done), channel_id=1, source_target_pairs={{0,1},{1,0},{2,3},{3,2},{4,5},{5,4},{6,7},{7,6},{8,9},{9,8},{10,11... | collective-permute-start | bytes 3145736 | tf_op jit(solution)/shard_map/ppermute | solution.py:342
  27.5 38.5 %collective-permute-start.5 = (bf16[128,4096]{1,0:T(8,128)(2,1)S(1)}, bf16[128,4096]{1,0:T(8,128)(2,1)}, u32[]{:S(2)}, u32[]{:S(2)}) collective-permute-start(bf16[128,4096]{1,0:T(8,128)(2,1)S(1)} %collective-permute-done.4.refs_2_), channel_id=1, source_target_pairs={{0,1},{1,0},{2,3},{3,2},{4,5},{5,4},{6,7},{7,6},{8,9},{9,8},{10,11... | collective-permute-start | bytes 3145736 | tf_op jit(solution)/shard_map/ppermute | solution.py:342
  27.5 38.5 %collective-permute-start.7 = (bf16[128,4096]{1,0:T(8,128)(2,1)}, bf16[128,4096]{1,0:T(8,128)(2,1)}, u32[]{:S(2)}, u32[]{:S(2)}) collective-permute-start(bf16[128,4096]{1,0:T(8,128)(2,1)} %collective-permute-done.6.refs_4_), channel_id=1, source_target_pairs={{0,1},{1,0},{2,3},{3,2},{4,5},{5,4},{6,7},{7,6},{8,9},{9,8},{10,11... | collective-permute-start | bytes 3145736 | tf_op jit(solution)/shard_map/ppermute | solution.py:342
  28.1 12.0 %collective-permute-start.11 = (bf16[8,66,384]{2,1,0:T(8,128)(2,1)S(1)}, bf16[8,66,384]{2,1,0:T(8,128)(2,1)S(1)}, u32[]{:S(2)}, u32[]{:S(2)}) collective-permute-start(bf16[8,66,384]{2,1,0:T(8,128)(2,1)S(1)} %fusion.1.refs_0_), channel_id=1, source_target_pairs={{0,2},{1,5},{2,0},{3,7},{4,6},{5,1},{6,4},{7,3},{8,10},{9,13},{10,... | collective-permute-start | bytes 1216520 | tf_op jit(solution)/shard_map/ppermute | solution.py:342
  29.5 18.2 %collective-permute-start.9 = (bf16[8,66,384]{2,1,0:T(8,128)(2,1)S(1)}, bf16[8,66,384]{2,1,0:T(8,128)(2,1)}, u32[]{:S(2)}, u32[]{:S(2)}) collective-permute-start(bf16[8,66,384]{2,1,0:T(8,128)(2,1)S(1)} %fusion.1.refs_0_), channel_id=1, source_target_pairs={{0,4},{1,3},{2,6},{3,1},{4,0},{5,7},{6,2},{7,5},{8,12},{9,11},{10,... | collective-permute-start | bytes 1216520 | tf_op jit(solution)/shard_map/ppermute | solution.py:342
  40.0 34.1 %collective-permute-start.15 = (bf16[128,4096]{1,0:T(8,128)(2,1)S(1)}, bf16[128,4096]{1,0:T(8,128)(2,1)}, u32[]{:S(2)}, u32[]{:S(2)}) collective-permute-start(bf16[128,4096]{1,0:T(8,128)(2,1)S(1)} %collective-permute-done.4.refs_2_), channel_id=1, source_target_pairs={{0,2},{1,5},{2,0},{3,7},{4,6},{5,1},{6,4},{7,3},{8,10},{9,13},{10,... | collective-permute-start | bytes 3145736 | tf_op jit(solution)/shard_map/ppermute | solution.py:342
  42.2 24.3 %all-to-all-start = ((bf16[32,32,256]{2,1,0:T(8,128)(2,1)}), bf16[32,32,256]{2,1,0:T(8,128)(2,1)S(1)}, u32[]{:S(2)}, u32[]{:S(2)}) async-start(bf16[32,32,256]{2,1,0:T(8,128)(2,1)} %bitcast.11), calls=%async_computation | async-start | bytes 1048576 | tf_op jit(solution)/shard_map/all_to_all | solution.py:146
  47.7 21.8 %copy-start.7 = (s32[16]{0:T(128)S(1)}, s32[16]{0:T(128)}, u32[]{:S(2)}) copy-start(s32[16]{0:T(128)} %shadow_ref.1) | copy-start | bytes 196
  47.7 17.8 %collective-permute-start.13 = (bf16[8,66,384]{2,1,0:T(8,128)(2,1)}, bf16[8,66,384]{2,1,0:T(8,128)(2,1)}, u32[]{:S(2)}, u32[]{:S(2)}) collective-permute-start(bf16[8,66,384]{2,1,0:T(8,128)(2,1)} %collective-permute-done.9.refs_2_), channel_id=1, source_target_pairs={{0,2},{1,5},{2,0},{3,7},{4,6},{5,1},{6,4},{7,3},{8,10},{9,13},{10,... | collective-permute-start | bytes 1216520 | tf_op jit(solution)/shard_map/ppermute | solution.py:342
  65.5 3.2 %collective-permute-start.8 = (bf16[8,66,384]{2,1,0:T(8,128)(2,1)S(1)}, bf16[8,66,384]{2,1,0:T(8,128)(2,1)}, u32[]{:S(2)}, u32[]{:S(2)}) collective-permute-start(bf16[8,66,384]{2,1,0:T(8,128)(2,1)S(1)} %fusion.1.refs_0_), channel_id=1, source_target_pairs={{0,1},{1,0},{2,3},{3,2},{4,5},{5,4},{6,7},{7,6},{8,9},{9,8},{10,11... | collective-permute-start | bytes 1216520 | tf_op jit(solution)/shard_map/ppermute | solution.py:342
  65.5 3.7 %collective-permute-start.10 = (bf16[8,66,384]{2,1,0:T(8,128)(2,1)}, bf16[8,66,384]{2,1,0:T(8,128)(2,1)}, u32[]{:S(2)}, u32[]{:S(2)}) collective-permute-start(bf16[8,66,384]{2,1,0:T(8,128)(2,1)} %collective-permute-done.9.refs_2_), channel_id=1, source_target_pairs={{0,1},{1,0},{2,3},{3,2},{4,5},{5,4},{6,7},{7,6},{8,9},{9,8},{10,11... | collective-permute-start | bytes 1216520 | tf_op jit(solution)/shard_map/ppermute | solution.py:342
  66.0 3.2 %collective-permute-start.12 = (bf16[8,66,384]{2,1,0:T(8,128)(2,1)S(1)}, bf16[8,66,384]{2,1,0:T(8,128)(2,1)}, u32[]{:S(2)}, u32[]{:S(2)}) collective-permute-start(bf16[8,66,384]{2,1,0:T(8,128)(2,1)S(1)} %collective-permute-done.11.refs_4_), channel_id=1, source_target_pairs={{0,1},{1,0},{2,3},{3,2},{4,5},{5,4},{6,7},{7,6},{8,9},{9,8},{10,11... | collective-permute-start | bytes 1216520 | tf_op jit(solution)/shard_map/ppermute | solution.py:342
  66.1 3.4 %collective-permute-start.14 = (bf16[8,66,384]{2,1,0:T(8,128)(2,1)}, bf16[8,66,384]{2,1,0:T(8,128)(2,1)}, u32[]{:S(2)}, u32[]{:S(2)}) collective-permute-start(bf16[8,66,384]{2,1,0:T(8,128)(2,1)} %collective-permute-done.13.refs_6_), channel_id=1, source_target_pairs={{0,1},{1,0},{2,3},{3,2},{4,5},{5,4},{6,7},{7,6},{8,9},{9,8},{10,11... | collective-permute-start | bytes 1216520 | tf_op jit(solution)/shard_map/ppermute | solution.py:342
  74.1 2.9 %collective-permute-start.16 = (bf16[128,4096]{1,0:T(8,128)(2,1)}, bf16[128,4096]{1,0:T(8,128)(2,1)S(1)}, u32[]{:S(2)}, u32[]{:S(2)}) collective-permute-start(bf16[128,4096]{1,0:T(8,128)(2,1)} %collective-permute-done.15.refs_6_), channel_id=1, source_target_pairs={{0,1},{1,0},{2,3},{3,2},{4,5},{5,4},{6,7},{7,6},{8,9},{9,8},{10,11... | collective-permute-start | bytes 3145736 | tf_op jit(solution)/shard_map/ppermute | solution.py:342

commit v6 on v4

--- a/solution.py
+++ b/solution.py
@@ -20,7 +20,8 @@
     place_ref, mask_ref, query_ref, grad_ref, out_ref, lse_ref, *rest
 ):
     cycle = mask_ref.shape[0]
-    pair_refs, (query_grad_ref, terms_ref, sums_ref, pairs_ref) = rest[:cycle], rest[cycle:]
+    pair_refs, query_grad_ref, term_refs = rest[:cycle], rest[cycle], rest[cycle + 1 : -3]
+    sums_ref, pairs_ref, terms_ref = rest[-3:]
     rows, width = pairs_ref.shape[1], pairs_ref.shape[2] // 2
     heads = lse_ref.shape[0]
     scale = 1.0 / math.sqrt(width)
@@ -62,23 +63,26 @@
         value_term = jnp.dot(
             jnp.concatenate(probs, axis=1), grads, preferred_element_type=jnp.float32
         )
-        terms_ref[mine - step, :, :width] = key_term.astype(jnp.bfloat16)
-        terms_ref[mine - step, :, width:] = value_term.astype(jnp.bfloat16)
+        terms_ref[step, :, :width] = key_term.astype(jnp.bfloat16)
+        terms_ref[step, :, width:] = value_term.astype(jnp.bfloat16)
 
     block(0, True)
 
-    @pl.loop(0, cycle)
-    def _(source):
-        seen = jnp.logical_and(source < mine, mask_ref[mine, source] > 0)
+    @pl.loop(1, cycle)
+    def _(step):
+        source = mine - step
+        seen = jnp.logical_and(source >= 0, mask_ref[mine, jnp.maximum(source, 0)] > 0)
 
         @pl.when(seen)
         def _():
-            block(mine - source, False)
-
-        @pl.when(jnp.logical_and(source != mine, jnp.logical_not(seen)))
+            block(step, False)
+
+        @pl.when(jnp.logical_not(seen))
         def _():
-            terms_ref[source] = jnp.zeros_like(terms_ref[source])
-
+            terms_ref[step] = jnp.zeros_like(terms_ref[step])
+
+    for step, term_ref in enumerate(term_refs):
+        term_ref[...] = terms_ref[step]
     query_grad_ref[...] = sums_ref[...].astype(jnp.bfloat16)
 
 
@@ -105,51 +109,59 @@
     mine = lax.axis_index("ctx")
     pair = arrived[0]
     operands = (queries, attn_out_grad, attn_out, lse_excess, *arrived)
-    return pl.pallas_call(
+    query_grad, *terms = pl.pallas_call(
         attention_kernel,
-        out_shape=(
-            jax.ShapeDtypeStruct(queries.shape, jnp.bfloat16),
-            jax.ShapeDtypeStruct((cycle,) + pair.shape, jnp.bfloat16),
-        ),
+        out_shape=[jax.ShapeDtypeStruct(queries.shape, jnp.bfloat16)]
+        + [jax.ShapeDtypeStruct(pair.shape, jnp.bfloat16)] * cycle,
         grid_spec=pltpu.PrefetchScalarGridSpec(
             num_scalar_prefetch=2,
             grid=(1,),
             in_specs=[full(operand.shape) for operand in operands],
-            out_specs=(full(queries.shape), full((cycle,) + pair.shape)),
+            out_specs=[full(queries.shape)] + [full(pair.shape)] * cycle,
             scratch_shapes=[
                 pltpu.VMEM(queries.shape, jnp.float32),
+                pltpu.VMEM((cycle,) + pair.shape, jnp.bfloat16),
                 pltpu.VMEM((cycle,) + pair.shape, jnp.bfloat16),
             ],
         ),
         compiler_params=pltpu.CompilerParams(vmem_limit_bytes=32 * 2**20),
         name="attention",
     )(mine.astype(jnp.int32)[None], block_mask, *operands)
+    return query_grad, terms
 
 
 def sum_kernel(parts_ref, key_ref, value_ref):
-    cycle, owners, rows, columns = parts_ref.shape
+    owners, rows, columns = parts_ref.shape
     kv_count = key_ref.shape[1] * 2 // columns
     group = owners // kv_count
     width = columns // 2
     for k in range(kv_count):
         total = jnp.zeros((rows, columns), jnp.float32)
-        for c in range(cycle):
-            for e in range(k * group, (k + 1) * group):
-                total += parts_ref[c, e].astype(jnp.float32)
+        for e in range(k * group, (k + 1) * group):
+            total += parts_ref[e].astype(jnp.float32)
         key_ref[:, k * width : (k + 1) * width] = total[:, :width].astype(jnp.bfloat16)
         value_ref[:, k * width : (k + 1) * width] = total[:, width:].astype(jnp.bfloat16)
 
 
-def summed_terms(terms, kv_columns, tiles):
-    cycle, owners = lax.axis_size("ctx"), lax.axis_size("exp")
-    rows, columns = terms.shape[1:]
+def block_terms(terms):
+    cycle = lax.axis_size("ctx")
+    total = terms[0].astype(jnp.float32)
+    for step in range(1, cycle):
+        pairs = [(c, c - step) for c in range(step, cycle)]
+        total = total + lax.ppermute(terms[step], "ctx", pairs).astype(jnp.float32)
+    return total.astype(jnp.bfloat16)
+
+
+def summed_terms(total, kv_columns, tiles):
+    owners = lax.axis_size("exp")
+    rows, columns = total.shape
     parts = lax.all_to_all(
-        terms.reshape(cycle * owners, rows // owners, columns),
-        ("ctx", "exp"),
+        total.reshape(owners, rows // owners, columns),
+        "exp",
         split_axis=0,
         concat_axis=0,
         tiled=True,
-    ).reshape(cycle, owners, rows // owners, columns)
+    )
     parts, tiles = lax.optimization_barrier((parts, tiles))
     shape = (rows // owners, kv_columns)
     out = jax.ShapeDtypeStruct(shape, jnp.bfloat16)
@@ -246,20 +258,21 @@
     )(own_index.astype(jnp.int32)[None], shadow_list, mixed, hidden, shadow_rows)
 
 
-def tile_kernel(weight_ref, *refs):
-    *block_refs, tile_ref, gathered_ref, held_ref, in_sems, out_sems = refs
-    per_dev, units, model = tile_ref.shape
+def tile_kernel(start, count, weight_ref, *refs):
+    block_refs = refs[:count]
+    tile_ref, gathered_ref, held_ref, in_sems, out_sems = refs[-5:]
+    per_dev, units, _ = tile_ref.shape
     tokens = block_refs[0].shape[0]
     steps = in_sems.shape[0]
-    step = model // steps
+    width = held_ref.shape[1]
+    step = width // steps
     arriving, leaving = [], []
     for i in range(steps):
-        columns = pl.ds(i * step, step)
         arriving.append(
             [
                 pltpu.make_async_copy(
-                    ref.at[:, columns],
-                    gathered_ref.at[pl.ds(n * tokens, tokens), columns],
+                    ref.at[:, pl.ds(i * step + (start if ref.shape[1] > width else 0), step)],
+                    gathered_ref.at[pl.ds(n * tokens, tokens), pl.ds(i * step, step)],
                     in_sems.at[i, n],
                 )
                 for n, ref in enumerate(block_refs)
@@ -280,7 +293,7 @@
             leaving.append(
                 pltpu.make_async_copy(
                     held_ref.at[pl.ds(j * units, units), pl.ds(i * step, step)],
-                    tile_ref.at[j, :, pl.ds(i * step, step)],
+                    tile_ref.at[j, :, pl.ds(start + i * step, step)],
                     out_sems.at[i, j],
                 )
             )
@@ -289,25 +302,28 @@
         copy.wait()
 
 
-def tile_sums(weighted, blocks, per_dev):
+def tile_sums(weighted, blocks, per_dev, start, tiles):
     tokens, model = blocks[0].shape
+    width = min(block.shape[1] for block in blocks)
     rows = weighted.shape[0]
-    steps = model // 1024
+    steps = width // 512
     anywhere = pl.BlockSpec(memory_space=pl.ANY)
+    earlier = [] if tiles is None else [tiles]
     return pl.pallas_call(
-        tile_kernel,
+        functools.partial(tile_kernel, start, len(blocks)),
         out_shape=jax.ShapeDtypeStruct((per_dev, rows // per_dev, model), jnp.float32),
-        in_specs=[pl.BlockSpec(memory_space=pltpu.VMEM)] + [anywhere] * len(blocks),
+        in_specs=[pl.BlockSpec(memory_space=pltpu.VMEM)] + [anywhere] * (len(blocks) + len(earlier)),
         out_specs=anywhere,
         scratch_shapes=[
-            pltpu.VMEM((len(blocks) * tokens, model), jnp.bfloat16),
-            pltpu.VMEM((rows, model), jnp.float32),
+            pltpu.VMEM((len(blocks) * tokens, width), jnp.bfloat16),
+            pltpu.VMEM((rows, width), jnp.float32),
             pltpu.SemaphoreType.DMA((steps, len(blocks))),
             pltpu.SemaphoreType.DMA((steps, per_dev)),
         ],
-        compiler_params=pltpu.CompilerParams(vmem_limit_bytes=32 * 2**20),
+        input_output_aliases={1 + len(blocks): 0} if earlier else {},
+        compiler_params=pltpu.CompilerParams(vmem_limit_bytes=20 * 2**20),
         name="tiles",
-    )(weighted, *blocks)
+    )(weighted, *blocks, *earlier)
 
 
 def swapped(value):
@@ -397,30 +413,37 @@
 ):
     steps = block_steps(lax.axis_size("exp"))
     tokens = expert_ids.shape[0]
+    per_dev = shadow_list.shape[0] // lax.axis_size("exp")
     first = moved(moe_grad, [held[1] for held in steps])
+    own_beside = beside(moe_grad)
     arrived = key_blocks(keys, values, queries.shape[1] // lse_excess.shape[0])
     payload = source_rows(expert_ids, route_probs, shadow_list, stored_hidden_state)
-    own_beside = beside(after(moe_grad, payload))
     mixed = swapped(payload)
-    second = moved(after(moe_grad, own_beside), [held[2] for held in steps])
-    per_dev = shadow_list.shape[0] // lax.axis_size("exp")
-    sent = after(picked_rows(shadow_list, mixed, payload.shape[1] - per_dev), arrived)
+    second = moved(after(moe_grad, mixed), [held[2] for held in steps])
+    sent = picked_rows(shadow_list, mixed, payload.shape[1] - per_dev)
+    sent = after(sent, arrived, own_beside)
     first_beside = beside(after(first, sent))
     shadow_rows = swapped(sent)
-    far = moved(after(first, first_beside), [held[2] for held in steps])
     query_grad, terms = attention(
-        queries, after(arrived, first_beside), attn_out, attn_out_grad, lse_excess, block_mask
-    )
-    weighted = expert_rows(
-        mixed, after(shadow_rows, query_grad), shadow_list, stored_hidden_state, tokens
-    )
+        queries, arrived, attn_out, attn_out_grad, lse_excess, block_mask
+    )
+    total = block_terms(terms)
+    parts = 2
+    first, second, shadow_rows, query_grad, first_beside = lax.optimization_barrier(
+        (first, second, shadow_rows, query_grad, first_beside)
+    )
+    far = [moved(part, [held[2] for held in steps]) for part in jnp.split(first, parts, axis=1)]
+    shadow_rows, total = lax.optimization_barrier((shadow_rows, total))
+    weighted = expert_rows(mixed, shadow_rows, shadow_list, stored_hidden_state, tokens)
     second_beside = beside(after(second, weighted))
-    far = after(far, second_beside)
-    blocks = all_blocks(
-        [(moe_grad, own_beside), (first, first_beside), (second, second_beside), (far, beside(far))]
-    )
-    tiles = tile_sums(weighted, blocks, per_dev)
-    key_grad, value_grad, expert_grad = summed_terms(terms, keys.shape[1], tiles)
+    near = [(moe_grad, own_beside), (first, first_beside), (second, second_beside)]
+    tiles, start = None, 0
+    for part in far:
+        part, _ = lax.optimization_barrier((part, weighted if tiles is None else tiles))
+        blocks = all_blocks(near + [(part, beside(part))])
+        tiles = tile_sums(weighted, blocks, per_dev, start, tiles)
+        start += part.shape[1]
+    key_grad, value_grad, expert_grad = summed_terms(total, keys.shape[1], tiles)
     return (query_grad, key_grad, value_grad, expert_grad)
 
 

time: 88.6 us -> 88.2 us (level); the launches traced: 87.9 us -> 86.6 us
  waiting for transfers between devices: 24.5 us -> 19 us
  Pallas kernels: 19.6 us -> 22.5 us
  local copies, waits for them, and re-layouts: 10.3 us -> 8.04 us
  starting transfers between devices: 31.1 us -> 32.9 us
  other arithmetic: 1.54 us -> 3.16 us
    ppermute x0 -> x3, waiting for transfers between devices: none -> 13.1 us  [block_terms(): total = total + lax.ppermute(terms[step], 'ctx', pairs).astype(jnp.float32)]
    all_to_all x2, waiting for transfers between devices: 9.28 us -> 0.97 us  [swapped(): return lax.all_to_all(value, 'exp', split_axis=0, concat_axis=0, tiled=True)]
    ppermute x7 -> x9, waiting for transfers between devices: 10.2 us -> 3.87 us  [moved(): lax.ppermute(value, 'exp', [(e, e ^ steps[e % 2]) for e in range(owners)])]
    ppermute x0 -> x3, starting transfers between devices: none -> 3.86 us  [block_terms(): total = total + lax.ppermute(terms[step], 'ctx', pairs).astype(jnp.float32)]
    all_to_all x1, starting transfers between devices: 7.67 us -> 3.98 us  [summed_terms(): lax.all_to_all(total.reshape(owners, rows // owners, columns), 'exp', spl...]
    pallas_call x2 -> x3, Pallas kernels: 14.7 us -> 17.7 us  [the longest x2 13.6 us: tile_sums(): pl.pallas_call(functools.partial(tile_kernel, start, len(blocks)), out_sh...]
    all_to_all x1, waiting for transfers between devices: 2.43 us -> 0.01 us  [summed_terms(): lax.all_to_all(total.reshape(owners, rows // owners, columns), 'exp', spl...]
    ppermute x7 -> x9, starting transfers between devices: 5.8 us -> 7.67 us  [moved(): lax.ppermute(value, 'exp', [(e, e ^ steps[e % 2]) for e in range(owners)])]
  transfers between devices with their start and end apart: 13 -> 18, of which waited for: 5 -> 7; matrix products, arithmetic and copies ran while one was open for 4% -> 5% of each run, Pallas kernels for 22% -> 25%
where the time goes in v6:
time: 88.2 us; the launch traced here: 86.6 us
  starting transfers between devices  32.9 us (37%)
  Pallas kernels  22.5 us (26%)
  waiting for transfers between devices  19 us (22%)
  local copies, waits for them, and re-layouts  8.04 us (9%)
  other arithmetic  3.16 us (4%)
  between operations  0.94 us (1%)
    pallas_call x2, Pallas kernels, tile_sums(): pl.pallas_call(functools.partial(tile_kernel, start, len(blocks)), out_sh...  13.6 us
    ppermute x3, waiting for transfers between devices, block_terms(): total = total + lax.ppermute(terms[step], 'ctx', pairs).astype(jnp.float32)  13.1 us
    ppermute x3, starting transfers between devices, key_blocks(): lax.ppermute(pair, 'ctx', [(c, c + step) for c in range(cycle - step)])  9.94 us
    unnamed x35, local copies, waits for them, and re-layouts  7.91 us
    ppermute x9, starting transfers between devices, moved(): lax.ppermute(value, 'exp', [(e, e ^ steps[e % 2]) for e in range(owners)])  7.67 us
    all_to_all x2, starting transfers between devices, swapped(): return lax.all_to_all(value, 'exp', split_axis=0, concat_axis=0, tiled=True)  7.43 us
    pallas_call x1, Pallas kernels, attention(): pl.pallas_call(attention_kernel, out_shape=[jax.ShapeDtypeStruct(queries....  4.07 us
    all_to_all x1, starting transfers between devices, summed_terms(): lax.all_to_all(total.reshape(owners, rows // owners, columns), 'exp', spl...  3.98 us
  transfers between devices with their start and end apart: 18, of which 7 were waited for; matrix products, arithmetic and copies ran while one was open for 5% of the time, Pallas kernels for 25%

profile of v6, /device:TPU:0, one launch (start us, length us, event | category | flops | bytes accessed | tf_op | source)
XLA Modules:
  0.0 86.6 jit_solution(12102801859851357106)
XLA Ops:
  0.6 0.5 collective-permute-start.5
  1.2 2.6 %collective-permute-start = (bf16[128,4096]{1,0:T(8,128)(2,1)}, bf16[128,4096]{1,0:T(8,128)(2,1)S(1)}, u32[]{:S(2)}, u32[]{:S(2)}) collective-permute-start(bf16[128,4096]{1,0:T(8,128)(2,1)} %refs_0_.3), channel_id=1, source_target_pairs={{0,4},{1,3},{2,6},{3,1},{4,0},{5,7},{6,2},{7,5},{8,12},{9,11},{10,... | collective-permute-start | bytes 3145736 | tf_op jit(solution)/shard_map/ppermute | solution.py:380
  3.8 0.7 convert_element_type.28
  4.4 1.5 %copy.21.hidden_ref = bf16[1,3,8,65,384]{4,3,2,1,0:T(8,128)(2,1)S(1)} copy(bf16[1,3,8,65,384]{4,2,3,1,0:T(8,128)(2,1)} %param.23) | data formatting | bytes 2396160 | tf_op args[11]
  5.9 0.0 copy-start.14
  5.9 0.0 copy-start.15
  5.9 0.0 copy-start.13
  6.0 0.0 copy-start
  6.0 1.1 %copy-done = bf16[1,3,8,65,384]{4,3,2,1,0:T(8,128)(2,1)} copy-done((bf16[1,3,8,65,384]{4,3,2,1,0:T(8,128)(2,1)}, bf16[1,3,8,65,384]{4,3,2,1,0:T(8,128)(2,1)S(1)}, u32[]{:S(2)}) %copy-start) | copy-done | bytes 1198104
  7.1 0.0 copy-start.12
  7.1 0.8 fusion.1
  7.9 3.5 %all-to-all-start = ((bf16[8,66,384]{2,1,0:T(8,128)(2,1)}), bf16[8,66,384]{2,1,0:T(8,128)(2,1)S(1)}, u32[]{:S(2)}, u32[]{:S(2)}) async-start(bf16[8,66,384]{2,1,0:T(8,128)(2,1)} %fusion.1), calls=%async_computation | async-start | bytes 884736 | tf_op jit(solution)/shard_map/all_to_all | solution.py:330
  11.5 5.5 %collective-permute-start.4 = (bf16[256,256]{1,0:T(8,128)(2,1)S(1)}, bf16[256,256]{1,0:T(8,128)(2,1)S(1)}, u32[]{:S(2)}, u32[]{:S(2)}) collective-permute-start(bf16[256,256]{1,0:T(8,128)(2,1)S(1)} %pad_maximum_fusion.rest_0_), channel_id=1, source_target_pairs={{0,24},{1,25},{2,26},{3,27},{4,28},{5,29},{6,30},{7,31}} | collective-permute-start | bytes 393224 | tf_op jit(solution)/shard_map/ppermute | solution.py:102
  17.0 1.3 %collective-permute-start.3 = (bf16[256,256]{1,0:T(8,128)(2,1)S(1)}, bf16[256,256]{1,0:T(8,128)(2,1)S(1)}, u32[]{:S(2)}, u32[]{:S(2)}) collective-permute-start(bf16[256,256]{1,0:T(8,128)(2,1)S(1)} %pad_maximum_fusion.rest_0_), channel_id=1, source_target_pairs={{0,16},{8,24},{1,17},{9,25},{2,18},{10,26},{3,19},{11,27},{4,20},{... | collective-permute-start | bytes 393224 | tf_op jit(solution)/shard_map/ppermute | solution.py:102
  18.3 3.1 %collective-permute-start.2 = (bf16[256,256]{1,0:T(8,128)(2,1)S(1)}, bf16[256,256]{1,0:T(8,128)(2,1)}, u32[]{:S(2)}, u32[]{:S(2)}) collective-permute-start(bf16[256,256]{1,0:T(8,128)(2,1)S(1)} %pad_maximum_fusion.rest_0_), channel_id=1, source_target_pairs={{0,8},{8,16},{16,24},{1,9},{9,17},{17,25},{2,10},{10,18},{18,26},{... | collective-permute-start | bytes 393224 | tf_op jit(solution)/shard_map/ppermute | solution.py:102
  21.4 1.0 %all-to-all-done.mixed_ref = bf16[8,66,384]{2,1,0:T(8,128)(2,1)S(1)} async-done(((bf16[8,66,384]{2,1,0:T(8,128)(2,1)}), bf16[8,66,384]{2,1,0:T(8,128)(2,1)S(1)}, u32[]{:S(2)}, u32[]{:S(2)}) %all-to-all-start) | async-done | bytes 405536 | tf_op jit(solution)/shard_map/all_to_all | solution.py:330
  22.4 1.3 %picked.1 = bf16[8,64,384]{2,1,0:T(8,128)(2,1)} custom-call(s32[16]{0:T(128)S(1)} %copy-done.13, bf16[8,66,384]{2,1,0:T(8,128)(2,1)S(1)} %all-to-all-done.mixed_ref), custom_call_target="tpu_custom_call" | custom-call | tf_op jit(solution)/shard_map/picked/pallas_call | solution.py:191
  23.8 1.1 %collective-permute-start.1 = (bf16[128,4096]{1,0:T(8,128)(2,1)S(1)}, bf16[128,4096]{1,0:T(8,128)(2,1)}, u32[]{:S(2)}, u32[]{:S(2)}) collective-permute-start(bf16[128,4096]{1,0:T(8,128)(2,1)S(1)} %copy-done.2), channel_id=1, source_target_pairs={{0,2},{1,5},{2,0},{3,7},{4,6},{5,1},{6,4},{7,3},{8,10},{9,13},{10,... | collective-permute-start | bytes 3145736 | tf_op jit(solution)/shard_map/ppermute | solution.py:380
  24.8 0.0 collective-permute-done.3.rest_2_
  24.8 1.1 %collective-permute-done.2.rest_1_ = bf16[256,256]{1,0:T(8,128)(2,1)} collective-permute-done((bf16[256,256]{1,0:T(8,128)(2,1)S(1)}, bf16[256,256]{1,0:T(8,128)(2,1)}, u32[]{:S(2)}, u32[]{:S(2)}) %collective-permute-start.2) | collective-permute-done | bytes 131104 | tf_op jit(solution)/shard_map/ppermute | solution.py:102
  25.9 0.0 collective-permute-done.5.refs_1_
  26.0 0.0 copy-start.9
  26.0 0.9 %copy-done.9 = bf16[256,512]{1,0:T(8,128)(2,1)S(1)} copy-done((bf16[256,512]{1,0:T(8,128)(2,1)S(1)}, bf16[256,512]{1,0:T(8,128)(2,1)}, u32[]{:S(2)}) %copy-start.9) | copy-done | bytes 262168
  26.9 4.1 %attention.1 = (bf16[256,512]{1,0:T(8,128)(2,1)}, bf16[256,256]{1,0:T(8,128)(2,1)S(1)}, bf16[256,256]{1,0:T(8,128)(2,1)}, bf16[256,256]{1,0:T(8,128)(2,1)}, bf16[256,256]{1,0:T(8,128)(2,1)}) custom-call(s32[1]{0:T(128)} %bitcast.3.place_ref, s32[4,4]{1,0:T(4,128)S(1)} %copy-done.12, bf16[256,512]{1,0:T(8,128)(2,1)S(1)} %copy-done.7, ...), custom_call_target="tpu_custom_call" | custom-call | tf_op jit(solution)/shard_map/attention/pallas_call | solution.py:112
  31.0 0.6 copy-done.10
  31.7 1.3 %collective-permute-start.7 = (bf16[256,256]{1,0:T(8,128)(2,1)}, bf16[256,256]{1,0:T(8,128)(2,1)S(1)}, u32[]{:S(2)}, u32[]{:S(2)}) collective-permute-start(bf16[256,256]{1,0:T(8,128)(2,1)} %get-tuple-element.33), channel_id=1, source_target_pairs={{8,0},{16,8},{24,16},{9,1},{17,9},{25,17},{10,2},{18,10},{26,18},{... | collective-permute-start | bytes 393224 | tf_op jit(solution)/shard_map/ppermute | solution.py:151
  32.9 1.3 %collective-permute-start.8 = (bf16[256,256]{1,0:T(8,128)(2,1)}, bf16[256,256]{1,0:T(8,128)(2,1)S(1)}, u32[]{:S(2)}, u32[]{:S(2)}) collective-permute-start(bf16[256,256]{1,0:T(8,128)(2,1)} %get-tuple-element.34), channel_id=1, source_target_pairs={{16,0},{24,8},{17,1},{25,9},{18,2},{26,10},{19,3},{27,11},{20,4},{... | collective-permute-start | bytes 393224 | tf_op jit(solution)/shard_map/ppermute | solution.py:151
  34.2 1.3 %collective-permute-start.9 = (bf16[256,256]{1,0:T(8,128)(2,1)}, bf16[256,256]{1,0:T(8,128)(2,1)S(1)}, u32[]{:S(2)}, u32[]{:S(2)}) collective-permute-start(bf16[256,256]{1,0:T(8,128)(2,1)} %get-tuple-element.35), channel_id=1, source_target_pairs={{24,0},{25,1},{26,2},{27,3},{28,4},{29,5},{30,6},{31,7}} | collective-permute-start | bytes 393224 | tf_op jit(solution)/shard_map/ppermute | solution.py:151
  35.5 4.0 %all-to-all-start.1 = ((bf16[8,64,384]{2,1,0:T(8,128)(2,1)}), bf16[8,64,384]{2,1,0:T(8,128)(2,1)S(1)}, u32[]{:S(2)}, u32[]{:S(2)}) async-start(bf16[8,64,384]{2,1,0:T(8,128)(2,1)} %picked.1), calls=%async_computation.1 | async-start | bytes 786432 | tf_op jit(solution)/shard_map/all_to_all | solution.py:330
  39.5 2.6 %collective-permute-done.7 = bf16[256,256]{1,0:T(8,128)(2,1)S(1)} collective-permute-done((bf16[256,256]{1,0:T(8,128)(2,1)}, bf16[256,256]{1,0:T(8,128)(2,1)S(1)}, u32[]{:S(2)}, u32[]{:S(2)}) %collective-permute-start.7) | collective-permute-done | bytes 131104 | tf_op jit(solution)/shard_map/ppermute | solution.py:151
  42.1 10.4 %collective-permute-done.8 = bf16[256,256]{1,0:T(8,128)(2,1)S(1)} collective-permute-done((bf16[256,256]{1,0:T(8,128)(2,1)}, bf16[256,256]{1,0:T(8,128)(2,1)S(1)}, u32[]{:S(2)}, u32[]{:S(2)}) %collective-permute-start.8) | collective-permute-done | bytes 131104 | tf_op jit(solution)/shard_map/ppermute | solution.py:151
  52.6 1.6 %add_convert_fusion = bf16[256,256]{1,0:T(8,128)(2,1)} fusion(bf16[256,256]{1,0:T(8,128)(2,1)S(1)} %collective-permute-done.9, bf16[256,256]{1,0:T(8,128)(2,1)S(1)} %collective-permute-done.8, bf16[256,256]{1,0:T(8,128)(2,1)S(1)} %collective-permute-done.7, bf16[256,256]{1,0:T(8,128)(2,1)} %copy-done.10), kind=kLoop, calls=%fused_computation.4 | loop fusion | flops 524288 | bytes 655360 | tf_op jit(solution)/shard_map/convert_element_type | solution.py:152
  54.2 0.1 fusion.2
  54.3 1.7 %collective-permute-start.12 = (bf16[128,2048]{1,0:T(8,128)(2,1)S(1)}, bf16[128,2048]{1,0:T(8,128)(2,1)S(1)}, u32[]{:S(2)}, u32[]{:S(2)}) collective-permute-start(bf16[128,2048]{1,0:T(8,128)(2,1)S(1)} %get-tuple-element.48), channel_id=1, source_target_pairs={{0,2},{1,5},{2,0},{3,7},{4,6},{5,1},{6,4},{7,3},{8,10},{9,13},{10,... | collective-permute-start | bytes 1572872 | tf_op jit(solution)/shard_map/ppermute | solution.py:380
  56.0 1.3 %copy-done.1 = bf16[1,3,8,65,384]{4,3,2,1,0:T(8,128)(2,1)S(1)} copy-done((bf16[1,3,8,65,384]{4,3,2,1,0:T(8,128)(2,1)S(1)}, bf16[1,3,8,65,384]{4,3,2,1,0:T(8,128)(2,1)}, u32[]{:S(2)}) %copy-start.1) | copy-done | bytes 1198104
  57.3 2.9 %weighted.1.weight_ref = bf16[768,1024]{1,0:T(8,128)(2,1)S(1)} custom-call(s32[1]{0:T(128)} %bitcast.5.own_ref, s32[16]{0:T(128)S(1)} %copy-done.13, bf16[8,66,384]{2,1,0:T(8,128)(2,1)S(1)} %all-to-all-done.mixed_ref, bf16[1,3,8,65,384]{4,3,2,1,0:T(8,128)(2,1)S(1)} %copy-done.1, bf16[8,64,384]{2,1,0:T(8,128)(2,1)S(1)} %all-to-all-done.1.side_ref), custom_call_target="tpu_custom_call" | custom-call | tf_op jit(solution)/shard_map/weighted/pallas_call | solution.py:243
  60.2 0.1 collective-permute-start.10
  60.3 3.2 %collective-permute-done.12.refs_6_ = bf16[128,2048]{1,0:T(8,128)(2,1)S(1)} collective-permute-done((bf16[128,2048]{1,0:T(8,128)(2,1)S(1)}, bf16[128,2048]{1,0:T(8,128)(2,1)S(1)}, u32[]{:S(2)}, u32[]{:S(2)}) %collective-permute-start.12) | collective-permute-done | bytes 524320 | tf_op jit(solution)/shard_map/ppermute | solution.py:380
  63.5 1.7 %collective-permute-start.11 = (bf16[128,2048]{1,0:T(8,128)(2,1)S(1)}, bf16[128,2048]{1,0:T(8,128)(2,1)S(1)}, u32[]{:S(2)}, u32[]{:S(2)}) collective-permute-start(bf16[128,2048]{1,0:T(8,128)(2,1)S(1)} %get-tuple-element.49), channel_id=1, source_target_pairs={{0,2},{1,5},{2,0},{3,7},{4,6},{5,1},{6,4},{7,3},{8,10},{9,13},{10,... | collective-permute-start | bytes 1572872 | tf_op jit(solution)/shard_map/ppermute | solution.py:380
  65.2 0.2 collective-permute-done.13.refs_7_
  65.5 6.9 %tiles.2.refs_8_ = f32[2,384,4096]{2,1,0:T(8,128)} custom-call(bf16[768,1024]{1,0:T(8,128)(2,1)S(1)} %weighted.1.weight_ref, bf16[128,4096]{1,0:T(8,128)(2,1)S(1)} %copy-done.3, bf16[128,4096]{1,0:T(8,128)(2,1)} %collective-permute-done.5.refs_1_, bf16[128,4096]{1,0:T(8,128)(2,1)S(1)} %collective-permute-done.refs_2_, ...), custom_call_target="tpu_custom_call" | custom-call | tf_op jit(solution)/shard_map/tiles/pallas_call | solution.py:312
  72.3 0.4 collective-permute-done.11.refs_6_
  72.7 4.0 %all-to-all-start.2 = ((bf16[8,32,256]{2,1,0:T(8,128)(2,1)}), bf16[8,32,256]{2,1,0:T(8,128)(2,1)S(1)}, u32[]{:S(2)}, u32[]{:S(2)}) async-start(bf16[8,32,256]{2,1,0:T(8,128)(2,1)} %bitcast.4), calls=%async_computation.2 | async-start | bytes 262144 | tf_op jit(solution)/shard_map/all_to_all | solution.py:158
  76.7 0.0 copy-start.4
  76.7 1.2 %copy-done.4 = bf16[128,4096]{1,0:T(8,128)(2,1)S(1)} copy-done((bf16[128,4096]{1,0:T(8,128)(2,1)S(1)}, bf16[128,4096]{1,0:T(8,128)(2,1)}, u32[]{:S(2)}) %copy-start.4) | copy-done | bytes 1048600
  77.9 1.2 %copy-done.6 = bf16[128,4096]{1,0:T(8,128)(2,1)S(1)} copy-done((bf16[128,4096]{1,0:T(8,128)(2,1)S(1)}, bf16[128,4096]{1,0:T(8,128)(2,1)}, u32[]{:S(2)}) %copy-start.6) | copy-done | bytes 1048600
  79.2 6.7 %tiles.3 = f32[2,384,4096]{2,1,0:T(8,128)} custom-call(bf16[768,1024]{1,0:T(8,128)(2,1)S(1)} %weighted.1.weight_ref, bf16[128,4096]{1,0:T(8,128)(2,1)S(1)} %copy-done.4, bf16[128,4096]{1,0:T(8,128)(2,1)} %collective-permute-done.5.refs_1_, bf16[128,4096]{1,0:T(8,128)(2,1)S(1)} %collective-permute-done.refs_2_, ...), custom_call_target="tpu_custom_call", output_to_operand_aliasing={{}: (9, {})} | custom-call | tf_op jit(solution)/shard_map/tiles/pallas_call | solution.py:312
  85.9 0.6 sums.1
  (37 shorter events, 0.2 us)
Async XLA Ops:
  0.6 5.3 %copy-start.16 = (s32[128,8]{0,1:T(8,128)S(1)}, s32[128,8]{0,1:T(8,128)}, u32[]{:S(2)}) copy-start(s32[128,8]{0,1:T(8,128)} %param.19) | copy-start | bytes 12292
  0.6 25.3 %collective-permute-start.5 = (bf16[128,4096]{1,0:T(8,128)(2,1)}, bf16[128,4096]{1,0:T(8,128)(2,1)}, u32[]{:S(2)}, u32[]{:S(2)}) collective-permute-start(bf16[128,4096]{1,0:T(8,128)(2,1)} %refs_0_.3), channel_id=1, source_target_pairs={{0,1},{1,0},{2,3},{3,2},{4,5},{5,4},{6,7},{7,6},{8,9},{9,8},{10,11... | collective-permute-start | bytes 3145736 | tf_op jit(solution)/shard_map/ppermute | solution.py:380
  1.2 24.8 %collective-permute-start = (bf16[128,4096]{1,0:T(8,128)(2,1)}, bf16[128,4096]{1,0:T(8,128)(2,1)S(1)}, u32[]{:S(2)}, u32[]{:S(2)}) collective-permute-start(bf16[128,4096]{1,0:T(8,128)(2,1)} %refs_0_.3), channel_id=1, source_target_pairs={{0,4},{1,3},{2,6},{3,1},{4,0},{5,7},{6,2},{7,5},{8,12},{9,11},{10,... | collective-permute-start | bytes 3145736 | tf_op jit(solution)/shard_map/ppermute | solution.py:380
  5.9 5.5 %copy-start.14 = (bf16[256,256]{1,0:T(8,128)(2,1)S(1)}, bf16[256,256]{1,0:T(8,128)(2,1)}, u32[]{:S(2)}) copy-start(bf16[256,256]{1,0:T(8,128)(2,1)} %param.14) | copy-start | bytes 393220
  5.9 5.5 %copy-start.15 = (bf16[256,256]{1,0:T(8,128)(2,1)S(1)}, bf16[256,256]{1,0:T(8,128)(2,1)}, u32[]{:S(2)}) copy-start(bf16[256,256]{1,0:T(8,128)(2,1)} %param.13) | copy-start | bytes 393220
  5.9 16.5 %copy-start.13 = (s32[16]{0:T(128)S(1)}, s32[16]{0:T(128)}, u32[]{:S(2)}) copy-start(s32[16]{0:T(128)} %shadow_ref.3) | copy-start | bytes 196
  6.0 1.1 %copy-start = (bf16[1,3,8,65,384]{4,3,2,1,0:T(8,128)(2,1)}, bf16[1,3,8,65,384]{4,3,2,1,0:T(8,128)(2,1)S(1)}, u32[]{:S(2)}) copy-start(bf16[1,3,8,65,384]{4,3,2,1,0:T(8,128)(2,1)S(1)} %copy.21.hidden_ref) | copy-start | bytes 3594244
  7.1 16.7 %copy-start.2 = (bf16[128,4096]{1,0:T(8,128)(2,1)S(1)}, bf16[128,4096]{1,0:T(8,128)(2,1)}, u32[]{:S(2)}) copy-start(bf16[128,4096]{1,0:T(8,128)(2,1)} %refs_0_.3) | copy-start | bytes 3145732
  7.1 18.9 %copy-start.7 = (bf16[256,512]{1,0:T(8,128)(2,1)S(1)}, bf16[256,512]{1,0:T(8,128)(2,1)}, u32[]{:S(2)}) copy-start(bf16[256,512]{1,0:T(8,128)(2,1)} %query_ref.1) | copy-start | bytes 786436
  7.1 18.9 %copy-start.8 = (bf16[256,512]{1,0:T(8,128)(2,1)S(1)}, bf16[256,512]{1,0:T(8,128)(2,1)}, u32[]{:S(2)}) copy-start(bf16[256,512]{1,0:T(8,128)(2,1)} %grad_ref.1) | copy-start | bytes 786436
  7.1 18.9 %copy-start.11 = (f32[4,256]{1,0:T(4,128)S(1)}, f32[4,256]{1,0:T(4,128)}, u32[]{:S(2)}) copy-start(f32[4,256]{1,0:T(4,128)} %lse_ref.1) | copy-start | bytes 12292
  7.1 18.9 %copy-start.12 = (s32[4,4]{1,0:T(4,128)S(1)}, s32[4,4]{1,0:T(4,128)}, u32[]{:S(2)}) copy-start(s32[4,4]{1,0:T(4,128)} %mask_ref.1) | copy-start | bytes 196
  7.9 14.5 %all-to-all-start = ((bf16[8,66,384]{2,1,0:T(8,128)(2,1)}), bf16[8,66,384]{2,1,0:T(8,128)(2,1)S(1)}, u32[]{:S(2)}, u32[]{:S(2)}) async-start(bf16[8,66,384]{2,1,0:T(8,128)(2,1)} %fusion.1), calls=%async_computation | async-start | bytes 884736 | tf_op jit(solution)/shard_map/all_to_all | solution.py:330
  11.5 12.3 %collective-permute-start.4 = (bf16[256,256]{1,0:T(8,128)(2,1)S(1)}, bf16[256,256]{1,0:T(8,128)(2,1)S(1)}, u32[]{:S(2)}, u32[]{:S(2)}) collective-permute-start(bf16[256,256]{1,0:T(8,128)(2,1)S(1)} %pad_maximum_fusion.rest_0_), channel_id=1, source_target_pairs={{0,24},{1,25},{2,26},{3,27},{4,28},{5,29},{6,30},{7,31}} | collective-permute-start | bytes 393224 | tf_op jit(solution)/shard_map/ppermute | solution.py:102
  17.0 7.8 %collective-permute-start.3 = (bf16[256,256]{1,0:T(8,128)(2,1)S(1)}, bf16[256,256]{1,0:T(8,128)(2,1)S(1)}, u32[]{:S(2)}, u32[]{:S(2)}) collective-permute-start(bf16[256,256]{1,0:T(8,128)(2,1)S(1)} %pad_maximum_fusion.rest_0_), channel_id=1, source_target_pairs={{0,16},{8,24},{1,17},{9,25},{2,18},{10,26},{3,19},{11,27},{4,20},{... | collective-permute-start | bytes 393224 | tf_op jit(solution)/shard_map/ppermute | solution.py:102
  18.3 7.6 %collective-permute-start.2 = (bf16[256,256]{1,0:T(8,128)(2,1)S(1)}, bf16[256,256]{1,0:T(8,128)(2,1)}, u32[]{:S(2)}, u32[]{:S(2)}) collective-permute-start(bf16[256,256]{1,0:T(8,128)(2,1)S(1)} %pad_maximum_fusion.rest_0_), channel_id=1, source_target_pairs={{0,8},{8,16},{16,24},{1,9},{9,17},{17,25},{2,10},{10,18},{18,26},{... | collective-permute-start | bytes 393224 | tf_op jit(solution)/shard_map/ppermute | solution.py:102
  23.8 30.5 %collective-permute-start.1 = (bf16[128,4096]{1,0:T(8,128)(2,1)S(1)}, bf16[128,4096]{1,0:T(8,128)(2,1)}, u32[]{:S(2)}, u32[]{:S(2)}) collective-permute-start(bf16[128,4096]{1,0:T(8,128)(2,1)S(1)} %copy-done.2), channel_id=1, source_target_pairs={{0,2},{1,5},{2,0},{3,7},{4,6},{5,1},{6,4},{7,3},{8,10},{9,13},{10,... | collective-permute-start | bytes 3145736 | tf_op jit(solution)/shard_map/ppermute | solution.py:380
  25.9 28.3 %collective-permute-start.6 = (bf16[128,4096]{1,0:T(8,128)(2,1)S(1)}, bf16[128,4096]{1,0:T(8,128)(2,1)}, u32[]{:S(2)}, u32[]{:S(2)}) collective-permute-start(bf16[128,4096]{1,0:T(8,128)(2,1)S(1)} %collective-permute-done.refs_2_), channel_id=1, source_target_pairs={{0,1},{1,0},{2,3},{3,2},{4,5},{5,4},{6,7},{7,6},{8,9},{9,8},{10,11... | collective-permute-start | bytes 3145736 | tf_op jit(solution)/shard_map/ppermute | solution.py:380
  26.0 1.0 %copy-start.9 = (bf16[256,512]{1,0:T(8,128)(2,1)S(1)}, bf16[256,512]{1,0:T(8,128)(2,1)}, u32[]{:S(2)}) copy-start(bf16[256,512]{1,0:T(8,128)(2,1)} %out_ref.1) | copy-start | bytes 786436
  31.0 0.6 copy-start.10
  31.7 10.5 %collective-permute-start.7 = (bf16[256,256]{1,0:T(8,128)(2,1)}, bf16[256,256]{1,0:T(8,128)(2,1)S(1)}, u32[]{:S(2)}, u32[]{:S(2)}) collective-permute-start(bf16[256,256]{1,0:T(8,128)(2,1)} %get-tuple-element.33), channel_id=1, source_target_pairs={{8,0},{16,8},{24,16},{9,1},{17,9},{25,17},{10,2},{18,10},{26,18},{... | collective-permute-start | bytes 393224 | tf_op jit(solution)/shard_map/ppermute | solution.py:151
  32.9 19.6 %collective-permute-start.8 = (bf16[256,256]{1,0:T(8,128)(2,1)}, bf16[256,256]{1,0:T(8,128)(2,1)S(1)}, u32[]{:S(2)}, u32[]{:S(2)}) collective-permute-start(bf16[256,256]{1,0:T(8,128)(2,1)} %get-tuple-element.34), channel_id=1, source_target_pairs={{16,0},{24,8},{17,1},{25,9},{18,2},{26,10},{19,3},{27,11},{20,4},{... | collective-permute-start | bytes 393224 | tf_op jit(solution)/shard_map/ppermute | solution.py:151
  34.2 18.3 %collective-permute-start.9 = (bf16[256,256]{1,0:T(8,128)(2,1)}, bf16[256,256]{1,0:T(8,128)(2,1)S(1)}, u32[]{:S(2)}, u32[]{:S(2)}) collective-permute-start(bf16[256,256]{1,0:T(8,128)(2,1)} %get-tuple-element.35), channel_id=1, source_target_pairs={{24,0},{25,1},{26,2},{27,3},{28,4},{29,5},{30,6},{31,7}} | collective-permute-start | bytes 393224 | tf_op jit(solution)/shard_map/ppermute | solution.py:151
  35.5 18.7 %all-to-all-start.1 = ((bf16[8,64,384]{2,1,0:T(8,128)(2,1)}), bf16[8,64,384]{2,1,0:T(8,128)(2,1)S(1)}, u32[]{:S(2)}, u32[]{:S(2)}) async-start(bf16[8,64,384]{2,1,0:T(8,128)(2,1)} %picked.1), calls=%async_computation.1 | async-start | bytes 786432 | tf_op jit(solution)/shard_map/all_to_all | solution.py:330
  54.3 9.2 %collective-permute-start.12 = (bf16[128,2048]{1,0:T(8,128)(2,1)S(1)}, bf16[128,2048]{1,0:T(8,128)(2,1)S(1)}, u32[]{:S(2)}, u32[]{:S(2)}) collective-permute-start(bf16[128,2048]{1,0:T(8,128)(2,1)S(1)} %get-tuple-element.48), channel_id=1, source_target_pairs={{0,2},{1,5},{2,0},{3,7},{4,6},{5,1},{6,4},{7,3},{8,10},{9,13},{10,... | collective-permute-start | bytes 1572872 | tf_op jit(solution)/shard_map/ppermute | solution.py:380
  56.0 1.3 %copy-start.1 = (bf16[1,3,8,65,384]{4,3,2,1,0:T(8,128)(2,1)S(1)}, bf16[1,3,8,65,384]{4,3,2,1,0:T(8,128)(2,1)}, u32[]{:S(2)}) copy-start(bf16[1,3,8,65,384]{4,3,2,1,0:T(8,128)(2,1)} %copy-done) | copy-start | bytes 3594244
  57.3 8.1 %copy-start.3 = (bf16[128,4096]{1,0:T(8,128)(2,1)S(1)}, bf16[128,4096]{1,0:T(8,128)(2,1)}, u32[]{:S(2)}) copy-start(bf16[128,4096]{1,0:T(8,128)(2,1)} %refs_0_.3) | copy-start | bytes 3145732
  60.2 5.0 %collective-permute-start.10 = (bf16[128,4096]{1,0:T(8,128)(2,1)}, bf16[128,4096]{1,0:T(8,128)(2,1)S(1)}, u32[]{:S(2)}, u32[]{:S(2)}) collective-permute-start(bf16[128,4096]{1,0:T(8,128)(2,1)} %collective-permute-done.1.refs_4_), channel_id=1, source_target_pairs={{0,1},{1,0},{2,3},{3,2},{4,5},{5,4},{6,7},{7,6},{8,9},{9,8},{10,11... | collective-permute-start | bytes 3145736 | tf_op jit(solution)/shard_map/ppermute | solution.py:380
  63.5 1.9 %collective-permute-start.13 = (bf16[128,2048]{1,0:T(8,128)(2,1)S(1)}, bf16[128,2048]{1,0:T(8,128)(2,1)S(1)}, u32[]{:S(2)}, u32[]{:S(2)}) collective-permute-start(bf16[128,2048]{1,0:T(8,128)(2,1)S(1)} %collective-permute-done.12.refs_6_), channel_id=1, source_target_pairs={{0,1},{1,0},{2,3},{3,2},{4,5},{5,4},{6,7},{7,6},{8,9},{9,8},{10,11... | collective-permute-start | bytes 1572872 | tf_op jit(solution)/shard_map/ppermute | solution.py:380
  63.5 9.2 %collective-permute-start.11 = (bf16[128,2048]{1,0:T(8,128)(2,1)S(1)}, bf16[128,2048]{1,0:T(8,128)(2,1)S(1)}, u32[]{:S(2)}, u32[]{:S(2)}) collective-permute-start(bf16[128,2048]{1,0:T(8,128)(2,1)S(1)} %get-tuple-element.49), channel_id=1, source_target_pairs={{0,2},{1,5},{2,0},{3,7},{4,6},{5,1},{6,4},{7,3},{8,10},{9,13},{10,... | collective-permute-start | bytes 1572872 | tf_op jit(solution)/shard_map/ppermute | solution.py:380
  65.2 7.1 %copy-start.5 = (bf16[128,4096]{1,0:T(8,128)(2,1)}, bf16[128,4096]{1,0:T(8,128)(2,1)S(1)}, u32[]{:S(2)}) copy-start(bf16[128,4096]{1,0:T(8,128)(2,1)S(1)} %collective-permute-done.10.refs_5_) | copy-start | bytes 3145732
  72.7 4.0 %collective-permute-start.14 = (bf16[128,2048]{1,0:T(8,128)(2,1)S(1)}, bf16[128,2048]{1,0:T(8,128)(2,1)}, u32[]{:S(2)}, u32[]{:S(2)}) collective-permute-start(bf16[128,2048]{1,0:T(8,128)(2,1)S(1)} %collective-permute-done.11.refs_6_), channel_id=1, source_target_pairs={{0,1},{1,0},{2,3},{3,2},{4,5},{5,4},{6,7},{7,6},{8,9},{9,8},{10,11... | collective-permute-start | bytes 1572872 | tf_op jit(solution)/shard_map/ppermute | solution.py:380
  72.7 13.2 %all-to-all-start.2 = ((bf16[8,32,256]{2,1,0:T(8,128)(2,1)}), bf16[8,32,256]{2,1,0:T(8,128)(2,1)S(1)}, u32[]{:S(2)}, u32[]{:S(2)}) async-start(bf16[8,32,256]{2,1,0:T(8,128)(2,1)} %bitcast.4), calls=%async_computation.2 | async-start | bytes 262144 | tf_op jit(solution)/shard_map/all_to_all | solution.py:158
  76.7 1.2 %copy-start.4 = (bf16[128,4096]{1,0:T(8,128)(2,1)S(1)}, bf16[128,4096]{1,0:T(8,128)(2,1)}, u32[]{:S(2)}) copy-start(bf16[128,4096]{1,0:T(8,128)(2,1)} %refs_0_.3) | copy-start | bytes 3145732
  77.9 1.2 %copy-start.6 = (bf16[128,4096]{1,0:T(8,128)(2,1)S(1)}, bf16[128,4096]{1,0:T(8,128)(2,1)}, u32[]{:S(2)}) copy-start(bf16[128,4096]{1,0:T(8,128)(2,1)} %copy-done.5) | copy-start | bytes 3145732

commit v7 on v6

--- a/solution.py
+++ b/solution.py
@@ -258,21 +258,20 @@
     )(own_index.astype(jnp.int32)[None], shadow_list, mixed, hidden, shadow_rows)
 
 
-def tile_kernel(start, count, weight_ref, *refs):
-    block_refs = refs[:count]
-    tile_ref, gathered_ref, held_ref, in_sems, out_sems = refs[-5:]
-    per_dev, units, _ = tile_ref.shape
+def tile_kernel(weight_ref, *refs):
+    *block_refs, tile_ref, gathered_ref, held_ref, in_sems, out_sems = refs
+    per_dev, units, model = tile_ref.shape
     tokens = block_refs[0].shape[0]
     steps = in_sems.shape[0]
-    width = held_ref.shape[1]
-    step = width // steps
+    step = model // steps
     arriving, leaving = [], []
     for i in range(steps):
+        columns = pl.ds(i * step, step)
         arriving.append(
             [
                 pltpu.make_async_copy(
-                    ref.at[:, pl.ds(i * step + (start if ref.shape[1] > width else 0), step)],
-                    gathered_ref.at[pl.ds(n * tokens, tokens), pl.ds(i * step, step)],
+                    ref.at[:, columns],
+                    gathered_ref.at[pl.ds(n * tokens, tokens), columns],
                     in_sems.at[i, n],
                 )
                 for n, ref in enumerate(block_refs)
@@ -293,7 +292,7 @@
             leaving.append(
                 pltpu.make_async_copy(
                     held_ref.at[pl.ds(j * units, units), pl.ds(i * step, step)],
-                    tile_ref.at[j, :, pl.ds(start + i * step, step)],
+                    tile_ref.at[j, :, pl.ds(i * step, step)],
                     out_sems.at[i, j],
                 )
             )
@@ -302,28 +301,25 @@
         copy.wait()
 
 
-def tile_sums(weighted, blocks, per_dev, start, tiles):
+def tile_sums(weighted, blocks, per_dev):
     tokens, model = blocks[0].shape
-    width = min(block.shape[1] for block in blocks)
     rows = weighted.shape[0]
-    steps = width // 512
+    steps = model // 1024
     anywhere = pl.BlockSpec(memory_space=pl.ANY)
-    earlier = [] if tiles is None else [tiles]
     return pl.pallas_call(
-        functools.partial(tile_kernel, start, len(blocks)),
+        tile_kernel,
         out_shape=jax.ShapeDtypeStruct((per_dev, rows // per_dev, model), jnp.float32),
-        in_specs=[pl.BlockSpec(memory_space=pltpu.VMEM)] + [anywhere] * (len(blocks) + len(earlier)),
+        in_specs=[pl.BlockSpec(memory_space=pltpu.VMEM)] + [anywhere] * len(blocks),
         out_specs=anywhere,
         scratch_shapes=[
-            pltpu.VMEM((len(blocks) * tokens, width), jnp.bfloat16),
-            pltpu.VMEM((rows, width), jnp.float32),
+            pltpu.VMEM((len(blocks) * tokens, model), jnp.bfloat16),
+            pltpu.VMEM((rows, model), jnp.float32),
             pltpu.SemaphoreType.DMA((steps, len(blocks))),
             pltpu.SemaphoreType.DMA((steps, per_dev)),
         ],
-        input_output_aliases={1 + len(blocks): 0} if earlier else {},
-        compiler_params=pltpu.CompilerParams(vmem_limit_bytes=20 * 2**20),
+        compiler_params=pltpu.CompilerParams(vmem_limit_bytes=32 * 2**20),
         name="tiles",
-    )(weighted, *blocks, *earlier)
+    )(weighted, *blocks)
 
 
 def swapped(value):
@@ -415,34 +411,24 @@
     tokens = expert_ids.shape[0]
     per_dev = shadow_list.shape[0] // lax.axis_size("exp")
     first = moved(moe_grad, [held[1] for held in steps])
-    own_beside = beside(moe_grad)
-    arrived = key_blocks(keys, values, queries.shape[1] // lse_excess.shape[0])
+    second = moved(moe_grad, [held[2] for held in steps])
     payload = source_rows(expert_ids, route_probs, shadow_list, stored_hidden_state)
     mixed = swapped(payload)
-    second = moved(after(moe_grad, mixed), [held[2] for held in steps])
-    sent = picked_rows(shadow_list, mixed, payload.shape[1] - per_dev)
-    sent = after(sent, arrived, own_beside)
-    first_beside = beside(after(first, sent))
-    shadow_rows = swapped(sent)
+    arrived = key_blocks(after(keys, payload), values, queries.shape[1] // lse_excess.shape[0])
     query_grad, terms = attention(
         queries, arrived, attn_out, attn_out_grad, lse_excess, block_mask
     )
     total = block_terms(terms)
-    parts = 2
-    first, second, shadow_rows, query_grad, first_beside = lax.optimization_barrier(
-        (first, second, shadow_rows, query_grad, first_beside)
-    )
-    far = [moved(part, [held[2] for held in steps]) for part in jnp.split(first, parts, axis=1)]
+    far = moved(after(first, query_grad), [held[2] for held in steps])
+    mixed, _ = lax.optimization_barrier((mixed, query_grad))
+    sent = picked_rows(shadow_list, mixed, payload.shape[1] - per_dev)
+    sent, first, second = lax.optimization_barrier((sent, first, second))
+    shadow_rows = swapped(sent)
     shadow_rows, total = lax.optimization_barrier((shadow_rows, total))
     weighted = expert_rows(mixed, shadow_rows, shadow_list, stored_hidden_state, tokens)
-    second_beside = beside(after(second, weighted))
-    near = [(moe_grad, own_beside), (first, first_beside), (second, second_beside)]
-    tiles, start = None, 0
-    for part in far:
-        part, _ = lax.optimization_barrier((part, weighted if tiles is None else tiles))
-        blocks = all_blocks(near + [(part, beside(part))])
-        tiles = tile_sums(weighted, blocks, per_dev, start, tiles)
-        start += part.shape[1]
+    far = after(far, weighted)
+    blocks = all_blocks([(block, beside(block)) for block in (moe_grad, first, second, far)])
+    tiles = tile_sums(weighted, blocks, per_dev)
     key_grad, value_grad, expert_grad = summed_terms(total, keys.shape[1], tiles)
     return (query_grad, key_grad, value_grad, expert_grad)
 

time: 88.2 us -> 82.4 us (0.934); the launches traced: 86.6 us -> 81.7 us
  waiting for transfers between devices: 19 us -> 24.6 us
  Pallas kernels: 22.5 us -> 18.6 us
  local copies, waits for them, and re-layouts: 8.04 us -> 4.62 us
  starting transfers between devices: 32.9 us -> 30.7 us
  other arithmetic: 3.16 us -> 2.27 us
    all_to_all x2, waiting for transfers between devices: 0.97 us -> 19.2 us  [swapped(): return lax.all_to_all(value, 'exp', split_axis=0, concat_axis=0, tiled=True)]
    ppermute x3, waiting for transfers between devices: 13.1 us -> 0.01 us  [block_terms(): total = total + lax.ppermute(terms[step], 'ctx', pairs).astype(jnp.float32)]
    unnamed x35 -> x27, local copies, waits for them, and re-layouts: 7.91 us -> 4.57 us
    ppermute x3, waiting for transfers between devices: 1.1 us -> 4.04 us  [key_blocks(): lax.ppermute(pair, 'ctx', [(c, c + step) for c in range(cycle - step)])]
    pallas_call x2 -> x1, Pallas kernels: 13.6 us -> 10.7 us  [tile_sums(): pl.pallas_call(tile_kernel, out_shape=jax.ShapeDtypeStruct((per_dev, rows...]
    ppermute x9 -> x7, waiting for transfers between devices: 3.87 us -> 1.4 us  [moved(): lax.ppermute(value, 'exp', [(e, e ^ steps[e % 2]) for e in range(owners)])]
    pallas_call x1, Pallas kernels: 4.07 us -> 3.07 us  [attention(): pl.pallas_call(attention_kernel, out_shape=[jax.ShapeDtypeStruct(queries....]
    convert_element_type x1, other arithmetic: 1.62 us -> 0.73 us  [block_terms(): return total.astype(jnp.bfloat16)]
  transfers between devices with their start and end apart: 18 -> 16, of which waited for: 7 -> 6; matrix products, arithmetic and copies ran while one was open for 5% -> 5% of each run, Pallas kernels for 25% -> 22%
where the time goes in v7:
time: 82.4 us; the launch traced here: 81.7 us
  starting transfers between devices  30.7 us (37%)
  waiting for transfers between devices  24.6 us (30%)
  Pallas kernels  18.6 us (23%)
  local copies, waits for them, and re-layouts  4.62 us (6%)
  other arithmetic  2.27 us (3%)
  between operations  0.9 us (1%)
    all_to_all x2, waiting for transfers between devices, swapped(): return lax.all_to_all(value, 'exp', split_axis=0, concat_axis=0, tiled=True)  19.2 us
    pallas_call x1, Pallas kernels, tile_sums(): pl.pallas_call(tile_kernel, out_shape=jax.ShapeDtypeStruct((per_dev, rows...  10.7 us
    ppermute x3, starting transfers between devices, key_blocks(): lax.ppermute(pair, 'ctx', [(c, c + step) for c in range(cycle - step)])  9.28 us
    all_to_all x2, starting transfers between devices, swapped(): return lax.all_to_all(value, 'exp', split_axis=0, concat_axis=0, tiled=True)  7.18 us
    ppermute x7, starting transfers between devices, moved(): lax.ppermute(value, 'exp', [(e, e ^ steps[e % 2]) for e in range(owners)])  6.98 us
    unnamed x27, local copies, waits for them, and re-layouts  4.57 us
    ppermute x3, waiting for transfers between devices, key_blocks(): lax.ppermute(pair, 'ctx', [(c, c + step) for c in range(cycle - step)])  4.04 us
    ppermute x3, starting transfers between devices, block_terms(): total = total + lax.ppermute(terms[step], 'ctx', pairs).astype(jnp.float32)  3.86 us
  transfers between devices with their start and end apart: 16, of which 6 were waited for; matrix products, arithmetic and copies ran while one was open for 5% of the time, Pallas kernels for 22%

profile of v7, /device:TPU:0, one launch (start us, length us, event | category | flops | bytes accessed | tf_op | source)
XLA Modules:
  0.0 81.7 jit_solution(8040056577519588760)
XLA Ops:
  0.6 3.0 %collective-permute-start.3 = (bf16[128,4096]{1,0:T(8,128)(2,1)}, bf16[128,4096]{1,0:T(8,128)(2,1)}, u32[]{:S(2)}, u32[]{:S(2)}) collective-permute-start(bf16[128,4096]{1,0:T(8,128)(2,1)} %refs_0_.1), channel_id=1, source_target_pairs={{0,4},{1,3},{2,6},{3,1},{4,0},{5,7},{6,2},{7,5},{8,12},{9,11},{10,... | collective-permute-start | bytes 3145736 | tf_op jit(solution)/shard_map/ppermute | solution.py:376
  3.7 1.5 %collective-permute-start.4 = (bf16[128,4096]{1,0:T(8,128)(2,1)}, bf16[128,4096]{1,0:T(8,128)(2,1)}, u32[]{:S(2)}, u32[]{:S(2)}) collective-permute-start(bf16[128,4096]{1,0:T(8,128)(2,1)} %refs_0_.1), channel_id=1, source_target_pairs={{0,2},{1,5},{2,0},{3,7},{4,6},{5,1},{6,4},{7,3},{8,10},{9,13},{10,... | collective-permute-start | bytes 3145736 | tf_op jit(solution)/shard_map/ppermute | solution.py:376
  5.2 0.7 convert_element_type.28
  5.8 1.5 %copy.20.hidden_ref = bf16[1,3,8,65,384]{4,3,2,1,0:T(8,128)(2,1)S(1)} copy(bf16[1,3,8,65,384]{4,2,3,1,0:T(8,128)(2,1)} %param.23) | data formatting | bytes 2396160 | tf_op args[11]
  7.3 0.0 copy-start.10
  7.3 0.0 copy-start.11
  7.3 0.0 copy-start.2
  7.3 0.0 copy-start.3
  7.4 0.0 copy-start.4
  7.4 0.0 copy-start.5
  7.4 0.0 copy-start.6
  7.5 0.8 fusion.1
  8.3 5.5 %collective-permute-start.2 = (bf16[256,256]{1,0:T(8,128)(2,1)S(1)}, bf16[256,256]{1,0:T(8,128)(2,1)S(1)}, u32[]{:S(2)}, u32[]{:S(2)}) collective-permute-start(bf16[256,256]{1,0:T(8,128)(2,1)S(1)} %pad_maximum_fusion.rest_0_), channel_id=1, source_target_pairs={{0,24},{1,25},{2,26},{3,27},{4,28},{5,29},{6,30},{7,31}} | collective-permute-start | bytes 393224 | tf_op jit(solution)/shard_map/ppermute | solution.py:102
  13.9 1.3 %collective-permute-start.1 = (bf16[256,256]{1,0:T(8,128)(2,1)S(1)}, bf16[256,256]{1,0:T(8,128)(2,1)S(1)}, u32[]{:S(2)}, u32[]{:S(2)}) collective-permute-start(bf16[256,256]{1,0:T(8,128)(2,1)S(1)} %pad_maximum_fusion.rest_0_), channel_id=1, source_target_pairs={{0,16},{8,24},{1,17},{9,25},{2,18},{10,26},{3,19},{11,27},{4,20},{... | collective-permute-start | bytes 393224 | tf_op jit(solution)/shard_map/ppermute | solution.py:102
  15.2 2.5 %collective-permute-start = (bf16[256,256]{1,0:T(8,128)(2,1)S(1)}, bf16[256,256]{1,0:T(8,128)(2,1)S(1)}, u32[]{:S(2)}, u32[]{:S(2)}) collective-permute-start(bf16[256,256]{1,0:T(8,128)(2,1)S(1)} %pad_maximum_fusion.rest_0_), channel_id=1, source_target_pairs={{0,8},{8,16},{16,24},{1,9},{9,17},{17,25},{2,10},{10,18},{18,26},{... | collective-permute-start | bytes 393224 | tf_op jit(solution)/shard_map/ppermute | solution.py:102
  17.6 0.2 collective-permute-done.2.rest_3_
  17.8 2.5 %collective-permute-done.1.rest_2_ = bf16[256,256]{1,0:T(8,128)(2,1)S(1)} collective-permute-done((bf16[256,256]{1,0:T(8,128)(2,1)S(1)}, bf16[256,256]{1,0:T(8,128)(2,1)S(1)}, u32[]{:S(2)}, u32[]{:S(2)}) %collective-permute-start.1) | collective-permute-done | bytes 131104 | tf_op jit(solution)/shard_map/ppermute | solution.py:102
  20.3 1.4 %collective-permute-done.rest_1_ = bf16[256,256]{1,0:T(8,128)(2,1)S(1)} collective-permute-done((bf16[256,256]{1,0:T(8,128)(2,1)S(1)}, bf16[256,256]{1,0:T(8,128)(2,1)S(1)}, u32[]{:S(2)}, u32[]{:S(2)}) %collective-permute-start) | collective-permute-done | bytes 131104 | tf_op jit(solution)/shard_map/ppermute | solution.py:102
  21.7 3.1 %attention.1 = (bf16[256,512]{1,0:T(8,128)(2,1)}, bf16[256,256]{1,0:T(8,128)(2,1)S(1)}, bf16[256,256]{1,0:T(8,128)(2,1)S(1)}, bf16[256,256]{1,0:T(8,128)(2,1)S(1)}, bf16[256,256]{1,0:T(8,128)(2,1)S(1)}) custom-call(s32[1]{0:T(128)} %bitcast.place_ref, s32[4,4]{1,0:T(4,128)S(1)} %copy-done.6, bf16[256,512]{1,0:T(8,128)(2,1)S(1)} %copy-done.2, ...), custom_call_target="tpu_custom_call" | custom-call | tf_op jit(solution)/shard_map/attention/pallas_call | solution.py:112
  24.8 0.7 copy-done.8
  25.5 0.7 copy-done.9
  26.1 1.4 %collective-permute-done.3.refs_2_ = bf16[128,4096]{1,0:T(8,128)(2,1)} collective-permute-done((bf16[128,4096]{1,0:T(8,128)(2,1)}, bf16[128,4096]{1,0:T(8,128)(2,1)}, u32[]{:S(2)}, u32[]{:S(2)}) %collective-permute-start.3) | collective-permute-done | bytes 1048608 | tf_op jit(solution)/shard_map/ppermute | solution.py:376
  27.5 1.5 %collective-permute-start.11 = (bf16[128,4096]{1,0:T(8,128)(2,1)}, bf16[128,4096]{1,0:T(8,128)(2,1)}, u32[]{:S(2)}, u32[]{:S(2)}) collective-permute-start(bf16[128,4096]{1,0:T(8,128)(2,1)} %collective-permute-done.3.refs_2_), channel_id=1, source_target_pairs={{0,2},{1,5},{2,0},{3,7},{4,6},{5,1},{6,4},{7,3},{8,10},{9,13},{10,... | collective-permute-start | bytes 3145736 | tf_op jit(solution)/shard_map/ppermute | solution.py:376
  29.0 3.7 %all-to-all-start = ((bf16[8,66,384]{2,1,0:T(8,128)(2,1)}), bf16[8,66,384]{2,1,0:T(8,128)(2,1)S(1)}, u32[]{:S(2)}, u32[]{:S(2)}) async-start(bf16[8,66,384]{2,1,0:T(8,128)(2,1)} %fusion.1), calls=%async_computation | async-start | bytes 884736 | tf_op jit(solution)/shard_map/all_to_all | solution.py:326
  32.7 1.3 %collective-permute-start.5 = (bf16[256,256]{1,0:T(8,128)(2,1)}, bf16[256,256]{1,0:T(8,128)(2,1)S(1)}, u32[]{:S(2)}, u32[]{:S(2)}) collective-permute-start(bf16[256,256]{1,0:T(8,128)(2,1)} %copy-done.9), channel_id=1, source_target_pairs={{8,0},{16,8},{24,16},{9,1},{17,9},{25,17},{10,2},{18,10},{26,18},{... | collective-permute-start | bytes 393224 | tf_op jit(solution)/shard_map/ppermute | solution.py:151
  34.0 1.3 %collective-permute-start.6 = (bf16[256,256]{1,0:T(8,128)(2,1)}, bf16[256,256]{1,0:T(8,128)(2,1)S(1)}, u32[]{:S(2)}, u32[]{:S(2)}) collective-permute-start(bf16[256,256]{1,0:T(8,128)(2,1)} %copy-done.8), channel_id=1, source_target_pairs={{16,0},{24,8},{17,1},{25,9},{18,2},{26,10},{19,3},{27,11},{20,4},{... | collective-permute-start | bytes 393224 | tf_op jit(solution)/shard_map/ppermute | solution.py:151
  35.3 1.3 %collective-permute-start.7 = (bf16[256,256]{1,0:T(8,128)(2,1)S(1)}, bf16[256,256]{1,0:T(8,128)(2,1)S(1)}, u32[]{:S(2)}, u32[]{:S(2)}) collective-permute-start(bf16[256,256]{1,0:T(8,128)(2,1)S(1)} %get-tuple-element.29), channel_id=1, source_target_pairs={{24,0},{25,1},{26,2},{27,3},{28,4},{29,5},{30,6},{31,7}} | collective-permute-start | bytes 393224 | tf_op jit(solution)/shard_map/ppermute | solution.py:151
  36.6 12.6 %all-to-all-done.mixed_ref = bf16[8,66,384]{2,1,0:T(8,128)(2,1)S(1)} async-done(((bf16[8,66,384]{2,1,0:T(8,128)(2,1)}), bf16[8,66,384]{2,1,0:T(8,128)(2,1)S(1)}, u32[]{:S(2)}, u32[]{:S(2)}) %all-to-all-start) | async-done | bytes 405536 | tf_op jit(solution)/shard_map/all_to_all | solution.py:326
  49.1 1.3 %picked.1 = bf16[8,64,384]{2,1,0:T(8,128)(2,1)} custom-call(s32[16]{0:T(128)S(1)} %copy-done.7, bf16[8,66,384]{2,1,0:T(8,128)(2,1)S(1)} %all-to-all-done.mixed_ref), custom_call_target="tpu_custom_call" | custom-call | tf_op jit(solution)/shard_map/picked/pallas_call | solution.py:191
  50.5 0.0 collective-permute-done.4.refs_4_
  50.5 3.5 %all-to-all-start.1 = ((bf16[8,64,384]{2,1,0:T(8,128)(2,1)}), bf16[8,64,384]{2,1,0:T(8,128)(2,1)S(1)}, u32[]{:S(2)}, u32[]{:S(2)}) async-start(bf16[8,64,384]{2,1,0:T(8,128)(2,1)} %picked.1), calls=%async_computation.1 | async-start | bytes 786432 | tf_op jit(solution)/shard_map/all_to_all | solution.py:326
  53.9 0.4 collective-permute-start.8
  54.3 0.7 add_convert_fusion
  55.1 0.2 collective-permute-start.9
  55.2 0.3 collective-permute-start.10
  55.6 6.6 %all-to-all-done.1.side_ref = bf16[8,64,384]{2,1,0:T(8,128)(2,1)S(1)} async-done(((bf16[8,64,384]{2,1,0:T(8,128)(2,1)}), bf16[8,64,384]{2,1,0:T(8,128)(2,1)S(1)}, u32[]{:S(2)}, u32[]{:S(2)}) %all-to-all-start.1) | async-done | bytes 393248 | tf_op jit(solution)/shard_map/all_to_all | solution.py:326
  62.2 0.7 copy-done
  63.0 1.0 %copy-done.1 = bf16[8,64,384]{2,1,0:T(8,128)(2,1)S(1)} copy-done((bf16[8,64,384]{2,1,0:T(8,128)(2,1)S(1)}, bf16[8,64,384]{2,1,0:T(8,128)(2,1)}, u32[]{:S(2)}) %copy-start.1) | copy-done | bytes 393240
  63.9 2.9 %weighted.1.weight_ref = bf16[768,1024]{1,0:T(8,128)(2,1)S(1)} custom-call(s32[1]{0:T(128)} %bitcast.5.own_ref, s32[16]{0:T(128)S(1)} %copy-done.7, bf16[8,66,384]{2,1,0:T(8,128)(2,1)S(1)} %all-to-all-done.mixed_ref, bf16[1,3,8,65,384]{4,3,2,1,0:T(8,128)(2,1)S(1)} %copy.20.hidden_ref, bf16[8,64,384]{2,1,0:T(8,128)(2,1)S(1)} %copy-done.1), custom_call_target="tpu_custom_call" | custom-call | tf_op jit(solution)/shard_map/weighted/pallas_call | solution.py:243
  66.8 0.0 collective-permute-done.11.refs_6_
  66.9 0.1 collective-permute-start.12
  66.9 3.4 %all-to-all-start.2 = ((bf16[8,32,256]{2,1,0:T(8,128)(2,1)}), bf16[8,32,256]{2,1,0:T(8,128)(2,1)S(1)}, u32[]{:S(2)}, u32[]{:S(2)}) async-start(bf16[8,32,256]{2,1,0:T(8,128)(2,1)} %bitcast.8), calls=%async_computation.2 | async-start | bytes 262144 | tf_op jit(solution)/shard_map/all_to_all | solution.py:158
  70.3 0.0 collective-permute-done.8.refs_1_
  70.3 0.0 collective-permute-done.9.refs_3_
  70.4 0.0 collective-permute-done.12.refs_7_
  70.4 10.7 %tiles.1 = f32[2,384,4096]{2,1,0:T(8,128)} custom-call(bf16[768,1024]{1,0:T(8,128)(2,1)S(1)} %weighted.1.weight_ref, bf16[128,4096]{1,0:T(8,128)(2,1)} %refs_0_.1, bf16[128,4096]{1,0:T(8,128)(2,1)} %collective-permute-done.8.refs_1_, bf16[128,4096]{1,0:T(8,128)(2,1)} %collective-permute-done.3.refs_2_, bf16[128,4096]{1,0:T(8,128)(2,1)} %collective-permute-done.9.refs_3_, ...), custom_call_target="tpu_custom_call" | custom-call | tf_op jit(solution)/shard_map/tiles/pallas_call | solution.py:309
  81.1 0.0 all-to-all-done.2.parts_ref
  81.1 0.6 sums.1
  (23 shorter events, 0.1 us)
Async XLA Ops:
  0.6 6.7 %copy-start.12 = (s32[128,8]{0,1:T(8,128)S(1)}, s32[128,8]{0,1:T(8,128)}, u32[]{:S(2)}) copy-start(s32[128,8]{0,1:T(8,128)} %param.19) | copy-start | bytes 12292
  0.6 26.8 %collective-permute-start.3 = (bf16[128,4096]{1,0:T(8,128)(2,1)}, bf16[128,4096]{1,0:T(8,128)(2,1)}, u32[]{:S(2)}, u32[]{:S(2)}) collective-permute-start(bf16[128,4096]{1,0:T(8,128)(2,1)} %refs_0_.1), channel_id=1, source_target_pairs={{0,4},{1,3},{2,6},{3,1},{4,0},{5,7},{6,2},{7,5},{8,12},{9,11},{10,... | collective-permute-start | bytes 3145736 | tf_op jit(solution)/shard_map/ppermute | solution.py:376
  3.7 46.8 %collective-permute-start.4 = (bf16[128,4096]{1,0:T(8,128)(2,1)}, bf16[128,4096]{1,0:T(8,128)(2,1)}, u32[]{:S(2)}, u32[]{:S(2)}) collective-permute-start(bf16[128,4096]{1,0:T(8,128)(2,1)} %refs_0_.1), channel_id=1, source_target_pairs={{0,2},{1,5},{2,0},{3,7},{4,6},{5,1},{6,4},{7,3},{8,10},{9,13},{10,... | collective-permute-start | bytes 3145736 | tf_op jit(solution)/shard_map/ppermute | solution.py:376
  7.3 1.0 %copy-start.10 = (bf16[256,256]{1,0:T(8,128)(2,1)S(1)}, bf16[256,256]{1,0:T(8,128)(2,1)}, u32[]{:S(2)}) copy-start(bf16[256,256]{1,0:T(8,128)(2,1)} %param.14) | copy-start | bytes 393220
  7.3 1.0 %copy-start.11 = (bf16[256,256]{1,0:T(8,128)(2,1)S(1)}, bf16[256,256]{1,0:T(8,128)(2,1)}, u32[]{:S(2)}) copy-start(bf16[256,256]{1,0:T(8,128)(2,1)} %param.13) | copy-start | bytes 393220
  7.3 14.4 %copy-start.2 = (bf16[256,512]{1,0:T(8,128)(2,1)S(1)}, bf16[256,512]{1,0:T(8,128)(2,1)}, u32[]{:S(2)}) copy-start(bf16[256,512]{1,0:T(8,128)(2,1)} %query_ref.1) | copy-start | bytes 786436
  7.3 14.3 %copy-start.3 = (bf16[256,512]{1,0:T(8,128)(2,1)S(1)}, bf16[256,512]{1,0:T(8,128)(2,1)}, u32[]{:S(2)}) copy-start(bf16[256,512]{1,0:T(8,128)(2,1)} %grad_ref.1) | copy-start | bytes 786436
  7.4 14.3 %copy-start.4 = (bf16[256,512]{1,0:T(8,128)(2,1)S(1)}, bf16[256,512]{1,0:T(8,128)(2,1)}, u32[]{:S(2)}) copy-start(bf16[256,512]{1,0:T(8,128)(2,1)} %out_ref.1) | copy-start | bytes 786436
  7.4 14.3 %copy-start.5 = (f32[4,256]{1,0:T(4,128)S(1)}, f32[4,256]{1,0:T(4,128)}, u32[]{:S(2)}) copy-start(f32[4,256]{1,0:T(4,128)} %lse_ref.1) | copy-start | bytes 12292
  7.4 14.3 %copy-start.6 = (s32[4,4]{1,0:T(4,128)S(1)}, s32[4,4]{1,0:T(4,128)}, u32[]{:S(2)}) copy-start(s32[4,4]{1,0:T(4,128)} %mask_ref.1) | copy-start | bytes 196
  8.3 40.8 %copy-start.7 = (s32[16]{0:T(128)S(1)}, s32[16]{0:T(128)}, u32[]{:S(2)}) copy-start(s32[16]{0:T(128)} %shadow_ref.3) | copy-start | bytes 196
  8.3 9.5 %collective-permute-start.2 = (bf16[256,256]{1,0:T(8,128)(2,1)S(1)}, bf16[256,256]{1,0:T(8,128)(2,1)S(1)}, u32[]{:S(2)}, u32[]{:S(2)}) collective-permute-start(bf16[256,256]{1,0:T(8,128)(2,1)S(1)} %pad_maximum_fusion.rest_0_), channel_id=1, source_target_pairs={{0,24},{1,25},{2,26},{3,27},{4,28},{5,29},{6,30},{7,31}} | collective-permute-start | bytes 393224 | tf_op jit(solution)/shard_map/ppermute | solution.py:102
  13.9 6.4 %collective-permute-start.1 = (bf16[256,256]{1,0:T(8,128)(2,1)S(1)}, bf16[256,256]{1,0:T(8,128)(2,1)S(1)}, u32[]{:S(2)}, u32[]{:S(2)}) collective-permute-start(bf16[256,256]{1,0:T(8,128)(2,1)S(1)} %pad_maximum_fusion.rest_0_), channel_id=1, source_target_pairs={{0,16},{8,24},{1,17},{9,25},{2,18},{10,26},{3,19},{11,27},{4,20},{... | collective-permute-start | bytes 393224 | tf_op jit(solution)/shard_map/ppermute | solution.py:102
  15.2 6.5 %collective-permute-start = (bf16[256,256]{1,0:T(8,128)(2,1)S(1)}, bf16[256,256]{1,0:T(8,128)(2,1)S(1)}, u32[]{:S(2)}, u32[]{:S(2)}) collective-permute-start(bf16[256,256]{1,0:T(8,128)(2,1)S(1)} %pad_maximum_fusion.rest_0_), channel_id=1, source_target_pairs={{0,8},{8,16},{16,24},{1,9},{9,17},{17,25},{2,10},{10,18},{18,26},{... | collective-permute-start | bytes 393224 | tf_op jit(solution)/shard_map/ppermute | solution.py:102
  24.8 0.7 copy-start.8
  25.4 0.7 copy-start.9
  27.5 39.4 %collective-permute-start.11 = (bf16[128,4096]{1,0:T(8,128)(2,1)}, bf16[128,4096]{1,0:T(8,128)(2,1)}, u32[]{:S(2)}, u32[]{:S(2)}) collective-permute-start(bf16[128,4096]{1,0:T(8,128)(2,1)} %collective-permute-done.3.refs_2_), channel_id=1, source_target_pairs={{0,2},{1,5},{2,0},{3,7},{4,6},{5,1},{6,4},{7,3},{8,10},{9,13},{10,... | collective-permute-start | bytes 3145736 | tf_op jit(solution)/shard_map/ppermute | solution.py:376
  29.0 20.2 %all-to-all-start = ((bf16[8,66,384]{2,1,0:T(8,128)(2,1)}), bf16[8,66,384]{2,1,0:T(8,128)(2,1)S(1)}, u32[]{:S(2)}, u32[]{:S(2)}) async-start(bf16[8,66,384]{2,1,0:T(8,128)(2,1)} %fusion.1), calls=%async_computation | async-start | bytes 884736 | tf_op jit(solution)/shard_map/all_to_all | solution.py:326
  32.7 21.7 %collective-permute-start.5 = (bf16[256,256]{1,0:T(8,128)(2,1)}, bf16[256,256]{1,0:T(8,128)(2,1)S(1)}, u32[]{:S(2)}, u32[]{:S(2)}) collective-permute-start(bf16[256,256]{1,0:T(8,128)(2,1)} %copy-done.9), channel_id=1, source_target_pairs={{8,0},{16,8},{24,16},{9,1},{17,9},{25,17},{10,2},{18,10},{26,18},{... | collective-permute-start | bytes 393224 | tf_op jit(solution)/shard_map/ppermute | solution.py:151
  34.0 20.4 %collective-permute-start.6 = (bf16[256,256]{1,0:T(8,128)(2,1)}, bf16[256,256]{1,0:T(8,128)(2,1)S(1)}, u32[]{:S(2)}, u32[]{:S(2)}) collective-permute-start(bf16[256,256]{1,0:T(8,128)(2,1)} %copy-done.8), channel_id=1, source_target_pairs={{16,0},{24,8},{17,1},{25,9},{18,2},{26,10},{19,3},{27,11},{20,4},{... | collective-permute-start | bytes 393224 | tf_op jit(solution)/shard_map/ppermute | solution.py:151
  35.3 19.1 %collective-permute-start.7 = (bf16[256,256]{1,0:T(8,128)(2,1)S(1)}, bf16[256,256]{1,0:T(8,128)(2,1)S(1)}, u32[]{:S(2)}, u32[]{:S(2)}) collective-permute-start(bf16[256,256]{1,0:T(8,128)(2,1)S(1)} %get-tuple-element.29), channel_id=1, source_target_pairs={{24,0},{25,1},{26,2},{27,3},{28,4},{29,5},{30,6},{31,7}} | collective-permute-start | bytes 393224 | tf_op jit(solution)/shard_map/ppermute | solution.py:151
  50.5 11.7 %all-to-all-start.1 = ((bf16[8,64,384]{2,1,0:T(8,128)(2,1)}), bf16[8,64,384]{2,1,0:T(8,128)(2,1)S(1)}, u32[]{:S(2)}, u32[]{:S(2)}) async-start(bf16[8,64,384]{2,1,0:T(8,128)(2,1)} %picked.1), calls=%async_computation.1 | async-start | bytes 786432 | tf_op jit(solution)/shard_map/all_to_all | solution.py:326
  53.9 16.4 %collective-permute-start.8 = (bf16[128,4096]{1,0:T(8,128)(2,1)}, bf16[128,4096]{1,0:T(8,128)(2,1)}, u32[]{:S(2)}, u32[]{:S(2)}) collective-permute-start(bf16[128,4096]{1,0:T(8,128)(2,1)} %refs_0_.1), channel_id=1, source_target_pairs={{0,1},{1,0},{2,3},{3,2},{4,5},{5,4},{6,7},{7,6},{8,9},{9,8},{10,11... | collective-permute-start | bytes 3145736 | tf_op jit(solution)/shard_map/ppermute | solution.py:376
  55.1 15.3 %collective-permute-start.9 = (bf16[128,4096]{1,0:T(8,128)(2,1)}, bf16[128,4096]{1,0:T(8,128)(2,1)}, u32[]{:S(2)}, u32[]{:S(2)}) collective-permute-start(bf16[128,4096]{1,0:T(8,128)(2,1)} %collective-permute-done.3.refs_2_), channel_id=1, source_target_pairs={{0,1},{1,0},{2,3},{3,2},{4,5},{5,4},{6,7},{7,6},{8,9},{9,8},{10,11... | collective-permute-start | bytes 3145736 | tf_op jit(solution)/shard_map/ppermute | solution.py:376
  55.2 15.1 %collective-permute-start.10 = (bf16[128,4096]{1,0:T(8,128)(2,1)}, bf16[128,4096]{1,0:T(8,128)(2,1)}, u32[]{:S(2)}, u32[]{:S(2)}) collective-permute-start(bf16[128,4096]{1,0:T(8,128)(2,1)} %collective-permute-done.4.refs_4_), channel_id=1, source_target_pairs={{0,1},{1,0},{2,3},{3,2},{4,5},{5,4},{6,7},{7,6},{8,9},{9,8},{10,11... | collective-permute-start | bytes 3145736 | tf_op jit(solution)/shard_map/ppermute | solution.py:376
  62.2 0.7 copy-start
  62.9 1.0 %copy-start.1 = (bf16[8,64,384]{2,1,0:T(8,128)(2,1)S(1)}, bf16[8,64,384]{2,1,0:T(8,128)(2,1)}, u32[]{:S(2)}) copy-start(bf16[8,64,384]{2,1,0:T(8,128)(2,1)} %copy-done) | copy-start | bytes 1179652
  66.9 3.5 %collective-permute-start.12 = (bf16[128,4096]{1,0:T(8,128)(2,1)}, bf16[128,4096]{1,0:T(8,128)(2,1)S(1)}, u32[]{:S(2)}, u32[]{:S(2)}) collective-permute-start(bf16[128,4096]{1,0:T(8,128)(2,1)} %collective-permute-done.11.refs_6_), channel_id=1, source_target_pairs={{0,1},{1,0},{2,3},{3,2},{4,5},{5,4},{6,7},{7,6},{8,9},{9,8},{10,11... | collective-permute-start | bytes 3145736 | tf_op jit(solution)/shard_map/ppermute | solution.py:376
  66.9 14.2 %all-to-all-start.2 = ((bf16[8,32,256]{2,1,0:T(8,128)(2,1)}), bf16[8,32,256]{2,1,0:T(8,128)(2,1)S(1)}, u32[]{:S(2)}, u32[]{:S(2)}) async-start(bf16[8,32,256]{2,1,0:T(8,128)(2,1)} %bitcast.8), calls=%async_computation.2 | async-start | bytes 262144 | tf_op jit(solution)/shard_map/all_to_all | solution.py:158

commit v8 on v3

--- a/solution.py
+++ b/solution.py
@@ -401,14 +401,16 @@
     first = moved(moe_grad, [held[1] for held in steps])
     arrived = key_blocks(keys, values, queries.shape[1] // lse_excess.shape[0])
     mixed, sent = source_rows(expert_ids, route_probs, shadow_list, stored_hidden_state)
-    moe_grad, first = lax.optimization_barrier((moe_grad, first))
-    second = moved(moe_grad, [held[2] for held in steps])
+    ready, mixed = lax.optimization_barrier((moe_grad, mixed))
+    second = moved(ready, [held[2] for held in steps])
     sent, arrived = lax.optimization_barrier((sent, arrived))
     shadow_rows = swapped(sent)
     query_grad, terms = attention(
         queries, arrived, attn_out, attn_out_grad, lse_excess, block_mask
     )
-    first, shadow_rows, query_grad = lax.optimization_barrier((first, shadow_rows, query_grad))
+    first, second, shadow_rows, query_grad = lax.optimization_barrier(
+        (first, second, shadow_rows, query_grad)
+    )
     weighted = expert_rows(
         mixed, shadow_rows, shadow_list, stored_hidden_state, expert_ids.shape[0]
     )

time: 88.6 us -> 83.3 us (0.940)
  waiting for transfers between devices: 32.9 us -> 29.8 us
  starting transfers between devices: 29.4 us -> 27.3 us
    ppermute x7, waiting for transfers between devices: 19.9 us -> 10.6 us  [moved(): lax.ppermute(value, 'exp', [(e, e ^ steps[e % 2]) for e in range(owners)])]
    all_to_all x2, waiting for transfers between devices: 6.32 us -> 12.9 us  [swapped(): return lax.all_to_all(value, 'exp', split_axis=0, concat_axis=0, tiled=True)]
    ppermute x7, starting transfers between devices: 6.08 us -> 2.81 us  [moved(): lax.ppermute(value, 'exp', [(e, e ^ steps[e % 2]) for e in range(owners)])]
    all_to_all x2, starting transfers between devices: 7.48 us -> 9.72 us  [swapped(): return lax.all_to_all(value, 'exp', split_axis=0, concat_axis=0, tiled=True)]
    all_to_all x1, starting transfers between devices: 6.51 us -> 5.49 us  [summed_terms(): lax.all_to_all(terms.reshape(cycle * owners, rows // owners, columns), ('...]
  transfers between devices with their start and end apart: 13 -> 13, of which waited for: 6 -> 6; matrix products, arithmetic and copies ran while one was open for 3% -> 0% of each run, Pallas kernels for 21% -> 22%
where the time goes in v8:
time: 83.3 us; the launch traced here: 82.2 us
  waiting for transfers between devices  29.8 us (36%)
  starting transfers between devices  27.3 us (33%)
  Pallas kernels  18.7 us (22%)
  local copies, waits for them, and re-layouts  4.12 us (5%)
  other arithmetic  1.54 us (2%)
  between operations  0.84 us (1%)
    all_to_all x2, waiting for transfers between devices, swapped(): return lax.all_to_all(value, 'exp', split_axis=0, concat_axis=0, tiled=True)  12.9 us
    pallas_call x1, Pallas kernels, tile_sums(): pl.pallas_call(tile_kernel, out_shape=jax.ShapeDtypeStruct((per_dev, rows...  10.7 us
    ppermute x7, waiting for transfers between devices, moved(): lax.ppermute(value, 'exp', [(e, e ^ steps[e % 2]) for e in range(owners)])  10.6 us
    all_to_all x2, starting transfers between devices, swapped(): return lax.all_to_all(value, 'exp', split_axis=0, concat_axis=0, tiled=True)  9.72 us
    ppermute x3, starting transfers between devices, key_blocks(): lax.ppermute(pair, 'ctx', [(c, c + step) for c in range(cycle - step)])  9.28 us
    all_to_all x1, starting transfers between devices, summed_terms(): lax.all_to_all(terms.reshape(cycle * owners, rows // owners, columns), ('...  5.49 us
    all_to_all x1, waiting for transfers between devices, summed_terms(): lax.all_to_all(terms.reshape(cycle * owners, rows // owners, columns), ('...  4.77 us
    unnamed x25, local copies, waits for them, and re-layouts  4.07 us
  transfers between devices with their start and end apart: 13, of which 6 were waited for; matrix products, arithmetic and copies ran while one was open for 0% of the time, Pallas kernels for 22%

profile of v8, /device:TPU:0, one launch (start us, length us, event | category | flops | bytes accessed | tf_op | source)
XLA Modules:
  0.0 82.2 jit_solution(6444854166783011030)
XLA Ops:
  0.6 0.7 convert_element_type.13
  1.3 1.5 %copy.20.hidden_ref = bf16[1,3,8,65,384]{4,3,2,1,0:T(8,128)(2,1)S(1)} copy(bf16[1,3,8,65,384]{4,2,3,1,0:T(8,128)(2,1)} %param.23) | data formatting | bytes 2396160 | tf_op args[11]
  2.8 0.0 copy-start.9
  2.8 0.0 copy-start.10
  2.9 0.0 copy-done.11
  2.9 0.0 copy-start.8
  2.9 0.8 fusion.1
  3.7 0.0 copy-start.7
  3.7 5.3 %all-to-all-start = ((bf16[8,66,384]{2,1,0:T(8,128)(2,1)}), bf16[8,66,384]{2,1,0:T(8,128)(2,1)S(1)}, u32[]{:S(2)}, u32[]{:S(2)}) async-start(bf16[8,66,384]{2,1,0:T(8,128)(2,1)} %fusion.1), calls=%async_computation | async-start | bytes 884736 | tf_op jit(solution)/shard_map/all_to_all | solution.py:314
  9.1 2.0 %collective-permute-start = (bf16[128,4096]{1,0:T(8,128)(2,1)}, bf16[128,4096]{1,0:T(8,128)(2,1)}, u32[]{:S(2)}, u32[]{:S(2)}) collective-permute-start(bf16[128,4096]{1,0:T(8,128)(2,1)} %refs_0_.1), channel_id=1, source_target_pairs={{0,4},{1,3},{2,6},{3,1},{4,0},{5,7},{6,2},{7,5},{8,12},{9,11},{10,... | collective-permute-start | bytes 3145736 | tf_op jit(solution)/shard_map/ppermute | solution.py:366
  11.1 7.3 %all-to-all-done.mixed_ref = bf16[8,66,384]{2,1,0:T(8,128)(2,1)S(1)} async-done(((bf16[8,66,384]{2,1,0:T(8,128)(2,1)}), bf16[8,66,384]{2,1,0:T(8,128)(2,1)S(1)}, u32[]{:S(2)}, u32[]{:S(2)}) %all-to-all-start) | async-done | bytes 405536 | tf_op jit(solution)/shard_map/all_to_all | solution.py:314
  18.4 0.1 collective-permute-start.1
  18.5 0.0 copy-done.9
  18.5 0.0 copy-done.10
  18.5 5.5 %collective-permute-start.4 = (bf16[256,256]{1,0:T(8,128)(2,1)S(1)}, bf16[256,256]{1,0:T(8,128)(2,1)S(1)}, u32[]{:S(2)}, u32[]{:S(2)}) collective-permute-start(bf16[256,256]{1,0:T(8,128)(2,1)S(1)} %pad_maximum_fusion.rest_0_), channel_id=1, source_target_pairs={{0,24},{1,25},{2,26},{3,27},{4,28},{5,29},{6,30},{7,31}} | collective-permute-start | bytes 393224 | tf_op jit(solution)/shard_map/ppermute | solution.py:98
  24.1 1.3 %collective-permute-start.3 = (bf16[256,256]{1,0:T(8,128)(2,1)S(1)}, bf16[256,256]{1,0:T(8,128)(2,1)S(1)}, u32[]{:S(2)}, u32[]{:S(2)}) collective-permute-start(bf16[256,256]{1,0:T(8,128)(2,1)S(1)} %pad_maximum_fusion.rest_0_), channel_id=1, source_target_pairs={{0,16},{8,24},{1,17},{9,25},{2,18},{10,26},{3,19},{11,27},{4,20},{... | collective-permute-start | bytes 393224 | tf_op jit(solution)/shard_map/ppermute | solution.py:98
  25.4 2.5 %collective-permute-start.2 = (bf16[256,256]{1,0:T(8,128)(2,1)S(1)}, bf16[256,256]{1,0:T(8,128)(2,1)S(1)}, u32[]{:S(2)}, u32[]{:S(2)}) collective-permute-start(bf16[256,256]{1,0:T(8,128)(2,1)S(1)} %pad_maximum_fusion.rest_0_), channel_id=1, source_target_pairs={{0,8},{8,16},{16,24},{1,9},{9,17},{17,25},{2,10},{10,18},{18,26},{... | collective-permute-start | bytes 393224 | tf_op jit(solution)/shard_map/ppermute | solution.py:98
  27.8 0.0 copy-done.8
  27.9 1.3 %picked.1 = bf16[8,64,384]{2,1,0:T(8,128)(2,1)} custom-call(s32[16]{0:T(128)S(1)} %copy-done.8, bf16[8,66,384]{2,1,0:T(8,128)(2,1)S(1)} %all-to-all-done.mixed_ref), custom_call_target="tpu_custom_call" | custom-call | tf_op jit(solution)/shard_map/picked/pallas_call | solution.py:179
  29.2 0.0 collective-permute-done.4.rest_3_
  29.2 0.1 collective-permute-done.3.rest_2_
  29.3 1.4 %collective-permute-done.2.rest_1_ = bf16[256,256]{1,0:T(8,128)(2,1)S(1)} collective-permute-done((bf16[256,256]{1,0:T(8,128)(2,1)S(1)}, bf16[256,256]{1,0:T(8,128)(2,1)S(1)}, u32[]{:S(2)}, u32[]{:S(2)}) %collective-permute-start.2) | collective-permute-done | bytes 131104 | tf_op jit(solution)/shard_map/ppermute | solution.py:98
  30.7 4.4 %all-to-all-start.1 = ((bf16[8,64,384]{2,1,0:T(8,128)(2,1)}), bf16[8,64,384]{2,1,0:T(8,128)(2,1)S(1)}, u32[]{:S(2)}, u32[]{:S(2)}) async-start(bf16[8,64,384]{2,1,0:T(8,128)(2,1)} %picked.1), calls=%async_computation.1 | async-start | bytes 786432 | tf_op jit(solution)/shard_map/all_to_all | solution.py:314
  35.1 0.0 copy-done.3
  35.1 0.0 copy-done.4
  35.2 0.0 copy-done.5
  35.2 3.1 %attention.1 = (bf16[256,512]{1,0:T(8,128)(2,1)}, bf16[4,256,256]{2,1,0:T(8,128)(2,1)S(1)}) custom-call(s32[1]{0:T(128)} %bitcast.3.place_ref, s32[4,4]{1,0:T(4,128)S(1)} %copy-done.7, bf16[256,512]{1,0:T(8,128)(2,1)S(1)} %copy-done.3, bf16[256,512]{1,0:T(8,128)(2,1)S(1)} %copy-done.4, bf16[256,512]{1,0:T(8,128)(2,1)S(1)} %copy-done.5, ...), custom_call_target="tpu_custom_call" | custom-call | tf_op jit(solution)/shard_map/attention/pallas_call | solution.py:108
  38.3 0.8 copy-done.2
  39.1 5.5 %all-to-all-done.1.side_ref = bf16[8,64,384]{2,1,0:T(8,128)(2,1)S(1)} async-done(((bf16[8,64,384]{2,1,0:T(8,128)(2,1)}), bf16[8,64,384]{2,1,0:T(8,128)(2,1)S(1)}, u32[]{:S(2)}, u32[]{:S(2)}) %all-to-all-start.1) | async-done | bytes 393248 | tf_op jit(solution)/shard_map/all_to_all | solution.py:314
  44.6 0.7 copy-done
  45.4 0.0 collective-permute-done.refs_2_
  45.4 0.0 collective-permute-done.1.refs_4_
  45.4 0.2 collective-permute-start.8
  45.6 0.0 collective-permute-start.5
  45.6 0.5 collective-permute-start.6
  46.1 0.0 collective-permute-start.7
  46.1 1.0 %copy-done.1 = bf16[8,64,384]{2,1,0:T(8,128)(2,1)S(1)} copy-done((bf16[8,64,384]{2,1,0:T(8,128)(2,1)S(1)}, bf16[8,64,384]{2,1,0:T(8,128)(2,1)}, u32[]{:S(2)}) %copy-start.1) | copy-done | bytes 393240
  47.1 2.8 %weighted.1.weight_ref = bf16[768,1024]{1,0:T(8,128)(2,1)S(1)} custom-call(s32[1]{0:T(128)} %bitcast.6.own_ref, s32[16]{0:T(128)S(1)} %copy-done.8, bf16[8,66,384]{2,1,0:T(8,128)(2,1)S(1)} %all-to-all-done.mixed_ref, bf16[1,3,8,65,384]{4,3,2,1,0:T(8,128)(2,1)S(1)} %copy.20.hidden_ref, bf16[8,64,384]{2,1,0:T(8,128)(2,1)S(1)} %copy-done.1), custom_call_target="tpu_custom_call" | custom-call | tf_op jit(solution)/shard_map/weighted/pallas_call | solution.py:231
  49.9 10.6 %collective-permute-done.8.refs_6_ = bf16[128,4096]{1,0:T(8,128)(2,1)} collective-permute-done((bf16[128,4096]{1,0:T(8,128)(2,1)}, bf16[128,4096]{1,0:T(8,128)(2,1)}, u32[]{:S(2)}, u32[]{:S(2)}) %collective-permute-start.8) | collective-permute-done | bytes 1048608 | tf_op jit(solution)/shard_map/ppermute | solution.py:366
  60.5 0.0 collective-permute-start.9
  60.5 5.5 %all-to-all-start.2 = ((bf16[32,32,256]{2,1,0:T(8,128)(2,1)}), bf16[32,32,256]{2,1,0:T(8,128)(2,1)S(1)}, u32[]{:S(2)}, u32[]{:S(2)}) async-start(bf16[32,32,256]{2,1,0:T(8,128)(2,1)} %bitcast.10), calls=%async_computation.2 | async-start | bytes 1048576 | tf_op jit(solution)/shard_map/all_to_all | solution.py:146
  66.0 0.0 collective-permute-done.5.refs_1_
  66.0 0.0 collective-permute-done.7.refs_5_
  66.0 0.0 collective-permute-done.6.refs_3_
  66.0 0.0 collective-permute-done.9.refs_7_
  66.0 10.7 %tiles.1 = f32[2,384,4096]{2,1,0:T(8,128)} custom-call(bf16[768,1024]{1,0:T(8,128)(2,1)S(1)} %weighted.1.weight_ref, bf16[128,4096]{1,0:T(8,128)(2,1)} %refs_0_.1, bf16[128,4096]{1,0:T(8,128)(2,1)} %collective-permute-done.5.refs_1_, bf16[128,4096]{1,0:T(8,128)(2,1)} %collective-permute-done.refs_2_, bf16[128,4096]{1,0:T(8,128)(2,1)} %collective-permute-done.6.refs_3_, ...), custom_call_target="tpu_custom_call" | custom-call | tf_op jit(solution)/shard_map/tiles/pallas_call | solution.py:297
  76.8 4.8 %all-to-all-done.2 = bf16[32,32,256]{2,1,0:T(8,128)(2,1)S(1)} async-done(((bf16[32,32,256]{2,1,0:T(8,128)(2,1)}), bf16[32,32,256]{2,1,0:T(8,128)(2,1)S(1)}, u32[]{:S(2)}, u32[]{:S(2)}) %all-to-all-start.2) | async-done | bytes 524320 | tf_op jit(solution)/shard_map/all_to_all | solution.py:146
  81.5 0.7 sums.1
  (14 shorter events, 0.1 us)
Async XLA Ops:
  1.3 1.5 %copy-start.11 = (s32[128,8]{0,1:T(8,128)S(1)}, s32[128,8]{0,1:T(8,128)}, u32[]{:S(2)}) copy-start(s32[128,8]{0,1:T(8,128)} %param.19) | copy-start | bytes 12292
  2.8 15.7 %copy-start.9 = (bf16[256,256]{1,0:T(8,128)(2,1)S(1)}, bf16[256,256]{1,0:T(8,128)(2,1)}, u32[]{:S(2)}) copy-start(bf16[256,256]{1,0:T(8,128)(2,1)} %param.14) | copy-start | bytes 393220
  2.8 15.7 %copy-start.10 = (bf16[256,256]{1,0:T(8,128)(2,1)S(1)}, bf16[256,256]{1,0:T(8,128)(2,1)}, u32[]{:S(2)}) copy-start(bf16[256,256]{1,0:T(8,128)(2,1)} %param.13) | copy-start | bytes 393220
  2.9 25.0 %copy-start.8 = (s32[16]{0:T(128)S(1)}, s32[16]{0:T(128)}, u32[]{:S(2)}) copy-start(s32[16]{0:T(128)} %shadow_ref.3) | copy-start | bytes 196
  3.7 31.4 %copy-start.3 = (bf16[256,512]{1,0:T(8,128)(2,1)S(1)}, bf16[256,512]{1,0:T(8,128)(2,1)}, u32[]{:S(2)}) copy-start(bf16[256,512]{1,0:T(8,128)(2,1)} %query_ref.1) | copy-start | bytes 786436
  3.7 31.4 %copy-start.4 = (bf16[256,512]{1,0:T(8,128)(2,1)S(1)}, bf16[256,512]{1,0:T(8,128)(2,1)}, u32[]{:S(2)}) copy-start(bf16[256,512]{1,0:T(8,128)(2,1)} %grad_ref.1) | copy-start | bytes 786436
  3.7 31.4 %copy-start.5 = (bf16[256,512]{1,0:T(8,128)(2,1)S(1)}, bf16[256,512]{1,0:T(8,128)(2,1)}, u32[]{:S(2)}) copy-start(bf16[256,512]{1,0:T(8,128)(2,1)} %out_ref.1) | copy-start | bytes 786436
  3.7 31.4 %copy-start.6 = (f32[4,256]{1,0:T(4,128)S(1)}, f32[4,256]{1,0:T(4,128)}, u32[]{:S(2)}) copy-start(f32[4,256]{1,0:T(4,128)} %lse_ref.1) | copy-start | bytes 12292
  3.7 31.4 %copy-start.7 = (s32[4,4]{1,0:T(4,128)S(1)}, s32[4,4]{1,0:T(4,128)}, u32[]{:S(2)}) copy-start(s32[4,4]{1,0:T(4,128)} %mask_ref.1) | copy-start | bytes 196
  3.7 14.7 %all-to-all-start = ((bf16[8,66,384]{2,1,0:T(8,128)(2,1)}), bf16[8,66,384]{2,1,0:T(8,128)(2,1)S(1)}, u32[]{:S(2)}, u32[]{:S(2)}) async-start(bf16[8,66,384]{2,1,0:T(8,128)(2,1)} %fusion.1), calls=%async_computation | async-start | bytes 884736 | tf_op jit(solution)/shard_map/all_to_all | solution.py:314
  9.1 36.3 %collective-permute-start = (bf16[128,4096]{1,0:T(8,128)(2,1)}, bf16[128,4096]{1,0:T(8,128)(2,1)}, u32[]{:S(2)}, u32[]{:S(2)}) collective-permute-start(bf16[128,4096]{1,0:T(8,128)(2,1)} %refs_0_.1), channel_id=1, source_target_pairs={{0,4},{1,3},{2,6},{3,1},{4,0},{5,7},{6,2},{7,5},{8,12},{9,11},{10,... | collective-permute-start | bytes 3145736 | tf_op jit(solution)/shard_map/ppermute | solution.py:366
  18.4 27.0 %collective-permute-start.1 = (bf16[128,4096]{1,0:T(8,128)(2,1)}, bf16[128,4096]{1,0:T(8,128)(2,1)}, u32[]{:S(2)}, u32[]{:S(2)}) collective-permute-start(bf16[128,4096]{1,0:T(8,128)(2,1)} %refs_0_.1), channel_id=1, source_target_pairs={{0,2},{1,5},{2,0},{3,7},{4,6},{5,1},{6,4},{7,3},{8,10},{9,13},{10,... | collective-permute-start | bytes 3145736 | tf_op jit(solution)/shard_map/ppermute | solution.py:366
  18.5 10.6 %collective-permute-start.4 = (bf16[256,256]{1,0:T(8,128)(2,1)S(1)}, bf16[256,256]{1,0:T(8,128)(2,1)S(1)}, u32[]{:S(2)}, u32[]{:S(2)}) collective-permute-start(bf16[256,256]{1,0:T(8,128)(2,1)S(1)} %pad_maximum_fusion.rest_0_), channel_id=1, source_target_pairs={{0,24},{1,25},{2,26},{3,27},{4,28},{5,29},{6,30},{7,31}} | collective-permute-start | bytes 393224 | tf_op jit(solution)/shard_map/ppermute | solution.py:98
  24.1 5.3 %collective-permute-start.3 = (bf16[256,256]{1,0:T(8,128)(2,1)S(1)}, bf16[256,256]{1,0:T(8,128)(2,1)S(1)}, u32[]{:S(2)}, u32[]{:S(2)}) collective-permute-start(bf16[256,256]{1,0:T(8,128)(2,1)S(1)} %pad_maximum_fusion.rest_0_), channel_id=1, source_target_pairs={{0,16},{8,24},{1,17},{9,25},{2,18},{10,26},{3,19},{11,27},{4,20},{... | collective-permute-start | bytes 393224 | tf_op jit(solution)/shard_map/ppermute | solution.py:98
  25.4 5.4 %collective-permute-start.2 = (bf16[256,256]{1,0:T(8,128)(2,1)S(1)}, bf16[256,256]{1,0:T(8,128)(2,1)S(1)}, u32[]{:S(2)}, u32[]{:S(2)}) collective-permute-start(bf16[256,256]{1,0:T(8,128)(2,1)S(1)} %pad_maximum_fusion.rest_0_), channel_id=1, source_target_pairs={{0,8},{8,16},{16,24},{1,9},{9,17},{17,25},{2,10},{10,18},{18,26},{... | collective-permute-start | bytes 393224 | tf_op jit(solution)/shard_map/ppermute | solution.py:98
  30.7 13.9 %all-to-all-start.1 = ((bf16[8,64,384]{2,1,0:T(8,128)(2,1)}), bf16[8,64,384]{2,1,0:T(8,128)(2,1)S(1)}, u32[]{:S(2)}, u32[]{:S(2)}) async-start(bf16[8,64,384]{2,1,0:T(8,128)(2,1)} %picked.1), calls=%async_computation.1 | async-start | bytes 786432 | tf_op jit(solution)/shard_map/all_to_all | solution.py:314
  38.3 0.8 copy-start.2
  44.6 0.7 copy-start
  45.4 15.1 %collective-permute-start.8 = (bf16[128,4096]{1,0:T(8,128)(2,1)}, bf16[128,4096]{1,0:T(8,128)(2,1)}, u32[]{:S(2)}, u32[]{:S(2)}) collective-permute-start(bf16[128,4096]{1,0:T(8,128)(2,1)} %collective-permute-done.refs_2_), channel_id=1, source_target_pairs={{0,2},{1,5},{2,0},{3,7},{4,6},{5,1},{6,4},{7,3},{8,10},{9,13},{10,... | collective-permute-start | bytes 3145736 | tf_op jit(solution)/shard_map/ppermute | solution.py:366
  45.6 20.4 %collective-permute-start.5 = (bf16[128,4096]{1,0:T(8,128)(2,1)}, bf16[128,4096]{1,0:T(8,128)(2,1)}, u32[]{:S(2)}, u32[]{:S(2)}) collective-permute-start(bf16[128,4096]{1,0:T(8,128)(2,1)} %refs_0_.1), channel_id=1, source_target_pairs={{0,1},{1,0},{2,3},{3,2},{4,5},{5,4},{6,7},{7,6},{8,9},{9,8},{10,11... | collective-permute-start | bytes 3145736 | tf_op jit(solution)/shard_map/ppermute | solution.py:366
  45.6 20.5 %collective-permute-start.6 = (bf16[128,4096]{1,0:T(8,128)(2,1)}, bf16[128,4096]{1,0:T(8,128)(2,1)}, u32[]{:S(2)}, u32[]{:S(2)}) collective-permute-start(bf16[128,4096]{1,0:T(8,128)(2,1)} %collective-permute-done.refs_2_), channel_id=1, source_target_pairs={{0,1},{1,0},{2,3},{3,2},{4,5},{5,4},{6,7},{7,6},{8,9},{9,8},{10,11... | collective-permute-start | bytes 3145736 | tf_op jit(solution)/shard_map/ppermute | solution.py:366
  46.1 19.9 %collective-permute-start.7 = (bf16[128,4096]{1,0:T(8,128)(2,1)}, bf16[128,4096]{1,0:T(8,128)(2,1)}, u32[]{:S(2)}, u32[]{:S(2)}) collective-permute-start(bf16[128,4096]{1,0:T(8,128)(2,1)} %collective-permute-done.1.refs_4_), channel_id=1, source_target_pairs={{0,1},{1,0},{2,3},{3,2},{4,5},{5,4},{6,7},{7,6},{8,9},{9,8},{10,11... | collective-permute-start | bytes 3145736 | tf_op jit(solution)/shard_map/ppermute | solution.py:366
  46.1 1.0 %copy-start.1 = (bf16[8,64,384]{2,1,0:T(8,128)(2,1)S(1)}, bf16[8,64,384]{2,1,0:T(8,128)(2,1)}, u32[]{:S(2)}) copy-start(bf16[8,64,384]{2,1,0:T(8,128)(2,1)} %copy-done) | copy-start | bytes 1179652
  60.5 5.5 %collective-permute-start.9 = (bf16[128,4096]{1,0:T(8,128)(2,1)}, bf16[128,4096]{1,0:T(8,128)(2,1)}, u32[]{:S(2)}, u32[]{:S(2)}) collective-permute-start(bf16[128,4096]{1,0:T(8,128)(2,1)} %collective-permute-done.8.refs_6_), channel_id=1, source_target_pairs={{0,1},{1,0},{2,3},{3,2},{4,5},{5,4},{6,7},{7,6},{8,9},{9,8},{10,11... | collective-permute-start | bytes 3145736 | tf_op jit(solution)/shard_map/ppermute | solution.py:366
  60.5 21.0 %all-to-all-start.2 = ((bf16[32,32,256]{2,1,0:T(8,128)(2,1)}), bf16[32,32,256]{2,1,0:T(8,128)(2,1)S(1)}, u32[]{:S(2)}, u32[]{:S(2)}) async-start(bf16[32,32,256]{2,1,0:T(8,128)(2,1)} %bitcast.10), calls=%async_computation.2 | async-start | bytes 1048576 | tf_op jit(solution)/shard_map/all_to_all | solution.py:146

commit v9 on v8

--- a/solution.py
+++ b/solution.py
@@ -403,8 +403,8 @@
     mixed, sent = source_rows(expert_ids, route_probs, shadow_list, stored_hidden_state)
     ready, mixed = lax.optimization_barrier((moe_grad, mixed))
     second = moved(ready, [held[2] for held in steps])
-    sent, arrived = lax.optimization_barrier((sent, arrived))
     shadow_rows = swapped(sent)
+    arrived, _ = lax.optimization_barrier((arrived, sent))
     query_grad, terms = attention(
         queries, arrived, attn_out, attn_out_grad, lse_excess, block_mask
     )

time: 83.3 us -> 84.7 us (1.017); the launches traced: 82.2 us -> 85.8 us
  starting transfers between devices: 27.3 us -> 29.9 us
  waiting for transfers between devices: 29.8 us -> 30.7 us
    ppermute x3, waiting for transfers between devices: 1.55 us -> 5.13 us  [key_blocks(): lax.ppermute(pair, 'ctx', [(c, c + step) for c in range(cycle - step)])]
    all_to_all x1, starting transfers between devices: 5.49 us -> 9.03 us  [summed_terms(): lax.all_to_all(terms.reshape(cycle * owners, rows // owners, columns), ('...]
    all_to_all x2, waiting for transfers between devices: 12.9 us -> 10.2 us  [swapped(): return lax.all_to_all(value, 'exp', split_axis=0, concat_axis=0, tiled=True)]
    all_to_all x2, starting transfers between devices: 9.72 us -> 8.77 us  [swapped(): return lax.all_to_all(value, 'exp', split_axis=0, concat_axis=0, tiled=True)]
  transfers between devices with their start and end apart: 13 -> 13, of which waited for: 6 -> 7; matrix products, arithmetic and copies ran while one was open for 0% -> 0% of each run, Pallas kernels for 22% -> 21%
where the time goes in v9:
time: 84.7 us; the launch traced here: 85.8 us
  waiting for transfers between devices  30.7 us (36%)
  starting transfers between devices  29.9 us (35%)
  Pallas kernels  18.7 us (22%)
  local copies, waits for them, and re-layouts  4.13 us (5%)
  other arithmetic  1.54 us (2%)
    pallas_call x1, Pallas kernels, tile_sums(): pl.pallas_call(tile_kernel, out_shape=jax.ShapeDtypeStruct((per_dev, rows...  10.7 us
    ppermute x7, waiting for transfers between devices, moved(): lax.ppermute(value, 'exp', [(e, e ^ steps[e % 2]) for e in range(owners)])  10.6 us
    all_to_all x2, waiting for transfers between devices, swapped(): return lax.all_to_all(value, 'exp', split_axis=0, concat_axis=0, tiled=True)  10.2 us
    ppermute x3, starting transfers between devices, key_blocks(): lax.ppermute(pair, 'ctx', [(c, c + step) for c in range(cycle - step)])  9.31 us
    all_to_all x1, starting transfers between devices, summed_terms(): lax.all_to_all(terms.reshape(cycle * owners, rows // owners, columns), ('...  9.03 us
    all_to_all x2, starting transfers between devices, swapped(): return lax.all_to_all(value, 'exp', split_axis=0, concat_axis=0, tiled=True)  8.77 us
    ppermute x3, waiting for transfers between devices, key_blocks(): lax.ppermute(pair, 'ctx', [(c, c + step) for c in range(cycle - step)])  5.13 us
    all_to_all x1, waiting for transfers between devices, summed_terms(): lax.all_to_all(terms.reshape(cycle * owners, rows // owners, columns), ('...  4.77 us
  transfers between devices with their start and end apart: 13, of which 7 were waited for; matrix products, arithmetic and copies ran while one was open for 0% of the time, Pallas kernels for 21%

profile of v9, /device:TPU:0, one launch (start us, length us, event | category | flops | bytes accessed | tf_op | source)
XLA Modules:
  0.0 85.8 jit_solution(3251579117171467186)
XLA Ops:
  0.6 0.7 convert_element_type.13
  1.3 1.5 %copy.20.hidden_ref = bf16[1,3,8,65,384]{4,3,2,1,0:T(8,128)(2,1)S(1)} copy(bf16[1,3,8,65,384]{4,2,3,1,0:T(8,128)(2,1)} %param.23) | data formatting | bytes 2396160 | tf_op args[11]
  2.8 0.0 copy-start.8
  2.8 0.0 copy-done.11
  2.9 0.8 fusion.1
  3.7 0.0 copy-start.5
  3.7 0.0 copy-start.6
  3.7 0.0 copy-start.7
  3.7 5.3 %all-to-all-start = ((bf16[8,66,384]{2,1,0:T(8,128)(2,1)}), bf16[8,66,384]{2,1,0:T(8,128)(2,1)S(1)}, u32[]{:S(2)}, u32[]{:S(2)}) async-start(bf16[8,66,384]{2,1,0:T(8,128)(2,1)} %fusion.1), calls=%async_computation | async-start | bytes 884736 | tf_op jit(solution)/shard_map/all_to_all | solution.py:314
  9.1 2.0 %collective-permute-start = (bf16[128,4096]{1,0:T(8,128)(2,1)}, bf16[128,4096]{1,0:T(8,128)(2,1)}, u32[]{:S(2)}, u32[]{:S(2)}) collective-permute-start(bf16[128,4096]{1,0:T(8,128)(2,1)} %refs_0_.1), channel_id=1, source_target_pairs={{0,4},{1,3},{2,6},{3,1},{4,0},{5,7},{6,2},{7,5},{8,12},{9,11},{10,... | collective-permute-start | bytes 3145736 | tf_op jit(solution)/shard_map/ppermute | solution.py:366
  11.1 7.3 %all-to-all-done.mixed_ref = bf16[8,66,384]{2,1,0:T(8,128)(2,1)S(1)} async-done(((bf16[8,66,384]{2,1,0:T(8,128)(2,1)}), bf16[8,66,384]{2,1,0:T(8,128)(2,1)S(1)}, u32[]{:S(2)}, u32[]{:S(2)}) %all-to-all-start) | async-done | bytes 405536 | tf_op jit(solution)/shard_map/all_to_all | solution.py:314
  18.4 0.1 collective-permute-start.1
  18.5 0.0 copy-done.8
  18.5 1.3 %picked.1 = bf16[8,64,384]{2,1,0:T(8,128)(2,1)} custom-call(s32[16]{0:T(128)S(1)} %copy-done.8, bf16[8,66,384]{2,1,0:T(8,128)(2,1)S(1)} %all-to-all-done.mixed_ref), custom_call_target="tpu_custom_call" | custom-call | tf_op jit(solution)/shard_map/picked/pallas_call | solution.py:179
  19.8 3.5 %all-to-all-start.1 = ((bf16[8,64,384]{2,1,0:T(8,128)(2,1)}), bf16[8,64,384]{2,1,0:T(8,128)(2,1)S(1)}, u32[]{:S(2)}, u32[]{:S(2)}) async-start(bf16[8,64,384]{2,1,0:T(8,128)(2,1)} %picked.1), calls=%async_computation.1 | async-start | bytes 786432 | tf_op jit(solution)/shard_map/all_to_all | solution.py:314
  23.3 0.0 copy-done.9
  23.3 0.0 copy-done.10
  23.4 5.5 %collective-permute-start.4 = (bf16[256,256]{1,0:T(8,128)(2,1)S(1)}, bf16[256,256]{1,0:T(8,128)(2,1)S(1)}, u32[]{:S(2)}, u32[]{:S(2)}) collective-permute-start(bf16[256,256]{1,0:T(8,128)(2,1)S(1)} %pad_maximum_fusion.rest_0_), channel_id=1, source_target_pairs={{0,24},{1,25},{2,26},{3,27},{4,28},{5,29},{6,30},{7,31}} | collective-permute-start | bytes 393224 | tf_op jit(solution)/shard_map/ppermute | solution.py:98
  28.9 1.3 %collective-permute-start.3 = (bf16[256,256]{1,0:T(8,128)(2,1)S(1)}, bf16[256,256]{1,0:T(8,128)(2,1)S(1)}, u32[]{:S(2)}, u32[]{:S(2)}) collective-permute-start(bf16[256,256]{1,0:T(8,128)(2,1)S(1)} %pad_maximum_fusion.rest_0_), channel_id=1, source_target_pairs={{0,16},{8,24},{1,17},{9,25},{2,18},{10,26},{3,19},{11,27},{4,20},{... | collective-permute-start | bytes 393224 | tf_op jit(solution)/shard_map/ppermute | solution.py:98
  30.2 2.5 %collective-permute-start.2 = (bf16[256,256]{1,0:T(8,128)(2,1)S(1)}, bf16[256,256]{1,0:T(8,128)(2,1)S(1)}, u32[]{:S(2)}, u32[]{:S(2)}) collective-permute-start(bf16[256,256]{1,0:T(8,128)(2,1)S(1)} %pad_maximum_fusion.rest_0_), channel_id=1, source_target_pairs={{0,8},{8,16},{16,24},{1,9},{9,17},{17,25},{2,10},{10,18},{18,26},{... | collective-permute-start | bytes 393224 | tf_op jit(solution)/shard_map/ppermute | solution.py:98
  32.7 0.1 collective-permute-done.4.rest_3_
  32.8 2.8 %collective-permute-done.3.rest_2_ = bf16[256,256]{1,0:T(8,128)(2,1)S(1)} collective-permute-done((bf16[256,256]{1,0:T(8,128)(2,1)S(1)}, bf16[256,256]{1,0:T(8,128)(2,1)S(1)}, u32[]{:S(2)}, u32[]{:S(2)}) %collective-permute-start.3) | collective-permute-done | bytes 131104 | tf_op jit(solution)/shard_map/ppermute | solution.py:98
  35.6 2.3 %collective-permute-done.2.rest_1_ = bf16[256,256]{1,0:T(8,128)(2,1)S(1)} collective-permute-done((bf16[256,256]{1,0:T(8,128)(2,1)S(1)}, bf16[256,256]{1,0:T(8,128)(2,1)S(1)}, u32[]{:S(2)}, u32[]{:S(2)}) %collective-permute-start.2) | collective-permute-done | bytes 131104 | tf_op jit(solution)/shard_map/ppermute | solution.py:98
  37.8 0.0 copy-done.3
  37.8 0.0 copy-done.4
  37.8 0.0 copy-done.5
  37.9 3.1 %attention.1 = (bf16[256,512]{1,0:T(8,128)(2,1)}, bf16[4,256,256]{2,1,0:T(8,128)(2,1)S(1)}) custom-call(s32[1]{0:T(128)} %bitcast.3.place_ref, s32[4,4]{1,0:T(4,128)S(1)} %copy-done.7, bf16[256,512]{1,0:T(8,128)(2,1)S(1)} %copy-done.3, bf16[256,512]{1,0:T(8,128)(2,1)S(1)} %copy-done.4, bf16[256,512]{1,0:T(8,128)(2,1)S(1)} %copy-done.5, ...), custom_call_target="tpu_custom_call" | custom-call | tf_op jit(solution)/shard_map/attention/pallas_call | solution.py:108
  40.9 0.8 copy-done.2
  41.7 2.9 %all-to-all-done.1.side_ref = bf16[8,64,384]{2,1,0:T(8,128)(2,1)S(1)} async-done(((bf16[8,64,384]{2,1,0:T(8,128)(2,1)}), bf16[8,64,384]{2,1,0:T(8,128)(2,1)S(1)}, u32[]{:S(2)}, u32[]{:S(2)}) %all-to-all-start.1) | async-done | bytes 393248 | tf_op jit(solution)/shard_map/all_to_all | solution.py:314
  44.6 0.7 copy-done
  45.4 0.0 collective-permute-done.refs_2_
  45.4 0.0 collective-permute-done.1.refs_4_
  45.4 0.1 collective-permute-start.8
  45.5 0.0 collective-permute-start.5
  45.5 0.5 collective-permute-start.6
  46.0 0.1 collective-permute-start.7
  46.0 1.0 %copy-done.1 = bf16[8,64,384]{2,1,0:T(8,128)(2,1)S(1)} copy-done((bf16[8,64,384]{2,1,0:T(8,128)(2,1)S(1)}, bf16[8,64,384]{2,1,0:T(8,128)(2,1)}, u32[]{:S(2)}) %copy-start.1) | copy-done | bytes 393240
  47.0 2.9 %weighted.1.weight_ref = bf16[768,1024]{1,0:T(8,128)(2,1)S(1)} custom-call(s32[1]{0:T(128)} %bitcast.6.own_ref, s32[16]{0:T(128)S(1)} %copy-done.8, bf16[8,66,384]{2,1,0:T(8,128)(2,1)S(1)} %all-to-all-done.mixed_ref, bf16[1,3,8,65,384]{4,3,2,1,0:T(8,128)(2,1)S(1)} %copy.20.hidden_ref, bf16[8,64,384]{2,1,0:T(8,128)(2,1)S(1)} %copy-done.1), custom_call_target="tpu_custom_call" | custom-call | tf_op jit(solution)/shard_map/weighted/pallas_call | solution.py:231
  49.9 10.6 %collective-permute-done.8.refs_6_ = bf16[128,4096]{1,0:T(8,128)(2,1)} collective-permute-done((bf16[128,4096]{1,0:T(8,128)(2,1)}, bf16[128,4096]{1,0:T(8,128)(2,1)}, u32[]{:S(2)}, u32[]{:S(2)}) %collective-permute-start.8) | collective-permute-done | bytes 1048608 | tf_op jit(solution)/shard_map/ppermute | solution.py:366
  60.5 0.0 collective-permute-start.9
  60.5 9.0 %all-to-all-start.2 = ((bf16[32,32,256]{2,1,0:T(8,128)(2,1)}), bf16[32,32,256]{2,1,0:T(8,128)(2,1)S(1)}, u32[]{:S(2)}, u32[]{:S(2)}) async-start(bf16[32,32,256]{2,1,0:T(8,128)(2,1)} %bitcast.10), calls=%async_computation.2 | async-start | bytes 1048576 | tf_op jit(solution)/shard_map/all_to_all | solution.py:146
  69.5 0.0 collective-permute-done.5.refs_1_
  69.5 0.0 collective-permute-done.7.refs_5_
  69.5 0.0 collective-permute-done.6.refs_3_
  69.5 0.0 collective-permute-done.9.refs_7_
  69.6 10.7 %tiles.1 = f32[2,384,4096]{2,1,0:T(8,128)} custom-call(bf16[768,1024]{1,0:T(8,128)(2,1)S(1)} %weighted.1.weight_ref, bf16[128,4096]{1,0:T(8,128)(2,1)} %refs_0_.1, bf16[128,4096]{1,0:T(8,128)(2,1)} %collective-permute-done.5.refs_1_, bf16[128,4096]{1,0:T(8,128)(2,1)} %collective-permute-done.refs_2_, bf16[128,4096]{1,0:T(8,128)(2,1)} %collective-permute-done.6.refs_3_, ...), custom_call_target="tpu_custom_call" | custom-call | tf_op jit(solution)/shard_map/tiles/pallas_call | solution.py:297
  80.3 4.8 %all-to-all-done.2 = bf16[32,32,256]{2,1,0:T(8,128)(2,1)S(1)} async-done(((bf16[32,32,256]{2,1,0:T(8,128)(2,1)}), bf16[32,32,256]{2,1,0:T(8,128)(2,1)S(1)}, u32[]{:S(2)}, u32[]{:S(2)}) %all-to-all-start.2) | async-done | bytes 524320 | tf_op jit(solution)/shard_map/all_to_all | solution.py:146
  85.1 0.7 sums.1
  (14 shorter events, 0.1 us)
Async XLA Ops:
  1.3 1.5 %copy-start.11 = (s32[128,8]{0,1:T(8,128)S(1)}, s32[128,8]{0,1:T(8,128)}, u32[]{:S(2)}) copy-start(s32[128,8]{0,1:T(8,128)} %param.19) | copy-start | bytes 12292
  2.8 15.7 %copy-start.8 = (s32[16]{0:T(128)S(1)}, s32[16]{0:T(128)}, u32[]{:S(2)}) copy-start(s32[16]{0:T(128)} %shadow_ref.3) | copy-start | bytes 196
  3.7 19.6 %copy-start.9 = (bf16[256,256]{1,0:T(8,128)(2,1)S(1)}, bf16[256,256]{1,0:T(8,128)(2,1)}, u32[]{:S(2)}) copy-start(bf16[256,256]{1,0:T(8,128)(2,1)} %param.14) | copy-start | bytes 393220
  3.7 19.6 %copy-start.10 = (bf16[256,256]{1,0:T(8,128)(2,1)S(1)}, bf16[256,256]{1,0:T(8,128)(2,1)}, u32[]{:S(2)}) copy-start(bf16[256,256]{1,0:T(8,128)(2,1)} %param.13) | copy-start | bytes 393220
  3.7 34.1 %copy-start.3 = (bf16[256,512]{1,0:T(8,128)(2,1)S(1)}, bf16[256,512]{1,0:T(8,128)(2,1)}, u32[]{:S(2)}) copy-start(bf16[256,512]{1,0:T(8,128)(2,1)} %query_ref.1) | copy-start | bytes 786436
  3.7 34.1 %copy-start.4 = (bf16[256,512]{1,0:T(8,128)(2,1)S(1)}, bf16[256,512]{1,0:T(8,128)(2,1)}, u32[]{:S(2)}) copy-start(bf16[256,512]{1,0:T(8,128)(2,1)} %grad_ref.1) | copy-start | bytes 786436
  3.7 34.1 %copy-start.5 = (bf16[256,512]{1,0:T(8,128)(2,1)S(1)}, bf16[256,512]{1,0:T(8,128)(2,1)}, u32[]{:S(2)}) copy-start(bf16[256,512]{1,0:T(8,128)(2,1)} %out_ref.1) | copy-start | bytes 786436
  3.7 34.1 %copy-start.6 = (f32[4,256]{1,0:T(4,128)S(1)}, f32[4,256]{1,0:T(4,128)}, u32[]{:S(2)}) copy-start(f32[4,256]{1,0:T(4,128)} %lse_ref.1) | copy-start | bytes 12292
  3.7 34.1 %copy-start.7 = (s32[4,4]{1,0:T(4,128)S(1)}, s32[4,4]{1,0:T(4,128)}, u32[]{:S(2)}) copy-start(s32[4,4]{1,0:T(4,128)} %mask_ref.1) | copy-start | bytes 196
  3.7 14.7 %all-to-all-start = ((bf16[8,66,384]{2,1,0:T(8,128)(2,1)}), bf16[8,66,384]{2,1,0:T(8,128)(2,1)S(1)}, u32[]{:S(2)}, u32[]{:S(2)}) async-start(bf16[8,66,384]{2,1,0:T(8,128)(2,1)} %fusion.1), calls=%async_computation | async-start | bytes 884736 | tf_op jit(solution)/shard_map/all_to_all | solution.py:314
  9.1 36.3 %collective-permute-start = (bf16[128,4096]{1,0:T(8,128)(2,1)}, bf16[128,4096]{1,0:T(8,128)(2,1)}, u32[]{:S(2)}, u32[]{:S(2)}) collective-permute-start(bf16[128,4096]{1,0:T(8,128)(2,1)} %refs_0_.1), channel_id=1, source_target_pairs={{0,4},{1,3},{2,6},{3,1},{4,0},{5,7},{6,2},{7,5},{8,12},{9,11},{10,... | collective-permute-start | bytes 3145736 | tf_op jit(solution)/shard_map/ppermute | solution.py:366
  18.4 27.0 %collective-permute-start.1 = (bf16[128,4096]{1,0:T(8,128)(2,1)}, bf16[128,4096]{1,0:T(8,128)(2,1)}, u32[]{:S(2)}, u32[]{:S(2)}) collective-permute-start(bf16[128,4096]{1,0:T(8,128)(2,1)} %refs_0_.1), channel_id=1, source_target_pairs={{0,2},{1,5},{2,0},{3,7},{4,6},{5,1},{6,4},{7,3},{8,10},{9,13},{10,... | collective-permute-start | bytes 3145736 | tf_op jit(solution)/shard_map/ppermute | solution.py:366
  19.8 24.8 %all-to-all-start.1 = ((bf16[8,64,384]{2,1,0:T(8,128)(2,1)}), bf16[8,64,384]{2,1,0:T(8,128)(2,1)S(1)}, u32[]{:S(2)}, u32[]{:S(2)}) async-start(bf16[8,64,384]{2,1,0:T(8,128)(2,1)} %picked.1), calls=%async_computation.1 | async-start | bytes 786432 | tf_op jit(solution)/shard_map/all_to_all | solution.py:314
  23.4 9.4 %collective-permute-start.4 = (bf16[256,256]{1,0:T(8,128)(2,1)S(1)}, bf16[256,256]{1,0:T(8,128)(2,1)S(1)}, u32[]{:S(2)}, u32[]{:S(2)}) collective-permute-start(bf16[256,256]{1,0:T(8,128)(2,1)S(1)} %pad_maximum_fusion.rest_0_), channel_id=1, source_target_pairs={{0,24},{1,25},{2,26},{3,27},{4,28},{5,29},{6,30},{7,31}} | collective-permute-start | bytes 393224 | tf_op jit(solution)/shard_map/ppermute | solution.py:98
  28.9 6.7 %collective-permute-start.3 = (bf16[256,256]{1,0:T(8,128)(2,1)S(1)}, bf16[256,256]{1,0:T(8,128)(2,1)S(1)}, u32[]{:S(2)}, u32[]{:S(2)}) collective-permute-start(bf16[256,256]{1,0:T(8,128)(2,1)S(1)} %pad_maximum_fusion.rest_0_), channel_id=1, source_target_pairs={{0,16},{8,24},{1,17},{9,25},{2,18},{10,26},{3,19},{11,27},{4,20},{... | collective-permute-start | bytes 393224 | tf_op jit(solution)/shard_map/ppermute | solution.py:98
  30.2 7.6 %collective-permute-start.2 = (bf16[256,256]{1,0:T(8,128)(2,1)S(1)}, bf16[256,256]{1,0:T(8,128)(2,1)S(1)}, u32[]{:S(2)}, u32[]{:S(2)}) collective-permute-start(bf16[256,256]{1,0:T(8,128)(2,1)S(1)} %pad_maximum_fusion.rest_0_), channel_id=1, source_target_pairs={{0,8},{8,16},{16,24},{1,9},{9,17},{17,25},{2,10},{10,18},{18,26},{... | collective-permute-start | bytes 393224 | tf_op jit(solution)/shard_map/ppermute | solution.py:98
  40.9 0.8 copy-start.2
  44.6 0.7 copy-start
  45.4 15.1 %collective-permute-start.8 = (bf16[128,4096]{1,0:T(8,128)(2,1)}, bf16[128,4096]{1,0:T(8,128)(2,1)}, u32[]{:S(2)}, u32[]{:S(2)}) collective-permute-start(bf16[128,4096]{1,0:T(8,128)(2,1)} %collective-permute-done.refs_2_), channel_id=1, source_target_pairs={{0,2},{1,5},{2,0},{3,7},{4,6},{5,1},{6,4},{7,3},{8,10},{9,13},{10,... | collective-permute-start | bytes 3145736 | tf_op jit(solution)/shard_map/ppermute | solution.py:366
  45.5 24.1 %collective-permute-start.5 = (bf16[128,4096]{1,0:T(8,128)(2,1)}, bf16[128,4096]{1,0:T(8,128)(2,1)}, u32[]{:S(2)}, u32[]{:S(2)}) collective-permute-start(bf16[128,4096]{1,0:T(8,128)(2,1)} %refs_0_.1), channel_id=1, source_target_pairs={{0,1},{1,0},{2,3},{3,2},{4,5},{5,4},{6,7},{7,6},{8,9},{9,8},{10,11... | collective-permute-start | bytes 3145736 | tf_op jit(solution)/shard_map/ppermute | solution.py:366
  45.5 24.1 %collective-permute-start.6 = (bf16[128,4096]{1,0:T(8,128)(2,1)}, bf16[128,4096]{1,0:T(8,128)(2,1)}, u32[]{:S(2)}, u32[]{:S(2)}) collective-permute-start(bf16[128,4096]{1,0:T(8,128)(2,1)} %collective-permute-done.refs_2_), channel_id=1, source_target_pairs={{0,1},{1,0},{2,3},{3,2},{4,5},{5,4},{6,7},{7,6},{8,9},{9,8},{10,11... | collective-permute-start | bytes 3145736 | tf_op jit(solution)/shard_map/ppermute | solution.py:366
  46.0 23.6 %collective-permute-start.7 = (bf16[128,4096]{1,0:T(8,128)(2,1)}, bf16[128,4096]{1,0:T(8,128)(2,1)}, u32[]{:S(2)}, u32[]{:S(2)}) collective-permute-start(bf16[128,4096]{1,0:T(8,128)(2,1)} %collective-permute-done.1.refs_4_), channel_id=1, source_target_pairs={{0,1},{1,0},{2,3},{3,2},{4,5},{5,4},{6,7},{7,6},{8,9},{9,8},{10,11... | collective-permute-start | bytes 3145736 | tf_op jit(solution)/shard_map/ppermute | solution.py:366
  46.0 1.0 %copy-start.1 = (bf16[8,64,384]{2,1,0:T(8,128)(2,1)S(1)}, bf16[8,64,384]{2,1,0:T(8,128)(2,1)}, u32[]{:S(2)}) copy-start(bf16[8,64,384]{2,1,0:T(8,128)(2,1)} %copy-done) | copy-start | bytes 1179652
  60.5 9.1 %collective-permute-start.9 = (bf16[128,4096]{1,0:T(8,128)(2,1)}, bf16[128,4096]{1,0:T(8,128)(2,1)}, u32[]{:S(2)}, u32[]{:S(2)}) collective-permute-start(bf16[128,4096]{1,0:T(8,128)(2,1)} %collective-permute-done.8.refs_6_), channel_id=1, source_target_pairs={{0,1},{1,0},{2,3},{3,2},{4,5},{5,4},{6,7},{7,6},{8,9},{9,8},{10,11... | collective-permute-start | bytes 3145736 | tf_op jit(solution)/shard_map/ppermute | solution.py:366
  60.5 24.6 %all-to-all-start.2 = ((bf16[32,32,256]{2,1,0:T(8,128)(2,1)}), bf16[32,32,256]{2,1,0:T(8,128)(2,1)S(1)}, u32[]{:S(2)}, u32[]{:S(2)}) async-start(bf16[32,32,256]{2,1,0:T(8,128)(2,1)} %bitcast.10), calls=%async_computation.2 | async-start | bytes 1048576 | tf_op jit(solution)/shard_map/all_to_all | solution.py:146

commit v10 on v9

--- a/solution.py
+++ b/solution.py
@@ -366,13 +366,13 @@
     return lax.ppermute(value, "exp", [(e, e ^ steps[e % 2]) for e in range(owners)])
 
 
-def expert_tiles(weighted, near, per_dev):
+def expert_tiles(weighted, near, anchor, per_dev):
     owners = lax.axis_size("exp")
     steps = block_steps(owners)
     far = moved(near[1], [held[2] for held in steps])
     held = list(near)
     blocks = [block for part in held for block in (part, moved(part, (1, 1)))]
-    far, _ = lax.optimization_barrier((far, weighted))
+    far, _ = lax.optimization_barrier((far, (weighted, anchor)))
     held = held + [far]
     rest = [far]
     for turn in range(len(steps[0]).bit_length() - 3):
@@ -404,18 +404,16 @@
     ready, mixed = lax.optimization_barrier((moe_grad, mixed))
     second = moved(ready, [held[2] for held in steps])
     shadow_rows = swapped(sent)
-    arrived, _ = lax.optimization_barrier((arrived, sent))
+    first, second, shadow_rows = lax.optimization_barrier((first, second, shadow_rows))
+    arrived, _ = lax.optimization_barrier((arrived, shadow_rows))
     query_grad, terms = attention(
         queries, arrived, attn_out, attn_out_grad, lse_excess, block_mask
     )
-    first, second, shadow_rows, query_grad = lax.optimization_barrier(
-        (first, second, shadow_rows, query_grad)
-    )
     weighted = expert_rows(
         mixed, shadow_rows, shadow_list, stored_hidden_state, expert_ids.shape[0]
     )
     per_dev = shadow_list.shape[0] // lax.axis_size("exp")
-    tiles = expert_tiles(weighted, (moe_grad, first, second), per_dev)
+    tiles = expert_tiles(weighted, (moe_grad, first, second), query_grad, per_dev)
     key_grad, value_grad, expert_grad = summed_terms(terms, keys.shape[1], tiles)
     return (query_grad, key_grad, value_grad, expert_grad)
 

time: 84.7 us -> 93.4 us (1.10); the launches traced: 85.8 us -> 91.6 us
  blocking collectives: 0 us -> 25.6 us
  waiting for transfers between devices: 30.7 us -> 14.4 us
  starting transfers between devices: 29.9 us -> 26.4 us
    all_to_all x0 -> x1, blocking collectives: none -> 25.6 us  [swapped(): return lax.all_to_all(value, 'exp', split_axis=0, concat_axis=0, tiled=True)]
    ppermute x7, waiting for transfers between devices: 10.6 us -> 0.02 us  [moved(): lax.ppermute(value, 'exp', [(e, e ^ steps[e % 2]) for e in range(owners)])]
    all_to_all x2 -> x1, starting transfers between devices: 8.77 us -> 5.3 us  [swapped(): return lax.all_to_all(value, 'exp', split_axis=0, concat_axis=0, tiled=True)]
    all_to_all x2 -> x1, waiting for transfers between devices: 10.2 us -> 7.32 us  [swapped(): return lax.all_to_all(value, 'exp', split_axis=0, concat_axis=0, tiled=True)]
    ppermute x3, waiting for transfers between devices: 5.13 us -> 2.31 us  [key_blocks(): lax.ppermute(pair, 'ctx', [(c, c + step) for c in range(cycle - step)])]
    unnamed x25 -> x33, local copies, waits for them, and re-layouts: 4.07 us -> 4.49 us
  transfers between devices with their start and end apart: 13 -> 12, of which waited for: 7 -> 5; matrix products, arithmetic and copies ran while one was open for 0% -> 0% of each run, Pallas kernels for 21% -> 19%
where the time goes in v10:
time: 93.4 us; the launch traced here: 91.6 us
  starting transfers between devices  26.4 us (28%)
  blocking collectives  25.6 us (27%)
  Pallas kernels  18.1 us (19%)
  waiting for transfers between devices  14.4 us (15%)
  local copies, waits for them, and re-layouts  4.54 us (5%)
  other arithmetic  1.54 us (2%)
    all_to_all x1, blocking collectives, swapped(): return lax.all_to_all(value, 'exp', split_axis=0, concat_axis=0, tiled=True)  25.6 us
    pallas_call x1, Pallas kernels, tile_sums(): pl.pallas_call(tile_kernel, out_shape=jax.ShapeDtypeStruct((per_dev, rows...  10.7 us
    ppermute x3, starting transfers between devices, key_blocks(): lax.ppermute(pair, 'ctx', [(c, c + step) for c in range(cycle - step)])  9.28 us
    all_to_all x1, starting transfers between devices, summed_terms(): lax.all_to_all(terms.reshape(cycle * owners, rows // owners, columns), ('...  8.38 us
    all_to_all x1, waiting for transfers between devices, swapped(): return lax.all_to_all(value, 'exp', split_axis=0, concat_axis=0, tiled=True)  7.32 us
    all_to_all x1, starting transfers between devices, swapped(): return lax.all_to_all(value, 'exp', split_axis=0, concat_axis=0, tiled=True)  5.3 us
    all_to_all x1, waiting for transfers between devices, summed_terms(): lax.all_to_all(terms.reshape(cycle * owners, rows // owners, columns), ('...  4.78 us
    unnamed x33, local copies, waits for them, and re-layouts  4.49 us
  transfers between devices with their start and end apart: 12, of which 5 were waited for; matrix products, arithmetic and copies ran while one was open for 0% of the time, Pallas kernels for 19%

profile of v10, /device:TPU:0, one launch (start us, length us, event | category | flops | bytes accessed | tf_op | source)
XLA Modules:
  0.0 91.6 jit_solution(954492888177759028)
XLA Ops:
  0.6 0.7 convert_element_type.13
  1.3 1.5 %copy.20.hidden_ref = bf16[1,3,8,65,384]{4,3,2,1,0:T(8,128)(2,1)S(1)} copy(bf16[1,3,8,65,384]{4,2,3,1,0:T(8,128)(2,1)} %param.23) | data formatting | bytes 2396160 | tf_op args[11]
  2.8 0.0 copy-start.12
  2.8 0.0 copy-done.15
  2.9 0.8 fusion.1
  3.7 5.3 %all-to-all-start = ((bf16[8,66,384]{2,1,0:T(8,128)(2,1)}), bf16[8,66,384]{2,1,0:T(8,128)(2,1)S(1)}, u32[]{:S(2)}, u32[]{:S(2)}) async-start(bf16[8,66,384]{2,1,0:T(8,128)(2,1)} %fusion.1), calls=%async_computation | async-start | bytes 884736 | tf_op jit(solution)/shard_map/all_to_all | solution.py:314
  9.0 2.0 %collective-permute-start.3 = (bf16[128,4096]{1,0:T(8,128)(2,1)}, bf16[128,4096]{1,0:T(8,128)(2,1)}, u32[]{:S(2)}, u32[]{:S(2)}) collective-permute-start(bf16[128,4096]{1,0:T(8,128)(2,1)} %refs_0_.1), channel_id=1, source_target_pairs={{0,4},{1,3},{2,6},{3,1},{4,0},{5,7},{6,2},{7,5},{8,12},{9,11},{10,... | collective-permute-start | bytes 3145736 | tf_op jit(solution)/shard_map/ppermute | solution.py:366
  11.0 7.3 %all-to-all-done.mixed_ref = bf16[8,66,384]{2,1,0:T(8,128)(2,1)S(1)} async-done(((bf16[8,66,384]{2,1,0:T(8,128)(2,1)}), bf16[8,66,384]{2,1,0:T(8,128)(2,1)S(1)}, u32[]{:S(2)}, u32[]{:S(2)}) %all-to-all-start) | async-done | bytes 405536 | tf_op jit(solution)/shard_map/all_to_all | solution.py:314
  18.4 0.1 collective-permute-start.4
  18.4 0.0 copy-done.12
  18.4 0.6 picked.1
  19.0 25.6 %all_to_all.15.side_ref = bf16[8,64,384]{2,1,0:T(8,128)(2,1)} all-to-all(bf16[8,64,384]{2,1,0:T(8,128)(2,1)S(1)} %picked.1), channel_id=1, replica_groups=mesh['ctx'=4,'exp'=8] {'exp'}, dimensions={0} | all-to-all | bytes 786432 | tf_op jit(solution)/shard_map/all_to_all | solution.py:314
  44.7 0.0 collective-permute-done.3.refs_2_
  44.7 0.0 collective-permute-done.4.refs_4_
  44.7 0.4 collective-permute-start.8
  45.1 0.0 copy-done.13
  45.1 0.0 copy-done.14
  45.1 5.5 %collective-permute-start.2 = (bf16[256,256]{1,0:T(8,128)(2,1)S(1)}, bf16[256,256]{1,0:T(8,128)(2,1)S(1)}, u32[]{:S(2)}, u32[]{:S(2)}) collective-permute-start(bf16[256,256]{1,0:T(8,128)(2,1)S(1)} %pad_maximum_fusion.rest_0_), channel_id=1, source_target_pairs={{0,24},{1,25},{2,26},{3,27},{4,28},{5,29},{6,30},{7,31}} | collective-permute-start | bytes 393224 | tf_op jit(solution)/shard_map/ppermute | solution.py:98
  50.6 1.3 %collective-permute-start.1 = (bf16[256,256]{1,0:T(8,128)(2,1)S(1)}, bf16[256,256]{1,0:T(8,128)(2,1)S(1)}, u32[]{:S(2)}, u32[]{:S(2)}) collective-permute-start(bf16[256,256]{1,0:T(8,128)(2,1)S(1)} %pad_maximum_fusion.rest_0_), channel_id=1, source_target_pairs={{0,16},{8,24},{1,17},{9,25},{2,18},{10,26},{3,19},{11,27},{4,20},{... | collective-permute-start | bytes 393224 | tf_op jit(solution)/shard_map/ppermute | solution.py:98
  51.9 2.5 %collective-permute-start = (bf16[256,256]{1,0:T(8,128)(2,1)S(1)}, bf16[256,256]{1,0:T(8,128)(2,1)S(1)}, u32[]{:S(2)}, u32[]{:S(2)}) collective-permute-start(bf16[256,256]{1,0:T(8,128)(2,1)S(1)} %pad_maximum_fusion.rest_0_), channel_id=1, source_target_pairs={{0,8},{8,16},{16,24},{1,9},{9,17},{17,25},{2,10},{10,18},{18,26},{... | collective-permute-start | bytes 393224 | tf_op jit(solution)/shard_map/ppermute | solution.py:98
  54.4 0.1 collective-permute-start.5
  54.5 0.1 collective-permute-done.2.rest_3_
  54.6 0.7 copy-done.4
  55.3 0.4 collective-permute-start.6
  55.7 1.5 %collective-permute-done.1.rest_2_ = bf16[256,256]{1,0:T(8,128)(2,1)S(1)} collective-permute-done((bf16[256,256]{1,0:T(8,128)(2,1)S(1)}, bf16[256,256]{1,0:T(8,128)(2,1)S(1)}, u32[]{:S(2)}, u32[]{:S(2)}) %collective-permute-start.1) | collective-permute-done | bytes 131104 | tf_op jit(solution)/shard_map/ppermute | solution.py:98
  57.1 0.7 copy-done.6
  57.8 0.7 collective-permute-done.rest_1_
  58.5 0.7 copy-done.8
  59.2 0.0 collective-permute-start.7
  59.2 1.0 %copy-done = bf16[8,64,384]{2,1,0:T(8,128)(2,1)S(1)} copy-done((bf16[8,64,384]{2,1,0:T(8,128)(2,1)S(1)}, bf16[8,64,384]{2,1,0:T(8,128)(2,1)}, u32[]{:S(2)}) %copy-start) | copy-done | bytes 393240
  60.2 0.0 copy-start.7
  60.2 0.0 copy-start.9
  60.2 0.0 copy-start.10
  60.2 0.0 copy-start.11
  60.3 2.9 %weighted.1.weight_ref = bf16[768,1024]{1,0:T(8,128)(2,1)S(1)} custom-call(s32[1]{0:T(128)} %bitcast.6.own_ref, s32[16]{0:T(128)S(1)} %copy-done.12, bf16[8,66,384]{2,1,0:T(8,128)(2,1)S(1)} %all-to-all-done.mixed_ref, bf16[1,3,8,65,384]{4,3,2,1,0:T(8,128)(2,1)S(1)} %copy.20.hidden_ref, bf16[8,64,384]{2,1,0:T(8,128)(2,1)S(1)} %copy-done), custom_call_target="tpu_custom_call" | custom-call | tf_op jit(solution)/shard_map/weighted/pallas_call | solution.py:231
  63.1 0.0 copy-done.1
  63.2 0.0 copy-done.2
  63.2 3.2 %attention.1 = (bf16[256,512]{1,0:T(8,128)(2,1)}, bf16[4,256,256]{2,1,0:T(8,128)(2,1)}) custom-call(s32[1]{0:T(128)} %bitcast.place_ref, s32[4,4]{1,0:T(4,128)S(1)} %copy-done.11, bf16[256,512]{1,0:T(8,128)(2,1)S(1)} %copy-done.1, bf16[256,512]{1,0:T(8,128)(2,1)S(1)} %copy-done.2, bf16[256,512]{1,0:T(8,128)(2,1)S(1)} %copy-done.3, f32[4,256]{1,0:T(4,128)S(1)} %copy-done.10, ...), custom_call_target="tpu_custom_call" | custom-call | tf_op jit(solution)/shard_map/attention/pallas_call | solution.py:108
  66.5 0.0 collective-permute-done.8.refs_6_
  66.5 0.5 collective-permute-start.9
  67.0 8.4 %all-to-all-start.2 = ((bf16[32,32,256]{2,1,0:T(8,128)(2,1)}), bf16[32,32,256]{2,1,0:T(8,128)(2,1)S(1)}, u32[]{:S(2)}, u32[]{:S(2)}) async-start(bf16[32,32,256]{2,1,0:T(8,128)(2,1)} %bitcast.4), calls=%async_computation.2 | async-start | bytes 1048576 | tf_op jit(solution)/shard_map/all_to_all | solution.py:146
  75.4 0.0 collective-permute-done.5.refs_1_
  75.4 0.0 collective-permute-done.7.refs_5_
  75.4 0.0 collective-permute-done.6.refs_3_
  75.4 0.0 collective-permute-done.9.refs_7_
  75.4 10.7 %tiles.1 = f32[2,384,4096]{2,1,0:T(8,128)} custom-call(bf16[768,1024]{1,0:T(8,128)(2,1)S(1)} %weighted.1.weight_ref, bf16[128,4096]{1,0:T(8,128)(2,1)} %refs_0_.1, bf16[128,4096]{1,0:T(8,128)(2,1)} %collective-permute-done.5.refs_1_, bf16[128,4096]{1,0:T(8,128)(2,1)} %collective-permute-done.3.refs_2_, bf16[128,4096]{1,0:T(8,128)(2,1)} %collective-permute-done.6.refs_3_, ...), custom_call_target="tpu_custom_call" | custom-call | tf_op jit(solution)/shard_map/tiles/pallas_call | solution.py:297
  86.1 4.8 %all-to-all-done.2 = bf16[32,32,256]{2,1,0:T(8,128)(2,1)S(1)} async-done(((bf16[32,32,256]{2,1,0:T(8,128)(2,1)}), bf16[32,32,256]{2,1,0:T(8,128)(2,1)S(1)}, u32[]{:S(2)}, u32[]{:S(2)}) %all-to-all-start.2) | async-done | bytes 524320 | tf_op jit(solution)/shard_map/all_to_all | solution.py:146
  90.9 0.7 sums.1
  (21 shorter events, 0.1 us)
Async XLA Ops:
  1.3 1.5 %copy-start.15 = (s32[128,8]{0,1:T(8,128)S(1)}, s32[128,8]{0,1:T(8,128)}, u32[]{:S(2)}) copy-start(s32[128,8]{0,1:T(8,128)} %param.19) | copy-start | bytes 12292
  2.8 15.7 %copy-start.12 = (s32[16]{0:T(128)S(1)}, s32[16]{0:T(128)}, u32[]{:S(2)}) copy-start(s32[16]{0:T(128)} %shadow_ref.3) | copy-start | bytes 196
  3.7 41.4 %copy-start.13 = (bf16[256,256]{1,0:T(8,128)(2,1)S(1)}, bf16[256,256]{1,0:T(8,128)(2,1)}, u32[]{:S(2)}) copy-start(bf16[256,256]{1,0:T(8,128)(2,1)} %param.14) | copy-start | bytes 393220
  3.7 41.4 %copy-start.14 = (bf16[256,256]{1,0:T(8,128)(2,1)S(1)}, bf16[256,256]{1,0:T(8,128)(2,1)}, u32[]{:S(2)}) copy-start(bf16[256,256]{1,0:T(8,128)(2,1)} %param.13) | copy-start | bytes 393220
  3.7 14.6 %all-to-all-start = ((bf16[8,66,384]{2,1,0:T(8,128)(2,1)}), bf16[8,66,384]{2,1,0:T(8,128)(2,1)S(1)}, u32[]{:S(2)}, u32[]{:S(2)}) async-start(bf16[8,66,384]{2,1,0:T(8,128)(2,1)} %fusion.1), calls=%async_computation | async-start | bytes 884736 | tf_op jit(solution)/shard_map/all_to_all | solution.py:314
  9.0 35.7 %collective-permute-start.3 = (bf16[128,4096]{1,0:T(8,128)(2,1)}, bf16[128,4096]{1,0:T(8,128)(2,1)}, u32[]{:S(2)}, u32[]{:S(2)}) collective-permute-start(bf16[128,4096]{1,0:T(8,128)(2,1)} %refs_0_.1), channel_id=1, source_target_pairs={{0,4},{1,3},{2,6},{3,1},{4,0},{5,7},{6,2},{7,5},{8,12},{9,11},{10,... | collective-permute-start | bytes 3145736 | tf_op jit(solution)/shard_map/ppermute | solution.py:366
  18.4 26.3 %collective-permute-start.4 = (bf16[128,4096]{1,0:T(8,128)(2,1)}, bf16[128,4096]{1,0:T(8,128)(2,1)}, u32[]{:S(2)}, u32[]{:S(2)}) collective-permute-start(bf16[128,4096]{1,0:T(8,128)(2,1)} %refs_0_.1), channel_id=1, source_target_pairs={{0,2},{1,5},{2,0},{3,7},{4,6},{5,1},{6,4},{7,3},{8,10},{9,13},{10,... | collective-permute-start | bytes 3145736 | tf_op jit(solution)/shard_map/ppermute | solution.py:366
  44.7 21.8 %collective-permute-start.8 = (bf16[128,4096]{1,0:T(8,128)(2,1)}, bf16[128,4096]{1,0:T(8,128)(2,1)}, u32[]{:S(2)}, u32[]{:S(2)}) collective-permute-start(bf16[128,4096]{1,0:T(8,128)(2,1)} %collective-permute-done.3.refs_2_), channel_id=1, source_target_pairs={{0,2},{1,5},{2,0},{3,7},{4,6},{5,1},{6,4},{7,3},{8,10},{9,13},{10,... | collective-permute-start | bytes 3145736 | tf_op jit(solution)/shard_map/ppermute | solution.py:366
  45.1 9.5 %collective-permute-start.2 = (bf16[256,256]{1,0:T(8,128)(2,1)S(1)}, bf16[256,256]{1,0:T(8,128)(2,1)S(1)}, u32[]{:S(2)}, u32[]{:S(2)}) collective-permute-start(bf16[256,256]{1,0:T(8,128)(2,1)S(1)} %pad_maximum_fusion.rest_0_), channel_id=1, source_target_pairs={{0,24},{1,25},{2,26},{3,27},{4,28},{5,29},{6,30},{7,31}} | collective-permute-start | bytes 393224 | tf_op jit(solution)/shard_map/ppermute | solution.py:98
  50.6 6.5 %collective-permute-start.1 = (bf16[256,256]{1,0:T(8,128)(2,1)S(1)}, bf16[256,256]{1,0:T(8,128)(2,1)S(1)}, u32[]{:S(2)}, u32[]{:S(2)}) collective-permute-start(bf16[256,256]{1,0:T(8,128)(2,1)S(1)} %pad_maximum_fusion.rest_0_), channel_id=1, source_target_pairs={{0,16},{8,24},{1,17},{9,25},{2,18},{10,26},{3,19},{11,27},{4,20},{... | collective-permute-start | bytes 393224 | tf_op jit(solution)/shard_map/ppermute | solution.py:98
  51.9 6.6 %collective-permute-start = (bf16[256,256]{1,0:T(8,128)(2,1)S(1)}, bf16[256,256]{1,0:T(8,128)(2,1)S(1)}, u32[]{:S(2)}, u32[]{:S(2)}) collective-permute-start(bf16[256,256]{1,0:T(8,128)(2,1)S(1)} %pad_maximum_fusion.rest_0_), channel_id=1, source_target_pairs={{0,8},{8,16},{16,24},{1,9},{9,17},{17,25},{2,10},{10,18},{18,26},{... | collective-permute-start | bytes 393224 | tf_op jit(solution)/shard_map/ppermute | solution.py:98
  54.4 20.9 %collective-permute-start.5 = (bf16[128,4096]{1,0:T(8,128)(2,1)}, bf16[128,4096]{1,0:T(8,128)(2,1)}, u32[]{:S(2)}, u32[]{:S(2)}) collective-permute-start(bf16[128,4096]{1,0:T(8,128)(2,1)} %refs_0_.1), channel_id=1, source_target_pairs={{0,1},{1,0},{2,3},{3,2},{4,5},{5,4},{6,7},{7,6},{8,9},{9,8},{10,11... | collective-permute-start | bytes 3145736 | tf_op jit(solution)/shard_map/ppermute | solution.py:366
  54.6 0.7 copy-start.4
  55.3 20.1 %collective-permute-start.6 = (bf16[128,4096]{1,0:T(8,128)(2,1)}, bf16[128,4096]{1,0:T(8,128)(2,1)}, u32[]{:S(2)}, u32[]{:S(2)}) collective-permute-start(bf16[128,4096]{1,0:T(8,128)(2,1)} %collective-permute-done.3.refs_2_), channel_id=1, source_target_pairs={{0,1},{1,0},{2,3},{3,2},{4,5},{5,4},{6,7},{7,6},{8,9},{9,8},{10,11... | collective-permute-start | bytes 3145736 | tf_op jit(solution)/shard_map/ppermute | solution.py:366
  57.1 0.7 copy-start.6
  58.5 0.7 copy-start.8
  59.2 16.2 %collective-permute-start.7 = (bf16[128,4096]{1,0:T(8,128)(2,1)}, bf16[128,4096]{1,0:T(8,128)(2,1)}, u32[]{:S(2)}, u32[]{:S(2)}) collective-permute-start(bf16[128,4096]{1,0:T(8,128)(2,1)} %collective-permute-done.4.refs_4_), channel_id=1, source_target_pairs={{0,1},{1,0},{2,3},{3,2},{4,5},{5,4},{6,7},{7,6},{8,9},{9,8},{10,11... | collective-permute-start | bytes 3145736 | tf_op jit(solution)/shard_map/ppermute | solution.py:366
  59.2 1.0 %copy-start = (bf16[8,64,384]{2,1,0:T(8,128)(2,1)S(1)}, bf16[8,64,384]{2,1,0:T(8,128)(2,1)}, u32[]{:S(2)}) copy-start(bf16[8,64,384]{2,1,0:T(8,128)(2,1)} %all_to_all.15.side_ref) | copy-start | bytes 1179652
  60.2 3.0 %copy-start.1 = (bf16[256,512]{1,0:T(8,128)(2,1)S(1)}, bf16[256,512]{1,0:T(8,128)(2,1)}, u32[]{:S(2)}) copy-start(bf16[256,512]{1,0:T(8,128)(2,1)} %query_ref.1) | copy-start | bytes 786436
  60.2 3.0 %copy-start.2 = (bf16[256,512]{1,0:T(8,128)(2,1)S(1)}, bf16[256,512]{1,0:T(8,128)(2,1)}, u32[]{:S(2)}) copy-start(bf16[256,512]{1,0:T(8,128)(2,1)} %grad_ref.1) | copy-start | bytes 786436
  60.2 3.0 %copy-start.3 = (bf16[256,512]{1,0:T(8,128)(2,1)S(1)}, bf16[256,512]{1,0:T(8,128)(2,1)}, u32[]{:S(2)}) copy-start(bf16[256,512]{1,0:T(8,128)(2,1)} %out_ref.1) | copy-start | bytes 786436
  60.2 3.0 %copy-start.5 = (bf16[256,256]{1,0:T(8,128)(2,1)S(1)}, bf16[256,256]{1,0:T(8,128)(2,1)}, u32[]{:S(2)}) copy-start(bf16[256,256]{1,0:T(8,128)(2,1)} %copy-done.4) | copy-start | bytes 393220
  60.2 3.0 %copy-start.7 = (bf16[256,256]{1,0:T(8,128)(2,1)S(1)}, bf16[256,256]{1,0:T(8,128)(2,1)}, u32[]{:S(2)}) copy-start(bf16[256,256]{1,0:T(8,128)(2,1)} %copy-done.6) | copy-start | bytes 393220
  60.2 3.0 %copy-start.9 = (bf16[256,256]{1,0:T(8,128)(2,1)S(1)}, bf16[256,256]{1,0:T(8,128)(2,1)}, u32[]{:S(2)}) copy-start(bf16[256,256]{1,0:T(8,128)(2,1)} %copy-done.8) | copy-start | bytes 393220
  60.2 3.0 %copy-start.10 = (f32[4,256]{1,0:T(4,128)S(1)}, f32[4,256]{1,0:T(4,128)}, u32[]{:S(2)}) copy-start(f32[4,256]{1,0:T(4,128)} %lse_ref.1) | copy-start | bytes 12292
  60.2 3.0 %copy-start.11 = (s32[4,4]{1,0:T(4,128)S(1)}, s32[4,4]{1,0:T(4,128)}, u32[]{:S(2)}) copy-start(s32[4,4]{1,0:T(4,128)} %mask_ref.1) | copy-start | bytes 196
  66.5 8.9 %collective-permute-start.9 = (bf16[128,4096]{1,0:T(8,128)(2,1)}, bf16[128,4096]{1,0:T(8,128)(2,1)}, u32[]{:S(2)}, u32[]{:S(2)}) collective-permute-start(bf16[128,4096]{1,0:T(8,128)(2,1)} %collective-permute-done.8.refs_6_), channel_id=1, source_target_pairs={{0,1},{1,0},{2,3},{3,2},{4,5},{5,4},{6,7},{7,6},{8,9},{9,8},{10,11... | collective-permute-start | bytes 3145736 | tf_op jit(solution)/shard_map/ppermute | solution.py:366
  67.0 23.9 %all-to-all-start.2 = ((bf16[32,32,256]{2,1,0:T(8,128)(2,1)}), bf16[32,32,256]{2,1,0:T(8,128)(2,1)S(1)}, u32[]{:S(2)}, u32[]{:S(2)}) async-start(bf16[32,32,256]{2,1,0:T(8,128)(2,1)} %bitcast.4), calls=%async_computation.2 | async-start | bytes 1048576 | tf_op jit(solution)/shard_map/all_to_all | solution.py:146

commit v11 on v10

--- a/solution.py
+++ b/solution.py
@@ -401,10 +401,9 @@
     first = moved(moe_grad, [held[1] for held in steps])
     arrived = key_blocks(keys, values, queries.shape[1] // lse_excess.shape[0])
     mixed, sent = source_rows(expert_ids, route_probs, shadow_list, stored_hidden_state)
-    ready, mixed = lax.optimization_barrier((moe_grad, mixed))
+    shadow_rows = swapped(sent)
+    ready, first, _ = lax.optimization_barrier((moe_grad, first, shadow_rows))
     second = moved(ready, [held[2] for held in steps])
-    shadow_rows = swapped(sent)
-    first, second, shadow_rows = lax.optimization_barrier((first, second, shadow_rows))
     arrived, _ = lax.optimization_barrier((arrived, shadow_rows))
     query_grad, terms = attention(
         queries, arrived, attn_out, attn_out_grad, lse_excess, block_mask

time: 93.4 us -> 81.9 us (0.88); the launches traced: 91.6 us -> 81.5 us
  starting transfers between devices: 26.4 us -> 18.9 us
  blocking collectives: 25.6 us -> 27.8 us
  local copies, waits for them, and re-layouts: 4.54 us -> 2.35 us
  waiting for transfers between devices: 14.4 us -> 12.9 us
    all_to_all x1 -> x0, waiting for transfers between devices: 7.32 us -> none  [swapped(): return lax.all_to_all(value, 'exp', split_axis=0, concat_axis=0, tiled=True)]
    all_to_all x1 -> x0, starting transfers between devices: 5.3 us -> none  [swapped(): return lax.all_to_all(value, 'exp', split_axis=0, concat_axis=0, tiled=True)]
    all_to_all x1, starting transfers between devices: 8.38 us -> 3.97 us  [summed_terms(): lax.all_to_all(terms.reshape(cycle * owners, rows // owners, columns), ('...]
    ppermute x7, waiting for transfers between devices: 0.02 us -> 4.25 us  [moved(): lax.ppermute(value, 'exp', [(e, e ^ steps[e % 2]) for e in range(owners)])]
    unnamed x33 -> x23, local copies, waits for them, and re-layouts: 4.49 us -> 2.29 us
    all_to_all x1 -> x2, blocking collectives: 25.6 us -> 27.8 us  [swapped(): return lax.all_to_all(value, 'exp', split_axis=0, concat_axis=0, tiled=True)]
    ppermute x7, starting transfers between devices: 3.47 us -> 5.64 us  [moved(): lax.ppermute(value, 'exp', [(e, e ^ steps[e % 2]) for e in range(owners)])]
    ppermute x3, waiting for transfers between devices: 2.31 us -> 3.83 us  [key_blocks(): lax.ppermute(pair, 'ctx', [(c, c + step) for c in range(cycle - step)])]
  transfers between devices with their start and end apart: 12 -> 11, of which waited for: 5 -> 5; matrix products, arithmetic and copies ran while one was open for 0% -> 3% of each run, Pallas kernels for 19% -> 21%
where the time goes in v11:
time: 81.9 us; the launch traced here: 81.5 us
  blocking collectives  27.8 us (34%)
  starting transfers between devices  18.9 us (23%)
  Pallas kernels  18 us (22%)
  waiting for transfers between devices  12.9 us (16%)
  local copies, waits for them, and re-layouts  2.35 us (3%)
  between operations  0.88 us (1%)
    all_to_all x2, blocking collectives, swapped(): return lax.all_to_all(value, 'exp', split_axis=0, concat_axis=0, tiled=True)  27.8 us
    pallas_call x1, Pallas kernels, tile_sums(): pl.pallas_call(tile_kernel, out_shape=jax.ShapeDtypeStruct((per_dev, rows...  10.7 us
    ppermute x3, starting transfers between devices, key_blocks(): lax.ppermute(pair, 'ctx', [(c, c + step) for c in range(cycle - step)])  9.28 us
    ppermute x7, starting transfers between devices, moved(): lax.ppermute(value, 'exp', [(e, e ^ steps[e % 2]) for e in range(owners)])  5.64 us
    all_to_all x1, waiting for transfers between devices, summed_terms(): lax.all_to_all(terms.reshape(cycle * owners, rows // owners, columns), ('...  4.77 us
    ppermute x7, waiting for transfers between devices, moved(): lax.ppermute(value, 'exp', [(e, e ^ steps[e % 2]) for e in range(owners)])  4.25 us
    all_to_all x1, starting transfers between devices, summed_terms(): lax.all_to_all(terms.reshape(cycle * owners, rows // owners, columns), ('...  3.97 us
    ppermute x3, waiting for transfers between devices, key_blocks(): lax.ppermute(pair, 'ctx', [(c, c + step) for c in range(cycle - step)])  3.83 us
  transfers between devices with their start and end apart: 11, of which 5 were waited for; matrix products, arithmetic and copies ran while one was open for 3% of the time, Pallas kernels for 21%

profile of v11, /device:TPU:0, one launch (start us, length us, event | category | flops | bytes accessed | tf_op | source)
XLA Modules:
  0.0 81.5 jit_solution(6411016444804457304)
XLA Ops:
  0.6 0.0 copy-start.10
  0.6 3.0 %collective-permute-start.4 = (bf16[128,4096]{1,0:T(8,128)(2,1)}, bf16[128,4096]{1,0:T(8,128)(2,1)}, u32[]{:S(2)}, u32[]{:S(2)}) collective-permute-start(bf16[128,4096]{1,0:T(8,128)(2,1)} %refs_0_.1), channel_id=1, source_target_pairs={{0,4},{1,3},{2,6},{3,1},{4,0},{5,7},{6,2},{7,5},{8,12},{9,11},{10,... | collective-permute-start | bytes 3145736 | tf_op jit(solution)/shard_map/ppermute | solution.py:366
  3.7 0.7 convert_element_type.13
  4.4 1.5 %copy.20.hidden_ref = bf16[1,3,8,65,384]{4,3,2,1,0:T(8,128)(2,1)S(1)} copy(bf16[1,3,8,65,384]{4,2,3,1,0:T(8,128)(2,1)} %param.23) | data formatting | bytes 2396160 | tf_op args[11]
  5.8 0.0 copy-done.10
  5.8 0.0 copy-start.7
  6.0 0.0 copy-start.8
  6.0 0.0 copy-start.9
  6.0 0.0 copy-start.2
  6.0 0.0 copy-start.3
  6.0 0.0 copy-start.4
  6.0 0.0 copy-start.5
  6.0 0.0 copy-start.6
  6.1 15.7 %all_to_all.15.mixed_ref = bf16[8,66,384]{2,1,0:T(8,128)(2,1)S(1)} all-to-all(bf16[8,66,384]{2,1,0:T(8,128)(2,1)S(1)} %fusion.1), channel_id=1, replica_groups=mesh['ctx'=4,'exp'=8] {'exp'}, dimensions={0} | all-to-all | bytes 811008 | tf_op jit(solution)/shard_map/all_to_all | solution.py:314
  21.7 0.0 copy-done.7
  21.7 0.6 picked.1
  22.3 12.1 %all_to_all.16.side_ref = bf16[8,64,384]{2,1,0:T(8,128)(2,1)} all-to-all(bf16[8,64,384]{2,1,0:T(8,128)(2,1)S(1)} %picked.1), channel_id=1, replica_groups=mesh['ctx'=4,'exp'=8] {'exp'}, dimensions={0} | all-to-all | bytes 786432 | tf_op jit(solution)/shard_map/all_to_all | solution.py:314
  34.5 0.0 collective-permute-done.4.refs_2_
  34.5 0.6 collective-permute-start.8
  35.0 1.5 %collective-permute-start.6 = (bf16[128,4096]{1,0:T(8,128)(2,1)}, bf16[128,4096]{1,0:T(8,128)(2,1)}, u32[]{:S(2)}, u32[]{:S(2)}) collective-permute-start(bf16[128,4096]{1,0:T(8,128)(2,1)} %refs_0_.1), channel_id=1, source_target_pairs={{0,2},{1,5},{2,0},{3,7},{4,6},{5,1},{6,4},{7,3},{8,10},{9,13},{10,... | collective-permute-start | bytes 3145736 | tf_op jit(solution)/shard_map/ppermute | solution.py:366
  36.5 0.0 copy-done.8
  36.5 0.0 copy-done.9
  36.5 5.5 %collective-permute-start.2 = (bf16[256,256]{1,0:T(8,128)(2,1)S(1)}, bf16[256,256]{1,0:T(8,128)(2,1)S(1)}, u32[]{:S(2)}, u32[]{:S(2)}) collective-permute-start(bf16[256,256]{1,0:T(8,128)(2,1)S(1)} %pad_maximum_fusion.rest_0_), channel_id=1, source_target_pairs={{0,24},{1,25},{2,26},{3,27},{4,28},{5,29},{6,30},{7,31}} | collective-permute-start | bytes 393224 | tf_op jit(solution)/shard_map/ppermute | solution.py:98
  42.1 1.3 %collective-permute-start.1 = (bf16[256,256]{1,0:T(8,128)(2,1)S(1)}, bf16[256,256]{1,0:T(8,128)(2,1)S(1)}, u32[]{:S(2)}, u32[]{:S(2)}) collective-permute-start(bf16[256,256]{1,0:T(8,128)(2,1)S(1)} %pad_maximum_fusion.rest_0_), channel_id=1, source_target_pairs={{0,16},{8,24},{1,17},{9,25},{2,18},{10,26},{3,19},{11,27},{4,20},{... | collective-permute-start | bytes 393224 | tf_op jit(solution)/shard_map/ppermute | solution.py:98
  43.4 2.5 %collective-permute-start = (bf16[256,256]{1,0:T(8,128)(2,1)S(1)}, bf16[256,256]{1,0:T(8,128)(2,1)S(1)}, u32[]{:S(2)}, u32[]{:S(2)}) collective-permute-start(bf16[256,256]{1,0:T(8,128)(2,1)S(1)} %pad_maximum_fusion.rest_0_), channel_id=1, source_target_pairs={{0,8},{8,16},{16,24},{1,9},{9,17},{17,25},{2,10},{10,18},{18,26},{... | collective-permute-start | bytes 393224 | tf_op jit(solution)/shard_map/ppermute | solution.py:98
  45.8 0.0 copy-start
  45.9 0.2 collective-permute-done.2.rest_3_
  46.0 0.0 collective-permute-start.3
  46.0 2.3 %collective-permute-done.1.rest_2_ = bf16[256,256]{1,0:T(8,128)(2,1)S(1)} collective-permute-done((bf16[256,256]{1,0:T(8,128)(2,1)S(1)}, bf16[256,256]{1,0:T(8,128)(2,1)S(1)}, u32[]{:S(2)}, u32[]{:S(2)}) %collective-permute-start.1) | collective-permute-done | bytes 131104 | tf_op jit(solution)/shard_map/ppermute | solution.py:98
  48.3 1.4 %collective-permute-done.rest_1_ = bf16[256,256]{1,0:T(8,128)(2,1)S(1)} collective-permute-done((bf16[256,256]{1,0:T(8,128)(2,1)S(1)}, bf16[256,256]{1,0:T(8,128)(2,1)S(1)}, u32[]{:S(2)}, u32[]{:S(2)}) %collective-permute-start) | collective-permute-done | bytes 131104 | tf_op jit(solution)/shard_map/ppermute | solution.py:98
  49.7 0.0 copy-done.5
  49.7 0.0 copy-done.6
  49.7 3.1 %attention.1 = (bf16[256,512]{1,0:T(8,128)(2,1)}, bf16[4,256,256]{2,1,0:T(8,128)(2,1)S(1)}) custom-call(s32[1]{0:T(128)} %bitcast.place_ref, s32[4,4]{1,0:T(4,128)S(1)} %copy-done.6, bf16[256,512]{1,0:T(8,128)(2,1)S(1)} %copy-done.2, bf16[256,512]{1,0:T(8,128)(2,1)S(1)} %copy-done.3, bf16[256,512]{1,0:T(8,128)(2,1)S(1)} %copy-done.4, ...), custom_call_target="tpu_custom_call" | custom-call | tf_op jit(solution)/shard_map/attention/pallas_call | solution.py:108
  52.8 0.8 copy-done.1
  53.6 2.9 %weighted.1.weight_ref = bf16[768,1024]{1,0:T(8,128)(2,1)S(1)} custom-call(s32[1]{0:T(128)} %bitcast.6.own_ref, s32[16]{0:T(128)S(1)} %copy-done.7, bf16[8,66,384]{2,1,0:T(8,128)(2,1)S(1)} %all_to_all.15.mixed_ref, bf16[1,3,8,65,384]{4,3,2,1,0:T(8,128)(2,1)S(1)} %copy.20.hidden_ref, bf16[8,64,384]{2,1,0:T(8,128)(2,1)S(1)} %copy-done), custom_call_target="tpu_custom_call" | custom-call | tf_op jit(solution)/shard_map/weighted/pallas_call | solution.py:231
  56.5 0.1 collective-permute-start.5
  56.6 0.0 collective-permute-done.8.refs_6_
  56.6 4.2 %collective-permute-done.6.refs_4_ = bf16[128,4096]{1,0:T(8,128)(2,1)} collective-permute-done((bf16[128,4096]{1,0:T(8,128)(2,1)}, bf16[128,4096]{1,0:T(8,128)(2,1)}, u32[]{:S(2)}, u32[]{:S(2)}) %collective-permute-start.6) | collective-permute-done | bytes 1048608 | tf_op jit(solution)/shard_map/ppermute | solution.py:366
  60.8 0.0 collective-permute-start.7
  60.8 0.5 collective-permute-start.9
  61.3 4.0 %all-to-all-start.2 = ((bf16[32,32,256]{2,1,0:T(8,128)(2,1)}), bf16[32,32,256]{2,1,0:T(8,128)(2,1)S(1)}, u32[]{:S(2)}, u32[]{:S(2)}) async-start(bf16[32,32,256]{2,1,0:T(8,128)(2,1)} %bitcast.10), calls=%async_computation.2 | async-start | bytes 1048576 | tf_op jit(solution)/shard_map/all_to_all | solution.py:146
  65.3 0.0 collective-permute-done.3.refs_1_
  65.3 0.0 collective-permute-done.5.refs_3_
  65.3 0.0 collective-permute-done.7.refs_5_
  65.3 0.0 collective-permute-done.9.refs_7_
  65.3 10.7 %tiles.1 = f32[2,384,4096]{2,1,0:T(8,128)} custom-call(bf16[768,1024]{1,0:T(8,128)(2,1)S(1)} %weighted.1.weight_ref, bf16[128,4096]{1,0:T(8,128)(2,1)} %refs_0_.1, bf16[128,4096]{1,0:T(8,128)(2,1)} %collective-permute-done.3.refs_1_, bf16[128,4096]{1,0:T(8,128)(2,1)} %collective-permute-done.4.refs_2_, bf16[128,4096]{1,0:T(8,128)(2,1)} %collective-permute-done.5.refs_3_, ...), custom_call_target="tpu_custom_call" | custom-call | tf_op jit(solution)/shard_map/tiles/pallas_call | solution.py:297
  76.1 4.8 %all-to-all-done.2 = bf16[32,32,256]{2,1,0:T(8,128)(2,1)S(1)} async-done(((bf16[32,32,256]{2,1,0:T(8,128)(2,1)}), bf16[32,32,256]{2,1,0:T(8,128)(2,1)S(1)}, u32[]{:S(2)}, u32[]{:S(2)}) %all-to-all-start.2) | async-done | bytes 524320 | tf_op jit(solution)/shard_map/all_to_all | solution.py:146
  80.8 0.7 sums.1
  (10 shorter events, 0.2 us)
Async XLA Ops:
  0.6 5.2 %copy-start.10 = (s32[128,8]{0,1:T(8,128)S(1)}, s32[128,8]{0,1:T(8,128)}, u32[]{:S(2)}) copy-start(s32[128,8]{0,1:T(8,128)} %param.19) | copy-start | bytes 12292
  0.6 33.8 %collective-permute-start.4 = (bf16[128,4096]{1,0:T(8,128)(2,1)}, bf16[128,4096]{1,0:T(8,128)(2,1)}, u32[]{:S(2)}, u32[]{:S(2)}) collective-permute-start(bf16[128,4096]{1,0:T(8,128)(2,1)} %refs_0_.1), channel_id=1, source_target_pairs={{0,4},{1,3},{2,6},{3,1},{4,0},{5,7},{6,2},{7,5},{8,12},{9,11},{10,... | collective-permute-start | bytes 3145736 | tf_op jit(solution)/shard_map/ppermute | solution.py:366
  5.8 15.9 %copy-start.7 = (s32[16]{0:T(128)S(1)}, s32[16]{0:T(128)}, u32[]{:S(2)}) copy-start(s32[16]{0:T(128)} %shadow_ref.3) | copy-start | bytes 196
  6.0 30.5 %copy-start.8 = (bf16[256,256]{1,0:T(8,128)(2,1)S(1)}, bf16[256,256]{1,0:T(8,128)(2,1)}, u32[]{:S(2)}) copy-start(bf16[256,256]{1,0:T(8,128)(2,1)} %param.14) | copy-start | bytes 393220
  6.0 30.5 %copy-start.9 = (bf16[256,256]{1,0:T(8,128)(2,1)S(1)}, bf16[256,256]{1,0:T(8,128)(2,1)}, u32[]{:S(2)}) copy-start(bf16[256,256]{1,0:T(8,128)(2,1)} %param.13) | copy-start | bytes 393220
  6.0 43.7 %copy-start.2 = (bf16[256,512]{1,0:T(8,128)(2,1)S(1)}, bf16[256,512]{1,0:T(8,128)(2,1)}, u32[]{:S(2)}) copy-start(bf16[256,512]{1,0:T(8,128)(2,1)} %query_ref.1) | copy-start | bytes 786436
  6.0 43.7 %copy-start.3 = (bf16[256,512]{1,0:T(8,128)(2,1)S(1)}, bf16[256,512]{1,0:T(8,128)(2,1)}, u32[]{:S(2)}) copy-start(bf16[256,512]{1,0:T(8,128)(2,1)} %grad_ref.1) | copy-start | bytes 786436
  6.0 43.7 %copy-start.4 = (bf16[256,512]{1,0:T(8,128)(2,1)S(1)}, bf16[256,512]{1,0:T(8,128)(2,1)}, u32[]{:S(2)}) copy-start(bf16[256,512]{1,0:T(8,128)(2,1)} %out_ref.1) | copy-start | bytes 786436
  6.0 43.7 %copy-start.5 = (f32[4,256]{1,0:T(4,128)S(1)}, f32[4,256]{1,0:T(4,128)}, u32[]{:S(2)}) copy-start(f32[4,256]{1,0:T(4,128)} %lse_ref.1) | copy-start | bytes 12292
  6.0 43.7 %copy-start.6 = (s32[4,4]{1,0:T(4,128)S(1)}, s32[4,4]{1,0:T(4,128)}, u32[]{:S(2)}) copy-start(s32[4,4]{1,0:T(4,128)} %mask_ref.1) | copy-start | bytes 196
  34.5 22.1 %collective-permute-start.8 = (bf16[128,4096]{1,0:T(8,128)(2,1)}, bf16[128,4096]{1,0:T(8,128)(2,1)}, u32[]{:S(2)}, u32[]{:S(2)}) collective-permute-start(bf16[128,4096]{1,0:T(8,128)(2,1)} %collective-permute-done.4.refs_2_), channel_id=1, source_target_pairs={{0,2},{1,5},{2,0},{3,7},{4,6},{5,1},{6,4},{7,3},{8,10},{9,13},{10,... | collective-permute-start | bytes 3145736 | tf_op jit(solution)/shard_map/ppermute | solution.py:366
  35.0 25.8 %collective-permute-start.6 = (bf16[128,4096]{1,0:T(8,128)(2,1)}, bf16[128,4096]{1,0:T(8,128)(2,1)}, u32[]{:S(2)}, u32[]{:S(2)}) collective-permute-start(bf16[128,4096]{1,0:T(8,128)(2,1)} %refs_0_.1), channel_id=1, source_target_pairs={{0,2},{1,5},{2,0},{3,7},{4,6},{5,1},{6,4},{7,3},{8,10},{9,13},{10,... | collective-permute-start | bytes 3145736 | tf_op jit(solution)/shard_map/ppermute | solution.py:366
  36.5 9.5 %collective-permute-start.2 = (bf16[256,256]{1,0:T(8,128)(2,1)S(1)}, bf16[256,256]{1,0:T(8,128)(2,1)S(1)}, u32[]{:S(2)}, u32[]{:S(2)}) collective-permute-start(bf16[256,256]{1,0:T(8,128)(2,1)S(1)} %pad_maximum_fusion.rest_0_), channel_id=1, source_target_pairs={{0,24},{1,25},{2,26},{3,27},{4,28},{5,29},{6,30},{7,31}} | collective-permute-start | bytes 393224 | tf_op jit(solution)/shard_map/ppermute | solution.py:98
  42.1 6.2 %collective-permute-start.1 = (bf16[256,256]{1,0:T(8,128)(2,1)S(1)}, bf16[256,256]{1,0:T(8,128)(2,1)S(1)}, u32[]{:S(2)}, u32[]{:S(2)}) collective-permute-start(bf16[256,256]{1,0:T(8,128)(2,1)S(1)} %pad_maximum_fusion.rest_0_), channel_id=1, source_target_pairs={{0,16},{8,24},{1,17},{9,25},{2,18},{10,26},{3,19},{11,27},{4,20},{... | collective-permute-start | bytes 393224 | tf_op jit(solution)/shard_map/ppermute | solution.py:98
  43.4 6.3 %collective-permute-start = (bf16[256,256]{1,0:T(8,128)(2,1)S(1)}, bf16[256,256]{1,0:T(8,128)(2,1)S(1)}, u32[]{:S(2)}, u32[]{:S(2)}) collective-permute-start(bf16[256,256]{1,0:T(8,128)(2,1)S(1)} %pad_maximum_fusion.rest_0_), channel_id=1, source_target_pairs={{0,8},{8,16},{16,24},{1,9},{9,17},{17,25},{2,10},{10,18},{18,26},{... | collective-permute-start | bytes 393224 | tf_op jit(solution)/shard_map/ppermute | solution.py:98
  45.8 7.7 %copy-start = (bf16[8,64,384]{2,1,0:T(8,128)(2,1)S(1)}, bf16[8,64,384]{2,1,0:T(8,128)(2,1)}, u32[]{:S(2)}) copy-start(bf16[8,64,384]{2,1,0:T(8,128)(2,1)} %all_to_all.16.side_ref) | copy-start | bytes 1179652
  46.0 19.3 %collective-permute-start.3 = (bf16[128,4096]{1,0:T(8,128)(2,1)}, bf16[128,4096]{1,0:T(8,128)(2,1)}, u32[]{:S(2)}, u32[]{:S(2)}) collective-permute-start(bf16[128,4096]{1,0:T(8,128)(2,1)} %refs_0_.1), channel_id=1, source_target_pairs={{0,1},{1,0},{2,3},{3,2},{4,5},{5,4},{6,7},{7,6},{8,9},{9,8},{10,11... | collective-permute-start | bytes 3145736 | tf_op jit(solution)/shard_map/ppermute | solution.py:366
  52.8 0.8 copy-start.1
  56.5 8.8 %collective-permute-start.5 = (bf16[128,4096]{1,0:T(8,128)(2,1)}, bf16[128,4096]{1,0:T(8,128)(2,1)}, u32[]{:S(2)}, u32[]{:S(2)}) collective-permute-start(bf16[128,4096]{1,0:T(8,128)(2,1)} %collective-permute-done.4.refs_2_), channel_id=1, source_target_pairs={{0,1},{1,0},{2,3},{3,2},{4,5},{5,4},{6,7},{7,6},{8,9},{9,8},{10,11... | collective-permute-start | bytes 3145736 | tf_op jit(solution)/shard_map/ppermute | solution.py:366
  60.8 4.5 %collective-permute-start.7 = (bf16[128,4096]{1,0:T(8,128)(2,1)}, bf16[128,4096]{1,0:T(8,128)(2,1)}, u32[]{:S(2)}, u32[]{:S(2)}) collective-permute-start(bf16[128,4096]{1,0:T(8,128)(2,1)} %collective-permute-done.6.refs_4_), channel_id=1, source_target_pairs={{0,1},{1,0},{2,3},{3,2},{4,5},{5,4},{6,7},{7,6},{8,9},{9,8},{10,11... | collective-permute-start | bytes 3145736 | tf_op jit(solution)/shard_map/ppermute | solution.py:366
  60.8 4.5 %collective-permute-start.9 = (bf16[128,4096]{1,0:T(8,128)(2,1)}, bf16[128,4096]{1,0:T(8,128)(2,1)}, u32[]{:S(2)}, u32[]{:S(2)}) collective-permute-start(bf16[128,4096]{1,0:T(8,128)(2,1)} %collective-permute-done.8.refs_6_), channel_id=1, source_target_pairs={{0,1},{1,0},{2,3},{3,2},{4,5},{5,4},{6,7},{7,6},{8,9},{9,8},{10,11... | collective-permute-start | bytes 3145736 | tf_op jit(solution)/shard_map/ppermute | solution.py:366
  61.3 19.5 %all-to-all-start.2 = ((bf16[32,32,256]{2,1,0:T(8,128)(2,1)}), bf16[32,32,256]{2,1,0:T(8,128)(2,1)S(1)}, u32[]{:S(2)}, u32[]{:S(2)}) async-start(bf16[32,32,256]{2,1,0:T(8,128)(2,1)} %bitcast.10), calls=%async_computation.2 | async-start | bytes 1048576 | tf_op jit(solution)/shard_map/all_to_all | solution.py:146

commit v12 on v11

--- a/solution.py
+++ b/solution.py
@@ -333,8 +333,7 @@
         ((0, 0), (0, limit - used), (0, lanes - units)),
     )
     mixed = jnp.concatenate([rows, jnp.pad(table, ((0, 0), (0, 0), (0, lanes - tokens)))], axis=1)
-    mixed = swapped(mixed)
-    return mixed, picked_rows(shadow_list, mixed, limit)
+    return mixed
 
 
 def expert_rows(mixed, shadow_rows, shadow_list, stored_hidden_state, tokens):
@@ -364,6 +363,19 @@
 def moved(value, steps):
     owners = lax.axis_size("exp")
     return lax.ppermute(value, "exp", [(e, e ^ steps[e % 2]) for e in range(owners)])
+
+
+def paired_half(block):
+    rows = block.shape[0] // 2
+    return lax.dynamic_slice_in_dim(block, lax.axis_index("ctx") % 2 * rows, rows, 0)
+
+
+def paired_whole(half):
+    other = lax.ppermute(half, "ctx", [(c, c ^ 1) for c in range(lax.axis_size("ctx"))])
+    lower = lax.axis_index("ctx") % 2 == 0
+    return jnp.where(
+        lower, jnp.concatenate([half, other], axis=0), jnp.concatenate([other, half], axis=0)
+    )
 
 
 def expert_tiles(weighted, near, anchor, per_dev):
@@ -398,20 +410,25 @@
     stored_hidden_state,
 ):
     steps = block_steps(lax.axis_size("exp"))
-    first = moved(moe_grad, [held[1] for held in steps])
+    half = paired_half(moe_grad)
+    first = moved(half, [held[1] for held in steps])
+    second = moved(half, [held[2] for held in steps])
     arrived = key_blocks(keys, values, queries.shape[1] // lse_excess.shape[0])
-    mixed, sent = source_rows(expert_ids, route_probs, shadow_list, stored_hidden_state)
+    payload = source_rows(expert_ids, route_probs, shadow_list, stored_hidden_state)
+    mixed, arrived = lax.optimization_barrier((swapped(payload), arrived))
+    per_dev = shadow_list.shape[0] // lax.axis_size("exp")
+    sent = picked_rows(shadow_list, mixed, payload.shape[1] - per_dev)
+    sent, first, second = lax.optimization_barrier((sent, first, second))
+    first, second = paired_whole(first), paired_whole(second)
     shadow_rows = swapped(sent)
-    ready, first, _ = lax.optimization_barrier((moe_grad, first, shadow_rows))
-    second = moved(ready, [held[2] for held in steps])
-    arrived, _ = lax.optimization_barrier((arrived, shadow_rows))
+    arrived, _ = lax.optimization_barrier((arrived, sent))
     query_grad, terms = attention(
         queries, arrived, attn_out, attn_out_grad, lse_excess, block_mask
     )
+    first, shadow_rows = lax.optimization_barrier((first, shadow_rows))
     weighted = expert_rows(
         mixed, shadow_rows, shadow_list, stored_hidden_state, expert_ids.shape[0]
     )
-    per_dev = shadow_list.shape[0] // lax.axis_size("exp")
     tiles = expert_tiles(weighted, (moe_grad, first, second), query_grad, per_dev)
     key_grad, value_grad, expert_grad = summed_terms(terms, keys.shape[1], tiles)
     return (query_grad, key_grad, value_grad, expert_grad)

time: 81.9 us -> 92.5 us (1.13)
  blocking collectives: 27.8 us -> 0 us
  starting transfers between devices: 18.9 us -> 34.6 us
  waiting for transfers between devices: 12.9 us -> 26.4 us
  other arithmetic: 0.78 us -> 6.77 us
  local copies, waits for them, and re-layouts: 2.35 us -> 4.47 us
    all_to_all x2 -> x0, blocking collectives: 27.8 us -> none  [swapped(): return lax.all_to_all(value, 'exp', split_axis=0, concat_axis=0, tiled=True)]
    ppermute x0 -> x2, waiting for transfers between devices: none -> 16.5 us  [paired_whole(): lax.ppermute(half, 'ctx', [(c, c ^ 1) for c in range(lax.axis_size('ctx'))])]
    all_to_all x0 -> x2, starting transfers between devices: none -> 7.33 us  [swapped(): return lax.all_to_all(value, 'exp', split_axis=0, concat_axis=0, tiled=True)]
    ppermute x0 -> x2, starting transfers between devices: none -> 5.99 us  [paired_whole(): lax.ppermute(half, 'ctx', [(c, c ^ 1) for c in range(lax.axis_size('ctx'))])]
    select_n x0 -> x2, other arithmetic: none -> 5.23 us  [paired_whole(): jnp.where(lower, jnp.concatenate([half, other], axis=0), jnp.concatenate(...]
    ppermute x7, waiting for transfers between devices: 4.25 us -> 0.02 us  [moved(): lax.ppermute(value, 'exp', [(e, e ^ steps[e % 2]) for e in range(owners)])]
    dynamic_slice x0 -> x1, local copies, waits for them, and re-layouts: none -> 1.87 us  [paired_half(): lax.dynamic_slice_in_dim(block, lax.axis_index('ctx') % 2 * rows, rows, 0)]
    ppermute x7, starting transfers between devices: 5.64 us -> 7.18 us  [moved(): lax.ppermute(value, 'exp', [(e, e ^ steps[e % 2]) for e in range(owners)])]
  transfers between devices with their start and end apart: 11 -> 15, of which waited for: 5 -> 6; matrix products, arithmetic and copies ran while one was open for 3% -> 9% of each run, Pallas kernels for 21% -> 20%
where the time goes in v12:
time: 92.5 us; the launch traced here: 91.9 us
  starting transfers between devices  34.6 us (37%)
  waiting for transfers between devices  26.4 us (29%)
  Pallas kernels  18.7 us (20%)
  other arithmetic  6.77 us (7%)
  local copies, waits for them, and re-layouts  4.47 us (5%)
  between operations  0.93 us (1%)
    ppermute x2, waiting for transfers between devices, paired_whole(): lax.ppermute(half, 'ctx', [(c, c ^ 1) for c in range(lax.axis_size('ctx'))])  16.5 us
    pallas_call x1, Pallas kernels, tile_sums(): pl.pallas_call(tile_kernel, out_shape=jax.ShapeDtypeStruct((per_dev, rows...  10.7 us
    ppermute x3, starting transfers between devices, key_blocks(): lax.ppermute(pair, 'ctx', [(c, c + step) for c in range(cycle - step)])  9.43 us
    all_to_all x2, starting transfers between devices, swapped(): return lax.all_to_all(value, 'exp', split_axis=0, concat_axis=0, tiled=True)  7.33 us
    ppermute x7, starting transfers between devices, moved(): lax.ppermute(value, 'exp', [(e, e ^ steps[e % 2]) for e in range(owners)])  7.18 us
    ppermute x2, starting transfers between devices, paired_whole(): lax.ppermute(half, 'ctx', [(c, c ^ 1) for c in range(lax.axis_size('ctx'))])  5.99 us
    select_n x2, other arithmetic, paired_whole(): jnp.where(lower, jnp.concatenate([half, other], axis=0), jnp.concatenate(...  5.23 us
    ppermute x3, waiting for transfers between devices, key_blocks(): lax.ppermute(pair, 'ctx', [(c, c + step) for c in range(cycle - step)])  5.14 us
  transfers between devices with their start and end apart: 15, of which 6 were waited for; matrix products, arithmetic and copies ran while one was open for 9% of the time, Pallas kernels for 20%

profile of v12, /device:TPU:0, one launch (start us, length us, event | category | flops | bytes accessed | tf_op | source)
XLA Modules:
  0.0 91.9 jit_solution(6577929771518547118)
XLA Ops:
  0.7 1.9 %constant_dynamic-slice_fusion = bf16[64,4096]{1,0:T(8,128)(2,1)} fusion(bf16[128,4096]{1,0:T(8,128)(2,1)} %refs_0_.1, s32[]{:T(128)S(6)} %select_n.42), kind=kLoop, calls=%fused_computation.9 | loop fusion | bytes 1048580 | tf_op jit(solution)/shard_map/dynamic_slice | solution.py:370
  2.5 2.9 %collective-permute-start.4 = (bf16[64,4096]{1,0:T(8,128)(2,1)}, bf16[64,4096]{1,0:T(8,128)(2,1)}, u32[]{:S(2)}, u32[]{:S(2)}) collective-permute-start(bf16[64,4096]{1,0:T(8,128)(2,1)} %constant_dynamic-slice_fusion), channel_id=1, source_target_pairs={{0,2},{1,5},{2,0},{3,7},{4,6},{5,1},{6,4},{7,3},{8,10},{9,13},{10,... | collective-permute-start | bytes 1572872 | tf_op jit(solution)/shard_map/ppermute | solution.py:365
  5.5 1.5 %collective-permute-start.3 = (bf16[64,4096]{1,0:T(8,128)(2,1)}, bf16[64,4096]{1,0:T(8,128)(2,1)}, u32[]{:S(2)}, u32[]{:S(2)}) collective-permute-start(bf16[64,4096]{1,0:T(8,128)(2,1)} %constant_dynamic-slice_fusion), channel_id=1, source_target_pairs={{0,4},{1,3},{2,6},{3,1},{4,0},{5,7},{6,2},{7,5},{8,12},{9,11},{10,... | collective-permute-start | bytes 1572872 | tf_op jit(solution)/shard_map/ppermute | solution.py:365
  7.0 0.7 convert_element_type.13
  7.7 1.5 %copy.20.hidden_ref = bf16[1,3,8,65,384]{4,3,2,1,0:T(8,128)(2,1)S(1)} copy(bf16[1,3,8,65,384]{4,2,3,1,0:T(8,128)(2,1)} %param.23) | data formatting | bytes 2396160 | tf_op args[11]
  9.2 0.0 copy-start.8
  9.3 0.8 fusion.1
  10.1 3.5 %all-to-all-start = ((bf16[8,66,384]{2,1,0:T(8,128)(2,1)}), bf16[8,66,384]{2,1,0:T(8,128)(2,1)S(1)}, u32[]{:S(2)}, u32[]{:S(2)}) async-start(bf16[8,66,384]{2,1,0:T(8,128)(2,1)} %fusion.1), calls=%async_computation | async-start | bytes 884736 | tf_op jit(solution)/shard_map/all_to_all | solution.py:314
  13.6 0.0 copy-start.3
  13.6 0.0 copy-start.4
  13.6 0.0 copy-start.5
  13.6 0.0 copy-start.6
  13.7 0.0 copy-start.7
  13.7 5.7 %collective-permute-start.2 = (bf16[256,256]{1,0:T(8,128)(2,1)S(1)}, bf16[256,256]{1,0:T(8,128)(2,1)S(1)}, u32[]{:S(2)}, u32[]{:S(2)}) collective-permute-start(bf16[256,256]{1,0:T(8,128)(2,1)S(1)} %pad_maximum_fusion.rest_0_), channel_id=1, source_target_pairs={{0,24},{1,25},{2,26},{3,27},{4,28},{5,29},{6,30},{7,31}} | collective-permute-start | bytes 393224 | tf_op jit(solution)/shard_map/ppermute | solution.py:98
  19.4 1.3 %collective-permute-start.1 = (bf16[256,256]{1,0:T(8,128)(2,1)S(1)}, bf16[256,256]{1,0:T(8,128)(2,1)S(1)}, u32[]{:S(2)}, u32[]{:S(2)}) collective-permute-start(bf16[256,256]{1,0:T(8,128)(2,1)S(1)} %pad_maximum_fusion.rest_0_), channel_id=1, source_target_pairs={{0,16},{8,24},{1,17},{9,25},{2,18},{10,26},{3,19},{11,27},{4,20},{... | collective-permute-start | bytes 393224 | tf_op jit(solution)/shard_map/ppermute | solution.py:98
  20.7 2.5 %collective-permute-start = (bf16[256,256]{1,0:T(8,128)(2,1)S(1)}, bf16[256,256]{1,0:T(8,128)(2,1)S(1)}, u32[]{:S(2)}, u32[]{:S(2)}) collective-permute-start(bf16[256,256]{1,0:T(8,128)(2,1)S(1)} %pad_maximum_fusion.rest_0_), channel_id=1, source_target_pairs={{0,8},{8,16},{16,24},{1,9},{9,17},{17,25},{2,10},{10,18},{18,26},{... | collective-permute-start | bytes 393224 | tf_op jit(solution)/shard_map/ppermute | solution.py:98
  23.2 0.1 collective-permute-done.2.rest_3_
  23.2 2.8 %collective-permute-done.1.rest_2_ = bf16[256,256]{1,0:T(8,128)(2,1)S(1)} collective-permute-done((bf16[256,256]{1,0:T(8,128)(2,1)S(1)}, bf16[256,256]{1,0:T(8,128)(2,1)S(1)}, u32[]{:S(2)}, u32[]{:S(2)}) %collective-permute-start.1) | collective-permute-done | bytes 131104 | tf_op jit(solution)/shard_map/ppermute | solution.py:98
  26.1 2.3 %collective-permute-done.rest_1_ = bf16[256,256]{1,0:T(8,128)(2,1)S(1)} collective-permute-done((bf16[256,256]{1,0:T(8,128)(2,1)S(1)}, bf16[256,256]{1,0:T(8,128)(2,1)S(1)}, u32[]{:S(2)}, u32[]{:S(2)}) %collective-permute-start) | collective-permute-done | bytes 131104 | tf_op jit(solution)/shard_map/ppermute | solution.py:98
  28.3 0.0 all-to-all-done.mixed_ref
  28.3 1.3 %picked.1 = bf16[8,64,384]{2,1,0:T(8,128)(2,1)} custom-call(s32[16]{0:T(128)S(1)} %copy-done.8, bf16[8,66,384]{2,1,0:T(8,128)(2,1)S(1)} %all-to-all-done.mixed_ref), custom_call_target="tpu_custom_call" | custom-call | tf_op jit(solution)/shard_map/picked/pallas_call | solution.py:179
  29.6 0.0 collective-permute-done.4
  29.6 0.0 collective-permute-done.3
  29.7 4.3 %collective-permute-start.5 = (bf16[64,4096]{1,0:T(8,128)(2,1)}, bf16[64,4096]{1,0:T(8,128)(2,1)}, u32[]{:S(2)}, u32[]{:S(2)}) collective-permute-start(bf16[64,4096]{1,0:T(8,128)(2,1)} %collective-permute-done.3), channel_id=1, source_target_pairs={{0,8},{8,0},{16,24},{24,16},{1,9},{9,1},{17,25},{25,17},{2,10},{10... | collective-permute-start | bytes 1572872 | tf_op jit(solution)/shard_map/ppermute | solution.py:374
  33.9 3.9 %all-to-all-start.2 = ((bf16[8,64,384]{2,1,0:T(8,128)(2,1)}), bf16[8,64,384]{2,1,0:T(8,128)(2,1)S(1)}, u32[]{:S(2)}, u32[]{:S(2)}) async-start(bf16[8,64,384]{2,1,0:T(8,128)(2,1)} %picked.1), calls=%async_computation.2 | async-start | bytes 786432 | tf_op jit(solution)/shard_map/all_to_all | solution.py:314
  37.8 8.6 %collective-permute-done.5 = bf16[64,4096]{1,0:T(8,128)(2,1)} collective-permute-done((bf16[64,4096]{1,0:T(8,128)(2,1)}, bf16[64,4096]{1,0:T(8,128)(2,1)}, u32[]{:S(2)}, u32[]{:S(2)}) %collective-permute-start.5) | collective-permute-done | bytes 524320 | tf_op jit(solution)/shard_map/ppermute | solution.py:374
  46.3 2.7 %maximum_select_fusion.refs_2_ = bf16[128,4096]{1,0:T(8,128)(2,1)} fusion(bf16[64,4096]{1,0:T(8,128)(2,1)} %collective-permute-done.5, bf16[64,4096]{1,0:T(8,128)(2,1)} %collective-permute-done.3, pred[]{:T(512)S(6)} %eq.24), kind=kLoop, calls=%fused_computation | loop fusion | flops 4718592 | bytes 2097153 | tf_op jit(solution)/shard_map/jit(_where)/select_n | solution.py:376
  49.1 0.0 all-to-all-done.2.side_ref
  49.1 1.7 %collective-permute-start.10 = (bf16[128,4096]{1,0:T(8,128)(2,1)}, bf16[128,4096]{1,0:T(8,128)(2,1)}, u32[]{:S(2)}, u32[]{:S(2)}) collective-permute-start(bf16[128,4096]{1,0:T(8,128)(2,1)} %maximum_select_fusion.refs_2_), channel_id=1, source_target_pairs={{0,2},{1,5},{2,0},{3,7},{4,6},{5,1},{6,4},{7,3},{8,10},{9,13},{10,... | collective-permute-start | bytes 3145736 | tf_op jit(solution)/shard_map/ppermute | solution.py:365
  50.7 1.7 %collective-permute-start.8 = (bf16[64,4096]{1,0:T(8,128)(2,1)}, bf16[64,4096]{1,0:T(8,128)(2,1)S(1)}, u32[]{:S(2)}, u32[]{:S(2)}) collective-permute-start(bf16[64,4096]{1,0:T(8,128)(2,1)} %collective-permute-done.4), channel_id=1, source_target_pairs={{0,8},{8,0},{16,24},{24,16},{1,9},{9,1},{17,25},{25,17},{2,10},{10... | collective-permute-start | bytes 1572872 | tf_op jit(solution)/shard_map/ppermute | solution.py:374
  52.5 0.0 collective-permute-start.6
  52.5 3.1 %attention.1 = (bf16[256,512]{1,0:T(8,128)(2,1)}, bf16[4,256,256]{2,1,0:T(8,128)(2,1)S(1)}) custom-call(s32[1]{0:T(128)} %bitcast.place_ref, s32[4,4]{1,0:T(4,128)S(1)} %copy-done.7, bf16[256,512]{1,0:T(8,128)(2,1)S(1)} %copy-done.3, bf16[256,512]{1,0:T(8,128)(2,1)S(1)} %copy-done.4, bf16[256,512]{1,0:T(8,128)(2,1)S(1)} %copy-done.5, ...), custom_call_target="tpu_custom_call" | custom-call | tf_op jit(solution)/shard_map/attention/pallas_call | solution.py:108
  55.6 0.5 collective-permute-start.7
  56.1 7.9 %collective-permute-done.8 = bf16[64,4096]{1,0:T(8,128)(2,1)S(1)} collective-permute-done((bf16[64,4096]{1,0:T(8,128)(2,1)}, bf16[64,4096]{1,0:T(8,128)(2,1)S(1)}, u32[]{:S(2)}, u32[]{:S(2)}) %collective-permute-start.8) | collective-permute-done | bytes 524320 | tf_op jit(solution)/shard_map/ppermute | solution.py:374
  64.0 2.5 %maximum_select_fusion.1.refs_4_ = bf16[128,4096]{1,0:T(8,128)(2,1)} fusion(bf16[64,4096]{1,0:T(8,128)(2,1)S(1)} %collective-permute-done.8, bf16[64,4096]{1,0:T(8,128)(2,1)} %collective-permute-done.4, pred[]{:T(512)S(6)} %eq.24), kind=kLoop, calls=%fused_computation.1 | loop fusion | flops 4718592 | bytes 2097153 | tf_op jit(solution)/shard_map/jit(_where)/select_n | solution.py:376
  66.5 0.0 collective-permute-start.9
  66.5 0.0 copy-start.1
  66.5 1.0 %copy-done.1 = bf16[8,64,384]{2,1,0:T(8,128)(2,1)S(1)} copy-done((bf16[8,64,384]{2,1,0:T(8,128)(2,1)S(1)}, bf16[8,64,384]{2,1,0:T(8,128)(2,1)}, u32[]{:S(2)}) %copy-start.1) | copy-done | bytes 393240
  67.5 2.9 %weighted.1.weight_ref = bf16[768,1024]{1,0:T(8,128)(2,1)S(1)} custom-call(s32[1]{0:T(128)} %bitcast.6.own_ref, s32[16]{0:T(128)S(1)} %copy-done.8, bf16[8,66,384]{2,1,0:T(8,128)(2,1)S(1)} %all-to-all-done.mixed_ref, bf16[1,3,8,65,384]{4,3,2,1,0:T(8,128)(2,1)S(1)} %copy.20.hidden_ref, bf16[8,64,384]{2,1,0:T(8,128)(2,1)S(1)} %copy-done.1), custom_call_target="tpu_custom_call" | custom-call | tf_op jit(solution)/shard_map/weighted/pallas_call | solution.py:231
  70.4 0.0 collective-permute-done.10.refs_6_
  70.4 0.6 collective-permute-start.11
  70.9 4.7 %all-to-all-start.1 = ((bf16[32,32,256]{2,1,0:T(8,128)(2,1)}), bf16[32,32,256]{2,1,0:T(8,128)(2,1)S(1)}, u32[]{:S(2)}, u32[]{:S(2)}) async-start(bf16[32,32,256]{2,1,0:T(8,128)(2,1)} %bitcast.10), calls=%async_computation.1 | async-start | bytes 1048576 | tf_op jit(solution)/shard_map/all_to_all | solution.py:146
  75.6 0.0 collective-permute-done.6.refs_1_
  75.6 0.0 collective-permute-done.9.refs_5_
  75.7 0.0 collective-permute-done.11.refs_7_
  75.7 10.7 %tiles.1 = f32[2,384,4096]{2,1,0:T(8,128)} custom-call(bf16[768,1024]{1,0:T(8,128)(2,1)S(1)} %weighted.1.weight_ref, bf16[128,4096]{1,0:T(8,128)(2,1)} %refs_0_.1, bf16[128,4096]{1,0:T(8,128)(2,1)} %collective-permute-done.6.refs_1_, bf16[128,4096]{1,0:T(8,128)(2,1)} %maximum_select_fusion.refs_2_, bf16[128,4096]{1,0:T(8,128)(2,1)} %collective-permute-done.7.refs_3_, ...), custom_call_target="tpu_custom_call" | custom-call | tf_op jit(solution)/shard_map/tiles/pallas_call | solution.py:297
  86.4 4.8 %all-to-all-done.1 = bf16[32,32,256]{2,1,0:T(8,128)(2,1)S(1)} async-done(((bf16[32,32,256]{2,1,0:T(8,128)(2,1)}), bf16[32,32,256]{2,1,0:T(8,128)(2,1)S(1)}, u32[]{:S(2)}, u32[]{:S(2)}) %all-to-all-start.1) | async-done | bytes 524320 | tf_op jit(solution)/shard_map/all_to_all | solution.py:146
  91.2 0.7 sums.1
  (21 shorter events, 0.1 us)
Async XLA Ops:
  0.6 8.6 %copy-start.11 = (s32[128,8]{0,1:T(8,128)S(1)}, s32[128,8]{0,1:T(8,128)}, u32[]{:S(2)}) copy-start(s32[128,8]{0,1:T(8,128)} %param.19) | copy-start | bytes 12292
  2.5 27.1 %collective-permute-start.4 = (bf16[64,4096]{1,0:T(8,128)(2,1)}, bf16[64,4096]{1,0:T(8,128)(2,1)}, u32[]{:S(2)}, u32[]{:S(2)}) collective-permute-start(bf16[64,4096]{1,0:T(8,128)(2,1)} %constant_dynamic-slice_fusion), channel_id=1, source_target_pairs={{0,2},{1,5},{2,0},{3,7},{4,6},{5,1},{6,4},{7,3},{8,10},{9,13},{10,... | collective-permute-start | bytes 1572872 | tf_op jit(solution)/shard_map/ppermute | solution.py:365
  5.5 24.2 %collective-permute-start.3 = (bf16[64,4096]{1,0:T(8,128)(2,1)}, bf16[64,4096]{1,0:T(8,128)(2,1)}, u32[]{:S(2)}, u32[]{:S(2)}) collective-permute-start(bf16[64,4096]{1,0:T(8,128)(2,1)} %constant_dynamic-slice_fusion), channel_id=1, source_target_pairs={{0,4},{1,3},{2,6},{3,1},{4,0},{5,7},{6,2},{7,5},{8,12},{9,11},{10,... | collective-permute-start | bytes 1572872 | tf_op jit(solution)/shard_map/ppermute | solution.py:365
  7.7 5.9 %copy-start.9 = (bf16[256,256]{1,0:T(8,128)(2,1)S(1)}, bf16[256,256]{1,0:T(8,128)(2,1)}, u32[]{:S(2)}) copy-start(bf16[256,256]{1,0:T(8,128)(2,1)} %param.14) | copy-start | bytes 393220
  7.7 5.9 %copy-start.10 = (bf16[256,256]{1,0:T(8,128)(2,1)S(1)}, bf16[256,256]{1,0:T(8,128)(2,1)}, u32[]{:S(2)}) copy-start(bf16[256,256]{1,0:T(8,128)(2,1)} %param.13) | copy-start | bytes 393220
  9.2 19.1 %copy-start.8 = (s32[16]{0:T(128)S(1)}, s32[16]{0:T(128)}, u32[]{:S(2)}) copy-start(s32[16]{0:T(128)} %shadow_ref.3) | copy-start | bytes 196
  10.1 18.2 %all-to-all-start = ((bf16[8,66,384]{2,1,0:T(8,128)(2,1)}), bf16[8,66,384]{2,1,0:T(8,128)(2,1)S(1)}, u32[]{:S(2)}, u32[]{:S(2)}) async-start(bf16[8,66,384]{2,1,0:T(8,128)(2,1)} %fusion.1), calls=%async_computation | async-start | bytes 884736 | tf_op jit(solution)/shard_map/all_to_all | solution.py:314
  13.6 38.9 %copy-start.3 = (bf16[256,512]{1,0:T(8,128)(2,1)S(1)}, bf16[256,512]{1,0:T(8,128)(2,1)}, u32[]{:S(2)}) copy-start(bf16[256,512]{1,0:T(8,128)(2,1)} %query_ref.1) | copy-start | bytes 786436
  13.6 38.9 %copy-start.4 = (bf16[256,512]{1,0:T(8,128)(2,1)S(1)}, bf16[256,512]{1,0:T(8,128)(2,1)}, u32[]{:S(2)}) copy-start(bf16[256,512]{1,0:T(8,128)(2,1)} %grad_ref.1) | copy-start | bytes 786436
  13.6 38.9 %copy-start.5 = (bf16[256,512]{1,0:T(8,128)(2,1)S(1)}, bf16[256,512]{1,0:T(8,128)(2,1)}, u32[]{:S(2)}) copy-start(bf16[256,512]{1,0:T(8,128)(2,1)} %out_ref.1) | copy-start | bytes 786436
  13.6 38.9 %copy-start.6 = (f32[4,256]{1,0:T(4,128)S(1)}, f32[4,256]{1,0:T(4,128)}, u32[]{:S(2)}) copy-start(f32[4,256]{1,0:T(4,128)} %lse_ref.1) | copy-start | bytes 12292
  13.7 38.9 %copy-start.7 = (s32[4,4]{1,0:T(4,128)S(1)}, s32[4,4]{1,0:T(4,128)}, u32[]{:S(2)}) copy-start(s32[4,4]{1,0:T(4,128)} %mask_ref.1) | copy-start | bytes 196
  13.7 9.5 %collective-permute-start.2 = (bf16[256,256]{1,0:T(8,128)(2,1)S(1)}, bf16[256,256]{1,0:T(8,128)(2,1)S(1)}, u32[]{:S(2)}, u32[]{:S(2)}) collective-permute-start(bf16[256,256]{1,0:T(8,128)(2,1)S(1)} %pad_maximum_fusion.rest_0_), channel_id=1, source_target_pairs={{0,24},{1,25},{2,26},{3,27},{4,28},{5,29},{6,30},{7,31}} | collective-permute-start | bytes 393224 | tf_op jit(solution)/shard_map/ppermute | solution.py:98
  19.4 6.7 %collective-permute-start.1 = (bf16[256,256]{1,0:T(8,128)(2,1)S(1)}, bf16[256,256]{1,0:T(8,128)(2,1)S(1)}, u32[]{:S(2)}, u32[]{:S(2)}) collective-permute-start(bf16[256,256]{1,0:T(8,128)(2,1)S(1)} %pad_maximum_fusion.rest_0_), channel_id=1, source_target_pairs={{0,16},{8,24},{1,17},{9,25},{2,18},{10,26},{3,19},{11,27},{4,20},{... | collective-permute-start | bytes 393224 | tf_op jit(solution)/shard_map/ppermute | solution.py:98
  20.7 7.6 %collective-permute-start = (bf16[256,256]{1,0:T(8,128)(2,1)S(1)}, bf16[256,256]{1,0:T(8,128)(2,1)S(1)}, u32[]{:S(2)}, u32[]{:S(2)}) collective-permute-start(bf16[256,256]{1,0:T(8,128)(2,1)S(1)} %pad_maximum_fusion.rest_0_), channel_id=1, source_target_pairs={{0,8},{8,16},{16,24},{1,9},{9,17},{17,25},{2,10},{10,18},{18,26},{... | collective-permute-start | bytes 393224 | tf_op jit(solution)/shard_map/ppermute | solution.py:98
  29.7 16.7 %collective-permute-start.5 = (bf16[64,4096]{1,0:T(8,128)(2,1)}, bf16[64,4096]{1,0:T(8,128)(2,1)}, u32[]{:S(2)}, u32[]{:S(2)}) collective-permute-start(bf16[64,4096]{1,0:T(8,128)(2,1)} %collective-permute-done.3), channel_id=1, source_target_pairs={{0,8},{8,0},{16,24},{24,16},{1,9},{9,1},{17,25},{25,17},{2,10},{10... | collective-permute-start | bytes 1572872 | tf_op jit(solution)/shard_map/ppermute | solution.py:374
  33.9 15.2 %all-to-all-start.2 = ((bf16[8,64,384]{2,1,0:T(8,128)(2,1)}), bf16[8,64,384]{2,1,0:T(8,128)(2,1)S(1)}, u32[]{:S(2)}, u32[]{:S(2)}) async-start(bf16[8,64,384]{2,1,0:T(8,128)(2,1)} %picked.1), calls=%async_computation.2 | async-start | bytes 786432 | tf_op jit(solution)/shard_map/all_to_all | solution.py:314
  49.1 17.4 %copy-start = (bf16[8,64,384]{2,1,0:T(8,128)(2,1)}, bf16[8,64,384]{2,1,0:T(8,128)(2,1)S(1)}, u32[]{:S(2)}) copy-start(bf16[8,64,384]{2,1,0:T(8,128)(2,1)S(1)} %all-to-all-done.2.side_ref) | copy-start | bytes 1179652
  49.1 21.3 %collective-permute-start.10 = (bf16[128,4096]{1,0:T(8,128)(2,1)}, bf16[128,4096]{1,0:T(8,128)(2,1)}, u32[]{:S(2)}, u32[]{:S(2)}) collective-permute-start(bf16[128,4096]{1,0:T(8,128)(2,1)} %maximum_select_fusion.refs_2_), channel_id=1, source_target_pairs={{0,2},{1,5},{2,0},{3,7},{4,6},{5,1},{6,4},{7,3},{8,10},{9,13},{10,... | collective-permute-start | bytes 3145736 | tf_op jit(solution)/shard_map/ppermute | solution.py:365
  50.7 13.3 %collective-permute-start.8 = (bf16[64,4096]{1,0:T(8,128)(2,1)}, bf16[64,4096]{1,0:T(8,128)(2,1)S(1)}, u32[]{:S(2)}, u32[]{:S(2)}) collective-permute-start(bf16[64,4096]{1,0:T(8,128)(2,1)} %collective-permute-done.4), channel_id=1, source_target_pairs={{0,8},{8,0},{16,24},{24,16},{1,9},{9,1},{17,25},{25,17},{2,10},{10... | collective-permute-start | bytes 1572872 | tf_op jit(solution)/shard_map/ppermute | solution.py:374
  52.5 23.1 %collective-permute-start.6 = (bf16[128,4096]{1,0:T(8,128)(2,1)}, bf16[128,4096]{1,0:T(8,128)(2,1)}, u32[]{:S(2)}, u32[]{:S(2)}) collective-permute-start(bf16[128,4096]{1,0:T(8,128)(2,1)} %refs_0_.1), channel_id=1, source_target_pairs={{0,1},{1,0},{2,3},{3,2},{4,5},{5,4},{6,7},{7,6},{8,9},{9,8},{10,11... | collective-permute-start | bytes 3145736 | tf_op jit(solution)/shard_map/ppermute | solution.py:365
  55.6 10.9 %copy-start.2 = (bf16[4,256,256]{2,1,0:T(8,128)(2,1)}, bf16[4,256,256]{2,1,0:T(8,128)(2,1)S(1)}, u32[]{:S(2)}) copy-start(bf16[4,256,256]{2,1,0:T(8,128)(2,1)S(1)} %get-tuple-element.36) | copy-start | bytes 1572868
  55.6 20.0 %collective-permute-start.7 = (bf16[128,4096]{1,0:T(8,128)(2,1)}, bf16[128,4096]{1,0:T(8,128)(2,1)}, u32[]{:S(2)}, u32[]{:S(2)}) collective-permute-start(bf16[128,4096]{1,0:T(8,128)(2,1)} %maximum_select_fusion.refs_2_), channel_id=1, source_target_pairs={{0,1},{1,0},{2,3},{3,2},{4,5},{5,4},{6,7},{7,6},{8,9},{9,8},{10,11... | collective-permute-start | bytes 3145736 | tf_op jit(solution)/shard_map/ppermute | solution.py:365
  66.5 9.1 %collective-permute-start.9 = (bf16[128,4096]{1,0:T(8,128)(2,1)}, bf16[128,4096]{1,0:T(8,128)(2,1)}, u32[]{:S(2)}, u32[]{:S(2)}) collective-permute-start(bf16[128,4096]{1,0:T(8,128)(2,1)} %maximum_select_fusion.1.refs_4_), channel_id=1, source_target_pairs={{0,1},{1,0},{2,3},{3,2},{4,5},{5,4},{6,7},{7,6},{8,9},{9,8},{10,11... | collective-permute-start | bytes 3145736 | tf_op jit(solution)/shard_map/ppermute | solution.py:365
  66.5 1.0 %copy-start.1 = (bf16[8,64,384]{2,1,0:T(8,128)(2,1)S(1)}, bf16[8,64,384]{2,1,0:T(8,128)(2,1)}, u32[]{:S(2)}) copy-start(bf16[8,64,384]{2,1,0:T(8,128)(2,1)} %copy-done) | copy-start | bytes 1179652
  70.4 5.3 %collective-permute-start.11 = (bf16[128,4096]{1,0:T(8,128)(2,1)}, bf16[128,4096]{1,0:T(8,128)(2,1)}, u32[]{:S(2)}, u32[]{:S(2)}) collective-permute-start(bf16[128,4096]{1,0:T(8,128)(2,1)} %collective-permute-done.10.refs_6_), channel_id=1, source_target_pairs={{0,1},{1,0},{2,3},{3,2},{4,5},{5,4},{6,7},{7,6},{8,9},{9,8},{10,11... | collective-permute-start | bytes 3145736 | tf_op jit(solution)/shard_map/ppermute | solution.py:365
  70.9 20.2 %all-to-all-start.1 = ((bf16[32,32,256]{2,1,0:T(8,128)(2,1)}), bf16[32,32,256]{2,1,0:T(8,128)(2,1)S(1)}, u32[]{:S(2)}, u32[]{:S(2)}) async-start(bf16[32,32,256]{2,1,0:T(8,128)(2,1)} %bitcast.10), calls=%async_computation.1 | async-start | bytes 1048576 | tf_op jit(solution)/shard_map/all_to_all | solution.py:146

commit v13 on v4

--- a/solution.py
+++ b/solution.py
@@ -246,11 +246,19 @@
     )(own_index.astype(jnp.int32)[None], shadow_list, mixed, hidden, shadow_rows)
 
 
-def tile_kernel(weight_ref, *refs):
-    *block_refs, tile_ref, gathered_ref, held_ref, in_sems, out_sems = refs
+def tile_kernel(halves, parity_ref, weight_ref, *refs):
+    *part_refs, tile_ref, gathered_ref, held_ref, in_sems, out_sems = refs
     per_dev, units, model = tile_ref.shape
-    tokens = block_refs[0].shape[0]
     steps = in_sems.shape[0]
+    tokens = gathered_ref.shape[0] // len(halves)
+    parity = parity_ref[0]
+    places = []
+    for n, count in enumerate(halves):
+        if count == 1:
+            places.append(n * tokens)
+        else:
+            places.append(pl.multiple_of(n * tokens + parity * (tokens // 2), 16))
+            places.append(pl.multiple_of(n * tokens + (1 - parity) * (tokens // 2), 16))
     step = model // steps
     arriving, leaving = [], []
     for i in range(steps):
@@ -259,10 +267,10 @@
             [
                 pltpu.make_async_copy(
                     ref.at[:, columns],
-                    gathered_ref.at[pl.ds(n * tokens, tokens), columns],
+                    gathered_ref.at[pl.ds(place, ref.shape[0]), columns],
                     in_sems.at[i, n],
                 )
-                for n, ref in enumerate(block_refs)
+                for n, (place, ref) in enumerate(zip(places, part_refs))
             ]
         )
     for copy in arriving[0] + arriving[1]:
@@ -290,24 +298,28 @@
 
 
 def tile_sums(weighted, blocks, per_dev):
-    tokens, model = blocks[0].shape
+    tokens, model = blocks[0][0].shape
     rows = weighted.shape[0]
     steps = model // 1024
+    halves = [len(block) for block in blocks]
+    parts = [part for block in blocks for part in block]
+    parity = (lax.axis_index("ctx") % 2).astype(jnp.int32)[None]
     anywhere = pl.BlockSpec(memory_space=pl.ANY)
     return pl.pallas_call(
-        tile_kernel,
+        functools.partial(tile_kernel, halves),
         out_shape=jax.ShapeDtypeStruct((per_dev, rows // per_dev, model), jnp.float32),
-        in_specs=[pl.BlockSpec(memory_space=pltpu.VMEM)] + [anywhere] * len(blocks),
+        in_specs=[pl.BlockSpec(memory_space=pltpu.SMEM), pl.BlockSpec(memory_space=pltpu.VMEM)]
+        + [anywhere] * len(parts),
         out_specs=anywhere,
         scratch_shapes=[
             pltpu.VMEM((len(blocks) * tokens, model), jnp.bfloat16),
             pltpu.VMEM((rows, model), jnp.float32),
-            pltpu.SemaphoreType.DMA((steps, len(blocks))),
+            pltpu.SemaphoreType.DMA((steps, len(parts))),
             pltpu.SemaphoreType.DMA((steps, per_dev)),
         ],
         compiler_params=pltpu.CompilerParams(vmem_limit_bytes=32 * 2**20),
         name="tiles",
-    )(weighted, *blocks)
+    )(parity, weighted, *parts)
 
 
 def swapped(value):
@@ -332,7 +344,8 @@
         stored_hidden_state[0, per_dev, :, :used],
         ((0, 0), (0, limit - used), (0, lanes - units)),
     )
-    return jnp.concatenate([rows, jnp.pad(table, ((0, 0), (0, 0), (0, lanes - tokens)))], axis=1)
+    mixed = jnp.concatenate([rows, jnp.pad(table, ((0, 0), (0, 0), (0, lanes - tokens)))], axis=1)
+    return mixed
 
 
 def expert_rows(mixed, shadow_rows, shadow_list, stored_hidden_state, tokens):
@@ -364,20 +377,25 @@
     return lax.ppermute(value, "exp", [(e, e ^ steps[e % 2]) for e in range(owners)])
 
 
-def after(value, *others):
-    return lax.optimization_barrier((value, others))[0]
+def paired_half(block):
+    rows = block.shape[0] // 2
+    return lax.dynamic_slice_in_dim(block, lax.axis_index("ctx") % 2 * rows, rows, 0)
+
+
+def from_pair(half):
+    return lax.ppermute(half, "ctx", [(c, c ^ 1) for c in range(lax.axis_size("ctx"))])
 
 
 def beside(block):
-    return moved(block, (1, 1))
+    return [moved(part, (1, 1)) for part in block]
 
 
 def all_blocks(held):
     steps = block_steps(lax.axis_size("exp"))[0]
     for turn in range(len(steps).bit_length() - 3):
         mask = steps[4 << turn]
-        more = [moved(part, (mask, mask)) for part, _ in held]
-        held = held + [(part, beside(part)) for part in more]
+        more = [[moved(part, (mask, mask)) for part in block] for block, _ in held]
+        held = held + [(block, beside(block)) for block in more]
     return [block for pair in held for block in pair]
 
 
@@ -396,30 +414,28 @@
     stored_hidden_state,
 ):
     steps = block_steps(lax.axis_size("exp"))
-    tokens = expert_ids.shape[0]
     first = moved(moe_grad, [held[1] for held in steps])
+    second = moved(paired_half(moe_grad), [held[2] for held in steps])
     arrived = key_blocks(keys, values, queries.shape[1] // lse_excess.shape[0])
     payload = source_rows(expert_ids, route_probs, shadow_list, stored_hidden_state)
-    own_beside = beside(after(moe_grad, payload))
-    mixed = swapped(payload)
-    second = moved(after(moe_grad, own_beside), [held[2] for held in steps])
+    mixed, arrived = lax.optimization_barrier((swapped(payload), arrived))
     per_dev = shadow_list.shape[0] // lax.axis_size("exp")
-    sent = after(picked_rows(shadow_list, mixed, payload.shape[1] - per_dev), arrived)
-    first_beside = beside(after(first, sent))
+    sent = picked_rows(shadow_list, mixed, payload.shape[1] - per_dev)
+    sent, second = lax.optimization_barrier((sent, second))
+    second = [second, from_pair(second)]
     shadow_rows = swapped(sent)
-    far = moved(after(first, first_beside), [held[2] for held in steps])
+    arrived, _ = lax.optimization_barrier((arrived, sent))
     query_grad, terms = attention(
-        queries, after(arrived, first_beside), attn_out, attn_out_grad, lse_excess, block_mask
-    )
+        queries, arrived, attn_out, attn_out_grad, lse_excess, block_mask
+    )
+    first, shadow_rows = lax.optimization_barrier((first, shadow_rows))
+    far = moved(first, [held[2] for held in steps])
     weighted = expert_rows(
-        mixed, after(shadow_rows, query_grad), shadow_list, stored_hidden_state, tokens
-    )
-    second_beside = beside(after(second, weighted))
-    far = after(far, second_beside)
-    blocks = all_blocks(
-        [(moe_grad, own_beside), (first, first_beside), (second, second_beside), (far, beside(far))]
-    )
-    tiles = tile_sums(weighted, blocks, per_dev)
+        mixed, shadow_rows, shadow_list, stored_hidden_state, expert_ids.shape[0]
+    )
+    near = [(block, beside(block)) for block in ([moe_grad], [first], second)]
+    far, _ = lax.optimization_barrier((far, (weighted, query_grad)))
+    tiles = tile_sums(weighted, all_blocks(near + [([far], beside([far]))]), per_dev)
     key_grad, value_grad, expert_grad = summed_terms(terms, keys.shape[1], tiles)
     return (query_grad, key_grad, value_grad, expert_grad)
 

time: 88.6 us -> 78.7 us (0.89)
  blocking collectives: 0 us -> 12 us
  waiting for transfers between devices: 24.5 us -> 12.5 us
  local copies, waits for them, and re-layouts: 10.3 us -> 4.26 us
  Pallas kernels: 19.6 us -> 18.1 us
  starting transfers between devices: 31.1 us -> 29.7 us
    all_to_all x0 -> x1, blocking collectives: none -> 12 us  [swapped(): return lax.all_to_all(value, 'exp', split_axis=0, concat_axis=0, tiled=True)]
    all_to_all x2 -> x1, waiting for transfers between devices: 9.28 us -> 0.01 us  [swapped(): return lax.all_to_all(value, 'exp', split_axis=0, concat_axis=0, tiled=True)]
    unnamed x31 -> x23, local copies, waits for them, and re-layouts: 9.42 us -> 2.3 us
    ppermute x7 -> x8, waiting for transfers between devices: 10.2 us -> 5.66 us  [moved(): lax.ppermute(value, 'exp', [(e, e ^ steps[e % 2]) for e in range(owners)])]
    ppermute x0 -> x1, starting transfers between devices: none -> 4.24 us  [from_pair(): lax.ppermute(half, 'ctx', [(c, c ^ 1) for c in range(lax.axis_size('ctx'))])]
    all_to_all x2 -> x1, starting transfers between devices: 7.06 us -> 3.61 us  [swapped(): return lax.all_to_all(value, 'exp', split_axis=0, concat_axis=0, tiled=True)]
    ppermute x3, waiting for transfers between devices: 2.53 us -> 5.14 us  [key_blocks(): lax.ppermute(pair, 'ctx', [(c, c + step) for c in range(cycle - step)])]
    dynamic_slice x0 -> x1, local copies, waits for them, and re-layouts: none -> 1.9 us  [paired_half(): lax.dynamic_slice_in_dim(block, lax.axis_index('ctx') % 2 * rows, rows, 0)]
  transfers between devices with their start and end apart: 13 -> 14, of which waited for: 5 -> 7; matrix products, arithmetic and copies ran while one was open for 4% -> 5% of each run, Pallas kernels for 22% -> 22%
where the time goes in v13:
time: 78.7 us; the launch traced here: 78.3 us
  starting transfers between devices  29.7 us (38%)
  Pallas kernels  18.1 us (23%)
  waiting for transfers between devices  12.5 us (16%)
  blocking collectives  12 us (15%)
  local copies, waits for them, and re-layouts  4.26 us (5%)
  other arithmetic  0.87 us (1%)
  between operations  0.85 us (1%)
    all_to_all x1, blocking collectives, swapped(): return lax.all_to_all(value, 'exp', split_axis=0, concat_axis=0, tiled=True)  12 us
    pallas_call x1, Pallas kernels, tile_sums(): pl.pallas_call(functools.partial(tile_kernel, halves), out_shape=jax.Shap...  10.9 us
    ppermute x3, starting transfers between devices, key_blocks(): lax.ppermute(pair, 'ctx', [(c, c + step) for c in range(cycle - step)])  9.29 us
    all_to_all x1, starting transfers between devices, summed_terms(): lax.all_to_all(terms.reshape(cycle * owners, rows // owners, columns), ('...  6.62 us
    ppermute x8, starting transfers between devices, moved(): lax.ppermute(value, 'exp', [(e, e ^ steps[e % 2]) for e in range(owners)])  5.9 us
    ppermute x8, waiting for transfers between devices, moved(): lax.ppermute(value, 'exp', [(e, e ^ steps[e % 2]) for e in range(owners)])  5.66 us
    ppermute x3, waiting for transfers between devices, key_blocks(): lax.ppermute(pair, 'ctx', [(c, c + step) for c in range(cycle - step)])  5.14 us
    ppermute x1, starting transfers between devices, from_pair(): lax.ppermute(half, 'ctx', [(c, c ^ 1) for c in range(lax.axis_size('ctx'))])  4.24 us
  transfers between devices with their start and end apart: 14, of which 7 were waited for; matrix products, arithmetic and copies ran while one was open for 5% of the time, Pallas kernels for 22%

profile of v13, /device:TPU:0, one launch (start us, length us, event | category | flops | bytes accessed | tf_op | source)
XLA Modules:
  0.0 78.3 jit_solution(17700610408390909022)
XLA Ops:
  0.6 3.0 %collective-permute-start.4 = (bf16[128,4096]{1,0:T(8,128)(2,1)}, bf16[128,4096]{1,0:T(8,128)(2,1)}, u32[]{:S(2)}, u32[]{:S(2)}) collective-permute-start(bf16[128,4096]{1,0:T(8,128)(2,1)} %refs_0_.1), channel_id=1, source_target_pairs={{0,4},{1,3},{2,6},{3,1},{4,0},{5,7},{6,2},{7,5},{8,12},{9,11},{10,... | collective-permute-start | bytes 3145736 | tf_op jit(solution)/shard_map/ppermute | solution.py:377
  3.7 1.9 %constant_dynamic-slice_fusion = bf16[64,4096]{1,0:T(8,128)(2,1)} fusion(bf16[128,4096]{1,0:T(8,128)(2,1)} %refs_0_.1, s32[]{:T(128)S(6)} %select_n.28), kind=kLoop, calls=%fused_computation.7 | loop fusion | bytes 1048580 | tf_op jit(solution)/shard_map/dynamic_slice | solution.py:382
  5.6 1.5 %collective-permute-start.3 = (bf16[64,4096]{1,0:T(8,128)(2,1)}, bf16[64,4096]{1,0:T(8,128)(2,1)}, u32[]{:S(2)}, u32[]{:S(2)}) collective-permute-start(bf16[64,4096]{1,0:T(8,128)(2,1)} %constant_dynamic-slice_fusion), channel_id=1, source_target_pairs={{0,2},{1,5},{2,0},{3,7},{4,6},{5,1},{6,4},{7,3},{8,10},{9,13},{10,... | collective-permute-start | bytes 1572872 | tf_op jit(solution)/shard_map/ppermute | solution.py:377
  7.1 1.5 %copy.20.hidden_ref = bf16[1,3,8,65,384]{4,3,2,1,0:T(8,128)(2,1)S(1)} copy(bf16[1,3,8,65,384]{4,2,3,1,0:T(8,128)(2,1)} %param.23) | data formatting | bytes 2396160 | tf_op args[11]
  8.5 0.0 copy-start.7
  8.5 0.0 copy-start.8
  8.6 0.0 copy-done.10
  8.6 0.0 copy-start.6
  8.6 0.0 copy-done.9
  8.7 0.8 %fusion.1 = bf16[8,66,384]{2,1,0:T(8,128)(2,1)} fusion(bf16[8,2,128]{2,1,0:T(2,128)(2,1)S(1)} %bitcast.12, bf16[8,64,384]{2,1,0:T(8,128)(2,1)S(1)} %slice_bitcast_fusion), kind=kLoop, calls=%fused_computation.2 | loop fusion | flops 1216512 | bytes 802816 | tf_op jit(solution)/shard_map/concatenate | solution.py:347
  9.5 0.0 copy-start.5
  9.5 3.6 %all-to-all-start = ((bf16[8,66,384]{2,1,0:T(8,128)(2,1)}), bf16[8,66,384]{2,1,0:T(8,128)(2,1)S(1)}, u32[]{:S(2)}, u32[]{:S(2)}) async-start(bf16[8,66,384]{2,1,0:T(8,128)(2,1)} %fusion.1), calls=%async_computation | async-start | bytes 884736 | tf_op jit(solution)/shard_map/all_to_all | solution.py:326
  13.1 0.0 copy-done.7
  13.1 0.0 copy-done.8
  13.2 5.5 %collective-permute-start.2 = (bf16[256,256]{1,0:T(8,128)(2,1)S(1)}, bf16[256,256]{1,0:T(8,128)(2,1)S(1)}, u32[]{:S(2)}, u32[]{:S(2)}) collective-permute-start(bf16[256,256]{1,0:T(8,128)(2,1)S(1)} %pad_maximum_fusion.rest_0_), channel_id=1, source_target_pairs={{0,24},{1,25},{2,26},{3,27},{4,28},{5,29},{6,30},{7,31}} | collective-permute-start | bytes 393224 | tf_op jit(solution)/shard_map/ppermute | solution.py:98
  18.7 1.3 %collective-permute-start.1 = (bf16[256,256]{1,0:T(8,128)(2,1)S(1)}, bf16[256,256]{1,0:T(8,128)(2,1)S(1)}, u32[]{:S(2)}, u32[]{:S(2)}) collective-permute-start(bf16[256,256]{1,0:T(8,128)(2,1)S(1)} %pad_maximum_fusion.rest_0_), channel_id=1, source_target_pairs={{0,16},{8,24},{1,17},{9,25},{2,18},{10,26},{3,19},{11,27},{4,20},{... | collective-permute-start | bytes 393224 | tf_op jit(solution)/shard_map/ppermute | solution.py:98
  20.0 2.5 %collective-permute-start = (bf16[256,256]{1,0:T(8,128)(2,1)S(1)}, bf16[256,256]{1,0:T(8,128)(2,1)S(1)}, u32[]{:S(2)}, u32[]{:S(2)}) collective-permute-start(bf16[256,256]{1,0:T(8,128)(2,1)S(1)} %pad_maximum_fusion.rest_0_), channel_id=1, source_target_pairs={{0,8},{8,16},{16,24},{1,9},{9,17},{17,25},{2,10},{10,18},{18,26},{... | collective-permute-start | bytes 393224 | tf_op jit(solution)/shard_map/ppermute | solution.py:98
  22.5 0.1 collective-permute-done.2.rest_3_
  22.6 2.8 %collective-permute-done.1.rest_2_ = bf16[256,256]{1,0:T(8,128)(2,1)S(1)} collective-permute-done((bf16[256,256]{1,0:T(8,128)(2,1)S(1)}, bf16[256,256]{1,0:T(8,128)(2,1)S(1)}, u32[]{:S(2)}, u32[]{:S(2)}) %collective-permute-start.1) | collective-permute-done | bytes 131104 | tf_op jit(solution)/shard_map/ppermute | solution.py:98
  25.4 2.3 %collective-permute-done.rest_1_ = bf16[256,256]{1,0:T(8,128)(2,1)S(1)} collective-permute-done((bf16[256,256]{1,0:T(8,128)(2,1)S(1)}, bf16[256,256]{1,0:T(8,128)(2,1)S(1)}, u32[]{:S(2)}, u32[]{:S(2)}) %collective-permute-start) | collective-permute-done | bytes 131104 | tf_op jit(solution)/shard_map/ppermute | solution.py:98
  27.7 0.0 all-to-all-done.mixed_ref
  27.7 0.0 copy-done.6
  27.7 0.6 picked.1
  28.3 0.0 collective-permute-done.3.refs_4_
  28.3 12.0 %all_to_all.15.side_ref = bf16[8,64,384]{2,1,0:T(8,128)(2,1)S(1)} all-to-all(bf16[8,64,384]{2,1,0:T(8,128)(2,1)S(1)} %picked.1), channel_id=1, replica_groups=mesh['ctx'=4,'exp'=8] {'exp'}, dimensions={0} | all-to-all | bytes 786432 | tf_op jit(solution)/shard_map/all_to_all | solution.py:326
  40.3 0.0 collective-permute-done.4.refs_2_
  40.3 0.6 collective-permute-start.10
  40.8 0.0 collective-permute-start.5
  40.8 4.2 %collective-permute-start.7 = (bf16[64,4096]{1,0:T(8,128)(2,1)}, bf16[64,4096]{1,0:T(8,128)(2,1)}, u32[]{:S(2)}, u32[]{:S(2)}) collective-permute-start(bf16[64,4096]{1,0:T(8,128)(2,1)} %collective-permute-done.3.refs_4_), channel_id=1, source_target_pairs={{0,8},{8,0},{16,24},{24,16},{1,9},{9,1},{17,25},{25,17},{2,10},{10... | collective-permute-start | bytes 1572872 | tf_op jit(solution)/shard_map/ppermute | solution.py:386
  45.1 0.0 copy-done.3
  45.1 3.1 %attention.1 = (bf16[256,512]{1,0:T(8,128)(2,1)}, bf16[4,256,256]{2,1,0:T(8,128)(2,1)S(1)}) custom-call(s32[1]{0:T(128)} %bitcast.place_ref, s32[4,4]{1,0:T(4,128)S(1)} %copy-done.5, bf16[256,512]{1,0:T(8,128)(2,1)S(1)} %copy-done.1, bf16[256,512]{1,0:T(8,128)(2,1)S(1)} %copy-done.2, bf16[256,512]{1,0:T(8,128)(2,1)S(1)} %copy-done.3, ...), custom_call_target="tpu_custom_call" | custom-call | tf_op jit(solution)/shard_map/attention/pallas_call | solution.py:108
  48.2 0.8 %copy-done = bf16[4,256,256]{2,1,0:T(8,128)(2,1)} copy-done((bf16[4,256,256]{2,1,0:T(8,128)(2,1)}, bf16[4,256,256]{2,1,0:T(8,128)(2,1)S(1)}, u32[]{:S(2)}) %copy-start) | copy-done | bytes 524312
  49.0 0.2 collective-permute-start.6
  49.2 2.9 %weighted.1.weight_ref = bf16[768,1024]{1,0:T(8,128)(2,1)S(1)} custom-call(s32[1]{0:T(128)} %bitcast.7.own_ref, s32[16]{0:T(128)S(1)} %copy-done.6, bf16[8,66,384]{2,1,0:T(8,128)(2,1)S(1)} %all-to-all-done.mixed_ref, bf16[1,3,8,65,384]{4,3,2,1,0:T(8,128)(2,1)S(1)} %copy.20.hidden_ref, bf16[8,64,384]{2,1,0:T(8,128)(2,1)S(1)} %all_to_all.15.side_ref), custom_call_target="tpu_custom_call" | custom-call | tf_op jit(solution)/shard_map/weighted/pallas_call | solution.py:231
  52.1 3.3 %collective-permute-done.10.refs_8_ = bf16[128,4096]{1,0:T(8,128)(2,1)} collective-permute-done((bf16[128,4096]{1,0:T(8,128)(2,1)}, bf16[128,4096]{1,0:T(8,128)(2,1)}, u32[]{:S(2)}, u32[]{:S(2)}) %collective-permute-start.10) | collective-permute-done | bytes 1048608 | tf_op jit(solution)/shard_map/ppermute | solution.py:377
  55.4 0.0 collective-permute-start.11
  55.4 6.6 %all-to-all-start.1 = ((bf16[32,32,256]{2,1,0:T(8,128)(2,1)}), bf16[32,32,256]{2,1,0:T(8,128)(2,1)S(1)}, u32[]{:S(2)}, u32[]{:S(2)}) async-start(bf16[32,32,256]{2,1,0:T(8,128)(2,1)} %bitcast.11), calls=%async_computation.1 | async-start | bytes 1048576 | tf_op jit(solution)/shard_map/all_to_all | solution.py:146
  62.0 0.3 collective-permute-start.8
  62.3 0.0 collective-permute-done.7.refs_5_
  62.4 0.3 collective-permute-start.9
  62.6 0.0 collective-permute-done.5.refs_1_
  62.6 1.6 %collective-permute-done.8.refs_6_ = bf16[64,4096]{1,0:T(8,128)(2,1)S(1)} collective-permute-done((bf16[64,4096]{1,0:T(8,128)(2,1)}, bf16[64,4096]{1,0:T(8,128)(2,1)S(1)}, u32[]{:S(2)}, u32[]{:S(2)}) %collective-permute-start.8) | collective-permute-done | bytes 524320 | tf_op jit(solution)/shard_map/ppermute | solution.py:377
  64.2 0.7 collective-permute-done.9.refs_7_
  65.0 0.0 collective-permute-done.6.refs_3_
  65.0 0.0 collective-permute-done.11.refs_9_
  65.0 10.9 %tiles.1 = f32[2,384,4096]{2,1,0:T(8,128)} custom-call(s32[1]{0:T(128)} %bitcast.6.parity_ref, bf16[768,1024]{1,0:T(8,128)(2,1)S(1)} %weighted.1.weight_ref, bf16[128,4096]{1,0:T(8,128)(2,1)} %refs_0_.1, bf16[128,4096]{1,0:T(8,128)(2,1)} %collective-permute-done.5.refs_1_, bf16[128,4096]{1,0:T(8,128)(2,1)} %collective-permute-done.4.refs_2_, ...), custom_call_target="tpu_custom_call" | custom-call | tf_op jit(solution)/shard_map/tiles/pallas_call | solution.py:308
  75.9 1.7 %all-to-all-done.1 = bf16[32,32,256]{2,1,0:T(8,128)(2,1)S(1)} async-done(((bf16[32,32,256]{2,1,0:T(8,128)(2,1)}), bf16[32,32,256]{2,1,0:T(8,128)(2,1)S(1)}, u32[]{:S(2)}, u32[]{:S(2)}) %all-to-all-start.1) | async-done | bytes 524320 | tf_op jit(solution)/shard_map/all_to_all | solution.py:146
  77.6 0.7 sums.1
  (16 shorter events, 0.1 us)
Async XLA Ops:
  0.6 39.6 %collective-permute-start.4 = (bf16[128,4096]{1,0:T(8,128)(2,1)}, bf16[128,4096]{1,0:T(8,128)(2,1)}, u32[]{:S(2)}, u32[]{:S(2)}) collective-permute-start(bf16[128,4096]{1,0:T(8,128)(2,1)} %refs_0_.1), channel_id=1, source_target_pairs={{0,4},{1,3},{2,6},{3,1},{4,0},{5,7},{6,2},{7,5},{8,12},{9,11},{10,... | collective-permute-start | bytes 3145736 | tf_op jit(solution)/shard_map/ppermute | solution.py:377
  5.6 3.0 %copy-start.10 = (bf16[128,8]{0,1:T(8,128)(2,1)S(1)}, bf16[128,8]{0,1:T(8,128)(2,1)}, u32[]{:S(2)}) copy-start(bf16[128,8]{0,1:T(8,128)(2,1)} %param.20) | copy-start | bytes 6148
  5.6 3.1 %copy-start.9 = (s32[128,8]{0,1:T(8,128)S(1)}, s32[128,8]{0,1:T(8,128)}, u32[]{:S(2)}) copy-start(s32[128,8]{0,1:T(8,128)} %param.19) | copy-start | bytes 12292
  5.6 22.7 %collective-permute-start.3 = (bf16[64,4096]{1,0:T(8,128)(2,1)}, bf16[64,4096]{1,0:T(8,128)(2,1)}, u32[]{:S(2)}, u32[]{:S(2)}) collective-permute-start(bf16[64,4096]{1,0:T(8,128)(2,1)} %constant_dynamic-slice_fusion), channel_id=1, source_target_pairs={{0,2},{1,5},{2,0},{3,7},{4,6},{5,1},{6,4},{7,3},{8,10},{9,13},{10,... | collective-permute-start | bytes 1572872 | tf_op jit(solution)/shard_map/ppermute | solution.py:377
  8.5 4.6 %copy-start.7 = (bf16[256,256]{1,0:T(8,128)(2,1)S(1)}, bf16[256,256]{1,0:T(8,128)(2,1)}, u32[]{:S(2)}) copy-start(bf16[256,256]{1,0:T(8,128)(2,1)} %param.14) | copy-start | bytes 393220
  8.5 4.6 %copy-start.8 = (bf16[256,256]{1,0:T(8,128)(2,1)S(1)}, bf16[256,256]{1,0:T(8,128)(2,1)}, u32[]{:S(2)}) copy-start(bf16[256,256]{1,0:T(8,128)(2,1)} %param.13) | copy-start | bytes 393220
  8.6 19.1 %copy-start.6 = (s32[16]{0:T(128)S(1)}, s32[16]{0:T(128)}, u32[]{:S(2)}) copy-start(s32[16]{0:T(128)} %shadow_ref.3) | copy-start | bytes 196
  9.5 35.6 %copy-start.1 = (bf16[256,512]{1,0:T(8,128)(2,1)S(1)}, bf16[256,512]{1,0:T(8,128)(2,1)}, u32[]{:S(2)}) copy-start(bf16[256,512]{1,0:T(8,128)(2,1)} %query_ref.1) | copy-start | bytes 786436
  9.5 35.6 %copy-start.2 = (bf16[256,512]{1,0:T(8,128)(2,1)S(1)}, bf16[256,512]{1,0:T(8,128)(2,1)}, u32[]{:S(2)}) copy-start(bf16[256,512]{1,0:T(8,128)(2,1)} %grad_ref.1) | copy-start | bytes 786436
  9.5 35.6 %copy-start.3 = (bf16[256,512]{1,0:T(8,128)(2,1)S(1)}, bf16[256,512]{1,0:T(8,128)(2,1)}, u32[]{:S(2)}) copy-start(bf16[256,512]{1,0:T(8,128)(2,1)} %out_ref.1) | copy-start | bytes 786436
  9.5 35.6 %copy-start.4 = (f32[4,256]{1,0:T(4,128)S(1)}, f32[4,256]{1,0:T(4,128)}, u32[]{:S(2)}) copy-start(f32[4,256]{1,0:T(4,128)} %lse_ref.1) | copy-start | bytes 12292
  9.5 35.6 %copy-start.5 = (s32[4,4]{1,0:T(4,128)S(1)}, s32[4,4]{1,0:T(4,128)}, u32[]{:S(2)}) copy-start(s32[4,4]{1,0:T(4,128)} %mask_ref.1) | copy-start | bytes 196
  9.5 18.2 %all-to-all-start = ((bf16[8,66,384]{2,1,0:T(8,128)(2,1)}), bf16[8,66,384]{2,1,0:T(8,128)(2,1)S(1)}, u32[]{:S(2)}, u32[]{:S(2)}) async-start(bf16[8,66,384]{2,1,0:T(8,128)(2,1)} %fusion.1), calls=%async_computation | async-start | bytes 884736 | tf_op jit(solution)/shard_map/all_to_all | solution.py:326
  13.2 9.4 %collective-permute-start.2 = (bf16[256,256]{1,0:T(8,128)(2,1)S(1)}, bf16[256,256]{1,0:T(8,128)(2,1)S(1)}, u32[]{:S(2)}, u32[]{:S(2)}) collective-permute-start(bf16[256,256]{1,0:T(8,128)(2,1)S(1)} %pad_maximum_fusion.rest_0_), channel_id=1, source_target_pairs={{0,24},{1,25},{2,26},{3,27},{4,28},{5,29},{6,30},{7,31}} | collective-permute-start | bytes 393224 | tf_op jit(solution)/shard_map/ppermute | solution.py:98
  18.7 6.7 %collective-permute-start.1 = (bf16[256,256]{1,0:T(8,128)(2,1)S(1)}, bf16[256,256]{1,0:T(8,128)(2,1)S(1)}, u32[]{:S(2)}, u32[]{:S(2)}) collective-permute-start(bf16[256,256]{1,0:T(8,128)(2,1)S(1)} %pad_maximum_fusion.rest_0_), channel_id=1, source_target_pairs={{0,16},{8,24},{1,17},{9,25},{2,18},{10,26},{3,19},{11,27},{4,20},{... | collective-permute-start | bytes 393224 | tf_op jit(solution)/shard_map/ppermute | solution.py:98
  20.0 7.6 %collective-permute-start = (bf16[256,256]{1,0:T(8,128)(2,1)S(1)}, bf16[256,256]{1,0:T(8,128)(2,1)S(1)}, u32[]{:S(2)}, u32[]{:S(2)}) collective-permute-start(bf16[256,256]{1,0:T(8,128)(2,1)S(1)} %pad_maximum_fusion.rest_0_), channel_id=1, source_target_pairs={{0,8},{8,16},{16,24},{1,9},{9,17},{17,25},{2,10},{10,18},{18,26},{... | collective-permute-start | bytes 393224 | tf_op jit(solution)/shard_map/ppermute | solution.py:98
  40.3 15.1 %collective-permute-start.10 = (bf16[128,4096]{1,0:T(8,128)(2,1)}, bf16[128,4096]{1,0:T(8,128)(2,1)}, u32[]{:S(2)}, u32[]{:S(2)}) collective-permute-start(bf16[128,4096]{1,0:T(8,128)(2,1)} %collective-permute-done.4.refs_2_), channel_id=1, source_target_pairs={{0,2},{1,5},{2,0},{3,7},{4,6},{5,1},{6,4},{7,3},{8,10},{9,13},{10,... | collective-permute-start | bytes 3145736 | tf_op jit(solution)/shard_map/ppermute | solution.py:377
  40.8 21.8 %collective-permute-start.5 = (bf16[128,4096]{1,0:T(8,128)(2,1)}, bf16[128,4096]{1,0:T(8,128)(2,1)}, u32[]{:S(2)}, u32[]{:S(2)}) collective-permute-start(bf16[128,4096]{1,0:T(8,128)(2,1)} %refs_0_.1), channel_id=1, source_target_pairs={{0,1},{1,0},{2,3},{3,2},{4,5},{5,4},{6,7},{7,6},{8,9},{9,8},{10,11... | collective-permute-start | bytes 3145736 | tf_op jit(solution)/shard_map/ppermute | solution.py:377
  40.8 21.5 %collective-permute-start.7 = (bf16[64,4096]{1,0:T(8,128)(2,1)}, bf16[64,4096]{1,0:T(8,128)(2,1)}, u32[]{:S(2)}, u32[]{:S(2)}) collective-permute-start(bf16[64,4096]{1,0:T(8,128)(2,1)} %collective-permute-done.3.refs_4_), channel_id=1, source_target_pairs={{0,8},{8,0},{16,24},{24,16},{1,9},{9,1},{17,25},{25,17},{2,10},{10... | collective-permute-start | bytes 1572872 | tf_op jit(solution)/shard_map/ppermute | solution.py:386
  48.2 0.8 %copy-start = (bf16[4,256,256]{2,1,0:T(8,128)(2,1)}, bf16[4,256,256]{2,1,0:T(8,128)(2,1)S(1)}, u32[]{:S(2)}) copy-start(bf16[4,256,256]{2,1,0:T(8,128)(2,1)S(1)} %get-tuple-element.35) | copy-start | bytes 1572868
  49.0 16.0 %collective-permute-start.6 = (bf16[128,4096]{1,0:T(8,128)(2,1)}, bf16[128,4096]{1,0:T(8,128)(2,1)}, u32[]{:S(2)}, u32[]{:S(2)}) collective-permute-start(bf16[128,4096]{1,0:T(8,128)(2,1)} %collective-permute-done.4.refs_2_), channel_id=1, source_target_pairs={{0,1},{1,0},{2,3},{3,2},{4,5},{5,4},{6,7},{7,6},{8,9},{9,8},{10,11... | collective-permute-start | bytes 3145736 | tf_op jit(solution)/shard_map/ppermute | solution.py:377
  55.4 9.6 %collective-permute-start.11 = (bf16[128,4096]{1,0:T(8,128)(2,1)}, bf16[128,4096]{1,0:T(8,128)(2,1)}, u32[]{:S(2)}, u32[]{:S(2)}) collective-permute-start(bf16[128,4096]{1,0:T(8,128)(2,1)} %collective-permute-done.10.refs_8_), channel_id=1, source_target_pairs={{0,1},{1,0},{2,3},{3,2},{4,5},{5,4},{6,7},{7,6},{8,9},{9,8},{10,11... | collective-permute-start | bytes 3145736 | tf_op jit(solution)/shard_map/ppermute | solution.py:377
  55.4 22.2 %all-to-all-start.1 = ((bf16[32,32,256]{2,1,0:T(8,128)(2,1)}), bf16[32,32,256]{2,1,0:T(8,128)(2,1)S(1)}, u32[]{:S(2)}, u32[]{:S(2)}) async-start(bf16[32,32,256]{2,1,0:T(8,128)(2,1)} %bitcast.11), calls=%async_computation.1 | async-start | bytes 1048576 | tf_op jit(solution)/shard_map/all_to_all | solution.py:146
  62.0 2.2 %collective-permute-start.8 = (bf16[64,4096]{1,0:T(8,128)(2,1)}, bf16[64,4096]{1,0:T(8,128)(2,1)S(1)}, u32[]{:S(2)}, u32[]{:S(2)}) collective-permute-start(bf16[64,4096]{1,0:T(8,128)(2,1)} %collective-permute-done.3.refs_4_), channel_id=1, source_target_pairs={{0,1},{1,0},{2,3},{3,2},{4,5},{5,4},{6,7},{7,6},{8,9},{9,8},{10,11... | collective-permute-start | bytes 1572872 | tf_op jit(solution)/shard_map/ppermute | solution.py:377
  62.4 2.6 %collective-permute-start.9 = (bf16[64,4096]{1,0:T(8,128)(2,1)}, bf16[64,4096]{1,0:T(8,128)(2,1)S(1)}, u32[]{:S(2)}, u32[]{:S(2)}) collective-permute-start(bf16[64,4096]{1,0:T(8,128)(2,1)} %collective-permute-done.7.refs_5_), channel_id=1, source_target_pairs={{0,1},{1,0},{2,3},{3,2},{4,5},{5,4},{6,7},{7,6},{8,9},{9,8},{10,11... | collective-permute-start | bytes 1572872 | tf_op jit(solution)/shard_map/ppermute | solution.py:377

commit v14 on v13

--- a/solution.py
+++ b/solution.py
@@ -20,15 +20,23 @@
     place_ref, mask_ref, query_ref, grad_ref, out_ref, lse_ref, *rest
 ):
     cycle = mask_ref.shape[0]
-    pair_refs, (query_grad_ref, terms_ref, sums_ref, pairs_ref) = rest[:cycle], rest[cycle:]
+    pair_ref, fetched_ref, swapped_ref, query_grad_ref, terms_ref, sums_ref, pairs_ref = rest
     rows, width = pairs_ref.shape[1], pairs_ref.shape[2] // 2
     heads = lse_ref.shape[0]
     scale = 1.0 / math.sqrt(width)
     mine = place_ref[0]
     offset = 0.5 * math.log(rows) + lse_ref[...]
     spans = [slice(h * width, (h + 1) * width) for h in range(heads)]
-    for step, pair_ref in enumerate(pair_refs):
-        pairs_ref[step] = pair_ref[...]
+    pairs_ref[0] = pair_ref[...]
+    for core, (key_ref, value_ref) in enumerate(
+        ((fetched_ref, swapped_ref), (swapped_ref, fetched_ref))
+    ):
+
+        @pl.when(place_ref[1] == core)
+        def _(key_ref=key_ref, value_ref=value_ref):
+            pairs_ref[1:, :, :width] = key_ref[...]
+            pairs_ref[1:, :, width:] = value_ref[...]
+
     delta = []
     for span in spans:
         both = grad_ref[:, span].astype(jnp.float32) * out_ref[:, span].astype(jnp.float32)
@@ -87,23 +95,23 @@
     owners = lax.axis_size("exp")
     kv_count = keys.shape[1] // width
     kv_head = lax.axis_index("exp") * kv_count // owners
-    pair = jnp.concatenate(
+    key = lax.dynamic_slice_in_dim(keys, kv_head * width, width, 1)
+    value = lax.dynamic_slice_in_dim(values, kv_head * width, width, 1)
+    half = jnp.where(lax.axis_index("exp") % 2 == 0, key, value)
+    fetched = jnp.stack(
         [
-            lax.dynamic_slice_in_dim(keys, kv_head * width, width, 1),
-            lax.dynamic_slice_in_dim(values, kv_head * width, width, 1),
-        ],
-        axis=1,
-    )
-    return [pair] + [
-        lax.ppermute(pair, "ctx", [(c, c + step) for c in range(cycle - step)])
-        for step in range(1, cycle)
-    ]
+            lax.ppermute(half, "ctx", [(c, c + step) for c in range(cycle - step)])
+            for step in range(1, cycle)
+        ]
+    )
+    return jnp.concatenate([key, value], axis=1), fetched
 
 
 def attention(queries, arrived, attn_out, attn_out_grad, lse_excess, block_mask):
     cycle = lax.axis_size("ctx")
     mine = lax.axis_index("ctx")
-    pair = arrived[0]
+    pair, fetched = arrived
+    arrived = (pair, fetched, moved(fetched, (1, 1)))
     operands = (queries, attn_out_grad, attn_out, lse_excess, *arrived)
     return pl.pallas_call(
         attention_kernel,
@@ -123,7 +131,7 @@
         ),
         compiler_params=pltpu.CompilerParams(vmem_limit_bytes=32 * 2**20),
         name="attention",
-    )(mine.astype(jnp.int32)[None], block_mask, *operands)
+    )(jnp.stack([mine, lax.axis_index("exp") % 2]).astype(jnp.int32), block_mask, *operands)
 
 
 def sum_kernel(parts_ref, key_ref, value_ref):
@@ -428,7 +436,7 @@
     query_grad, terms = attention(
         queries, arrived, attn_out, attn_out_grad, lse_excess, block_mask
     )
-    first, shadow_rows = lax.optimization_barrier((first, shadow_rows))
+    first, shadow_rows, query_grad = lax.optimization_barrier((first, shadow_rows, query_grad))
     far = moved(first, [held[2] for held in steps])
     weighted = expert_rows(
         mixed, shadow_rows, shadow_list, stored_hidden_state, expert_ids.shape[0]

time: 78.7 us -> 80.3 us (1.020)
  blocking collectives: 12 us -> 0 us
  waiting for transfers between devices: 12.5 us -> 21.4 us
  starting transfers between devices: 29.7 us -> 31.7 us
  local copies, waits for them, and re-layouts: 4.26 us -> 5.99 us
    all_to_all x1 -> x0, blocking collectives: 12 us -> none  [swapped(): return lax.all_to_all(value, 'exp', split_axis=0, concat_axis=0, tiled=True)]
    ppermute x8 -> x9, waiting for transfers between devices: 5.66 us -> 12.1 us  [moved(): lax.ppermute(value, 'exp', [(e, e ^ steps[e % 2]) for e in range(owners)])]
    all_to_all x1 -> x2, waiting for transfers between devices: 0.01 us -> 5.67 us  [swapped(): return lax.all_to_all(value, 'exp', split_axis=0, concat_axis=0, tiled=True)]
    all_to_all x1 -> x2, starting transfers between devices: 3.61 us -> 7.37 us  [swapped(): return lax.all_to_all(value, 'exp', split_axis=0, concat_axis=0, tiled=True)]
    ppermute x3, waiting for transfers between devices: 5.14 us -> 1.84 us  [key_blocks(): lax.ppermute(half, 'ctx', [(c, c + step) for c in range(cycle - step)])]
    ppermute x1, starting transfers between devices: 4.24 us -> 1.73 us  [from_pair(): lax.ppermute(half, 'ctx', [(c, c ^ 1) for c in range(lax.axis_size('ctx'))])]
    unnamed x23 -> x27, local copies, waits for them, and re-layouts: 2.3 us -> 4.05 us
    ppermute x8 -> x9, starting transfers between devices: 5.9 us -> 6.4 us  [moved(): lax.ppermute(value, 'exp', [(e, e ^ steps[e % 2]) for e in range(owners)])]
  transfers between devices with their start and end apart: 14 -> 16, of which waited for: 7 -> 8; matrix products, arithmetic and copies ran while one was open for 5% -> 6% of each run, Pallas kernels for 22% -> 23%
where the time goes in v14:
time: 80.3 us; the launch traced here: 79.7 us
  starting transfers between devices  31.7 us (39%)
  waiting for transfers between devices  21.4 us (27%)
  Pallas kernels  18.9 us (24%)
  local copies, waits for them, and re-layouts  5.99 us (7%)
  other arithmetic  1.01 us (1%)
  between operations  0.9 us (1%)
    ppermute x9, waiting for transfers between devices, moved(): lax.ppermute(value, 'exp', [(e, e ^ steps[e % 2]) for e in range(owners)])  12.1 us
    pallas_call x1, Pallas kernels, tile_sums(): pl.pallas_call(functools.partial(tile_kernel, halves), out_shape=jax.Shap...  10.8 us
    ppermute x3, starting transfers between devices, key_blocks(): lax.ppermute(half, 'ctx', [(c, c + step) for c in range(cycle - step)])  9.42 us
    all_to_all x2, starting transfers between devices, swapped(): return lax.all_to_all(value, 'exp', split_axis=0, concat_axis=0, tiled=True)  7.37 us
    all_to_all x1, starting transfers between devices, summed_terms(): lax.all_to_all(terms.reshape(cycle * owners, rows // owners, columns), ('...  6.74 us
    ppermute x9, starting transfers between devices, moved(): lax.ppermute(value, 'exp', [(e, e ^ steps[e % 2]) for e in range(owners)])  6.4 us
    all_to_all x2, waiting for transfers between devices, swapped(): return lax.all_to_all(value, 'exp', split_axis=0, concat_axis=0, tiled=True)  5.67 us
    unnamed x27, local copies, waits for them, and re-layouts  4.05 us
  transfers between devices with their start and end apart: 16, of which 8 were waited for; matrix products, arithmetic and copies ran while one was open for 6% of the time, Pallas kernels for 23%

profile of v14, /device:TPU:0, one launch (start us, length us, event | category | flops | bytes accessed | tf_op | source)
XLA Modules:
  0.0 79.7 jit_solution(11983189648838626817)
XLA Ops:
  0.6 3.0 %collective-permute-start = (bf16[128,4096]{1,0:T(8,128)(2,1)}, bf16[128,4096]{1,0:T(8,128)(2,1)}, u32[]{:S(2)}, u32[]{:S(2)}) collective-permute-start(bf16[128,4096]{1,0:T(8,128)(2,1)} %refs_0_.1), channel_id=1, source_target_pairs={{0,4},{1,3},{2,6},{3,1},{4,0},{5,7},{6,2},{7,5},{8,12},{9,11},{10,... | collective-permute-start | bytes 3145736 | tf_op jit(solution)/shard_map/ppermute | solution.py:385
  3.7 1.9 %constant_dynamic-slice_fusion = bf16[64,4096]{1,0:T(8,128)(2,1)} fusion(bf16[128,4096]{1,0:T(8,128)(2,1)} %refs_0_.1, s32[]{:T(128)S(6)} %select_n.45), kind=kLoop, calls=%fused_computation.9 | loop fusion | bytes 1048580 | tf_op jit(solution)/shard_map/dynamic_slice | solution.py:390
  5.6 1.5 %collective-permute-start.4 = (bf16[64,4096]{1,0:T(8,128)(2,1)}, bf16[64,4096]{1,0:T(8,128)(2,1)}, u32[]{:S(2)}, u32[]{:S(2)}) collective-permute-start(bf16[64,4096]{1,0:T(8,128)(2,1)} %constant_dynamic-slice_fusion), channel_id=1, source_target_pairs={{0,2},{1,5},{2,0},{3,7},{4,6},{5,1},{6,4},{7,3},{8,10},{9,13},{10,... | collective-permute-start | bytes 1572872 | tf_op jit(solution)/shard_map/ppermute | solution.py:385
  7.1 1.5 %copy.20.hidden_ref = bf16[1,3,8,65,384]{4,3,2,1,0:T(8,128)(2,1)S(1)} copy(bf16[1,3,8,65,384]{4,2,3,1,0:T(8,128)(2,1)} %param.23) | data formatting | bytes 2396160 | tf_op args[11]
  8.5 0.0 copy-start.9
  8.5 0.0 copy-start.10
  8.7 0.0 copy-start.8
  8.7 0.8 %fusion.1 = bf16[8,66,384]{2,1,0:T(8,128)(2,1)} fusion(bf16[8,2,128]{2,1,0:T(2,128)(2,1)S(1)} %bitcast.19, bf16[8,64,384]{2,1,0:T(8,128)(2,1)S(1)} %slice_bitcast_fusion), kind=kLoop, calls=%fused_computation.2 | loop fusion | flops 1216512 | bytes 802816 | tf_op jit(solution)/shard_map/concatenate | solution.py:355
  9.5 3.5 %all-to-all-start = ((bf16[8,66,384]{2,1,0:T(8,128)(2,1)}), bf16[8,66,384]{2,1,0:T(8,128)(2,1)S(1)}, u32[]{:S(2)}, u32[]{:S(2)}) async-start(bf16[8,66,384]{2,1,0:T(8,128)(2,1)} %fusion.1), calls=%async_computation | async-start | bytes 884736 | tf_op jit(solution)/shard_map/all_to_all | solution.py:334
  13.0 0.0 copy-start.3
  13.0 0.0 copy-start.4
  13.0 0.0 copy-start.5
  13.0 0.0 copy-start.6
  13.0 0.0 copy-start.7
  13.1 5.7 %collective-permute-start.3 = (bf16[256,128]{1,0:T(8,128)(2,1)S(1)}, bf16[256,128]{1,0:T(8,128)(2,1)S(1)}, u32[]{:S(2)}, u32[]{:S(2)}) collective-permute-start(bf16[256,128]{1,0:T(8,128)(2,1)S(1)} %get-tuple-element.38), channel_id=1, source_target_pairs={{0,24},{1,25},{2,26},{3,27},{4,28},{5,29},{6,30},{7,31}} | collective-permute-start | bytes 196616 | tf_op jit(solution)/shard_map/ppermute | solution.py:103
  18.8 1.3 %collective-permute-start.2 = (bf16[256,128]{1,0:T(8,128)(2,1)S(1)}, bf16[256,128]{1,0:T(8,128)(2,1)S(1)}, u32[]{:S(2)}, u32[]{:S(2)}) collective-permute-start(bf16[256,128]{1,0:T(8,128)(2,1)S(1)} %get-tuple-element.38), channel_id=1, source_target_pairs={{0,16},{8,24},{1,17},{9,25},{2,18},{10,26},{3,19},{11,27},{4,20},{... | collective-permute-start | bytes 196616 | tf_op jit(solution)/shard_map/ppermute | solution.py:103
  20.1 2.5 %collective-permute-start.1 = (bf16[256,128]{1,0:T(8,128)(2,1)S(1)}, bf16[256,128]{1,0:T(8,128)(2,1)S(1)}, u32[]{:S(2)}, u32[]{:S(2)}) collective-permute-start(bf16[256,128]{1,0:T(8,128)(2,1)S(1)} %get-tuple-element.38), channel_id=1, source_target_pairs={{0,8},{8,16},{16,24},{1,9},{9,17},{17,25},{2,10},{10,18},{18,26},{... | collective-permute-start | bytes 196616 | tf_op jit(solution)/shard_map/ppermute | solution.py:103
  22.6 0.0 collective-permute-done.3
  22.6 0.0 collective-permute-done.2
  22.6 1.8 %collective-permute-done.1 = bf16[256,128]{1,0:T(8,128)(2,1)S(1)} collective-permute-done((bf16[256,128]{1,0:T(8,128)(2,1)S(1)}, bf16[256,128]{1,0:T(8,128)(2,1)S(1)}, u32[]{:S(2)}, u32[]{:S(2)}) %collective-permute-start.1) | collective-permute-done | bytes 65568 | tf_op jit(solution)/shard_map/ppermute | solution.py:103
  24.5 2.9 %all-to-all-done.mixed_ref = bf16[8,66,384]{2,1,0:T(8,128)(2,1)S(1)} async-done(((bf16[8,66,384]{2,1,0:T(8,128)(2,1)}), bf16[8,66,384]{2,1,0:T(8,128)(2,1)S(1)}, u32[]{:S(2)}, u32[]{:S(2)}) %all-to-all-start) | async-done | bytes 405536 | tf_op jit(solution)/shard_map/all_to_all | solution.py:334
  27.3 1.3 %picked.1 = bf16[8,64,384]{2,1,0:T(8,128)(2,1)} custom-call(s32[16]{0:T(128)S(1)} %copy-done.8, bf16[8,66,384]{2,1,0:T(8,128)(2,1)S(1)} %all-to-all-done.mixed_ref), custom_call_target="tpu_custom_call" | custom-call | tf_op jit(solution)/shard_map/picked/pallas_call | solution.py:187
  28.7 0.0 collective-permute-done.4.refs_4_
  28.7 3.9 %all-to-all-start.1 = ((bf16[8,64,384]{2,1,0:T(8,128)(2,1)}), bf16[8,64,384]{2,1,0:T(8,128)(2,1)S(1)}, u32[]{:S(2)}, u32[]{:S(2)}) async-start(bf16[8,64,384]{2,1,0:T(8,128)(2,1)} %picked.1), calls=%async_computation.1 | async-start | bytes 786432 | tf_op jit(solution)/shard_map/all_to_all | solution.py:334
  32.6 0.5 collective-permute-start.5
  33.1 0.1 pad_add_fusion.place_ref
  33.1 1.0 %collective-permute-done.5.rest_2_ = bf16[3,256,128]{2,1,0:T(8,128)(2,1)S(1)} collective-permute-done((bf16[3,256,128]{2,1,0:T(8,128)(2,1)S(1)}, bf16[3,256,128]{2,1,0:T(8,128)(2,1)S(1)}, u32[]{:S(2)}, u32[]{:S(2)}) %collective-permute-start.5) | collective-permute-done | bytes 196640 | tf_op jit(solution)/shard_map/ppermute | solution.py:385
  34.2 3.1 %attention.1 = (bf16[256,512]{1,0:T(8,128)(2,1)}, bf16[4,256,256]{2,1,0:T(8,128)(2,1)S(1)}) custom-call(s32[2]{0:T(128)S(1)} %pad_add_fusion.place_ref, s32[4,4]{1,0:T(4,128)S(1)} %copy-done.7, bf16[256,512]{1,0:T(8,128)(2,1)S(1)} %copy-done.3, bf16[256,512]{1,0:T(8,128)(2,1)S(1)} %copy-done.4, bf16[256,512]{1,0:T(8,128)(2,1)S(1)} %copy-done.5, ...), custom_call_target="tpu_custom_call" | custom-call | tf_op jit(solution)/shard_map/attention/pallas_call | solution.py:116
  37.3 0.8 %copy-done.2 = bf16[4,256,256]{2,1,0:T(8,128)(2,1)} copy-done((bf16[4,256,256]{2,1,0:T(8,128)(2,1)}, bf16[4,256,256]{2,1,0:T(8,128)(2,1)S(1)}, u32[]{:S(2)}) %copy-start.2) | copy-done | bytes 524312
  38.1 2.8 %all-to-all-done.1.side_ref = bf16[8,64,384]{2,1,0:T(8,128)(2,1)S(1)} async-done(((bf16[8,64,384]{2,1,0:T(8,128)(2,1)}), bf16[8,64,384]{2,1,0:T(8,128)(2,1)S(1)}, u32[]{:S(2)}, u32[]{:S(2)}) %all-to-all-start.1) | async-done | bytes 393248 | tf_op jit(solution)/shard_map/all_to_all | solution.py:334
  40.9 0.7 copy-done
  41.7 0.0 collective-permute-done.refs_2_
  41.7 0.6 collective-permute-start.11
  42.2 0.0 collective-permute-start.6
  42.2 1.7 %collective-permute-start.8 = (bf16[64,4096]{1,0:T(8,128)(2,1)}, bf16[64,4096]{1,0:T(8,128)(2,1)}, u32[]{:S(2)}, u32[]{:S(2)}) collective-permute-start(bf16[64,4096]{1,0:T(8,128)(2,1)} %collective-permute-done.4.refs_4_), channel_id=1, source_target_pairs={{0,8},{8,0},{16,24},{24,16},{1,9},{9,1},{17,25},{25,17},{2,10},{10... | collective-permute-start | bytes 1572872 | tf_op jit(solution)/shard_map/ppermute | solution.py:394
  43.9 0.2 collective-permute-start.7
  44.2 1.0 %copy-done.1 = bf16[8,64,384]{2,1,0:T(8,128)(2,1)S(1)} copy-done((bf16[8,64,384]{2,1,0:T(8,128)(2,1)S(1)}, bf16[8,64,384]{2,1,0:T(8,128)(2,1)}, u32[]{:S(2)}) %copy-start.1) | copy-done | bytes 393240
  45.2 2.9 %weighted.1.weight_ref = bf16[768,1024]{1,0:T(8,128)(2,1)S(1)} custom-call(s32[1]{0:T(128)} %bitcast.11.own_ref, s32[16]{0:T(128)S(1)} %copy-done.8, bf16[8,66,384]{2,1,0:T(8,128)(2,1)S(1)} %all-to-all-done.mixed_ref, bf16[1,3,8,65,384]{4,3,2,1,0:T(8,128)(2,1)S(1)} %copy.20.hidden_ref, bf16[8,64,384]{2,1,0:T(8,128)(2,1)S(1)} %copy-done.1), custom_call_target="tpu_custom_call" | custom-call | tf_op jit(solution)/shard_map/weighted/pallas_call | solution.py:239
  48.1 8.7 %collective-permute-done.11.refs_8_ = bf16[128,4096]{1,0:T(8,128)(2,1)} collective-permute-done((bf16[128,4096]{1,0:T(8,128)(2,1)}, bf16[128,4096]{1,0:T(8,128)(2,1)}, u32[]{:S(2)}, u32[]{:S(2)}) %collective-permute-start.11) | collective-permute-done | bytes 1048608 | tf_op jit(solution)/shard_map/ppermute | solution.py:385
  56.8 0.0 collective-permute-start.12
  56.8 6.7 %all-to-all-start.2 = ((bf16[32,32,256]{2,1,0:T(8,128)(2,1)}), bf16[32,32,256]{2,1,0:T(8,128)(2,1)S(1)}, u32[]{:S(2)}, u32[]{:S(2)}) async-start(bf16[32,32,256]{2,1,0:T(8,128)(2,1)} %bitcast.15), calls=%async_computation.2 | async-start | bytes 1048576 | tf_op jit(solution)/shard_map/all_to_all | solution.py:154
  63.5 0.3 collective-permute-start.9
  63.8 0.3 collective-permute-start.10
  64.1 1.6 %collective-permute-done.9.refs_6_ = bf16[64,4096]{1,0:T(8,128)(2,1)S(1)} collective-permute-done((bf16[64,4096]{1,0:T(8,128)(2,1)}, bf16[64,4096]{1,0:T(8,128)(2,1)S(1)}, u32[]{:S(2)}, u32[]{:S(2)}) %collective-permute-start.9) | collective-permute-done | bytes 524320 | tf_op jit(solution)/shard_map/ppermute | solution.py:385
  65.7 0.7 collective-permute-done.10.refs_7_
  66.5 10.8 %tiles.1 = f32[2,384,4096]{2,1,0:T(8,128)} custom-call(s32[1]{0:T(128)} %bitcast.10.parity_ref, bf16[768,1024]{1,0:T(8,128)(2,1)S(1)} %weighted.1.weight_ref, bf16[128,4096]{1,0:T(8,128)(2,1)} %refs_0_.1, bf16[128,4096]{1,0:T(8,128)(2,1)} %collective-permute-done.6.refs_1_, bf16[128,4096]{1,0:T(8,128)(2,1)} %collective-permute-done.refs_2_, ...), custom_call_target="tpu_custom_call" | custom-call | tf_op jit(solution)/shard_map/tiles/pallas_call | solution.py:316
  77.3 1.8 %all-to-all-done.2 = bf16[32,32,256]{2,1,0:T(8,128)(2,1)S(1)} async-done(((bf16[32,32,256]{2,1,0:T(8,128)(2,1)}), bf16[32,32,256]{2,1,0:T(8,128)(2,1)S(1)}, u32[]{:S(2)}, u32[]{:S(2)}) %all-to-all-start.2) | async-done | bytes 524320 | tf_op jit(solution)/shard_map/all_to_all | solution.py:154
  79.1 0.7 sums.1
  (25 shorter events, 0.2 us)
Async XLA Ops:
  0.6 41.0 %collective-permute-start = (bf16[128,4096]{1,0:T(8,128)(2,1)}, bf16[128,4096]{1,0:T(8,128)(2,1)}, u32[]{:S(2)}, u32[]{:S(2)}) collective-permute-start(bf16[128,4096]{1,0:T(8,128)(2,1)} %refs_0_.1), channel_id=1, source_target_pairs={{0,4},{1,3},{2,6},{3,1},{4,0},{5,7},{6,2},{7,5},{8,12},{9,11},{10,... | collective-permute-start | bytes 3145736 | tf_op jit(solution)/shard_map/ppermute | solution.py:385
  5.6 3.0 %copy-start.12 = (bf16[128,8]{0,1:T(8,128)(2,1)S(1)}, bf16[128,8]{0,1:T(8,128)(2,1)}, u32[]{:S(2)}) copy-start(bf16[128,8]{0,1:T(8,128)(2,1)} %param.20) | copy-start | bytes 6148
  5.6 3.0 %copy-start.11 = (s32[128,8]{0,1:T(8,128)S(1)}, s32[128,8]{0,1:T(8,128)}, u32[]{:S(2)}) copy-start(s32[128,8]{0,1:T(8,128)} %param.19) | copy-start | bytes 12292
  5.6 23.1 %collective-permute-start.4 = (bf16[64,4096]{1,0:T(8,128)(2,1)}, bf16[64,4096]{1,0:T(8,128)(2,1)}, u32[]{:S(2)}, u32[]{:S(2)}) collective-permute-start(bf16[64,4096]{1,0:T(8,128)(2,1)} %constant_dynamic-slice_fusion), channel_id=1, source_target_pairs={{0,2},{1,5},{2,0},{3,7},{4,6},{5,1},{6,4},{7,3},{8,10},{9,13},{10,... | collective-permute-start | bytes 1572872 | tf_op jit(solution)/shard_map/ppermute | solution.py:385
  8.5 4.5 %copy-start.9 = (bf16[256,256]{1,0:T(8,128)(2,1)S(1)}, bf16[256,256]{1,0:T(8,128)(2,1)}, u32[]{:S(2)}) copy-start(bf16[256,256]{1,0:T(8,128)(2,1)} %param.13) | copy-start | bytes 393220
  8.5 4.5 %copy-start.10 = (bf16[256,256]{1,0:T(8,128)(2,1)S(1)}, bf16[256,256]{1,0:T(8,128)(2,1)}, u32[]{:S(2)}) copy-start(bf16[256,256]{1,0:T(8,128)(2,1)} %param.14) | copy-start | bytes 393220
  8.7 18.7 %copy-start.8 = (s32[16]{0:T(128)S(1)}, s32[16]{0:T(128)}, u32[]{:S(2)}) copy-start(s32[16]{0:T(128)} %shadow_ref.3) | copy-start | bytes 196
  9.5 17.9 %all-to-all-start = ((bf16[8,66,384]{2,1,0:T(8,128)(2,1)}), bf16[8,66,384]{2,1,0:T(8,128)(2,1)S(1)}, u32[]{:S(2)}, u32[]{:S(2)}) async-start(bf16[8,66,384]{2,1,0:T(8,128)(2,1)} %fusion.1), calls=%async_computation | async-start | bytes 884736 | tf_op jit(solution)/shard_map/all_to_all | solution.py:334
  13.0 21.2 %copy-start.3 = (bf16[256,512]{1,0:T(8,128)(2,1)S(1)}, bf16[256,512]{1,0:T(8,128)(2,1)}, u32[]{:S(2)}) copy-start(bf16[256,512]{1,0:T(8,128)(2,1)} %query_ref.1) | copy-start | bytes 786436
  13.0 21.2 %copy-start.4 = (bf16[256,512]{1,0:T(8,128)(2,1)S(1)}, bf16[256,512]{1,0:T(8,128)(2,1)}, u32[]{:S(2)}) copy-start(bf16[256,512]{1,0:T(8,128)(2,1)} %grad_ref.1) | copy-start | bytes 786436
  13.0 21.2 %copy-start.5 = (bf16[256,512]{1,0:T(8,128)(2,1)S(1)}, bf16[256,512]{1,0:T(8,128)(2,1)}, u32[]{:S(2)}) copy-start(bf16[256,512]{1,0:T(8,128)(2,1)} %out_ref.1) | copy-start | bytes 786436
  13.0 21.1 %copy-start.6 = (f32[4,256]{1,0:T(4,128)S(1)}, f32[4,256]{1,0:T(4,128)}, u32[]{:S(2)}) copy-start(f32[4,256]{1,0:T(4,128)} %lse_ref.1) | copy-start | bytes 12292
  13.0 21.1 %copy-start.7 = (s32[4,4]{1,0:T(4,128)S(1)}, s32[4,4]{1,0:T(4,128)}, u32[]{:S(2)}) copy-start(s32[4,4]{1,0:T(4,128)} %mask_ref.1) | copy-start | bytes 196
  13.1 9.5 %collective-permute-start.3 = (bf16[256,128]{1,0:T(8,128)(2,1)S(1)}, bf16[256,128]{1,0:T(8,128)(2,1)S(1)}, u32[]{:S(2)}, u32[]{:S(2)}) collective-permute-start(bf16[256,128]{1,0:T(8,128)(2,1)S(1)} %get-tuple-element.38), channel_id=1, source_target_pairs={{0,24},{1,25},{2,26},{3,27},{4,28},{5,29},{6,30},{7,31}} | collective-permute-start | bytes 196616 | tf_op jit(solution)/shard_map/ppermute | solution.py:103
  18.8 3.8 %collective-permute-start.2 = (bf16[256,128]{1,0:T(8,128)(2,1)S(1)}, bf16[256,128]{1,0:T(8,128)(2,1)S(1)}, u32[]{:S(2)}, u32[]{:S(2)}) collective-permute-start(bf16[256,128]{1,0:T(8,128)(2,1)S(1)} %get-tuple-element.38), channel_id=1, source_target_pairs={{0,16},{8,24},{1,17},{9,25},{2,18},{10,26},{3,19},{11,27},{4,20},{... | collective-permute-start | bytes 196616 | tf_op jit(solution)/shard_map/ppermute | solution.py:103
  20.1 4.4 %collective-permute-start.1 = (bf16[256,128]{1,0:T(8,128)(2,1)S(1)}, bf16[256,128]{1,0:T(8,128)(2,1)S(1)}, u32[]{:S(2)}, u32[]{:S(2)}) collective-permute-start(bf16[256,128]{1,0:T(8,128)(2,1)S(1)} %get-tuple-element.38), channel_id=1, source_target_pairs={{0,8},{8,16},{16,24},{1,9},{9,17},{17,25},{2,10},{10,18},{18,26},{... | collective-permute-start | bytes 196616 | tf_op jit(solution)/shard_map/ppermute | solution.py:103
  28.7 12.2 %all-to-all-start.1 = ((bf16[8,64,384]{2,1,0:T(8,128)(2,1)}), bf16[8,64,384]{2,1,0:T(8,128)(2,1)S(1)}, u32[]{:S(2)}, u32[]{:S(2)}) async-start(bf16[8,64,384]{2,1,0:T(8,128)(2,1)} %picked.1), calls=%async_computation.1 | async-start | bytes 786432 | tf_op jit(solution)/shard_map/all_to_all | solution.py:334
  32.6 1.6 %collective-permute-start.5 = (bf16[3,256,128]{2,1,0:T(8,128)(2,1)S(1)}, bf16[3,256,128]{2,1,0:T(8,128)(2,1)S(1)}, u32[]{:S(2)}, u32[]{:S(2)}) collective-permute-start(bf16[3,256,128]{2,1,0:T(8,128)(2,1)S(1)} %pad_maximum_fusion.rest_1_), channel_id=1, source_target_pairs={{0,1},{1,0},{2,3},{3,2},{4,5},{5,4},{6,7},{7,6},{8,9},{9,8},{10,11... | collective-permute-start | bytes 589832 | tf_op jit(solution)/shard_map/ppermute | solution.py:385
  37.3 0.8 %copy-start.2 = (bf16[4,256,256]{2,1,0:T(8,128)(2,1)}, bf16[4,256,256]{2,1,0:T(8,128)(2,1)S(1)}, u32[]{:S(2)}) copy-start(bf16[4,256,256]{2,1,0:T(8,128)(2,1)S(1)} %get-tuple-element.29) | copy-start | bytes 1572868
  40.9 0.7 copy-start
  41.7 15.1 %collective-permute-start.11 = (bf16[128,4096]{1,0:T(8,128)(2,1)}, bf16[128,4096]{1,0:T(8,128)(2,1)}, u32[]{:S(2)}, u32[]{:S(2)}) collective-permute-start(bf16[128,4096]{1,0:T(8,128)(2,1)} %collective-permute-done.refs_2_), channel_id=1, source_target_pairs={{0,2},{1,5},{2,0},{3,7},{4,6},{5,1},{6,4},{7,3},{8,10},{9,13},{10,... | collective-permute-start | bytes 3145736 | tf_op jit(solution)/shard_map/ppermute | solution.py:385
  42.2 21.9 %collective-permute-start.6 = (bf16[128,4096]{1,0:T(8,128)(2,1)}, bf16[128,4096]{1,0:T(8,128)(2,1)}, u32[]{:S(2)}, u32[]{:S(2)}) collective-permute-start(bf16[128,4096]{1,0:T(8,128)(2,1)} %refs_0_.1), channel_id=1, source_target_pairs={{0,1},{1,0},{2,3},{3,2},{4,5},{5,4},{6,7},{7,6},{8,9},{9,8},{10,11... | collective-permute-start | bytes 3145736 | tf_op jit(solution)/shard_map/ppermute | solution.py:385
  42.2 21.6 %collective-permute-start.8 = (bf16[64,4096]{1,0:T(8,128)(2,1)}, bf16[64,4096]{1,0:T(8,128)(2,1)}, u32[]{:S(2)}, u32[]{:S(2)}) collective-permute-start(bf16[64,4096]{1,0:T(8,128)(2,1)} %collective-permute-done.4.refs_4_), channel_id=1, source_target_pairs={{0,8},{8,0},{16,24},{24,16},{1,9},{9,1},{17,25},{25,17},{2,10},{10... | collective-permute-start | bytes 1572872 | tf_op jit(solution)/shard_map/ppermute | solution.py:394
  43.9 22.5 %collective-permute-start.7 = (bf16[128,4096]{1,0:T(8,128)(2,1)}, bf16[128,4096]{1,0:T(8,128)(2,1)}, u32[]{:S(2)}, u32[]{:S(2)}) collective-permute-start(bf16[128,4096]{1,0:T(8,128)(2,1)} %collective-permute-done.refs_2_), channel_id=1, source_target_pairs={{0,1},{1,0},{2,3},{3,2},{4,5},{5,4},{6,7},{7,6},{8,9},{9,8},{10,11... | collective-permute-start | bytes 3145736 | tf_op jit(solution)/shard_map/ppermute | solution.py:385
  44.2 1.0 %copy-start.1 = (bf16[8,64,384]{2,1,0:T(8,128)(2,1)S(1)}, bf16[8,64,384]{2,1,0:T(8,128)(2,1)}, u32[]{:S(2)}) copy-start(bf16[8,64,384]{2,1,0:T(8,128)(2,1)} %copy-done) | copy-start | bytes 1179652
  56.8 9.7 %collective-permute-start.12 = (bf16[128,4096]{1,0:T(8,128)(2,1)}, bf16[128,4096]{1,0:T(8,128)(2,1)}, u32[]{:S(2)}, u32[]{:S(2)}) collective-permute-start(bf16[128,4096]{1,0:T(8,128)(2,1)} %collective-permute-done.11.refs_8_), channel_id=1, source_target_pairs={{0,1},{1,0},{2,3},{3,2},{4,5},{5,4},{6,7},{7,6},{8,9},{9,8},{10,11... | collective-permute-start | bytes 3145736 | tf_op jit(solution)/shard_map/ppermute | solution.py:385
  56.8 22.3 %all-to-all-start.2 = ((bf16[32,32,256]{2,1,0:T(8,128)(2,1)}), bf16[32,32,256]{2,1,0:T(8,128)(2,1)S(1)}, u32[]{:S(2)}, u32[]{:S(2)}) async-start(bf16[32,32,256]{2,1,0:T(8,128)(2,1)} %bitcast.15), calls=%async_computation.2 | async-start | bytes 1048576 | tf_op jit(solution)/shard_map/all_to_all | solution.py:154
  63.5 2.2 %collective-permute-start.9 = (bf16[64,4096]{1,0:T(8,128)(2,1)}, bf16[64,4096]{1,0:T(8,128)(2,1)S(1)}, u32[]{:S(2)}, u32[]{:S(2)}) collective-permute-start(bf16[64,4096]{1,0:T(8,128)(2,1)} %collective-permute-done.4.refs_4_), channel_id=1, source_target_pairs={{0,1},{1,0},{2,3},{3,2},{4,5},{5,4},{6,7},{7,6},{8,9},{9,8},{10,11... | collective-permute-start | bytes 1572872 | tf_op jit(solution)/shard_map/ppermute | solution.py:385
  63.8 2.6 %collective-permute-start.10 = (bf16[64,4096]{1,0:T(8,128)(2,1)}, bf16[64,4096]{1,0:T(8,128)(2,1)S(1)}, u32[]{:S(2)}, u32[]{:S(2)}) collective-permute-start(bf16[64,4096]{1,0:T(8,128)(2,1)} %collective-permute-done.8.refs_5_), channel_id=1, source_target_pairs={{0,1},{1,0},{2,3},{3,2},{4,5},{5,4},{6,7},{7,6},{8,9},{9,8},{10,11... | collective-permute-start | bytes 1572872 | tf_op jit(solution)/shard_map/ppermute | solution.py:385

commit v15 on v14

--- a/solution.py
+++ b/solution.py
@@ -20,7 +20,8 @@
     place_ref, mask_ref, query_ref, grad_ref, out_ref, lse_ref, *rest
 ):
     cycle = mask_ref.shape[0]
-    pair_ref, fetched_ref, swapped_ref, query_grad_ref, terms_ref, sums_ref, pairs_ref = rest
+    pair_ref, fetched_ref, swapped_ref, query_grad_ref = rest[:4]
+    *term_refs, sums_ref, pairs_ref, terms_ref = rest[4:]
     rows, width = pairs_ref.shape[1], pairs_ref.shape[2] // 2
     heads = lse_ref.shape[0]
     scale = 1.0 / math.sqrt(width)
@@ -70,23 +71,26 @@
         value_term = jnp.dot(
             jnp.concatenate(probs, axis=1), grads, preferred_element_type=jnp.float32
         )
-        terms_ref[mine - step, :, :width] = key_term.astype(jnp.bfloat16)
-        terms_ref[mine - step, :, width:] = value_term.astype(jnp.bfloat16)
+        terms_ref[step, :, :width] = key_term.astype(jnp.bfloat16)
+        terms_ref[step, :, width:] = value_term.astype(jnp.bfloat16)
 
     block(0, True)
 
-    @pl.loop(0, cycle)
-    def _(source):
-        seen = jnp.logical_and(source < mine, mask_ref[mine, source] > 0)
+    @pl.loop(1, cycle)
+    def _(step):
+        source = mine - step
+        seen = jnp.logical_and(source >= 0, mask_ref[mine, jnp.maximum(source, 0)] > 0)
 
         @pl.when(seen)
         def _():
-            block(mine - source, False)
-
-        @pl.when(jnp.logical_and(source != mine, jnp.logical_not(seen)))
+            block(step, False)
+
+        @pl.when(jnp.logical_not(seen))
         def _():
-            terms_ref[source] = jnp.zeros_like(terms_ref[source])
-
+            terms_ref[step] = jnp.zeros_like(terms_ref[step])
+
+    for step, term_ref in enumerate(term_refs):
+        term_ref[...] = terms_ref[step]
     query_grad_ref[...] = sums_ref[...].astype(jnp.bfloat16)
 
 
@@ -113,51 +117,59 @@
     pair, fetched = arrived
     arrived = (pair, fetched, moved(fetched, (1, 1)))
     operands = (queries, attn_out_grad, attn_out, lse_excess, *arrived)
-    return pl.pallas_call(
+    query_grad, *terms = pl.pallas_call(
         attention_kernel,
-        out_shape=(
-            jax.ShapeDtypeStruct(queries.shape, jnp.bfloat16),
-            jax.ShapeDtypeStruct((cycle,) + pair.shape, jnp.bfloat16),
-        ),
+        out_shape=[jax.ShapeDtypeStruct(queries.shape, jnp.bfloat16)]
+        + [jax.ShapeDtypeStruct(pair.shape, jnp.bfloat16)] * cycle,
         grid_spec=pltpu.PrefetchScalarGridSpec(
             num_scalar_prefetch=2,
             grid=(1,),
             in_specs=[full(operand.shape) for operand in operands],
-            out_specs=(full(queries.shape), full((cycle,) + pair.shape)),
+            out_specs=[full(queries.shape)] + [full(pair.shape)] * cycle,
             scratch_shapes=[
                 pltpu.VMEM(queries.shape, jnp.float32),
+                pltpu.VMEM((cycle,) + pair.shape, jnp.bfloat16),
                 pltpu.VMEM((cycle,) + pair.shape, jnp.bfloat16),
             ],
         ),
         compiler_params=pltpu.CompilerParams(vmem_limit_bytes=32 * 2**20),
         name="attention",
     )(jnp.stack([mine, lax.axis_index("exp") % 2]).astype(jnp.int32), block_mask, *operands)
+    return query_grad, terms
 
 
 def sum_kernel(parts_ref, key_ref, value_ref):
-    cycle, owners, rows, columns = parts_ref.shape
+    owners, rows, columns = parts_ref.shape
     kv_count = key_ref.shape[1] * 2 // columns
     group = owners // kv_count
     width = columns // 2
     for k in range(kv_count):
         total = jnp.zeros((rows, columns), jnp.float32)
-        for c in range(cycle):
-            for e in range(k * group, (k + 1) * group):
-                total += parts_ref[c, e].astype(jnp.float32)
+        for e in range(k * group, (k + 1) * group):
+            total += parts_ref[e].astype(jnp.float32)
         key_ref[:, k * width : (k + 1) * width] = total[:, :width].astype(jnp.bfloat16)
         value_ref[:, k * width : (k + 1) * width] = total[:, width:].astype(jnp.bfloat16)
 
 
-def summed_terms(terms, kv_columns, tiles):
-    cycle, owners = lax.axis_size("ctx"), lax.axis_size("exp")
-    rows, columns = terms.shape[1:]
+def block_terms(terms):
+    cycle = lax.axis_size("ctx")
+    total = terms[0].astype(jnp.float32)
+    for step in range(1, cycle):
+        pairs = [(c, c - step) for c in range(step, cycle)]
+        total = total + lax.ppermute(terms[step], "ctx", pairs).astype(jnp.float32)
+    return total.astype(jnp.bfloat16)
+
+
+def summed_terms(total, kv_columns, tiles):
+    owners = lax.axis_size("exp")
+    rows, columns = total.shape
     parts = lax.all_to_all(
-        terms.reshape(cycle * owners, rows // owners, columns),
-        ("ctx", "exp"),
+        total.reshape(owners, rows // owners, columns),
+        "exp",
         split_axis=0,
         concat_axis=0,
         tiled=True,
-    ).reshape(cycle, owners, rows // owners, columns)
+    )
     parts, tiles = lax.optimization_barrier((parts, tiles))
     shape = (rows // owners, kv_columns)
     out = jax.ShapeDtypeStruct(shape, jnp.bfloat16)
@@ -430,21 +442,26 @@
     per_dev = shadow_list.shape[0] // lax.axis_size("exp")
     sent = picked_rows(shadow_list, mixed, payload.shape[1] - per_dev)
     sent, second = lax.optimization_barrier((sent, second))
+    own, first, _ = lax.optimization_barrier((moe_grad, first, sent))
     second = [second, from_pair(second)]
+    own_beside, first_beside = beside([own]), beside([first])
     shadow_rows = swapped(sent)
     arrived, _ = lax.optimization_barrier((arrived, sent))
     query_grad, terms = attention(
         queries, arrived, attn_out, attn_out_grad, lse_excess, block_mask
     )
-    first, shadow_rows, query_grad = lax.optimization_barrier((first, shadow_rows, query_grad))
+    first, second, shadow_rows, terms, own_beside, first_beside = lax.optimization_barrier(
+        (first, second, shadow_rows, terms, own_beside, first_beside)
+    )
     far = moved(first, [held[2] for held in steps])
+    total = block_terms(terms)
     weighted = expert_rows(
         mixed, shadow_rows, shadow_list, stored_hidden_state, expert_ids.shape[0]
     )
-    near = [(block, beside(block)) for block in ([moe_grad], [first], second)]
-    far, _ = lax.optimization_barrier((far, (weighted, query_grad)))
+    far, total, _ = lax.optimization_barrier((far, total, weighted))
+    near = [([moe_grad], own_beside), ([first], first_beside), (second, beside(second))]
     tiles = tile_sums(weighted, all_blocks(near + [([far], beside([far]))]), per_dev)
-    key_grad, value_grad, expert_grad = summed_terms(terms, keys.shape[1], tiles)
+    key_grad, value_grad, expert_grad = summed_terms(total, keys.shape[1], tiles)
     return (query_grad, key_grad, value_grad, expert_grad)
 
 

time: 80.3 us -> 83.3 us (1.037)
  waiting for transfers between devices: 21.4 us -> 14.6 us
  local copies, waits for them, and re-layouts: 5.99 us -> 11.9 us
  starting transfers between devices: 31.7 us -> 33.6 us
  other arithmetic: 1.01 us -> 2.41 us
    ppermute x9, waiting for transfers between devices: 12.1 us -> 1.62 us  [moved(): lax.ppermute(value, 'exp', [(e, e ^ steps[e % 2]) for e in range(owners)])]
    ppermute x0 -> x3, waiting for transfers between devices: none -> 8.88 us  [block_terms(): total = total + lax.ppermute(terms[step], 'ctx', pairs).astype(jnp.float32)]
    unnamed x27 -> x37, local copies, waits for them, and re-layouts: 4.05 us -> 9.92 us
    ppermute x0 -> x3, starting transfers between devices: none -> 3.86 us  [block_terms(): total = total + lax.ppermute(terms[step], 'ctx', pairs).astype(jnp.float32)]
    all_to_all x2, waiting for transfers between devices: 5.67 us -> 2.26 us  [swapped(): return lax.all_to_all(value, 'exp', split_axis=0, concat_axis=0, tiled=True)]
    all_to_all x1, starting transfers between devices: 6.74 us -> 3.37 us  [summed_terms(): lax.all_to_all(total.reshape(owners, rows // owners, columns), 'exp', spl...]
    all_to_all x1, waiting for transfers between devices: 1.79 us -> 0.01 us  [summed_terms(): lax.all_to_all(total.reshape(owners, rows // owners, columns), 'exp', spl...]
    ppermute x9, starting transfers between devices: 6.4 us -> 8.07 us  [moved(): lax.ppermute(value, 'exp', [(e, e ^ steps[e % 2]) for e in range(owners)])]
  transfers between devices with their start and end apart: 16 -> 19, of which waited for: 8 -> 6; matrix products, arithmetic and copies ran while one was open for 6% -> 7% of each run, Pallas kernels for 23% -> 22%
where the time goes in v15:
time: 83.3 us; the launch traced here: 82.1 us
  starting transfers between devices  33.6 us (40%)
  Pallas kernels  18.7 us (22%)
  waiting for transfers between devices  14.6 us (18%)
  local copies, waits for them, and re-layouts  11.9 us (14%)
  other arithmetic  2.41 us (3%)
  between operations  0.92 us (1%)
    pallas_call x1, Pallas kernels, tile_sums(): pl.pallas_call(functools.partial(tile_kernel, halves), out_shape=jax.Shap...  10.7 us
    unnamed x37, local copies, waits for them, and re-layouts  9.92 us
    ppermute x3, starting transfers between devices, key_blocks(): lax.ppermute(half, 'ctx', [(c, c + step) for c in range(cycle - step)])  9.27 us
    ppermute x3, waiting for transfers between devices, block_terms(): total = total + lax.ppermute(terms[step], 'ctx', pairs).astype(jnp.float32)  8.88 us
    ppermute x9, starting transfers between devices, moved(): lax.ppermute(value, 'exp', [(e, e ^ steps[e % 2]) for e in range(owners)])  8.07 us
    all_to_all x2, starting transfers between devices, swapped(): return lax.all_to_all(value, 'exp', split_axis=0, concat_axis=0, tiled=True)  7.32 us
    ppermute x3, starting transfers between devices, block_terms(): total = total + lax.ppermute(terms[step], 'ctx', pairs).astype(jnp.float32)  3.86 us
    all_to_all x1, starting transfers between devices, summed_terms(): lax.all_to_all(total.reshape(owners, rows // owners, columns), 'exp', spl...  3.37 us
  transfers between devices with their start and end apart: 19, of which 6 were waited for; matrix products, arithmetic and copies ran while one was open for 7% of the time, Pallas kernels for 22%

profile of v15, /device:TPU:0, one launch (start us, length us, event | category | flops | bytes accessed | tf_op | source)
XLA Modules:
  0.0 82.1 jit_solution(2792519229237068591)
XLA Ops:
  0.6 3.0 %collective-permute-start.5 = (bf16[128,4096]{1,0:T(8,128)(2,1)}, bf16[128,4096]{1,0:T(8,128)(2,1)}, u32[]{:S(2)}, u32[]{:S(2)}) collective-permute-start(bf16[128,4096]{1,0:T(8,128)(2,1)} %refs_0_.1), channel_id=1, source_target_pairs={{0,4},{1,3},{2,6},{3,1},{4,0},{5,7},{6,2},{7,5},{8,12},{9,11},{10,... | collective-permute-start | bytes 3145736 | tf_op jit(solution)/shard_map/ppermute | solution.py:397
  3.7 1.9 %constant_dynamic-slice_fusion = bf16[64,4096]{1,0:T(8,128)(2,1)} fusion(bf16[128,4096]{1,0:T(8,128)(2,1)} %refs_0_.1, s32[]{:T(128)S(6)} %select_n.45), kind=kLoop, calls=%fused_computation.10 | loop fusion | bytes 1048580 | tf_op jit(solution)/shard_map/dynamic_slice | solution.py:402
  5.6 1.5 %collective-permute-start.3 = (bf16[64,4096]{1,0:T(8,128)(2,1)}, bf16[64,4096]{1,0:T(8,128)(2,1)}, u32[]{:S(2)}, u32[]{:S(2)}) collective-permute-start(bf16[64,4096]{1,0:T(8,128)(2,1)} %constant_dynamic-slice_fusion), channel_id=1, source_target_pairs={{0,2},{1,5},{2,0},{3,7},{4,6},{5,1},{6,4},{7,3},{8,10},{9,13},{10,... | collective-permute-start | bytes 1572872 | tf_op jit(solution)/shard_map/ppermute | solution.py:397
  7.1 0.7 convert_element_type.28
  7.7 1.5 %copy.20.hidden_ref = bf16[1,3,8,65,384]{4,3,2,1,0:T(8,128)(2,1)S(1)} copy(bf16[1,3,8,65,384]{4,2,3,1,0:T(8,128)(2,1)} %param.23) | data formatting | bytes 2396160 | tf_op args[11]
  9.2 0.0 copy-start.16
  9.3 0.8 fusion.1
  10.1 3.6 %all-to-all-start = ((bf16[8,66,384]{2,1,0:T(8,128)(2,1)}), bf16[8,66,384]{2,1,0:T(8,128)(2,1)S(1)}, u32[]{:S(2)}, u32[]{:S(2)}) async-start(bf16[8,66,384]{2,1,0:T(8,128)(2,1)} %fusion.1), calls=%async_computation | async-start | bytes 884736 | tf_op jit(solution)/shard_map/all_to_all | solution.py:346
  13.8 0.0 copy-start.9
  13.8 0.0 copy-start.10
  13.9 5.5 %collective-permute-start.2 = (bf16[256,128]{1,0:T(8,128)(2,1)S(1)}, bf16[256,128]{1,0:T(8,128)(2,1)S(1)}, u32[]{:S(2)}, u32[]{:S(2)}) collective-permute-start(bf16[256,128]{1,0:T(8,128)(2,1)S(1)} %get-tuple-element.64), channel_id=1, source_target_pairs={{0,24},{1,25},{2,26},{3,27},{4,28},{5,29},{6,30},{7,31}} | collective-permute-start | bytes 196616 | tf_op jit(solution)/shard_map/ppermute | solution.py:107
  19.4 1.3 %collective-permute-start.1 = (bf16[256,128]{1,0:T(8,128)(2,1)S(1)}, bf16[256,128]{1,0:T(8,128)(2,1)S(1)}, u32[]{:S(2)}, u32[]{:S(2)}) collective-permute-start(bf16[256,128]{1,0:T(8,128)(2,1)S(1)} %get-tuple-element.64), channel_id=1, source_target_pairs={{0,16},{8,24},{1,17},{9,25},{2,18},{10,26},{3,19},{11,27},{4,20},{... | collective-permute-start | bytes 196616 | tf_op jit(solution)/shard_map/ppermute | solution.py:107
  20.7 2.5 %collective-permute-start = (bf16[256,128]{1,0:T(8,128)(2,1)S(1)}, bf16[256,128]{1,0:T(8,128)(2,1)S(1)}, u32[]{:S(2)}, u32[]{:S(2)}) collective-permute-start(bf16[256,128]{1,0:T(8,128)(2,1)S(1)} %get-tuple-element.64), channel_id=1, source_target_pairs={{0,8},{8,16},{16,24},{1,9},{9,17},{17,25},{2,10},{10,18},{18,26},{... | collective-permute-start | bytes 196616 | tf_op jit(solution)/shard_map/ppermute | solution.py:107
  23.2 1.8 %collective-permute-done = bf16[256,128]{1,0:T(8,128)(2,1)S(1)} collective-permute-done((bf16[256,128]{1,0:T(8,128)(2,1)S(1)}, bf16[256,128]{1,0:T(8,128)(2,1)S(1)}, u32[]{:S(2)}, u32[]{:S(2)}) %collective-permute-start) | collective-permute-done | bytes 65568 | tf_op jit(solution)/shard_map/ppermute | solution.py:107
  25.1 2.3 %all-to-all-done.mixed_ref = bf16[8,66,384]{2,1,0:T(8,128)(2,1)S(1)} async-done(((bf16[8,66,384]{2,1,0:T(8,128)(2,1)}), bf16[8,66,384]{2,1,0:T(8,128)(2,1)S(1)}, u32[]{:S(2)}, u32[]{:S(2)}) %all-to-all-start) | async-done | bytes 405536 | tf_op jit(solution)/shard_map/all_to_all | solution.py:346
  27.3 1.3 %picked.1 = bf16[8,64,384]{2,1,0:T(8,128)(2,1)} custom-call(s32[16]{0:T(128)S(1)} %copy-done.11, bf16[8,66,384]{2,1,0:T(8,128)(2,1)S(1)} %all-to-all-done.mixed_ref), custom_call_target="tpu_custom_call" | custom-call | tf_op jit(solution)/shard_map/picked/pallas_call | solution.py:199
  28.7 0.1 collective-permute-start.7
  28.8 0.5 collective-permute-start.8
  29.3 1.8 %collective-permute-start.6 = (bf16[64,4096]{1,0:T(8,128)(2,1)}, bf16[64,4096]{1,0:T(8,128)(2,1)}, u32[]{:S(2)}, u32[]{:S(2)}) collective-permute-start(bf16[64,4096]{1,0:T(8,128)(2,1)} %collective-permute-done.3.refs_4_), channel_id=1, source_target_pairs={{0,8},{8,0},{16,24},{24,16},{1,9},{9,1},{17,25},{25,17},{2,10},{10... | collective-permute-start | bytes 1572872 | tf_op jit(solution)/shard_map/ppermute | solution.py:406
  31.0 3.7 %all-to-all-start.1 = ((bf16[8,64,384]{2,1,0:T(8,128)(2,1)}), bf16[8,64,384]{2,1,0:T(8,128)(2,1)S(1)}, u32[]{:S(2)}, u32[]{:S(2)}) async-start(bf16[8,64,384]{2,1,0:T(8,128)(2,1)} %picked.1), calls=%async_computation.1 | async-start | bytes 786432 | tf_op jit(solution)/shard_map/all_to_all | solution.py:346
  34.7 0.5 collective-permute-start.4
  35.3 0.1 pad_add_fusion.place_ref
  35.3 1.0 %collective-permute-done.4.rest_2_ = bf16[3,256,128]{2,1,0:T(8,128)(2,1)S(1)} collective-permute-done((bf16[3,256,128]{2,1,0:T(8,128)(2,1)S(1)}, bf16[3,256,128]{2,1,0:T(8,128)(2,1)S(1)}, u32[]{:S(2)}, u32[]{:S(2)}) %collective-permute-start.4) | collective-permute-done | bytes 196640 | tf_op jit(solution)/shard_map/ppermute | solution.py:397
  36.3 0.9 %copy-done.4 = bf16[256,512]{1,0:T(8,128)(2,1)S(1)} copy-done((bf16[256,512]{1,0:T(8,128)(2,1)S(1)}, bf16[256,512]{1,0:T(8,128)(2,1)}, u32[]{:S(2)}) %copy-start.4) | copy-done | bytes 262168
  37.3 0.9 %copy-done.5 = bf16[256,512]{1,0:T(8,128)(2,1)S(1)} copy-done((bf16[256,512]{1,0:T(8,128)(2,1)S(1)}, bf16[256,512]{1,0:T(8,128)(2,1)}, u32[]{:S(2)}) %copy-start.5) | copy-done | bytes 262168
  38.2 0.9 %copy-done.6 = bf16[256,512]{1,0:T(8,128)(2,1)S(1)} copy-done((bf16[256,512]{1,0:T(8,128)(2,1)S(1)}, bf16[256,512]{1,0:T(8,128)(2,1)}, u32[]{:S(2)}) %copy-start.6) | copy-done | bytes 262168
  39.2 3.1 %attention.1 = (bf16[256,512]{1,0:T(8,128)(2,1)}, bf16[256,256]{1,0:T(8,128)(2,1)S(1)}, bf16[256,256]{1,0:T(8,128)(2,1)S(1)}, bf16[256,256]{1,0:T(8,128)(2,1)S(1)}, bf16[256,256]{1,0:T(8,128)(2,1)S(1)}) custom-call(s32[2]{0:T(128)S(1)} %pad_add_fusion.place_ref, s32[4,4]{1,0:T(4,128)S(1)} %copy-done.10, bf16[256,512]{1,0:T(8,128)(2,1)S(1)} %copy-done.4, ...), custom_call_target="tpu_custom_call" | custom-call | tf_op jit(solution)/shard_map/attention/pallas_call | solution.py:120
  42.3 0.7 copy-done.7
  43.0 0.6 copy-done.12
  43.6 0.6 copy-done.13
  44.3 0.7 copy-done.14
  44.9 0.7 copy-done.2
  45.7 2.0 %collective-permute-start.9 = (bf16[128,4096]{1,0:T(8,128)(2,1)}, bf16[128,4096]{1,0:T(8,128)(2,1)}, u32[]{:S(2)}, u32[]{:S(2)}) collective-permute-start(bf16[128,4096]{1,0:T(8,128)(2,1)} %collective-permute-done.5.refs_2_), channel_id=1, source_target_pairs={{0,2},{1,5},{2,0},{3,7},{4,6},{5,1},{6,4},{7,3},{8,10},{9,13},{10,... | collective-permute-start | bytes 3145736 | tf_op jit(solution)/shard_map/ppermute | solution.py:397
  47.6 1.3 %collective-permute-start.10 = (bf16[256,256]{1,0:T(8,128)(2,1)}, bf16[256,256]{1,0:T(8,128)(2,1)S(1)}, u32[]{:S(2)}, u32[]{:S(2)}) collective-permute-start(bf16[256,256]{1,0:T(8,128)(2,1)} %copy-done.14), channel_id=1, source_target_pairs={{8,0},{16,8},{24,16},{9,1},{17,9},{25,17},{10,2},{18,10},{26,18},{... | collective-permute-start | bytes 393224 | tf_op jit(solution)/shard_map/ppermute | solution.py:159
  48.9 1.3 %collective-permute-start.11 = (bf16[256,256]{1,0:T(8,128)(2,1)}, bf16[256,256]{1,0:T(8,128)(2,1)S(1)}, u32[]{:S(2)}, u32[]{:S(2)}) collective-permute-start(bf16[256,256]{1,0:T(8,128)(2,1)} %copy-done.13), channel_id=1, source_target_pairs={{16,0},{24,8},{17,1},{25,9},{18,2},{26,10},{19,3},{27,11},{20,4},{... | collective-permute-start | bytes 393224 | tf_op jit(solution)/shard_map/ppermute | solution.py:159
  50.2 1.3 %collective-permute-start.12 = (bf16[256,256]{1,0:T(8,128)(2,1)}, bf16[256,256]{1,0:T(8,128)(2,1)S(1)}, u32[]{:S(2)}, u32[]{:S(2)}) collective-permute-start(bf16[256,256]{1,0:T(8,128)(2,1)} %copy-done.12), channel_id=1, source_target_pairs={{24,0},{25,1},{26,2},{27,3},{28,4},{29,5},{30,6},{31,7}} | collective-permute-start | bytes 393224 | tf_op jit(solution)/shard_map/ppermute | solution.py:159
  51.5 0.0 copy-start.3
  51.5 1.0 %copy-done.3 = bf16[8,64,384]{2,1,0:T(8,128)(2,1)S(1)} copy-done((bf16[8,64,384]{2,1,0:T(8,128)(2,1)S(1)}, bf16[8,64,384]{2,1,0:T(8,128)(2,1)}, u32[]{:S(2)}) %copy-start.3) | copy-done | bytes 393240
  52.5 2.9 %weighted.1.weight_ref = bf16[768,1024]{1,0:T(8,128)(2,1)S(1)} custom-call(s32[1]{0:T(128)} %bitcast.8.own_ref, s32[16]{0:T(128)S(1)} %copy-done.11, bf16[8,66,384]{2,1,0:T(8,128)(2,1)S(1)} %all-to-all-done.mixed_ref, bf16[1,3,8,65,384]{4,3,2,1,0:T(8,128)(2,1)S(1)} %copy.20.hidden_ref, bf16[8,64,384]{2,1,0:T(8,128)(2,1)S(1)} %copy-done.3), custom_call_target="tpu_custom_call" | custom-call | tf_op jit(solution)/shard_map/weighted/pallas_call | solution.py:251
  55.4 8.9 %collective-permute-done.11 = bf16[256,256]{1,0:T(8,128)(2,1)S(1)} collective-permute-done((bf16[256,256]{1,0:T(8,128)(2,1)}, bf16[256,256]{1,0:T(8,128)(2,1)S(1)}, u32[]{:S(2)}, u32[]{:S(2)}) %collective-permute-start.11) | collective-permute-done | bytes 131104 | tf_op jit(solution)/shard_map/ppermute | solution.py:159
  64.3 0.7 add_convert_fusion
  65.0 0.5 collective-permute-start.13
  65.5 3.4 %all-to-all-start.2 = ((bf16[8,32,256]{2,1,0:T(8,128)(2,1)}), bf16[8,32,256]{2,1,0:T(8,128)(2,1)S(1)}, u32[]{:S(2)}, u32[]{:S(2)}) async-start(bf16[8,32,256]{2,1,0:T(8,128)(2,1)} %bitcast.9), calls=%async_computation.2 | async-start | bytes 262144 | tf_op jit(solution)/shard_map/all_to_all | solution.py:166
  68.9 0.5 collective-permute-done.13.refs_6_
  69.4 0.1 collective-permute-done.14.refs_7_
  69.5 1.2 %copy-done.1 = bf16[128,4096]{1,0:T(8,128)(2,1)S(1)} copy-done((bf16[128,4096]{1,0:T(8,128)(2,1)S(1)}, bf16[128,4096]{1,0:T(8,128)(2,1)}, u32[]{:S(2)}) %copy-start.1) | copy-done | bytes 1048600
  70.7 10.7 %tiles.1 = f32[2,384,4096]{2,1,0:T(8,128)} custom-call(s32[1]{0:T(128)} %bitcast.10.parity_ref, bf16[768,1024]{1,0:T(8,128)(2,1)S(1)} %weighted.1.weight_ref, bf16[128,4096]{1,0:T(8,128)(2,1)S(1)} %copy-done.1, bf16[128,4096]{1,0:T(8,128)(2,1)} %collective-permute-done.7.refs_1_, bf16[128,4096]{1,0:T(8,128)(2,1)} %collective-permute-done.5.refs_2_, ...), custom_call_target="tpu_custom_call" | custom-call | tf_op jit(solution)/shard_map/tiles/pallas_call | solution.py:328
  81.5 0.6 sums.1
  (42 shorter events, 0.2 us)
Async XLA Ops:
  0.6 28.1 %collective-permute-start.5 = (bf16[128,4096]{1,0:T(8,128)(2,1)}, bf16[128,4096]{1,0:T(8,128)(2,1)}, u32[]{:S(2)}, u32[]{:S(2)}) collective-permute-start(bf16[128,4096]{1,0:T(8,128)(2,1)} %refs_0_.1), channel_id=1, source_target_pairs={{0,4},{1,3},{2,6},{3,1},{4,0},{5,7},{6,2},{7,5},{8,12},{9,11},{10,... | collective-permute-start | bytes 3145736 | tf_op jit(solution)/shard_map/ppermute | solution.py:397
  5.6 23.1 %collective-permute-start.3 = (bf16[64,4096]{1,0:T(8,128)(2,1)}, bf16[64,4096]{1,0:T(8,128)(2,1)}, u32[]{:S(2)}, u32[]{:S(2)}) collective-permute-start(bf16[64,4096]{1,0:T(8,128)(2,1)} %constant_dynamic-slice_fusion), channel_id=1, source_target_pairs={{0,2},{1,5},{2,0},{3,7},{4,6},{5,1},{6,4},{7,3},{8,10},{9,13},{10,... | collective-permute-start | bytes 1572872 | tf_op jit(solution)/shard_map/ppermute | solution.py:397
  7.7 1.5 %copy-start.17 = (s32[128,8]{0,1:T(8,128)S(1)}, s32[128,8]{0,1:T(8,128)}, u32[]{:S(2)}) copy-start(s32[128,8]{0,1:T(8,128)} %param.19) | copy-start | bytes 12292
  9.2 4.6 %copy-start.15 = (bf16[256,256]{1,0:T(8,128)(2,1)S(1)}, bf16[256,256]{1,0:T(8,128)(2,1)}, u32[]{:S(2)}) copy-start(bf16[256,256]{1,0:T(8,128)(2,1)} %param.13) | copy-start | bytes 393220
  9.2 4.6 %copy-start.16 = (bf16[256,256]{1,0:T(8,128)(2,1)S(1)}, bf16[256,256]{1,0:T(8,128)(2,1)}, u32[]{:S(2)}) copy-start(bf16[256,256]{1,0:T(8,128)(2,1)} %param.14) | copy-start | bytes 393220
  9.3 18.0 %copy-start.11 = (s32[16]{0:T(128)S(1)}, s32[16]{0:T(128)}, u32[]{:S(2)}) copy-start(s32[16]{0:T(128)} %shadow_ref.3) | copy-start | bytes 196
  10.1 18.5 %copy-start = (bf16[128,4096]{1,0:T(8,128)(2,1)S(1)}, bf16[128,4096]{1,0:T(8,128)(2,1)}, u32[]{:S(2)}) copy-start(bf16[128,4096]{1,0:T(8,128)(2,1)} %refs_0_.1) | copy-start | bytes 3145732
  10.1 17.2 %all-to-all-start = ((bf16[8,66,384]{2,1,0:T(8,128)(2,1)}), bf16[8,66,384]{2,1,0:T(8,128)(2,1)S(1)}, u32[]{:S(2)}, u32[]{:S(2)}) async-start(bf16[8,66,384]{2,1,0:T(8,128)(2,1)} %fusion.1), calls=%async_computation | async-start | bytes 884736 | tf_op jit(solution)/shard_map/all_to_all | solution.py:346
  13.8 22.6 %copy-start.9 = (f32[4,256]{1,0:T(4,128)S(1)}, f32[4,256]{1,0:T(4,128)}, u32[]{:S(2)}) copy-start(f32[4,256]{1,0:T(4,128)} %lse_ref.1) | copy-start | bytes 12292
  13.8 22.6 %copy-start.10 = (s32[4,4]{1,0:T(4,128)S(1)}, s32[4,4]{1,0:T(4,128)}, u32[]{:S(2)}) copy-start(s32[4,4]{1,0:T(4,128)} %mask_ref.1) | copy-start | bytes 196
  13.9 9.3 %collective-permute-start.2 = (bf16[256,128]{1,0:T(8,128)(2,1)S(1)}, bf16[256,128]{1,0:T(8,128)(2,1)S(1)}, u32[]{:S(2)}, u32[]{:S(2)}) collective-permute-start(bf16[256,128]{1,0:T(8,128)(2,1)S(1)} %get-tuple-element.64), channel_id=1, source_target_pairs={{0,24},{1,25},{2,26},{3,27},{4,28},{5,29},{6,30},{7,31}} | collective-permute-start | bytes 196616 | tf_op jit(solution)/shard_map/ppermute | solution.py:107
  19.4 3.8 %collective-permute-start.1 = (bf16[256,128]{1,0:T(8,128)(2,1)S(1)}, bf16[256,128]{1,0:T(8,128)(2,1)S(1)}, u32[]{:S(2)}, u32[]{:S(2)}) collective-permute-start(bf16[256,128]{1,0:T(8,128)(2,1)S(1)} %get-tuple-element.64), channel_id=1, source_target_pairs={{0,16},{8,24},{1,17},{9,25},{2,18},{10,26},{3,19},{11,27},{4,20},{... | collective-permute-start | bytes 196616 | tf_op jit(solution)/shard_map/ppermute | solution.py:107
  20.7 4.4 %collective-permute-start = (bf16[256,128]{1,0:T(8,128)(2,1)S(1)}, bf16[256,128]{1,0:T(8,128)(2,1)S(1)}, u32[]{:S(2)}, u32[]{:S(2)}) collective-permute-start(bf16[256,128]{1,0:T(8,128)(2,1)S(1)} %get-tuple-element.64), channel_id=1, source_target_pairs={{0,8},{8,16},{16,24},{1,9},{9,17},{17,25},{2,10},{10,18},{18,26},{... | collective-permute-start | bytes 196616 | tf_op jit(solution)/shard_map/ppermute | solution.py:107
  28.7 17.0 %collective-permute-start.7 = (bf16[128,4096]{1,0:T(8,128)(2,1)S(1)}, bf16[128,4096]{1,0:T(8,128)(2,1)}, u32[]{:S(2)}, u32[]{:S(2)}) collective-permute-start(bf16[128,4096]{1,0:T(8,128)(2,1)S(1)} %copy-done), channel_id=1, source_target_pairs={{0,1},{1,0},{2,3},{3,2},{4,5},{5,4},{6,7},{7,6},{8,9},{9,8},{10,11... | collective-permute-start | bytes 3145736 | tf_op jit(solution)/shard_map/ppermute | solution.py:397
  28.8 16.9 %collective-permute-start.8 = (bf16[128,4096]{1,0:T(8,128)(2,1)}, bf16[128,4096]{1,0:T(8,128)(2,1)}, u32[]{:S(2)}, u32[]{:S(2)}) collective-permute-start(bf16[128,4096]{1,0:T(8,128)(2,1)} %collective-permute-done.5.refs_2_), channel_id=1, source_target_pairs={{0,1},{1,0},{2,3},{3,2},{4,5},{5,4},{6,7},{7,6},{8,9},{9,8},{10,11... | collective-permute-start | bytes 3145736 | tf_op jit(solution)/shard_map/ppermute | solution.py:397
  29.3 16.4 %collective-permute-start.6 = (bf16[64,4096]{1,0:T(8,128)(2,1)}, bf16[64,4096]{1,0:T(8,128)(2,1)}, u32[]{:S(2)}, u32[]{:S(2)}) collective-permute-start(bf16[64,4096]{1,0:T(8,128)(2,1)} %collective-permute-done.3.refs_4_), channel_id=1, source_target_pairs={{0,8},{8,0},{16,24},{24,16},{1,9},{9,1},{17,25},{25,17},{2,10},{10... | collective-permute-start | bytes 1572872 | tf_op jit(solution)/shard_map/ppermute | solution.py:406
  31.0 13.9 %all-to-all-start.1 = ((bf16[8,64,384]{2,1,0:T(8,128)(2,1)}), bf16[8,64,384]{2,1,0:T(8,128)(2,1)S(1)}, u32[]{:S(2)}, u32[]{:S(2)}) async-start(bf16[8,64,384]{2,1,0:T(8,128)(2,1)} %picked.1), calls=%async_computation.1 | async-start | bytes 786432 | tf_op jit(solution)/shard_map/all_to_all | solution.py:346
  34.7 1.6 %collective-permute-start.4 = (bf16[3,256,128]{2,1,0:T(8,128)(2,1)S(1)}, bf16[3,256,128]{2,1,0:T(8,128)(2,1)S(1)}, u32[]{:S(2)}, u32[]{:S(2)}) collective-permute-start(bf16[3,256,128]{2,1,0:T(8,128)(2,1)S(1)} %pad_maximum_fusion.rest_1_), channel_id=1, source_target_pairs={{0,1},{1,0},{2,3},{3,2},{4,5},{5,4},{6,7},{7,6},{8,9},{9,8},{10,11... | collective-permute-start | bytes 589832 | tf_op jit(solution)/shard_map/ppermute | solution.py:397
  36.3 1.0 %copy-start.4 = (bf16[256,512]{1,0:T(8,128)(2,1)S(1)}, bf16[256,512]{1,0:T(8,128)(2,1)}, u32[]{:S(2)}) copy-start(bf16[256,512]{1,0:T(8,128)(2,1)} %query_ref.1) | copy-start | bytes 786436
  37.3 0.9 %copy-start.5 = (bf16[256,512]{1,0:T(8,128)(2,1)S(1)}, bf16[256,512]{1,0:T(8,128)(2,1)}, u32[]{:S(2)}) copy-start(bf16[256,512]{1,0:T(8,128)(2,1)} %grad_ref.1) | copy-start | bytes 786436
  38.2 0.9 %copy-start.6 = (bf16[256,512]{1,0:T(8,128)(2,1)S(1)}, bf16[256,512]{1,0:T(8,128)(2,1)}, u32[]{:S(2)}) copy-start(bf16[256,512]{1,0:T(8,128)(2,1)} %out_ref.1) | copy-start | bytes 786436
  42.3 0.7 copy-start.7
  43.0 0.7 copy-start.12
  43.6 0.6 copy-start.13
  44.3 0.7 copy-start.14
  44.9 0.7 copy-start.2
  45.7 19.3 %collective-permute-start.9 = (bf16[128,4096]{1,0:T(8,128)(2,1)}, bf16[128,4096]{1,0:T(8,128)(2,1)}, u32[]{:S(2)}, u32[]{:S(2)}) collective-permute-start(bf16[128,4096]{1,0:T(8,128)(2,1)} %collective-permute-done.5.refs_2_), channel_id=1, source_target_pairs={{0,2},{1,5},{2,0},{3,7},{4,6},{5,1},{6,4},{7,3},{8,10},{9,13},{10,... | collective-permute-start | bytes 3145736 | tf_op jit(solution)/shard_map/ppermute | solution.py:397
  47.6 7.8 %collective-permute-start.10 = (bf16[256,256]{1,0:T(8,128)(2,1)}, bf16[256,256]{1,0:T(8,128)(2,1)S(1)}, u32[]{:S(2)}, u32[]{:S(2)}) collective-permute-start(bf16[256,256]{1,0:T(8,128)(2,1)} %copy-done.14), channel_id=1, source_target_pairs={{8,0},{16,8},{24,16},{9,1},{17,9},{25,17},{10,2},{18,10},{26,18},{... | collective-permute-start | bytes 393224 | tf_op jit(solution)/shard_map/ppermute | solution.py:159
  48.9 15.3 %collective-permute-start.11 = (bf16[256,256]{1,0:T(8,128)(2,1)}, bf16[256,256]{1,0:T(8,128)(2,1)S(1)}, u32[]{:S(2)}, u32[]{:S(2)}) collective-permute-start(bf16[256,256]{1,0:T(8,128)(2,1)} %copy-done.13), channel_id=1, source_target_pairs={{16,0},{24,8},{17,1},{25,9},{18,2},{26,10},{19,3},{27,11},{20,4},{... | collective-permute-start | bytes 393224 | tf_op jit(solution)/shard_map/ppermute | solution.py:159
  50.2 14.1 %collective-permute-start.12 = (bf16[256,256]{1,0:T(8,128)(2,1)}, bf16[256,256]{1,0:T(8,128)(2,1)S(1)}, u32[]{:S(2)}, u32[]{:S(2)}) collective-permute-start(bf16[256,256]{1,0:T(8,128)(2,1)} %copy-done.12), channel_id=1, source_target_pairs={{24,0},{25,1},{26,2},{27,3},{28,4},{29,5},{30,6},{31,7}} | collective-permute-start | bytes 393224 | tf_op jit(solution)/shard_map/ppermute | solution.py:159
  51.5 1.0 %copy-start.3 = (bf16[8,64,384]{2,1,0:T(8,128)(2,1)S(1)}, bf16[8,64,384]{2,1,0:T(8,128)(2,1)}, u32[]{:S(2)}) copy-start(bf16[8,64,384]{2,1,0:T(8,128)(2,1)} %copy-done.2) | copy-start | bytes 1179652
  52.5 11.8 %copy-start.8 = (bf16[256,256]{1,0:T(8,128)(2,1)S(1)}, bf16[256,256]{1,0:T(8,128)(2,1)}, u32[]{:S(2)}) copy-start(bf16[256,256]{1,0:T(8,128)(2,1)} %copy-done.7) | copy-start | bytes 393220
  65.0 4.5 %collective-permute-start.15 = (bf16[128,4096]{1,0:T(8,128)(2,1)}, bf16[128,4096]{1,0:T(8,128)(2,1)S(1)}, u32[]{:S(2)}, u32[]{:S(2)}) collective-permute-start(bf16[128,4096]{1,0:T(8,128)(2,1)} %collective-permute-done.9.refs_8_), channel_id=1, source_target_pairs={{0,1},{1,0},{2,3},{3,2},{4,5},{5,4},{6,7},{7,6},{8,9},{9,8},{10,11... | collective-permute-start | bytes 3145736 | tf_op jit(solution)/shard_map/ppermute | solution.py:397
  65.0 4.4 %collective-permute-start.13 = (bf16[64,4096]{1,0:T(8,128)(2,1)}, bf16[64,4096]{1,0:T(8,128)(2,1)S(1)}, u32[]{:S(2)}, u32[]{:S(2)}) collective-permute-start(bf16[64,4096]{1,0:T(8,128)(2,1)} %collective-permute-done.3.refs_4_), channel_id=1, source_target_pairs={{0,1},{1,0},{2,3},{3,2},{4,5},{5,4},{6,7},{7,6},{8,9},{9,8},{10,11... | collective-permute-start | bytes 1572872 | tf_op jit(solution)/shard_map/ppermute | solution.py:397
  65.5 4.0 %collective-permute-start.14 = (bf16[64,4096]{1,0:T(8,128)(2,1)}, bf16[64,4096]{1,0:T(8,128)(2,1)}, u32[]{:S(2)}, u32[]{:S(2)}) collective-permute-start(bf16[64,4096]{1,0:T(8,128)(2,1)} %collective-permute-done.6.refs_5_), channel_id=1, source_target_pairs={{0,1},{1,0},{2,3},{3,2},{4,5},{5,4},{6,7},{7,6},{8,9},{9,8},{10,11... | collective-permute-start | bytes 1572872 | tf_op jit(solution)/shard_map/ppermute | solution.py:397
  65.5 16.0 %all-to-all-start.2 = ((bf16[8,32,256]{2,1,0:T(8,128)(2,1)}), bf16[8,32,256]{2,1,0:T(8,128)(2,1)S(1)}, u32[]{:S(2)}, u32[]{:S(2)}) async-start(bf16[8,32,256]{2,1,0:T(8,128)(2,1)} %bitcast.9), calls=%async_computation.2 | async-start | bytes 262144 | tf_op jit(solution)/shard_map/all_to_all | solution.py:166
  69.5 1.2 %copy-start.1 = (bf16[128,4096]{1,0:T(8,128)(2,1)S(1)}, bf16[128,4096]{1,0:T(8,128)(2,1)}, u32[]{:S(2)}) copy-start(bf16[128,4096]{1,0:T(8,128)(2,1)} %refs_0_.1) | copy-start | bytes 3145732

commit v16 on v14

--- a/solution.py
+++ b/solution.py
@@ -423,20 +423,22 @@
 ):
     steps = block_steps(lax.axis_size("exp"))
     first = moved(moe_grad, [held[1] for held in steps])
-    second = moved(paired_half(moe_grad), [held[2] for held in steps])
     arrived = key_blocks(keys, values, queries.shape[1] // lse_excess.shape[0])
     payload = source_rows(expert_ids, route_probs, shadow_list, stored_hidden_state)
     mixed, arrived = lax.optimization_barrier((swapped(payload), arrived))
     per_dev = shadow_list.shape[0] // lax.axis_size("exp")
     sent = picked_rows(shadow_list, mixed, payload.shape[1] - per_dev)
-    sent, second = lax.optimization_barrier((sent, second))
-    second = [second, from_pair(second)]
+    half, _ = lax.optimization_barrier((paired_half(moe_grad), mixed))
+    second = moved(half, [held[2] for held in steps])
     shadow_rows = swapped(sent)
     arrived, _ = lax.optimization_barrier((arrived, sent))
     query_grad, terms = attention(
         queries, arrived, attn_out, attn_out_grad, lse_excess, block_mask
     )
-    first, shadow_rows, query_grad = lax.optimization_barrier((first, shadow_rows, query_grad))
+    first, second, shadow_rows, query_grad = lax.optimization_barrier(
+        (first, second, shadow_rows, query_grad)
+    )
+    second = [second, from_pair(second)]
     far = moved(first, [held[2] for held in steps])
     weighted = expert_rows(
         mixed, shadow_rows, shadow_list, stored_hidden_state, expert_ids.shape[0]

time: 80.3 us -> 82 us (1.021)
  starting transfers between devices: 31.7 us -> 25.9 us
  waiting for transfers between devices: 21.4 us -> 27.2 us
  other arithmetic: 1.01 us -> 2.54 us
    all_to_all x2, waiting for transfers between devices: 5.67 us -> 12.4 us  [swapped(): return lax.all_to_all(value, 'exp', split_axis=0, concat_axis=0, tiled=True)]
    all_to_all x1, starting transfers between devices: 6.74 us -> 2.6 us  [summed_terms(): lax.all_to_all(terms.reshape(cycle * owners, rows // owners, columns), ('...]
    ppermute x3, waiting for transfers between devices: 1.84 us -> 0.01 us  [key_blocks(): lax.ppermute(half, 'ctx', [(c, c + step) for c in range(cycle - step)])]
    ppermute x1, starting transfers between devices: 1.73 us -> 0.01 us  [from_pair(): lax.ppermute(half, 'ctx', [(c, c ^ 1) for c in range(lax.axis_size('ctx'))])]
    ppermute x3, starting transfers between devices: 9.42 us -> 10.7 us  [key_blocks(): lax.ppermute(half, 'ctx', [(c, c + step) for c in range(cycle - step)])]
    ppermute x9, waiting for transfers between devices: 12.1 us -> 13.1 us  [moved(): lax.ppermute(value, 'exp', [(e, e ^ steps[e % 2]) for e in range(owners)])]
    select_n x1, other arithmetic: 0.04 us -> 0.91 us  [key_blocks(): half = jnp.where(lax.axis_index('exp') % 2 == 0, key, value)]
    ppermute x9, starting transfers between devices: 6.4 us -> 5.54 us  [moved(): lax.ppermute(value, 'exp', [(e, e ^ steps[e % 2]) for e in range(owners)])]
  transfers between devices with their start and end apart: 16 -> 16, of which waited for: 8 -> 7; matrix products, arithmetic and copies ran while one was open for 6% -> 6% of each run, Pallas kernels for 23% -> 22%
where the time goes in v16:
time: 82 us; the launch traced here: 81.4 us
  waiting for transfers between devices  27.2 us (33%)
  starting transfers between devices  25.9 us (32%)
  Pallas kernels  18.9 us (23%)
  local copies, waits for them, and re-layouts  5.96 us (7%)
  other arithmetic  2.54 us (3%)
  between operations  0.86 us (1%)
    ppermute x9, waiting for transfers between devices, moved(): lax.ppermute(value, 'exp', [(e, e ^ steps[e % 2]) for e in range(owners)])  13.1 us
    all_to_all x2, waiting for transfers between devices, swapped(): return lax.all_to_all(value, 'exp', split_axis=0, concat_axis=0, tiled=True)  12.4 us
    pallas_call x1, Pallas kernels, tile_sums(): pl.pallas_call(functools.partial(tile_kernel, halves), out_shape=jax.Shap...  10.9 us
    ppermute x3, starting transfers between devices, key_blocks(): lax.ppermute(half, 'ctx', [(c, c + step) for c in range(cycle - step)])  10.7 us
    all_to_all x2, starting transfers between devices, swapped(): return lax.all_to_all(value, 'exp', split_axis=0, concat_axis=0, tiled=True)  7.05 us
    ppermute x9, starting transfers between devices, moved(): lax.ppermute(value, 'exp', [(e, e ^ steps[e % 2]) for e in range(owners)])  5.54 us
    unnamed x21, local copies, waits for them, and re-layouts  4.04 us
    pallas_call x1, Pallas kernels, attention(): pl.pallas_call(attention_kernel, out_shape=(jax.ShapeDtypeStruct(queries....  3.15 us
  transfers between devices with their start and end apart: 16, of which 7 were waited for; matrix products, arithmetic and copies ran while one was open for 6% of the time, Pallas kernels for 22%

profile of v16, /device:TPU:0, one launch (start us, length us, event | category | flops | bytes accessed | tf_op | source)
XLA Modules:
  0.0 81.4 jit_solution(13727847197754481616)
XLA Ops:
  0.7 0.9 %broadcast_select_fusion = (bf16[256,128]{1,0:T(8,128)(2,1)S(1)}, bf16[256,128]{1,0:T(8,128)(2,1)S(1)}, bf16[256,128]{1,0:T(8,128)(2,1)S(1)}) fusion(pred[]{:T(512)S(6)} %eq.24, bf16[256,256]{1,0:T(8,128)(2,1)} %param.13, s32[]{:T(128)S(6)} %select_n.42, bf16[256,256]{1,0:T(8,128)(2,1)} %param.14), kind=kLoop, calls=%fused_computation.8 | loop fusion | flops 32768 | bytes 327685 | tf_op jit(solution)/shard_map/jit(_where)/select_n | solution.py:100
  1.6 7.0 %collective-permute-start.3 = (bf16[256,128]{1,0:T(8,128)(2,1)S(1)}, bf16[256,128]{1,0:T(8,128)(2,1)S(1)}, u32[]{:S(2)}, u32[]{:S(2)}) collective-permute-start(bf16[256,128]{1,0:T(8,128)(2,1)S(1)} %get-tuple-element.38), channel_id=1, source_target_pairs={{0,24},{1,25},{2,26},{3,27},{4,28},{5,29},{6,30},{7,31}} | collective-permute-start | bytes 196616 | tf_op jit(solution)/shard_map/ppermute | solution.py:103
  8.5 1.3 %collective-permute-start.2 = (bf16[256,128]{1,0:T(8,128)(2,1)S(1)}, bf16[256,128]{1,0:T(8,128)(2,1)S(1)}, u32[]{:S(2)}, u32[]{:S(2)}) collective-permute-start(bf16[256,128]{1,0:T(8,128)(2,1)S(1)} %get-tuple-element.38), channel_id=1, source_target_pairs={{0,16},{8,24},{1,17},{9,25},{2,18},{10,26},{3,19},{11,27},{4,20},{... | collective-permute-start | bytes 196616 | tf_op jit(solution)/shard_map/ppermute | solution.py:103
  9.8 2.5 %collective-permute-start.1 = (bf16[256,128]{1,0:T(8,128)(2,1)S(1)}, bf16[256,128]{1,0:T(8,128)(2,1)S(1)}, u32[]{:S(2)}, u32[]{:S(2)}) collective-permute-start(bf16[256,128]{1,0:T(8,128)(2,1)S(1)} %get-tuple-element.38), channel_id=1, source_target_pairs={{0,8},{8,16},{16,24},{1,9},{9,17},{17,25},{2,10},{10,18},{18,26},{... | collective-permute-start | bytes 196616 | tf_op jit(solution)/shard_map/ppermute | solution.py:103
  12.3 1.6 %collective-permute-start = (bf16[128,4096]{1,0:T(8,128)(2,1)}, bf16[128,4096]{1,0:T(8,128)(2,1)}, u32[]{:S(2)}, u32[]{:S(2)}) collective-permute-start(bf16[128,4096]{1,0:T(8,128)(2,1)} %refs_0_.1), channel_id=1, source_target_pairs={{0,4},{1,3},{2,6},{3,1},{4,0},{5,7},{6,2},{7,5},{8,12},{9,11},{10,... | collective-permute-start | bytes 3145736 | tf_op jit(solution)/shard_map/ppermute | solution.py:385
  13.9 0.7 convert_element_type.13
  14.6 1.5 %copy.20.hidden_ref = bf16[1,3,8,65,384]{4,3,2,1,0:T(8,128)(2,1)S(1)} copy(bf16[1,3,8,65,384]{4,2,3,1,0:T(8,128)(2,1)} %param.23) | data formatting | bytes 2396160 | tf_op args[11]
  16.1 0.0 copy-done.9
  16.1 0.8 fusion.1
  16.9 3.6 %all-to-all-start = ((bf16[8,66,384]{2,1,0:T(8,128)(2,1)}), bf16[8,66,384]{2,1,0:T(8,128)(2,1)S(1)}, u32[]{:S(2)}, u32[]{:S(2)}) async-start(bf16[8,66,384]{2,1,0:T(8,128)(2,1)} %fusion.1), calls=%async_computation | async-start | bytes 884736 | tf_op jit(solution)/shard_map/all_to_all | solution.py:334
  20.6 1.9 %constant_dynamic-slice_fusion.2 = bf16[64,4096]{1,0:T(8,128)(2,1)} fusion(bf16[128,4096]{1,0:T(8,128)(2,1)} %refs_0_.1, s32[]{:T(128)S(6)} %select_n.39), kind=kLoop, calls=%fused_computation.11 | loop fusion | bytes 1048580 | tf_op jit(solution)/shard_map/dynamic_slice | solution.py:390
  22.5 0.0 copy-start.7
  22.5 0.0 collective-permute-done.3
  22.5 0.0 collective-permute-done.2
  22.5 0.0 collective-permute-done.1
  22.6 9.6 %all-to-all-done.mixed_ref = bf16[8,66,384]{2,1,0:T(8,128)(2,1)S(1)} async-done(((bf16[8,66,384]{2,1,0:T(8,128)(2,1)}), bf16[8,66,384]{2,1,0:T(8,128)(2,1)S(1)}, u32[]{:S(2)}, u32[]{:S(2)}) %all-to-all-start) | async-done | bytes 405536 | tf_op jit(solution)/shard_map/all_to_all | solution.py:334
  32.1 1.5 %collective-permute-start.4 = (bf16[64,4096]{1,0:T(8,128)(2,1)}, bf16[64,4096]{1,0:T(8,128)(2,1)}, u32[]{:S(2)}, u32[]{:S(2)}) collective-permute-start(bf16[64,4096]{1,0:T(8,128)(2,1)} %constant_dynamic-slice_fusion.2), channel_id=1, source_target_pairs={{0,2},{1,5},{2,0},{3,7},{4,6},{5,1},{6,4},{7,3},{8,10},{9,13},{10,... | collective-permute-start | bytes 1572872 | tf_op jit(solution)/shard_map/ppermute | solution.py:385
  33.6 1.3 %picked.1 = bf16[8,64,384]{2,1,0:T(8,128)(2,1)} custom-call(s32[16]{0:T(128)S(1)} %copy-done.8, bf16[8,66,384]{2,1,0:T(8,128)(2,1)S(1)} %all-to-all-done.mixed_ref), custom_call_target="tpu_custom_call" | custom-call | tf_op jit(solution)/shard_map/picked/pallas_call | solution.py:187
  34.9 3.5 %all-to-all-start.1 = ((bf16[8,64,384]{2,1,0:T(8,128)(2,1)}), bf16[8,64,384]{2,1,0:T(8,128)(2,1)S(1)}, u32[]{:S(2)}, u32[]{:S(2)}) async-start(bf16[8,64,384]{2,1,0:T(8,128)(2,1)} %picked.1), calls=%async_computation.1 | async-start | bytes 786432 | tf_op jit(solution)/shard_map/all_to_all | solution.py:334
  38.4 0.4 collective-permute-start.5
  38.8 0.1 pad_add_fusion.place_ref
  38.9 1.0 %collective-permute-done.5.rest_2_ = bf16[3,256,128]{2,1,0:T(8,128)(2,1)S(1)} collective-permute-done((bf16[3,256,128]{2,1,0:T(8,128)(2,1)S(1)}, bf16[3,256,128]{2,1,0:T(8,128)(2,1)S(1)}, u32[]{:S(2)}, u32[]{:S(2)}) %collective-permute-start.5) | collective-permute-done | bytes 196640 | tf_op jit(solution)/shard_map/ppermute | solution.py:385
  39.9 3.1 %attention.1 = (bf16[256,512]{1,0:T(8,128)(2,1)}, bf16[4,256,256]{2,1,0:T(8,128)(2,1)S(1)}) custom-call(s32[2]{0:T(128)S(1)} %pad_add_fusion.place_ref, s32[4,4]{1,0:T(4,128)S(1)} %copy-done.7, bf16[256,512]{1,0:T(8,128)(2,1)S(1)} %copy-done.3, bf16[256,512]{1,0:T(8,128)(2,1)S(1)} %copy-done.4, bf16[256,512]{1,0:T(8,128)(2,1)S(1)} %copy-done.5, ...), custom_call_target="tpu_custom_call" | custom-call | tf_op jit(solution)/shard_map/attention/pallas_call | solution.py:116
  43.1 0.8 copy-done.2
  43.9 2.8 %all-to-all-done.1.side_ref = bf16[8,64,384]{2,1,0:T(8,128)(2,1)S(1)} async-done(((bf16[8,64,384]{2,1,0:T(8,128)(2,1)}), bf16[8,64,384]{2,1,0:T(8,128)(2,1)S(1)}, u32[]{:S(2)}, u32[]{:S(2)}) %all-to-all-start.1) | async-done | bytes 393248 | tf_op jit(solution)/shard_map/all_to_all | solution.py:334
  46.7 0.8 copy-done
  47.4 0.0 collective-permute-done.4.refs_4_
  47.4 0.0 collective-permute-done.refs_2_
  47.5 1.0 %collective-permute-start.11 = (bf16[128,4096]{1,0:T(8,128)(2,1)}, bf16[128,4096]{1,0:T(8,128)(2,1)}, u32[]{:S(2)}, u32[]{:S(2)}) collective-permute-start(bf16[128,4096]{1,0:T(8,128)(2,1)} %collective-permute-done.refs_2_), channel_id=1, source_target_pairs={{0,2},{1,5},{2,0},{3,7},{4,6},{5,1},{6,4},{7,3},{8,10},{9,13},{10,... | collective-permute-start | bytes 3145736 | tf_op jit(solution)/shard_map/ppermute | solution.py:385
  48.4 0.0 collective-permute-start.6
  48.4 0.5 collective-permute-start.7
  48.9 0.0 collective-permute-start.8
  48.9 1.0 %copy-done.1 = bf16[8,64,384]{2,1,0:T(8,128)(2,1)S(1)} copy-done((bf16[8,64,384]{2,1,0:T(8,128)(2,1)S(1)}, bf16[8,64,384]{2,1,0:T(8,128)(2,1)}, u32[]{:S(2)}) %copy-start.1) | copy-done | bytes 393240
  49.9 2.9 %weighted.1.weight_ref = bf16[768,1024]{1,0:T(8,128)(2,1)S(1)} custom-call(s32[1]{0:T(128)} %bitcast.11.own_ref, s32[16]{0:T(128)S(1)} %copy-done.8, bf16[8,66,384]{2,1,0:T(8,128)(2,1)S(1)} %all-to-all-done.mixed_ref, bf16[1,3,8,65,384]{4,3,2,1,0:T(8,128)(2,1)S(1)} %copy.20.hidden_ref, bf16[8,64,384]{2,1,0:T(8,128)(2,1)S(1)} %copy-done.1), custom_call_target="tpu_custom_call" | custom-call | tf_op jit(solution)/shard_map/weighted/pallas_call | solution.py:239
  52.8 9.7 %collective-permute-done.11.refs_8_ = bf16[128,4096]{1,0:T(8,128)(2,1)} collective-permute-done((bf16[128,4096]{1,0:T(8,128)(2,1)}, bf16[128,4096]{1,0:T(8,128)(2,1)}, u32[]{:S(2)}, u32[]{:S(2)}) %collective-permute-start.11) | collective-permute-done | bytes 1048608 | tf_op jit(solution)/shard_map/ppermute | solution.py:385
  62.6 0.0 collective-permute-start.12
  62.6 2.6 %all-to-all-start.2 = ((bf16[32,32,256]{2,1,0:T(8,128)(2,1)}), bf16[32,32,256]{2,1,0:T(8,128)(2,1)S(1)}, u32[]{:S(2)}, u32[]{:S(2)}) async-start(bf16[32,32,256]{2,1,0:T(8,128)(2,1)} %bitcast.15), calls=%async_computation.2 | async-start | bytes 1048576 | tf_op jit(solution)/shard_map/all_to_all | solution.py:154
  65.2 0.3 collective-permute-start.9
  65.5 0.0 collective-permute-done.8.refs_5_
  65.5 0.3 collective-permute-start.10
  65.8 0.0 collective-permute-done.6.refs_1_
  65.8 1.6 %collective-permute-done.9.refs_6_ = bf16[64,4096]{1,0:T(8,128)(2,1)S(1)} collective-permute-done((bf16[64,4096]{1,0:T(8,128)(2,1)}, bf16[64,4096]{1,0:T(8,128)(2,1)S(1)}, u32[]{:S(2)}, u32[]{:S(2)}) %collective-permute-start.9) | collective-permute-done | bytes 524320 | tf_op jit(solution)/shard_map/ppermute | solution.py:385
  67.4 0.7 collective-permute-done.10.refs_7_
  68.1 0.0 collective-permute-done.7.refs_3_
  68.1 0.0 collective-permute-done.12.refs_9_
  68.1 10.9 %tiles.1 = f32[2,384,4096]{2,1,0:T(8,128)} custom-call(s32[1]{0:T(128)} %bitcast.10.parity_ref, bf16[768,1024]{1,0:T(8,128)(2,1)S(1)} %weighted.1.weight_ref, bf16[128,4096]{1,0:T(8,128)(2,1)} %refs_0_.1, bf16[128,4096]{1,0:T(8,128)(2,1)} %collective-permute-done.6.refs_1_, bf16[128,4096]{1,0:T(8,128)(2,1)} %collective-permute-done.refs_2_, ...), custom_call_target="tpu_custom_call" | custom-call | tf_op jit(solution)/shard_map/tiles/pallas_call | solution.py:316
  79.0 1.7 %all-to-all-done.2 = bf16[32,32,256]{2,1,0:T(8,128)(2,1)S(1)} async-done(((bf16[32,32,256]{2,1,0:T(8,128)(2,1)}), bf16[32,32,256]{2,1,0:T(8,128)(2,1)S(1)}, u32[]{:S(2)}, u32[]{:S(2)}) %all-to-all-start.2) | async-done | bytes 524320 | tf_op jit(solution)/shard_map/all_to_all | solution.py:154
  80.7 0.7 sums.1
  (19 shorter events, 0.1 us)
Async XLA Ops:
  1.6 20.9 %collective-permute-start.3 = (bf16[256,128]{1,0:T(8,128)(2,1)S(1)}, bf16[256,128]{1,0:T(8,128)(2,1)S(1)}, u32[]{:S(2)}, u32[]{:S(2)}) collective-permute-start(bf16[256,128]{1,0:T(8,128)(2,1)S(1)} %get-tuple-element.38), channel_id=1, source_target_pairs={{0,24},{1,25},{2,26},{3,27},{4,28},{5,29},{6,30},{7,31}} | collective-permute-start | bytes 196616 | tf_op jit(solution)/shard_map/ppermute | solution.py:103
  8.5 14.0 %collective-permute-start.2 = (bf16[256,128]{1,0:T(8,128)(2,1)S(1)}, bf16[256,128]{1,0:T(8,128)(2,1)S(1)}, u32[]{:S(2)}, u32[]{:S(2)}) collective-permute-start(bf16[256,128]{1,0:T(8,128)(2,1)S(1)} %get-tuple-element.38), channel_id=1, source_target_pairs={{0,16},{8,24},{1,17},{9,25},{2,18},{10,26},{3,19},{11,27},{4,20},{... | collective-permute-start | bytes 196616 | tf_op jit(solution)/shard_map/ppermute | solution.py:103
  9.8 12.7 %collective-permute-start.1 = (bf16[256,128]{1,0:T(8,128)(2,1)S(1)}, bf16[256,128]{1,0:T(8,128)(2,1)S(1)}, u32[]{:S(2)}, u32[]{:S(2)}) collective-permute-start(bf16[256,128]{1,0:T(8,128)(2,1)S(1)} %get-tuple-element.38), channel_id=1, source_target_pairs={{0,8},{8,16},{16,24},{1,9},{9,17},{17,25},{2,10},{10,18},{18,26},{... | collective-permute-start | bytes 196616 | tf_op jit(solution)/shard_map/ppermute | solution.py:103
  12.3 35.1 %collective-permute-start = (bf16[128,4096]{1,0:T(8,128)(2,1)}, bf16[128,4096]{1,0:T(8,128)(2,1)}, u32[]{:S(2)}, u32[]{:S(2)}) collective-permute-start(bf16[128,4096]{1,0:T(8,128)(2,1)} %refs_0_.1), channel_id=1, source_target_pairs={{0,4},{1,3},{2,6},{3,1},{4,0},{5,7},{6,2},{7,5},{8,12},{9,11},{10,... | collective-permute-start | bytes 3145736 | tf_op jit(solution)/shard_map/ppermute | solution.py:385
  14.6 1.5 %copy-start.9 = (s32[128,8]{0,1:T(8,128)S(1)}, s32[128,8]{0,1:T(8,128)}, u32[]{:S(2)}) copy-start(s32[128,8]{0,1:T(8,128)} %param.19) | copy-start | bytes 12292
  16.9 16.7 %copy-start.8 = (s32[16]{0:T(128)S(1)}, s32[16]{0:T(128)}, u32[]{:S(2)}) copy-start(s32[16]{0:T(128)} %shadow_ref.3) | copy-start | bytes 196
  16.9 15.2 %all-to-all-start = ((bf16[8,66,384]{2,1,0:T(8,128)(2,1)}), bf16[8,66,384]{2,1,0:T(8,128)(2,1)S(1)}, u32[]{:S(2)}, u32[]{:S(2)}) async-start(bf16[8,66,384]{2,1,0:T(8,128)(2,1)} %fusion.1), calls=%async_computation | async-start | bytes 884736 | tf_op jit(solution)/shard_map/all_to_all | solution.py:334
  22.4 17.5 %copy-start.3 = (bf16[256,512]{1,0:T(8,128)(2,1)S(1)}, bf16[256,512]{1,0:T(8,128)(2,1)}, u32[]{:S(2)}) copy-start(bf16[256,512]{1,0:T(8,128)(2,1)} %query_ref.1) | copy-start | bytes 786436
  22.4 17.5 %copy-start.4 = (bf16[256,512]{1,0:T(8,128)(2,1)S(1)}, bf16[256,512]{1,0:T(8,128)(2,1)}, u32[]{:S(2)}) copy-start(bf16[256,512]{1,0:T(8,128)(2,1)} %grad_ref.1) | copy-start | bytes 786436
  22.4 17.5 %copy-start.5 = (bf16[256,512]{1,0:T(8,128)(2,1)S(1)}, bf16[256,512]{1,0:T(8,128)(2,1)}, u32[]{:S(2)}) copy-start(bf16[256,512]{1,0:T(8,128)(2,1)} %out_ref.1) | copy-start | bytes 786436
  22.4 17.5 %copy-start.6 = (f32[4,256]{1,0:T(4,128)S(1)}, f32[4,256]{1,0:T(4,128)}, u32[]{:S(2)}) copy-start(f32[4,256]{1,0:T(4,128)} %lse_ref.1) | copy-start | bytes 12292
  22.5 17.5 %copy-start.7 = (s32[4,4]{1,0:T(4,128)S(1)}, s32[4,4]{1,0:T(4,128)}, u32[]{:S(2)}) copy-start(s32[4,4]{1,0:T(4,128)} %mask_ref.1) | copy-start | bytes 196
  32.1 15.3 %collective-permute-start.4 = (bf16[64,4096]{1,0:T(8,128)(2,1)}, bf16[64,4096]{1,0:T(8,128)(2,1)}, u32[]{:S(2)}, u32[]{:S(2)}) collective-permute-start(bf16[64,4096]{1,0:T(8,128)(2,1)} %constant_dynamic-slice_fusion.2), channel_id=1, source_target_pairs={{0,2},{1,5},{2,0},{3,7},{4,6},{5,1},{6,4},{7,3},{8,10},{9,13},{10,... | collective-permute-start | bytes 1572872 | tf_op jit(solution)/shard_map/ppermute | solution.py:385
  34.9 11.7 %all-to-all-start.1 = ((bf16[8,64,384]{2,1,0:T(8,128)(2,1)}), bf16[8,64,384]{2,1,0:T(8,128)(2,1)S(1)}, u32[]{:S(2)}, u32[]{:S(2)}) async-start(bf16[8,64,384]{2,1,0:T(8,128)(2,1)} %picked.1), calls=%async_computation.1 | async-start | bytes 786432 | tf_op jit(solution)/shard_map/all_to_all | solution.py:334
  38.4 1.5 %collective-permute-start.5 = (bf16[3,256,128]{2,1,0:T(8,128)(2,1)S(1)}, bf16[3,256,128]{2,1,0:T(8,128)(2,1)S(1)}, u32[]{:S(2)}, u32[]{:S(2)}) collective-permute-start(bf16[3,256,128]{2,1,0:T(8,128)(2,1)S(1)} %pad_maximum_fusion.rest_1_), channel_id=1, source_target_pairs={{0,1},{1,0},{2,3},{3,2},{4,5},{5,4},{6,7},{7,6},{8,9},{9,8},{10,11... | collective-permute-start | bytes 589832 | tf_op jit(solution)/shard_map/ppermute | solution.py:385
  43.1 0.8 copy-start.2
  46.7 0.8 copy-start
  47.5 15.1 %collective-permute-start.11 = (bf16[128,4096]{1,0:T(8,128)(2,1)}, bf16[128,4096]{1,0:T(8,128)(2,1)}, u32[]{:S(2)}, u32[]{:S(2)}) collective-permute-start(bf16[128,4096]{1,0:T(8,128)(2,1)} %collective-permute-done.refs_2_), channel_id=1, source_target_pairs={{0,2},{1,5},{2,0},{3,7},{4,6},{5,1},{6,4},{7,3},{8,10},{9,13},{10,... | collective-permute-start | bytes 3145736 | tf_op jit(solution)/shard_map/ppermute | solution.py:385
  48.4 17.3 %collective-permute-start.6 = (bf16[128,4096]{1,0:T(8,128)(2,1)}, bf16[128,4096]{1,0:T(8,128)(2,1)}, u32[]{:S(2)}, u32[]{:S(2)}) collective-permute-start(bf16[128,4096]{1,0:T(8,128)(2,1)} %refs_0_.1), channel_id=1, source_target_pairs={{0,1},{1,0},{2,3},{3,2},{4,5},{5,4},{6,7},{7,6},{8,9},{9,8},{10,11... | collective-permute-start | bytes 3145736 | tf_op jit(solution)/shard_map/ppermute | solution.py:385
  48.4 19.7 %collective-permute-start.7 = (bf16[128,4096]{1,0:T(8,128)(2,1)}, bf16[128,4096]{1,0:T(8,128)(2,1)}, u32[]{:S(2)}, u32[]{:S(2)}) collective-permute-start(bf16[128,4096]{1,0:T(8,128)(2,1)} %collective-permute-done.refs_2_), channel_id=1, source_target_pairs={{0,1},{1,0},{2,3},{3,2},{4,5},{5,4},{6,7},{7,6},{8,9},{9,8},{10,11... | collective-permute-start | bytes 3145736 | tf_op jit(solution)/shard_map/ppermute | solution.py:385
  48.9 16.6 %collective-permute-start.8 = (bf16[64,4096]{1,0:T(8,128)(2,1)}, bf16[64,4096]{1,0:T(8,128)(2,1)}, u32[]{:S(2)}, u32[]{:S(2)}) collective-permute-start(bf16[64,4096]{1,0:T(8,128)(2,1)} %collective-permute-done.4.refs_4_), channel_id=1, source_target_pairs={{0,8},{8,0},{16,24},{24,16},{1,9},{9,1},{17,25},{25,17},{2,10},{10... | collective-permute-start | bytes 1572872 | tf_op jit(solution)/shard_map/ppermute | solution.py:394
  48.9 1.0 %copy-start.1 = (bf16[8,64,384]{2,1,0:T(8,128)(2,1)S(1)}, bf16[8,64,384]{2,1,0:T(8,128)(2,1)}, u32[]{:S(2)}) copy-start(bf16[8,64,384]{2,1,0:T(8,128)(2,1)} %copy-done) | copy-start | bytes 1179652
  62.6 5.6 %collective-permute-start.12 = (bf16[128,4096]{1,0:T(8,128)(2,1)}, bf16[128,4096]{1,0:T(8,128)(2,1)}, u32[]{:S(2)}, u32[]{:S(2)}) collective-permute-start(bf16[128,4096]{1,0:T(8,128)(2,1)} %collective-permute-done.11.refs_8_), channel_id=1, source_target_pairs={{0,1},{1,0},{2,3},{3,2},{4,5},{5,4},{6,7},{7,6},{8,9},{9,8},{10,11... | collective-permute-start | bytes 3145736 | tf_op jit(solution)/shard_map/ppermute | solution.py:385
  62.6 18.2 %all-to-all-start.2 = ((bf16[32,32,256]{2,1,0:T(8,128)(2,1)}), bf16[32,32,256]{2,1,0:T(8,128)(2,1)S(1)}, u32[]{:S(2)}, u32[]{:S(2)}) async-start(bf16[32,32,256]{2,1,0:T(8,128)(2,1)} %bitcast.15), calls=%async_computation.2 | async-start | bytes 1048576 | tf_op jit(solution)/shard_map/all_to_all | solution.py:154
  65.2 2.2 %collective-permute-start.9 = (bf16[64,4096]{1,0:T(8,128)(2,1)}, bf16[64,4096]{1,0:T(8,128)(2,1)S(1)}, u32[]{:S(2)}, u32[]{:S(2)}) collective-permute-start(bf16[64,4096]{1,0:T(8,128)(2,1)} %collective-permute-done.4.refs_4_), channel_id=1, source_target_pairs={{0,1},{1,0},{2,3},{3,2},{4,5},{5,4},{6,7},{7,6},{8,9},{9,8},{10,11... | collective-permute-start | bytes 1572872 | tf_op jit(solution)/shard_map/ppermute | solution.py:385
  65.5 2.6 %collective-permute-start.10 = (bf16[64,4096]{1,0:T(8,128)(2,1)}, bf16[64,4096]{1,0:T(8,128)(2,1)S(1)}, u32[]{:S(2)}, u32[]{:S(2)}) collective-permute-start(bf16[64,4096]{1,0:T(8,128)(2,1)} %collective-permute-done.8.refs_5_), channel_id=1, source_target_pairs={{0,1},{1,0},{2,3},{3,2},{4,5},{5,4},{6,7},{7,6},{8,9},{9,8},{10,11... | collective-permute-start | bytes 1572872 | tf_op jit(solution)/shard_map/ppermute | solution.py:385

commit v17 on v13

--- a/solution.py
+++ b/solution.py
@@ -281,10 +281,11 @@
         for copy in arriving[i + 2] if i + 2 < steps else []:
             copy.start()
         columns = slice(i * step, (i + 1) * step)
-        held_ref[:, columns] = jnp.dot(
-            weight_ref[...], gathered_ref[:, columns], preferred_element_type=jnp.float32
-        )
         for j in range(per_dev):
+            expert = slice(j * units, (j + 1) * units)
+            held_ref[expert, columns] = jnp.dot(
+                weight_ref[expert], gathered_ref[:, columns], preferred_element_type=jnp.float32
+            )
             leaving.append(
                 pltpu.make_async_copy(
                     held_ref.at[pl.ds(j * units, units), pl.ds(i * step, step)],

time: 78.7 us -> 78.7 us (level)
  no operation moved by 1% of the time
where the time goes in v17:
time: 78.7 us; the launch traced here: 78.3 us
  starting transfers between devices  29.7 us (38%)
  Pallas kernels  17.5 us (22%)
  waiting for transfers between devices  13.1 us (17%)
  blocking collectives  12 us (15%)
  local copies, waits for them, and re-layouts  4.26 us (5%)
  other arithmetic  0.87 us (1%)
  between operations  0.85 us (1%)
    all_to_all x1, blocking collectives, swapped(): return lax.all_to_all(value, 'exp', split_axis=0, concat_axis=0, tiled=True)  12 us
    pallas_call x1, Pallas kernels, tile_sums(): pl.pallas_call(functools.partial(tile_kernel, halves), out_shape=jax.Shap...  10.3 us
    ppermute x3, starting transfers between devices, key_blocks(): lax.ppermute(pair, 'ctx', [(c, c + step) for c in range(cycle - step)])  9.29 us
    all_to_all x1, starting transfers between devices, summed_terms(): lax.all_to_all(terms.reshape(cycle * owners, rows // owners, columns), ('...  6.62 us
    ppermute x8, starting transfers between devices, moved(): lax.ppermute(value, 'exp', [(e, e ^ steps[e % 2]) for e in range(owners)])  5.9 us
    ppermute x8, waiting for transfers between devices, moved(): lax.ppermute(value, 'exp', [(e, e ^ steps[e % 2]) for e in range(owners)])  5.66 us
    ppermute x3, waiting for transfers between devices, key_blocks(): lax.ppermute(pair, 'ctx', [(c, c + step) for c in range(cycle - step)])  5.14 us
    ppermute x1, starting transfers between devices, from_pair(): lax.ppermute(half, 'ctx', [(c, c ^ 1) for c in range(lax.axis_size('ctx'))])  4.24 us
  transfers between devices with their start and end apart: 14, of which 7 were waited for; matrix products, arithmetic and copies ran while one was open for 5% of the time, Pallas kernels for 22%

profile of v17, /device:TPU:0, one launch (start us, length us, event | category | flops | bytes accessed | tf_op | source)
XLA Modules:
  0.0 78.3 jit_solution(3850276769912365907)
XLA Ops:
  0.6 3.0 %collective-permute-start.4 = (bf16[128,4096]{1,0:T(8,128)(2,1)}, bf16[128,4096]{1,0:T(8,128)(2,1)}, u32[]{:S(2)}, u32[]{:S(2)}) collective-permute-start(bf16[128,4096]{1,0:T(8,128)(2,1)} %refs_0_.1), channel_id=1, source_target_pairs={{0,4},{1,3},{2,6},{3,1},{4,0},{5,7},{6,2},{7,5},{8,12},{9,11},{10,... | collective-permute-start | bytes 3145736 | tf_op jit(solution)/shard_map/ppermute | solution.py:378
  3.7 1.9 %constant_dynamic-slice_fusion = bf16[64,4096]{1,0:T(8,128)(2,1)} fusion(bf16[128,4096]{1,0:T(8,128)(2,1)} %refs_0_.1, s32[]{:T(128)S(6)} %select_n.28), kind=kLoop, calls=%fused_computation.7 | loop fusion | bytes 1048580 | tf_op jit(solution)/shard_map/dynamic_slice | solution.py:383
  5.6 1.5 %collective-permute-start.3 = (bf16[64,4096]{1,0:T(8,128)(2,1)}, bf16[64,4096]{1,0:T(8,128)(2,1)}, u32[]{:S(2)}, u32[]{:S(2)}) collective-permute-start(bf16[64,4096]{1,0:T(8,128)(2,1)} %constant_dynamic-slice_fusion), channel_id=1, source_target_pairs={{0,2},{1,5},{2,0},{3,7},{4,6},{5,1},{6,4},{7,3},{8,10},{9,13},{10,... | collective-permute-start | bytes 1572872 | tf_op jit(solution)/shard_map/ppermute | solution.py:378
  7.1 1.5 %copy.20.hidden_ref = bf16[1,3,8,65,384]{4,3,2,1,0:T(8,128)(2,1)S(1)} copy(bf16[1,3,8,65,384]{4,2,3,1,0:T(8,128)(2,1)} %param.23) | data formatting | bytes 2396160 | tf_op args[11]
  8.5 0.0 copy-start.7
  8.5 0.0 copy-start.8
  8.6 0.0 copy-done.10
  8.6 0.0 copy-start.6
  8.6 0.0 copy-done.9
  8.7 0.8 %fusion.1 = bf16[8,66,384]{2,1,0:T(8,128)(2,1)} fusion(bf16[8,2,128]{2,1,0:T(2,128)(2,1)S(1)} %bitcast.12, bf16[8,64,384]{2,1,0:T(8,128)(2,1)S(1)} %slice_bitcast_fusion), kind=kLoop, calls=%fused_computation.2 | loop fusion | flops 1216512 | bytes 802816 | tf_op jit(solution)/shard_map/concatenate | solution.py:348
  9.5 0.0 copy-start.5
  9.5 3.6 %all-to-all-start = ((bf16[8,66,384]{2,1,0:T(8,128)(2,1)}), bf16[8,66,384]{2,1,0:T(8,128)(2,1)S(1)}, u32[]{:S(2)}, u32[]{:S(2)}) async-start(bf16[8,66,384]{2,1,0:T(8,128)(2,1)} %fusion.1), calls=%async_computation | async-start | bytes 884736 | tf_op jit(solution)/shard_map/all_to_all | solution.py:327
  13.1 0.0 copy-done.7
  13.1 0.0 copy-done.8
  13.2 5.5 %collective-permute-start.2 = (bf16[256,256]{1,0:T(8,128)(2,1)S(1)}, bf16[256,256]{1,0:T(8,128)(2,1)S(1)}, u32[]{:S(2)}, u32[]{:S(2)}) collective-permute-start(bf16[256,256]{1,0:T(8,128)(2,1)S(1)} %pad_maximum_fusion.rest_0_), channel_id=1, source_target_pairs={{0,24},{1,25},{2,26},{3,27},{4,28},{5,29},{6,30},{7,31}} | collective-permute-start | bytes 393224 | tf_op jit(solution)/shard_map/ppermute | solution.py:98
  18.7 1.3 %collective-permute-start.1 = (bf16[256,256]{1,0:T(8,128)(2,1)S(1)}, bf16[256,256]{1,0:T(8,128)(2,1)S(1)}, u32[]{:S(2)}, u32[]{:S(2)}) collective-permute-start(bf16[256,256]{1,0:T(8,128)(2,1)S(1)} %pad_maximum_fusion.rest_0_), channel_id=1, source_target_pairs={{0,16},{8,24},{1,17},{9,25},{2,18},{10,26},{3,19},{11,27},{4,20},{... | collective-permute-start | bytes 393224 | tf_op jit(solution)/shard_map/ppermute | solution.py:98
  20.0 2.5 %collective-permute-start = (bf16[256,256]{1,0:T(8,128)(2,1)S(1)}, bf16[256,256]{1,0:T(8,128)(2,1)S(1)}, u32[]{:S(2)}, u32[]{:S(2)}) collective-permute-start(bf16[256,256]{1,0:T(8,128)(2,1)S(1)} %pad_maximum_fusion.rest_0_), channel_id=1, source_target_pairs={{0,8},{8,16},{16,24},{1,9},{9,17},{17,25},{2,10},{10,18},{18,26},{... | collective-permute-start | bytes 393224 | tf_op jit(solution)/shard_map/ppermute | solution.py:98
  22.5 0.1 collective-permute-done.2.rest_3_
  22.6 2.8 %collective-permute-done.1.rest_2_ = bf16[256,256]{1,0:T(8,128)(2,1)S(1)} collective-permute-done((bf16[256,256]{1,0:T(8,128)(2,1)S(1)}, bf16[256,256]{1,0:T(8,128)(2,1)S(1)}, u32[]{:S(2)}, u32[]{:S(2)}) %collective-permute-start.1) | collective-permute-done | bytes 131104 | tf_op jit(solution)/shard_map/ppermute | solution.py:98
  25.4 2.3 %collective-permute-done.rest_1_ = bf16[256,256]{1,0:T(8,128)(2,1)S(1)} collective-permute-done((bf16[256,256]{1,0:T(8,128)(2,1)S(1)}, bf16[256,256]{1,0:T(8,128)(2,1)S(1)}, u32[]{:S(2)}, u32[]{:S(2)}) %collective-permute-start) | collective-permute-done | bytes 131104 | tf_op jit(solution)/shard_map/ppermute | solution.py:98
  27.7 0.0 all-to-all-done.mixed_ref
  27.7 0.0 copy-done.6
  27.7 0.6 picked.1
  28.3 0.0 collective-permute-done.3.refs_4_
  28.3 12.0 %all_to_all.15.side_ref = bf16[8,64,384]{2,1,0:T(8,128)(2,1)S(1)} all-to-all(bf16[8,64,384]{2,1,0:T(8,128)(2,1)S(1)} %picked.1), channel_id=1, replica_groups=mesh['ctx'=4,'exp'=8] {'exp'}, dimensions={0} | all-to-all | bytes 786432 | tf_op jit(solution)/shard_map/all_to_all | solution.py:327
  40.3 0.0 collective-permute-done.4.refs_2_
  40.3 0.6 collective-permute-start.10
  40.8 0.0 collective-permute-start.5
  40.8 4.2 %collective-permute-start.7 = (bf16[64,4096]{1,0:T(8,128)(2,1)}, bf16[64,4096]{1,0:T(8,128)(2,1)}, u32[]{:S(2)}, u32[]{:S(2)}) collective-permute-start(bf16[64,4096]{1,0:T(8,128)(2,1)} %collective-permute-done.3.refs_4_), channel_id=1, source_target_pairs={{0,8},{8,0},{16,24},{24,16},{1,9},{9,1},{17,25},{25,17},{2,10},{10... | collective-permute-start | bytes 1572872 | tf_op jit(solution)/shard_map/ppermute | solution.py:387
  45.1 0.0 copy-done.1
  45.1 3.1 %attention.1 = (bf16[256,512]{1,0:T(8,128)(2,1)}, bf16[4,256,256]{2,1,0:T(8,128)(2,1)S(1)}) custom-call(s32[1]{0:T(128)} %bitcast.place_ref, s32[4,4]{1,0:T(4,128)S(1)} %copy-done.5, bf16[256,512]{1,0:T(8,128)(2,1)S(1)} %copy-done.1, bf16[256,512]{1,0:T(8,128)(2,1)S(1)} %copy-done.2, bf16[256,512]{1,0:T(8,128)(2,1)S(1)} %copy-done.3, ...), custom_call_target="tpu_custom_call" | custom-call | tf_op jit(solution)/shard_map/attention/pallas_call | solution.py:108
  48.2 0.8 %copy-done = bf16[4,256,256]{2,1,0:T(8,128)(2,1)} copy-done((bf16[4,256,256]{2,1,0:T(8,128)(2,1)}, bf16[4,256,256]{2,1,0:T(8,128)(2,1)S(1)}, u32[]{:S(2)}) %copy-start) | copy-done | bytes 524312
  49.0 0.2 collective-permute-start.6
  49.2 2.9 %weighted.1.weight_ref = bf16[768,1024]{1,0:T(8,128)(2,1)S(1)} custom-call(s32[1]{0:T(128)} %bitcast.7.own_ref, s32[16]{0:T(128)S(1)} %copy-done.6, bf16[8,66,384]{2,1,0:T(8,128)(2,1)S(1)} %all-to-all-done.mixed_ref, bf16[1,3,8,65,384]{4,3,2,1,0:T(8,128)(2,1)S(1)} %copy.20.hidden_ref, bf16[8,64,384]{2,1,0:T(8,128)(2,1)S(1)} %all_to_all.15.side_ref), custom_call_target="tpu_custom_call" | custom-call | tf_op jit(solution)/shard_map/weighted/pallas_call | solution.py:231
  52.1 3.3 %collective-permute-done.10.refs_8_ = bf16[128,4096]{1,0:T(8,128)(2,1)} collective-permute-done((bf16[128,4096]{1,0:T(8,128)(2,1)}, bf16[128,4096]{1,0:T(8,128)(2,1)}, u32[]{:S(2)}, u32[]{:S(2)}) %collective-permute-start.10) | collective-permute-done | bytes 1048608 | tf_op jit(solution)/shard_map/ppermute | solution.py:378
  55.4 0.0 collective-permute-start.11
  55.4 6.6 %all-to-all-start.1 = ((bf16[32,32,256]{2,1,0:T(8,128)(2,1)}), bf16[32,32,256]{2,1,0:T(8,128)(2,1)S(1)}, u32[]{:S(2)}, u32[]{:S(2)}) async-start(bf16[32,32,256]{2,1,0:T(8,128)(2,1)} %bitcast.11), calls=%async_computation.1 | async-start | bytes 1048576 | tf_op jit(solution)/shard_map/all_to_all | solution.py:146
  62.0 0.3 collective-permute-start.8
  62.3 0.0 collective-permute-done.7.refs_5_
  62.4 0.3 collective-permute-start.9
  62.6 0.0 collective-permute-done.5.refs_1_
  62.6 1.6 %collective-permute-done.8.refs_6_ = bf16[64,4096]{1,0:T(8,128)(2,1)S(1)} collective-permute-done((bf16[64,4096]{1,0:T(8,128)(2,1)}, bf16[64,4096]{1,0:T(8,128)(2,1)S(1)}, u32[]{:S(2)}, u32[]{:S(2)}) %collective-permute-start.8) | collective-permute-done | bytes 524320 | tf_op jit(solution)/shard_map/ppermute | solution.py:378
  64.2 0.7 collective-permute-done.9.refs_7_
  65.0 0.0 collective-permute-done.6.refs_3_
  65.0 0.0 collective-permute-done.11.refs_9_
  65.0 10.3 %tiles.1 = f32[2,384,4096]{2,1,0:T(8,128)} custom-call(s32[1]{0:T(128)} %bitcast.6.parity_ref, bf16[768,1024]{1,0:T(8,128)(2,1)S(1)} %weighted.1.weight_ref, bf16[128,4096]{1,0:T(8,128)(2,1)} %refs_0_.1, bf16[128,4096]{1,0:T(8,128)(2,1)} %collective-permute-done.5.refs_1_, bf16[128,4096]{1,0:T(8,128)(2,1)} %collective-permute-done.4.refs_2_, ...), custom_call_target="tpu_custom_call" | custom-call | tf_op jit(solution)/shard_map/tiles/pallas_call | solution.py:309
  75.3 2.3 %all-to-all-done.1 = bf16[32,32,256]{2,1,0:T(8,128)(2,1)S(1)} async-done(((bf16[32,32,256]{2,1,0:T(8,128)(2,1)}), bf16[32,32,256]{2,1,0:T(8,128)(2,1)S(1)}, u32[]{:S(2)}, u32[]{:S(2)}) %all-to-all-start.1) | async-done | bytes 524320 | tf_op jit(solution)/shard_map/all_to_all | solution.py:146
  77.6 0.7 sums.1
  (16 shorter events, 0.1 us)
Async XLA Ops:
  0.6 39.6 %collective-permute-start.4 = (bf16[128,4096]{1,0:T(8,128)(2,1)}, bf16[128,4096]{1,0:T(8,128)(2,1)}, u32[]{:S(2)}, u32[]{:S(2)}) collective-permute-start(bf16[128,4096]{1,0:T(8,128)(2,1)} %refs_0_.1), channel_id=1, source_target_pairs={{0,4},{1,3},{2,6},{3,1},{4,0},{5,7},{6,2},{7,5},{8,12},{9,11},{10,... | collective-permute-start | bytes 3145736 | tf_op jit(solution)/shard_map/ppermute | solution.py:378
  5.6 3.0 %copy-start.10 = (bf16[128,8]{0,1:T(8,128)(2,1)S(1)}, bf16[128,8]{0,1:T(8,128)(2,1)}, u32[]{:S(2)}) copy-start(bf16[128,8]{0,1:T(8,128)(2,1)} %param.20) | copy-start | bytes 6148
  5.6 3.1 %copy-start.9 = (s32[128,8]{0,1:T(8,128)S(1)}, s32[128,8]{0,1:T(8,128)}, u32[]{:S(2)}) copy-start(s32[128,8]{0,1:T(8,128)} %param.19) | copy-start | bytes 12292
  5.6 22.7 %collective-permute-start.3 = (bf16[64,4096]{1,0:T(8,128)(2,1)}, bf16[64,4096]{1,0:T(8,128)(2,1)}, u32[]{:S(2)}, u32[]{:S(2)}) collective-permute-start(bf16[64,4096]{1,0:T(8,128)(2,1)} %constant_dynamic-slice_fusion), channel_id=1, source_target_pairs={{0,2},{1,5},{2,0},{3,7},{4,6},{5,1},{6,4},{7,3},{8,10},{9,13},{10,... | collective-permute-start | bytes 1572872 | tf_op jit(solution)/shard_map/ppermute | solution.py:378
  8.5 4.6 %copy-start.7 = (bf16[256,256]{1,0:T(8,128)(2,1)S(1)}, bf16[256,256]{1,0:T(8,128)(2,1)}, u32[]{:S(2)}) copy-start(bf16[256,256]{1,0:T(8,128)(2,1)} %param.14) | copy-start | bytes 393220
  8.5 4.6 %copy-start.8 = (bf16[256,256]{1,0:T(8,128)(2,1)S(1)}, bf16[256,256]{1,0:T(8,128)(2,1)}, u32[]{:S(2)}) copy-start(bf16[256,256]{1,0:T(8,128)(2,1)} %param.13) | copy-start | bytes 393220
  8.6 19.1 %copy-start.6 = (s32[16]{0:T(128)S(1)}, s32[16]{0:T(128)}, u32[]{:S(2)}) copy-start(s32[16]{0:T(128)} %shadow_ref.3) | copy-start | bytes 196
  9.5 35.6 %copy-start.1 = (bf16[256,512]{1,0:T(8,128)(2,1)S(1)}, bf16[256,512]{1,0:T(8,128)(2,1)}, u32[]{:S(2)}) copy-start(bf16[256,512]{1,0:T(8,128)(2,1)} %query_ref.1) | copy-start | bytes 786436
  9.5 35.6 %copy-start.2 = (bf16[256,512]{1,0:T(8,128)(2,1)S(1)}, bf16[256,512]{1,0:T(8,128)(2,1)}, u32[]{:S(2)}) copy-start(bf16[256,512]{1,0:T(8,128)(2,1)} %grad_ref.1) | copy-start | bytes 786436
  9.5 35.6 %copy-start.3 = (bf16[256,512]{1,0:T(8,128)(2,1)S(1)}, bf16[256,512]{1,0:T(8,128)(2,1)}, u32[]{:S(2)}) copy-start(bf16[256,512]{1,0:T(8,128)(2,1)} %out_ref.1) | copy-start | bytes 786436
  9.5 35.6 %copy-start.4 = (f32[4,256]{1,0:T(4,128)S(1)}, f32[4,256]{1,0:T(4,128)}, u32[]{:S(2)}) copy-start(f32[4,256]{1,0:T(4,128)} %lse_ref.1) | copy-start | bytes 12292
  9.5 35.6 %copy-start.5 = (s32[4,4]{1,0:T(4,128)S(1)}, s32[4,4]{1,0:T(4,128)}, u32[]{:S(2)}) copy-start(s32[4,4]{1,0:T(4,128)} %mask_ref.1) | copy-start | bytes 196
  9.5 18.2 %all-to-all-start = ((bf16[8,66,384]{2,1,0:T(8,128)(2,1)}), bf16[8,66,384]{2,1,0:T(8,128)(2,1)S(1)}, u32[]{:S(2)}, u32[]{:S(2)}) async-start(bf16[8,66,384]{2,1,0:T(8,128)(2,1)} %fusion.1), calls=%async_computation | async-start | bytes 884736 | tf_op jit(solution)/shard_map/all_to_all | solution.py:327
  13.2 9.4 %collective-permute-start.2 = (bf16[256,256]{1,0:T(8,128)(2,1)S(1)}, bf16[256,256]{1,0:T(8,128)(2,1)S(1)}, u32[]{:S(2)}, u32[]{:S(2)}) collective-permute-start(bf16[256,256]{1,0:T(8,128)(2,1)S(1)} %pad_maximum_fusion.rest_0_), channel_id=1, source_target_pairs={{0,24},{1,25},{2,26},{3,27},{4,28},{5,29},{6,30},{7,31}} | collective-permute-start | bytes 393224 | tf_op jit(solution)/shard_map/ppermute | solution.py:98
  18.7 6.7 %collective-permute-start.1 = (bf16[256,256]{1,0:T(8,128)(2,1)S(1)}, bf16[256,256]{1,0:T(8,128)(2,1)S(1)}, u32[]{:S(2)}, u32[]{:S(2)}) collective-permute-start(bf16[256,256]{1,0:T(8,128)(2,1)S(1)} %pad_maximum_fusion.rest_0_), channel_id=1, source_target_pairs={{0,16},{8,24},{1,17},{9,25},{2,18},{10,26},{3,19},{11,27},{4,20},{... | collective-permute-start | bytes 393224 | tf_op jit(solution)/shard_map/ppermute | solution.py:98
  20.0 7.6 %collective-permute-start = (bf16[256,256]{1,0:T(8,128)(2,1)S(1)}, bf16[256,256]{1,0:T(8,128)(2,1)S(1)}, u32[]{:S(2)}, u32[]{:S(2)}) collective-permute-start(bf16[256,256]{1,0:T(8,128)(2,1)S(1)} %pad_maximum_fusion.rest_0_), channel_id=1, source_target_pairs={{0,8},{8,16},{16,24},{1,9},{9,17},{17,25},{2,10},{10,18},{18,26},{... | collective-permute-start | bytes 393224 | tf_op jit(solution)/shard_map/ppermute | solution.py:98
  40.3 15.1 %collective-permute-start.10 = (bf16[128,4096]{1,0:T(8,128)(2,1)}, bf16[128,4096]{1,0:T(8,128)(2,1)}, u32[]{:S(2)}, u32[]{:S(2)}) collective-permute-start(bf16[128,4096]{1,0:T(8,128)(2,1)} %collective-permute-done.4.refs_2_), channel_id=1, source_target_pairs={{0,2},{1,5},{2,0},{3,7},{4,6},{5,1},{6,4},{7,3},{8,10},{9,13},{10,... | collective-permute-start | bytes 3145736 | tf_op jit(solution)/shard_map/ppermute | solution.py:378
  40.8 21.8 %collective-permute-start.5 = (bf16[128,4096]{1,0:T(8,128)(2,1)}, bf16[128,4096]{1,0:T(8,128)(2,1)}, u32[]{:S(2)}, u32[]{:S(2)}) collective-permute-start(bf16[128,4096]{1,0:T(8,128)(2,1)} %refs_0_.1), channel_id=1, source_target_pairs={{0,1},{1,0},{2,3},{3,2},{4,5},{5,4},{6,7},{7,6},{8,9},{9,8},{10,11... | collective-permute-start | bytes 3145736 | tf_op jit(solution)/shard_map/ppermute | solution.py:378
  40.8 21.5 %collective-permute-start.7 = (bf16[64,4096]{1,0:T(8,128)(2,1)}, bf16[64,4096]{1,0:T(8,128)(2,1)}, u32[]{:S(2)}, u32[]{:S(2)}) collective-permute-start(bf16[64,4096]{1,0:T(8,128)(2,1)} %collective-permute-done.3.refs_4_), channel_id=1, source_target_pairs={{0,8},{8,0},{16,24},{24,16},{1,9},{9,1},{17,25},{25,17},{2,10},{10... | collective-permute-start | bytes 1572872 | tf_op jit(solution)/shard_map/ppermute | solution.py:387
  48.2 0.8 %copy-start = (bf16[4,256,256]{2,1,0:T(8,128)(2,1)}, bf16[4,256,256]{2,1,0:T(8,128)(2,1)S(1)}, u32[]{:S(2)}) copy-start(bf16[4,256,256]{2,1,0:T(8,128)(2,1)S(1)} %get-tuple-element.35) | copy-start | bytes 1572868
  49.0 16.0 %collective-permute-start.6 = (bf16[128,4096]{1,0:T(8,128)(2,1)}, bf16[128,4096]{1,0:T(8,128)(2,1)}, u32[]{:S(2)}, u32[]{:S(2)}) collective-permute-start(bf16[128,4096]{1,0:T(8,128)(2,1)} %collective-permute-done.4.refs_2_), channel_id=1, source_target_pairs={{0,1},{1,0},{2,3},{3,2},{4,5},{5,4},{6,7},{7,6},{8,9},{9,8},{10,11... | collective-permute-start | bytes 3145736 | tf_op jit(solution)/shard_map/ppermute | solution.py:378
  55.4 9.6 %collective-permute-start.11 = (bf16[128,4096]{1,0:T(8,128)(2,1)}, bf16[128,4096]{1,0:T(8,128)(2,1)}, u32[]{:S(2)}, u32[]{:S(2)}) collective-permute-start(bf16[128,4096]{1,0:T(8,128)(2,1)} %collective-permute-done.10.refs_8_), channel_id=1, source_target_pairs={{0,1},{1,0},{2,3},{3,2},{4,5},{5,4},{6,7},{7,6},{8,9},{9,8},{10,11... | collective-permute-start | bytes 3145736 | tf_op jit(solution)/shard_map/ppermute | solution.py:378
  55.4 22.2 %all-to-all-start.1 = ((bf16[32,32,256]{2,1,0:T(8,128)(2,1)}), bf16[32,32,256]{2,1,0:T(8,128)(2,1)S(1)}, u32[]{:S(2)}, u32[]{:S(2)}) async-start(bf16[32,32,256]{2,1,0:T(8,128)(2,1)} %bitcast.11), calls=%async_computation.1 | async-start | bytes 1048576 | tf_op jit(solution)/shard_map/all_to_all | solution.py:146
  62.0 2.2 %collective-permute-start.8 = (bf16[64,4096]{1,0:T(8,128)(2,1)}, bf16[64,4096]{1,0:T(8,128)(2,1)S(1)}, u32[]{:S(2)}, u32[]{:S(2)}) collective-permute-start(bf16[64,4096]{1,0:T(8,128)(2,1)} %collective-permute-done.3.refs_4_), channel_id=1, source_target_pairs={{0,1},{1,0},{2,3},{3,2},{4,5},{5,4},{6,7},{7,6},{8,9},{9,8},{10,11... | collective-permute-start | bytes 1572872 | tf_op jit(solution)/shard_map/ppermute | solution.py:378
  62.4 2.6 %collective-permute-start.9 = (bf16[64,4096]{1,0:T(8,128)(2,1)}, bf16[64,4096]{1,0:T(8,128)(2,1)S(1)}, u32[]{:S(2)}, u32[]{:S(2)}) collective-permute-start(bf16[64,4096]{1,0:T(8,128)(2,1)} %collective-permute-done.7.refs_5_), channel_id=1, source_target_pairs={{0,1},{1,0},{2,3},{3,2},{4,5},{5,4},{6,7},{7,6},{8,9},{9,8},{10,11... | collective-permute-start | bytes 1572872 | tf_op jit(solution)/shard_map/ppermute | solution.py:378
